TPU v7x, 512 devices: a whole 4x4x16 slice. The times are simulated.
512 devices in a mesh: seq: 4 (over y), exp: 128 (over z, x, core).
Axes of the slice: x: 4, y: 4, z: 16, core: 2. Of those that a mesh axis runs over, the one named last changes fastest.
Arguments:
- states: bfloat16 [65536, 2048], P(('seq', 'exp')), may hold values from -6 to 6
- queries: bfloat16 [65536, 2048], P(('seq', 'exp')), may hold values from -36 to 36
- mem_keys: bfloat16 [256, 2048], P('seq'), may hold values from -4.1 to 4.1
- mem_values: bfloat16 [256, 2048], P('seq'), may hold values from -6 to 6
- expert_ids: int32 [65536], P(('seq', 'exp')), may hold values from 0 to 127, as said below
- send_counts: int32 [512, 4], P(('seq', 'exp')), may hold values from 0 to 2, as said below
- w_in: bfloat16 [4, 10240, 2048], P('seq', 'exp'), may hold values from -0.125 to 0.125
- w_out: bfloat16 [4, 10240, 2048], P('seq', 'exp'), may hold values from -0.125 to 0.125
- upstream: bfloat16 [65536, 2048], P(('seq', 'exp')), may hold values from -6 to 6
Outputs:
- grad_states: bfloat16 [65536, 2048], P(('seq', 'exp'))
- grad_queries: bfloat16 [65536, 2048], P(('seq', 'exp'))
- grad_keys: bfloat16 [256, 2048], P('seq')
- grad_values: bfloat16 [256, 2048], P('seq')
- grad_w_in: bfloat16 [4, 10240, 2048], P('seq', 'exp')
- grad_w_out: bfloat16 [4, 10240, 2048], P('seq', 'exp')
Inputs may be any that keep to these rules, and one draw needn't show every extreme that they name: `expert_ids`: for each window expert (0 to 3) the tokens of one device name it at most 2 times, and the tokens of the 4 devices with one index of exp name it at most 2 times together; in every such group some window expert is named 2 times by one device. send_counts[b, e] is the number of tokens of device block b whose expert is window expert e.
All inputs are finite; a program needn't handle non-finite values.
Results may differ from a plain program's by a relative error of at most 0.0063.
Values may be sent and summed in bfloat16 or wider, within the bound.
No kernel may reach another device: no remote copies, remote signals or barrier semaphores. Data moves between devices by JAX's collectives and lax.ppermute only.
A program may use at most 64 MiB of HBM per device.

v0:
```python
import jax
import jax.numpy as jnp
from jax import lax
from jax.sharding import PartitionSpec as P

HEAD = 64
CAP = 2
GCAP = 2


def contract(left, right, left_dim, right_dim):
    return lax.dot_general(
        left, right, (((left_dim,), (right_dim,)), ((), ())), preferred_element_type=jnp.float32
    )


def per_device(
    states, queries, mem_keys, mem_values, expert_ids, send_counts, w_in, w_out, upstream
):
    score_scale = HEAD ** (-0.5)
    row_count = states.shape[0]
    hidden_width = states.shape[1]
    head_count = hidden_width // HEAD
    window = lax.axis_size("seq")
    all_keys, all_values = (
        lax.all_gather(mem_keys, "seq", axis=0, tiled=True),
        lax.all_gather(mem_values, "seq", axis=0, tiled=True),
    )
    mem_count = all_keys.shape[0]
    key_per_head = all_keys.reshape(mem_count, head_count, HEAD)
    value_per_head = all_values.reshape(mem_count, head_count, HEAD)
    heads_of_query = queries.reshape(row_count, head_count, HEAD)
    attention_scores = (
        jnp.einsum("zyk,cyk->yzc", heads_of_query, key_per_head, preferred_element_type=jnp.float32)
        * score_scale
    )
    probs = jax.nn.softmax(attention_scores, axis=-1)
    broadcast_probabilities = probs.astype(jnp.bfloat16)
    attended_values = jnp.einsum(
        "fae,efb->afb", broadcast_probabilities, value_per_head, preferred_element_type=jnp.float32
    )
    mixed = (states.astype(jnp.float32) + attended_values.reshape(row_count, hidden_width)).astype(
        jnp.bfloat16
    )
    experts_here = jnp.arange(window, dtype=jnp.int32)
    onehot = (expert_ids[:, None] == experts_here[None, :]).astype(jnp.int32)
    rank = jnp.sum((jnp.cumsum(onehot, axis=0) - 1) * onehot, axis=1)
    limit = jnp.sum(onehot * send_counts, axis=1)
    slot = jnp.where(rank < limit, expert_ids * CAP + rank, -1)
    place = (jnp.arange(window * CAP, dtype=jnp.int32)[:, None] == slot[None, :]).astype(
        jnp.bfloat16
    )
    send_rows = jnp.dot(place, mixed, preferred_element_type=jnp.float32).astype(jnp.bfloat16)
    send_grads = jnp.dot(place, upstream, preferred_element_type=jnp.float32).astype(jnp.bfloat16)
    got_rows, got_grads, got_counts = (
        lax.all_to_all(send_rows, "seq", split_axis=0, concat_axis=0, tiled=True),
        lax.all_to_all(send_grads, "seq", split_axis=0, concat_axis=0, tiled=True),
        lax.all_to_all(
            send_counts.reshape(window, 1), "seq", split_axis=0, concat_axis=0, tiled=True
        ),
    )
    counts = got_counts[:, 0]
    offsets = jnp.cumsum(counts).astype(jnp.int32) - counts
    source = jnp.arange(window * CAP, dtype=jnp.int32)
    anchor = (source // CAP)[:, None] == experts_here[None, :]
    order = source % CAP
    source_offset = jnp.sum(anchor.astype(jnp.int32) * offsets[None, :], axis=1)
    source_count = jnp.sum(anchor.astype(jnp.int32) * counts[None, :], axis=1)
    target = source_offset + order
    target = jnp.where((order < source_count) & (target < GCAP), target, -1)
    pack = (jnp.arange(GCAP, dtype=jnp.int32)[:, None] == target[None, :]).astype(jnp.bfloat16)
    rows_here = jnp.dot(pack, got_rows, preferred_element_type=jnp.float32).astype(jnp.bfloat16)
    grads_here = jnp.dot(pack, got_grads, preferred_element_type=jnp.float32).astype(jnp.bfloat16)
    all_rows, all_grads = (
        lax.all_gather(rows_here, "exp", axis=0, tiled=True),
        lax.all_gather(grads_here, "exp", axis=0, tiled=True),
    )
    weight_in = w_in[0]
    weight_out = w_out[0]
    pre = contract(all_rows, weight_in, 1, 1)
    act, pullback = jax.vjp(jax.nn.gelu, pre)
    act_b = act.astype(jnp.bfloat16)
    d_act = contract(all_grads, weight_out, 1, 1)
    d_pre = pullback(d_act)[0].astype(jnp.bfloat16)
    grad_in = contract(d_pre, all_rows, 0, 0).astype(jnp.bfloat16)
    grad_out = contract(act_b, all_grads, 0, 0).astype(jnp.bfloat16)
    total = lax.psum(contract(d_pre, weight_in, 1, 0), "exp")
    mine = lax.dynamic_slice_in_dim(total, lax.axis_index("exp") * GCAP, GCAP, 0)
    mine_b = mine.astype(jnp.bfloat16)
    back = contract(pack, mine_b, 0, 0).astype(jnp.bfloat16)
    returned = lax.all_to_all(back, "seq", split_axis=0, concat_axis=0, tiled=True)
    moe_grad = contract(place, returned, 0, 0)
    grad_states = (upstream.astype(jnp.float32) + moe_grad).astype(jnp.bfloat16)
    head_gradients = grad_states.reshape(row_count, head_count, HEAD)
    probability_gradient = jnp.einsum(
        "zyk,cyk->yzc", head_gradients, value_per_head, preferred_element_type=jnp.float32
    )
    centre = jnp.sum(probs * probability_gradient, axis=-1, keepdims=True)
    score_gradient = (probs * (probability_gradient - centre) * score_scale).astype(jnp.bfloat16)
    grad_queries = jnp.einsum(
        "fae,efb->afb", score_gradient, key_per_head, preferred_element_type=jnp.float32
    )
    grad_queries = grad_queries.reshape(row_count, hidden_width).astype(jnp.bfloat16)
    key_portion = jnp.einsum(
        "vro,rvx->ovx", score_gradient, heads_of_query, preferred_element_type=jnp.float32
    )
    value_portion = jnp.einsum(
        "vro,rvx->ovx", broadcast_probabilities, head_gradients, preferred_element_type=jnp.float32
    )
    key_portion = key_portion.reshape(mem_count, hidden_width)
    value_portion = value_portion.reshape(mem_count, hidden_width)
    own_rows = mem_keys.shape[0]
    key_total, value_total = lax.psum((key_portion, value_portion), ("seq", "exp"))
    start = lax.axis_index("seq") * own_rows
    key_total = lax.dynamic_slice_in_dim(key_total, start, own_rows, 0)
    value_total = lax.dynamic_slice_in_dim(value_total, start, own_rows, 0)
    return (
        grad_states,
        grad_queries,
        key_total.astype(jnp.bfloat16),
        value_total.astype(jnp.bfloat16),
        grad_in[None],
        grad_out[None],
    )


def solution(mesh):
    placed = (
        P(("seq", "exp"), None),
        P(("seq", "exp"), None),
        P("seq", None),
        P("seq", None),
        P(("seq", "exp")),
        P(("seq", "exp"), None),
        P("seq", "exp", None),
        P("seq", "exp", None),
        P(("seq", "exp"), None),
    )
    return jax.shard_map(
        per_device,
        mesh=mesh,
        in_specs=placed,
        out_specs=(
            P(("seq", "exp"), None),
            P(("seq", "exp"), None),
            P("seq", None),
            P("seq", None),
            P("seq", "exp", None),
            P("seq", "exp", None),
        ),
        check_vma=False,
    )
```

profile of v0, /device:TPU:1, one launch (start us, length us, event | category | flops | bytes accessed | tf_op | source)
XLA Modules:
  0.0 1132.0 jit_solution(5430175312385256259)
XLA Ops:
  7.2 0.0 copy-start
  7.2 0.0 all-gather.9.cloned.1.call-start
  7.2 0.7 all-gather.9.cloned.1.call-update
  7.9 1.3 copy.51
  9.2 5.0 all-to-all-start
  14.2 0.7 all-gather.7.cloned.1.call-update
  15.0 0.7 fusion.46
  15.7 0.2 reduce_window_sum.18
  15.9 0.8 select_reduce_fusion
  16.7 0.7 compare_select_fusion
  17.4 1.2 convolution_convert_fusion.4
  18.6 0.7 all_to_all.32
  19.3 0.0 all-to-all-done
  19.3 4.2 all-to-all-start.1
  23.5 0.0 all-gather.11.cloned.1.call-start
  23.5 0.2 reduce
  23.7 0.2 reduce-window.8
  23.9 0.1 select_reduce_fusion.2
  24.0 3.8 all-to-all-done.1
  27.9 0.7 fusion.17
  28.6 0.0 all-gather.11.cloned.1.call-update
  28.6 0.0 all-gather.13.cloned.1.call-start
  28.7 1.3 copy.52
  30.0 0.0 copy-start.6
  30.0 16.2 %all-gather.9.cloned.1.call-done = bf16[256,2048]{1,0:T(8,128)(2,1)} async-done(((bf16[64,2048]{1,0:T(8,128)(2,1)}), bf16[256,2048]{1,0:T(8,128)(2,1)}) %all-gather.9.cloned.1.call-update) | async-done | bytes 1048592 | tf_op jit(solution)/shard_map/all_gather | solution.py:27
  46.2 1.5 copy.54
  47.7 0.0 copy-start.1
  47.7 32.7 %all-gather.7.cloned.1.call-done = bf16[256,2048]{1,0:T(8,128)(2,1)} async-done(((bf16[64,2048]{1,0:T(8,128)(2,1)}), bf16[256,2048]{1,0:T(8,128)(2,1)}) %all-gather.7.cloned.1.call-update) | async-done | bytes 1048592 | tf_op jit(solution)/shard_map/all_gather | solution.py:26
  80.4 1.5 copy.53
  81.9 3.2 fusion.67
  85.1 2.8 fusion.27
  87.9 0.3 copy.55
  88.3 0.0 copy-start.8
  88.3 1.3 convolution_convert_fusion.3
  89.6 7.2 all_to_all.45
  96.8 0.7 fusion.18
  97.6 0.0 all-gather.13.cloned.1.call-update
  97.6 118.8 %all-gather.11.cloned.1.call-done = bf16[128,2,2048]{2,1,0:T(2,128)(2,1)} async-done(((bf16[1,2,2048]{2,1,0:T(2,128)(2,1)}), bf16[128,2,2048]{2,1,0:T(2,128)(2,1)}) %all-gather.11.cloned.1.call-update) | async-done | bytes 1048592 | tf_op jit(solution)/shard_map/all_gather | solution.py:76
  216.4 1.5 reshape.126
  217.9 128.3 %all-gather.13.cloned.1.call-done = bf16[128,2,2048]{2,1,0:T(2,128)(2,1)} async-done(((bf16[1,2,2048]{2,1,0:T(2,128)(2,1)}), bf16[128,2,2048]{2,1,0:T(2,128)(2,1)}) %all-gather.13.cloned.1.call-update) | async-done | bytes 1048592 | tf_op jit(solution)/shard_map/all_gather | solution.py:75
  346.2 1.5 reshape.128
  347.6 0.4 fusion.31
  348.1 1.0 fusion.16
  349.1 0.5 fusion.43
  349.6 0.5 fusion.29
  350.1 507.2 %all-reduce.3 = bf16[256,2048]{1,0:T(8,128)(2,1)} all-reduce(f32[256,2048]{1,0:T(8,128)S(1)} %fusion.29), channel_id=1, replica_groups=mesh['seq'=4,'exp'=128] {'exp'}, use_global_device_ids=true, to_apply=%region_8.9 | all-reduce | flops 524288 | bytes 3145728 | tf_op jit(solution)/shard_map/psum | solution.py:87
  857.3 1.0 convolution_convert_fusion.2
  858.3 0.7 all_to_all.38
  859.0 4.0 all-to-all-start.3
  863.0 1.0 fusion.15
  864.0 3.3 all-to-all-done.3
  867.3 1.4 fusion.14
  868.7 0.0 copy-start.5
  868.7 0.3 copy.56
  869.0 2.7 fusion.68
  871.7 27.7 %fusion.22 = bf16[32,128,64]{1,2,0:T(8,128)(2,1)S(1)} fusion(bf16[256,32,64]{0,2,1:T(8,128)(2,1)S(1)} %bitcast.62, f32[32,128,256]{2,1,0:T(8,128)} %fusion.68, f32[32,128,256]{2,1,0:T(8,128)} %get-tuple-element.43, f32[32,128]{1,0:T(8,128)S(1)} %get-tuple-element.42), kind=kOutput, calls=%fused_computation.27 | convolution fusion | flops 141824256 | bytes 9977856 | tf_op jit(solution)/shard_map/fae,efb->afb/dot_general | solution.py:100
  899.5 0.0 copy-done.5
  899.5 28.8 %fusion.9 = f32[32,256,64]{1,2,0:T(8,128)} fusion(bf16[128,32,64]{0,2,1:T(8,128)(2,1)S(1)} %bitcast.66, f32[32,128,256]{2,1,0:T(8,128)} %fusion.68, f32[32,128,256]{2,1,0:T(8,128)} %get-tuple-element.43, f32[32,128]{1,0:T(8,128)S(1)} %get-tuple-element.42), kind=kOutput, calls=%fused_computation.9 | convolution fusion | flops 141562112 | bytes 11026432 | tf_op jit(solution)/shard_map/vro,rvx->ovx/dot_general | solution.py:104
  928.3 4.4 fusion.25
  932.6 1.0 copy.59
  933.6 1.9 copy.57
  935.6 3.0 copy.58
  938.5 185.1 %all-reduce.4 = (bf16[256,2048]{1,0:T(8,128)(2,1)S(1)}, bf16[256,2048]{1,0:T(8,128)(2,1)}) all-reduce(f32[256,2048]{1,0:T(8,128)S(1)} %copy.57, f32[256,2048]{1,0:T(8,128)} %copy.58), channel_id=1, replica_groups=mesh['seq'=4,'exp'=128] {'seq','exp'}, use_global_device_ids=true, to_apply=%region_10.11 | all-reduce | flops 1048576 | bytes 6291456 | tf_op jit(solution)/shard_map/psum | solution.py:113
  1123.6 1.8 dynamic-slice_convert_fusion
  (20 shorter events, 0.1 us)
Async XLA Ops:
  7.2 340.5 %copy-start = (bf16[1,80,2048]{2,1,0:T(8,128)(2,1)S(1)}, bf16[1,80,2048]{2,1,0:T(8,128)(2,1)}, u32[]{:S(2)}) copy-start(bf16[1,80,2048]{2,1,0:T(8,128)(2,1)} %param.15) | copy-start | bytes 983044
  7.2 39.0 %all-gather.9.cloned.1.call-start = ((), (), s32[]{:S(2)}) async-start(), calls=%async_computation.5 | async-start | bytes 1310720 | tf_op jit(solution)/shard_map/all_gather | solution.py:27
  9.2 10.1 all-to-all-start
  14.2 66.2 %all-gather.7.cloned.1.call-start = ((), (), s32[]{:S(2)}) async-start(), calls=%async_computation.4 | async-start | bytes 1310720 | tf_op jit(solution)/shard_map/all_gather | solution.py:26
  19.3 8.5 all-to-all-start.1
  23.5 192.9 %all-gather.11.cloned.1.call-start = ((), (), s32[]{:S(2)}) async-start(), calls=%async_computation.6 | async-start | bytes 1056768 | tf_op jit(solution)/shard_map/all_gather | solution.py:76
  28.6 317.6 %all-gather.13.cloned.1.call-start = ((), (), s32[]{:S(2)}) async-start(), calls=%async_computation.7 | async-start | bytes 1056768 | tf_op jit(solution)/shard_map/all_gather | solution.py:75
  30.0 55.1 %copy-start.6 = (bf16[128,2048]{0,1:T(8,128)(2,1)}, bf16[128,2048]{0,1:T(8,128)(2,1)S(1)}, u32[]{:S(2)}) copy-start(bf16[128,2048]{0,1:T(8,128)(2,1)S(1)} %copy.52) | copy-start | bytes 1572868
  47.7 40.2 %copy-start.1 = (bf16[256,2048]{0,1:T(8,128)(2,1)}, bf16[256,2048]{0,1:T(8,128)(2,1)S(1)}, u32[]{:S(2)}) copy-start(bf16[256,2048]{0,1:T(8,128)(2,1)S(1)} %copy.54) | copy-start | bytes 3145732
  81.9 6.0 copy-start.3
  88.3 260.9 %copy-start.8 = (bf16[1,80,2048]{2,1,0:T(8,128)(2,1)S(1)}, bf16[1,80,2048]{2,1,0:T(8,128)(2,1)}, u32[]{:S(2)}) copy-start(bf16[1,80,2048]{2,1,0:T(8,128)(2,1)} %param.16) | copy-start | bytes 983044
  857.3 11.7 %copy-start.2 = (bf16[256,2048]{0,1:T(8,128)(2,1)S(1)}, bf16[256,2048]{0,1:T(8,128)(2,1)}, u32[]{:S(2)}) copy-start(bf16[256,2048]{0,1:T(8,128)(2,1)} %copy-done.1) | copy-start | bytes 3145732
  859.0 8.3 all-to-all-start.3
  864.0 7.7 copy-start.4
  868.7 30.8 %copy-start.5 = (bf16[128,2048]{1,0:T(8,128)(2,1)}, bf16[128,2048]{1,0:T(8,128)(2,1)S(1)}, u32[]{:S(2)}) copy-start(bf16[128,2048]{1,0:T(8,128)(2,1)S(1)} %fusion.14) | copy-start | bytes 1572868
  871.7 27.8 %copy-start.7 = (bf16[128,2048]{0,1:T(8,128)(2,1)S(1)}, bf16[128,2048]{0,1:T(8,128)(2,1)}, u32[]{:S(2)}) copy-start(bf16[128,2048]{0,1:T(8,128)(2,1)} %copy-done.6) | copy-start | bytes 1572868
Sparse Core Ops, SparseCore 0:
  10.1 36.0 all-gather.8
  48.3 32.0 all-gather.6
  84.0 132.3 all-gather.10
  219.8 126.3 all-gather.12
where the time goes:
time: 1130 us
  blocking collectives  700 us (62%)
  waiting for transfers between devices  305 us (27%)
  matrix products  79.4 us (7%)
  local copies, waits for them, and re-layouts  18.2 us (2%)
  between operations  14 us (1%)
  starting transfers between devices  13.3 us (1%)
    psum x1, blocking collectives, per_device(): total = lax.psum(contract(d_pre, weight_in, 1, 0), 'exp')  507 us
    psum x1, blocking collectives, per_device(): lax.psum((key_portion, value_portion), ('seq', 'exp'))  185 us
    all_gather x1, waiting for transfers between devices, per_device(): lax.all_gather(rows_here, 'exp', axis=0, tiled=True)  128 us
    all_gather x1, waiting for transfers between devices, per_device(): lax.all_gather(grads_here, 'exp', axis=0, tiled=True)  119 us
    all_gather x1, waiting for transfers between devices, per_device(): lax.all_gather(mem_keys, 'seq', axis=0, tiled=True)  32.7 us
    dot_general x1, matrix products, per_device(): jnp.einsum('vro,rvx->ovx', score_gradient, heads_of_query, preferred_elem...  28.8 us
    dot_general x1, matrix products, per_device(): jnp.einsum('fae,efb->afb', score_gradient, key_per_head, preferred_elemen...  27.7 us
  transfers between devices with their start and end apart: 7, of which 6 were waited for; matrix products, arithmetic and copies ran while one was open for 2% of the time, Pallas kernels for 0%

commit v1 on v0

v1 whole, which is shorter than its diff:
```python
import functools

import jax
import jax.numpy as jnp
from jax import lax
from jax.experimental import pallas as pl
from jax.experimental.pallas import tpu as pltpu
from jax.sharding import Mesh, PartitionSpec as P

HEAD = 64
GCAP = 2
SCALE = HEAD ** (-0.5)
BF, F32 = jnp.bfloat16, jnp.float32
DEVICES = ("y", "z", "x", "c")
PLANE = ("z", "x", "c")


def dot(left, right, left_dim=1, right_dim=0):
    return lax.dot_general(
        left, right, (((left_dim,), (right_dim,)), ((), ())), preferred_element_type=F32
    )


def exchange(values, axes):
    return lax.all_to_all(values, axes, split_axis=0, concat_axis=0, tiled=True)


def spread(values, axis):
    n = lax.axis_size(axis)
    copies = jnp.broadcast_to(values[None], (n,) + values.shape).reshape(
        (n * values.shape[0],) + values.shape[1:]
    )
    return exchange(copies, axis)


def collect(values, axes):
    n = lax.axis_size(axes)
    got = exchange(values, axes)
    return jnp.sum(got.reshape((n, -1) + got.shape[1:]).astype(F32), axis=0)


def other_core(values):
    return lax.ppermute(values, "c", [(0, 1), (1, 0)])


def attention_backward_kernel(
    core_ref, place_ref, rows_ref, up_ref, q_ref, k_ref, v_ref, gs_ref, gq_ref, keep_ref, send_ref
):
    first = core_ref[0] == 0
    moe = dot(place_ref[...], rows_ref[...])
    gs_ref[...] = (up_ref[...].astype(F32) + moe).astype(BF)
    tokens = q_ref.shape[0]
    low = lax.broadcasted_iota(jnp.int32, (tokens, 2 * HEAD), 1) < HEAD

    def both(block):
        none = jnp.zeros_like(block)
        return jnp.concatenate([jnp.where(low, block, none), jnp.where(low, none, block)], axis=0)

    for pair in range(q_ref.shape[1] // (2 * HEAD)):
        cols = slice(pair * 2 * HEAD, (pair + 1) * 2 * HEAD)
        queries = both(q_ref[:, cols] * BF(SCALE))
        grads = both(gs_ref[:, cols])
        keys, values = k_ref[:, cols], v_ref[:, cols]
        scores = dot(keys, queries, 1, 1)
        exps = jnp.exp(scores - jnp.max(scores, axis=0, keepdims=True))
        probs = exps * (1.0 / jnp.sum(exps, axis=0, keepdims=True))
        d_probs = dot(values, grads, 1, 1)
        centre = jnp.sum(probs * d_probs, axis=0, keepdims=True)
        d_scores = (probs * (d_probs - centre)).astype(BF)
        g_keys = dot(d_scores, queries)
        g_values = dot(probs.astype(BF), grads)
        keep_ref[:, cols] = jnp.where(first, g_keys, g_values).astype(BF)
        send_ref[:, cols] = jnp.where(first, g_values, g_keys).astype(BF)
        g_queries = dot(keys, d_scores, 0, 0)
        g_queries = jnp.concatenate([g_queries[:HEAD, :tokens], g_queries[HEAD:, tokens:]], axis=0)
        gq_ref[:, cols] = (g_queries.T * SCALE).astype(BF)


def attention_backward(core, place, rows, upstream, queries, keys, values):
    tokens, width = queries.shape
    mem = keys.shape[0]
    block = 512
    column = lambda n: pl.BlockSpec((n, block), lambda i: (0, i))
    return pl.pallas_call(
        attention_backward_kernel,
        grid=(width // block,),
        in_specs=[
            pl.BlockSpec(memory_space=pltpu.SMEM),
            pl.BlockSpec(place.shape, lambda i: (0, 0)),
            column(rows.shape[0]),
            column(tokens),
            column(tokens),
            column(mem),
            column(mem),
        ],
        out_specs=[column(tokens), column(tokens), column(mem), column(mem)],
        out_shape=[
            jax.ShapeDtypeStruct((tokens, width), BF),
            jax.ShapeDtypeStruct((tokens, width), BF),
            jax.ShapeDtypeStruct((mem, width), BF),
            jax.ShapeDtypeStruct((mem, width), BF),
        ],
        cost_estimate=pl.CostEstimate(
            flops=12 * tokens * mem * width, bytes_accessed=8 * mem * width, transcendentals=0
        ),
    )(core, place, rows, upstream, queries, keys, values)


def per_device(
    states, queries, mem_keys, mem_values, expert_ids, send_counts, w_in, w_out, upstream
):
    tokens, width = states.shape
    heads = width // HEAD
    window = lax.axis_size("y")
    slots = window * GCAP
    mine, core = lax.axis_index("y"), lax.axis_index("c")
    all_keys = lax.all_gather(mem_keys, "y", axis=0, tiled=True)
    all_values = lax.all_gather(mem_values, "y", axis=0, tiled=True)

    experts = jnp.arange(window, dtype=jnp.int32)
    onehot = (expert_ids[:, None] == experts[None, :]).astype(jnp.int32)
    rank = jnp.sum((jnp.cumsum(onehot, axis=0) - 1) * onehot, axis=1)
    limit = jnp.sum(onehot * send_counts, axis=1)
    slot = jnp.where(rank < limit, expert_ids * GCAP + rank, -1)
    slot_ids = jnp.arange(slots, dtype=jnp.int32)
    place = (slot_ids[:, None] == slot[None, :]).astype(BF)
    payload = [dot(place, part).astype(BF) for part in (queries, states, upstream)]
    flags = jnp.broadcast_to(jnp.repeat(send_counts[0], GCAP).astype(BF)[:, None], (slots, 128))
    group = lax.all_gather(jnp.concatenate(payload + [flags], axis=1), "y", axis=0, tiled=True)

    counts = group[:, 3 * width].reshape(window, slots)[:, ::GCAP].astype(jnp.int32)
    offsets = jnp.cumsum(counts, axis=0).astype(jnp.int32) - counts
    order = jnp.arange(GCAP, dtype=jnp.int32)
    position = offsets[:, :, None] + order
    kept = (order < counts[:, :, None]) & (position < GCAP)
    target = jnp.where(kept, experts[None, :, None] * GCAP + position, -1).reshape(-1)
    pack = (slot_ids[:, None] == target[None, :]).astype(BF)
    filled = jnp.sum(pack.astype(F32), axis=1)
    routed = dot(pack, group[:, : 3 * width]).astype(BF)
    own_target = lax.dynamic_slice_in_dim(target, mine * slots, slots, 0)
    own = (own_target[:, None] == slot_ids[None, :]).astype(BF)
    place_back = dot(place, own, 0, 0).astype(BF)

    in_head = jnp.arange(heads)[:, None] == (jnp.arange(width) // HEAD)[None, :]
    by_head = jnp.where(in_head[:, None, :], routed[None, :, :width], 0).reshape(-1, width)
    scores = dot(by_head, mem_keys, 1, 1) * SCALE
    top = jnp.max(scores, axis=1, keepdims=True)
    exps = jnp.exp(scores - top)
    total = jnp.sum(exps, axis=1)
    part = dot(exps.astype(BF), mem_values).reshape(heads, slots, width)
    part = jnp.sum(jnp.where(in_head[:, None, :], part, 0.0), axis=0)
    tops, totals = top.reshape(heads, slots).T, total.reshape(heads, slots).T
    pad = jnp.zeros((slots, 128 - 2 * heads), F32)
    parts = exchange(jnp.concatenate([part, tops, totals, pad], axis=1), "y")
    parts = parts.reshape(window, GCAP, -1)
    tops, totals = parts[:, :, width : width + heads], parts[:, :, width + heads : width + 2 * heads]
    share = jnp.exp(tops - jnp.max(tops, axis=0))
    share = share / jnp.sum(share * totals, axis=0)
    share = jnp.dot(
        share.reshape(-1, heads), in_head.astype(F32), precision=lax.Precision.HIGHEST
    ).reshape(window, GCAP, width)
    attended = jnp.sum(parts[:, :, :width] * share, axis=0)
    here = lax.dynamic_slice_in_dim(routed, mine * GCAP, GCAP, 0)
    here_filled = lax.dynamic_slice_in_dim(filled, mine * GCAP, GCAP, 0)
    row = (here[:, width : 2 * width].astype(F32) + attended) * here_filled[:, None]
    pair = jnp.concatenate([row.astype(BF), here[:, 2 * width :]], axis=1)

    near = spread(spread(pair, "z"), "x")
    far = other_core(near)
    weight_in, weight_out = w_in[0], w_out[0]

    def expert(block):
        rows, grads = block[:, :width], block[:, width:]
        pre = dot(rows, weight_in, 1, 1)
        act, pullback = jax.vjp(jax.nn.gelu, pre)
        d_pre = pullback(dot(grads, weight_out, 1, 1))[0].astype(BF)
        return d_pre, dot(d_pre, rows, 0, 0), dot(act.astype(BF), grads, 0, 0), dot(d_pre, weight_in)

    _, far_in, far_out, far_back = expert(far)
    _, near_in, near_out, near_back = expert(near)
    grad_in, grad_out = (near_in + far_in).astype(BF), (near_out + far_out).astype(BF)

    back = (near_back + other_core(far_back.astype(BF)).astype(F32)).astype(BF)
    back = collect(back, "x").astype(BF)
    back = collect(back, "z").astype(BF)
    returned = lax.all_gather(back, "y", axis=0, tiled=True)

    grad_states, grad_queries, keep, send = attention_backward(
        core.reshape(1).astype(jnp.int32),
        place_back,
        returned,
        upstream,
        queries,
        all_keys,
        all_values,
    )

    memory = (keep.astype(F32) + other_core(send).astype(F32)).astype(BF)
    own_rows = mem_keys.shape[0]
    memory = collect(memory, ("y", "x")).astype(BF)
    memory = collect(memory, "z").astype(BF)
    memory = spread(spread(memory, "z"), "x")
    across = other_core(memory)
    grad_keys = jnp.where(core == 0, memory, across)
    grad_values = jnp.where(core == 0, across, memory)
    return grad_states, grad_queries, grad_keys, grad_values, grad_in[None], grad_out[None]


def solution(mesh):
    chips = Mesh(mesh.devices.reshape(4, 16, 4, 2), DEVICES)
    rows, memory, weights = P(DEVICES, None), P("y", None), P("y", PLANE, None)
    return jax.shard_map(
        per_device,
        mesh=chips,
        in_specs=(rows, rows, memory, memory, P(DEVICES), rows, weights, weights, rows),
        out_specs=(rows, rows, memory, memory, weights, weights),
        check_vma=False,
    )
```

time: 1130 us -> 253 us (0.22)
  blocking collectives: 700 us -> 95.7 us
  waiting for transfers between devices: 305 us -> 55.4 us
  matrix products: 79.4 us -> 10.4 us
  starting transfers between devices: 13.3 us -> 51.2 us
    psum x2 -> x0, blocking collectives: 692 us -> none  [the longest x1 507 us: per_device(): total = lax.psum(contract(d_pre, weight_in, 1, 0), 'exp')]
    all_gather x4 -> x2, waiting for transfers between devices: 296 us -> 7.34 us  [the longest x1 7.34 us: per_device(): all_values = lax.all_gather(mem_values, 'y', axis=0, tiled=True)]
    all_to_all x1 -> x4, blocking collectives: 7.22 us -> 75.3 us  [exchange(): return lax.all_to_all(values, axes, split_axis=0, concat_axis=0, tiled=True)]
    dot_general x16 -> x18, matrix products: 76.2 us -> 10.4 us  [the longest x17 10.1 us: dot(): lax.dot_general(left, right, (((left_dim,), (right_dim,)), ((), ())), pre...]
    all_to_all x3 -> x5, waiting for transfers between devices: 7.11 us -> 43.3 us  [exchange(): return lax.all_to_all(values, axes, split_axis=0, concat_axis=0, tiled=True)]
    ppermute x0 -> x4, starting transfers between devices: none -> 25.3 us  [other_core(): return lax.ppermute(values, 'c', [(0, 1), (1, 0)])]
    all_gather x0 -> x2, blocking collectives: none -> 20.4 us  [the longest x1 11 us: per_device(): lax.all_gather(jnp.concatenate(payload + [flags], axis=1), 'y', axis=0, t...]
    all_to_all x3 -> x5, starting transfers between devices: 13.3 us -> 25.9 us  [exchange(): return lax.all_to_all(values, axes, split_axis=0, concat_axis=0, tiled=True)]
  transfers between devices with their start and end apart: 7 -> 11, of which waited for: 6 -> 9; matrix products, arithmetic and copies ran while one was open for 2% -> 4% of each run, Pallas kernels for 0% -> 0%
where the time goes in v1:
time: 253 us; the launch traced here: 252 us
  blocking collectives  95.7 us (38%)
  waiting for transfers between devices  55.4 us (22%)
  starting transfers between devices  51.2 us (20%)
  between operations  14.4 us (6%)
  matrix products  10.4 us (4%)
  Pallas kernels  8.91 us (4%)
  other arithmetic  8.33 us (3%)
  local copies, waits for them, and re-layouts  7.55 us (3%)
    all_to_all x4, blocking collectives, exchange(): return lax.all_to_all(values, axes, split_axis=0, concat_axis=0, tiled=True)  75.3 us
    all_to_all x5, waiting for transfers between devices, exchange(): return lax.all_to_all(values, axes, split_axis=0, concat_axis=0, tiled=True)  43.3 us
    all_to_all x5, starting transfers between devices, exchange(): return lax.all_to_all(values, axes, split_axis=0, concat_axis=0, tiled=True)  25.9 us
    ppermute x4, starting transfers between devices, other_core(): return lax.ppermute(values, 'c', [(0, 1), (1, 0)])  25.3 us
    all_gather x1, blocking collectives, per_device(): lax.all_gather(jnp.concatenate(payload + [flags], axis=1), 'y', axis=0, t...  11 us
    dot_general x17, matrix products, dot(): lax.dot_general(left, right, (((left_dim,), (right_dim,)), ((), ())), pre...  10.1 us
    all_gather x1, blocking collectives, per_device(): returned = lax.all_gather(back, 'y', axis=0, tiled=True)  9.38 us
    pallas_call x1, Pallas kernels, attention_backward(): pl.pallas_call(attention_backward_kernel, grid=(width // block,), in_spec...  8.91 us
  transfers between devices with their start and end apart: 11, of which 9 were waited for; matrix products, arithmetic and copies ran while one was open for 4% of the time, Pallas kernels for 0%

profile of v1, /device:TPU:1, one launch (start us, length us, event | category | flops | bytes accessed | tf_op | source)
XLA Modules:
  0.0 251.9 jit_solution(12829729458429954134)
XLA Ops:
  7.2 0.8 fusion.37
  8.0 0.7 bitcast_convert_fusion
  8.7 0.2 reduce_window_sum.22
  8.9 0.8 select_reduce_fusion
  9.7 0.7 compare_select_fusion
  10.4 1.2 convolution_convert_fusion.2
  11.6 0.2 convolution_convert_fusion.3
  11.8 0.2 convolution_convert_fusion.4
  12.2 11.0 %all_gather.12 = bf16[32,6272]{1,0:T(8,128)(2,1)S(1)} all-gather(bf16[8,6272]{1,0:T(8,128)(2,1)S(1)} %pad_maximum_fusion), channel_id=1, replica_groups=mesh['y'=4,'z'=16,'x'=4,'c'=2] {'y'}, dimensions={0}, use_global_device_ids=true | all-gather | bytes 501760 | tf_op jit(solution)/shard_map/all_gather | solution.py:129
  23.8 0.2 convolution_convert_fusion
  24.1 0.5 fusion.95
  24.7 0.2 copy-done.6
  24.9 0.5 fusion.5
  25.7 0.7 all_to_all.50
  26.4 3.5 %all-to-all-start = ((f32[4,2,2176]{2,1,0:T(2,128)}), f32[4,2,2176]{2,1,0:T(2,128)S(1)}, u32[]{:S(2)}, u32[]{:S(2)}) async-start(f32[4,2,2176]{2,1,0:T(2,128)} %all_to_all.50), calls=%async_computation | async-start | bytes 139264 | tf_op jit(solution)/shard_map/all_to_all | solution.py:25
  30.2 4.2 %all-to-all-done = f32[4,2,2176]{2,1,0:T(2,128)S(1)} async-done(((f32[4,2,2176]{2,1,0:T(2,128)}), f32[4,2,2176]{2,1,0:T(2,128)S(1)}, u32[]{:S(2)}, u32[]{:S(2)}) %all-to-all-start) | async-done | bytes 69664 | tf_op jit(solution)/shard_map/all_to_all | solution.py:25
  34.5 0.3 fusion.6
  34.9 0.2 broadcast_in_dim.69
  35.1 28.3 %all_to_all.75 = bf16[16,2,4096]{2,1,0:T(2,128)(2,1)S(1)} all-to-all(bf16[16,2,4096]{2,1,0:T(2,128)(2,1)S(1)} %broadcast_in_dim.69), channel_id=1, replica_groups=mesh['y'=4,'z'=16,'x'=4,'c'=2] {'z'}, dimensions={0} | all-to-all | bytes 524288 | tf_op jit(solution)/shard_map/all_to_all | solution.py:25
  63.7 13.7 %all_to_all.76 = bf16[4,32,4096]{2,1,0:T(8,128)(2,1)S(1)} all-to-all(bf16[4,32,4096]{2,1,0:T(8,128)(2,1)S(1)} %broadcast_in_dim.116), channel_id=1, replica_groups=mesh['y'=4,'z'=16,'x'=4,'c'=2] {'x'}, dimensions={0} | all-to-all | bytes 2097152 | tf_op jit(solution)/shard_map/all_to_all | solution.py:25
  77.4 12.0 %collective-permute-start = (bf16[128,4096]{1,0:T(8,128)(2,1)S(1)}, bf16[128,4096]{1,0:T(8,128)(2,1)S(1)}, u32[]{:S(2)}, u32[]{:S(2)}) collective-permute-start(bf16[128,4096]{1,0:T(8,128)(2,1)S(1)} %bitcast.63), channel_id=1, source_target_pairs={{0,1},{1,0},{2,3},{3,2},{4,5},{5,4},{6,7},{7,6},{8,9},{9,8},{10,11... | collective-permute-start | bytes 3145736 | tf_op jit(solution)/shard_map/ppermute | solution.py:43
  89.5 2.2 collective-permute-done
  91.7 0.3 fusion.13
  92.0 0.3 fusion.53
  92.3 1.1 convolution_convert_fusion.1
  93.4 2.3 collective-permute-start.1
  95.7 0.3 fusion.20
  96.0 1.3 fusion.46
  97.4 0.3 add_convert_fusion.1
  97.8 11.6 %all_to_all.77 = bf16[4,32,2048]{2,1,0:T(8,128)(2,1)S(1)} all-to-all(bf16[4,32,2048]{2,1,0:T(8,128)(2,1)S(1)} %bitcast.69), channel_id=1, replica_groups=mesh['y'=4,'z'=16,'x'=4,'c'=2] {'x'}, dimensions={0} | all-to-all | bytes 1048576 | tf_op jit(solution)/shard_map/all_to_all | solution.py:25
  109.5 0.8 all_to_all.57
  110.3 3.6 %all-to-all-start.4 = ((bf16[16,2,2048]{2,1,0:T(2,128)(2,1)}), bf16[16,2,2048]{2,1,0:T(2,128)(2,1)S(1)}, u32[]{:S(2)}, u32[]{:S(2)}) async-start(bf16[16,2,2048]{2,1,0:T(2,128)(2,1)} %all_to_all.57), calls=%async_computation.4 | async-start | bytes 262144 | tf_op jit(solution)/shard_map/all_to_all | solution.py:25
  113.9 0.3 convolution_convert_fusion.5
  114.2 0.7 copy.49.place_ref
  114.9 10.9 %all-to-all-done.4 = bf16[16,2,2048]{2,1,0:T(2,128)(2,1)S(1)} async-done(((bf16[16,2,2048]{2,1,0:T(2,128)(2,1)}), bf16[16,2,2048]{2,1,0:T(2,128)(2,1)S(1)}, u32[]{:S(2)}, u32[]{:S(2)}) %all-to-all-start.4) | async-done | bytes 131104 | tf_op jit(solution)/shard_map/all_to_all | solution.py:25
  125.8 0.1 reduce_sum.119
  125.9 9.4 %all-gather = bf16[4,2,2048]{2,1,0:T(2,128)(2,1)S(1)} all-gather(bf16[1,2,2048]{2,1,0:T(2,128)(2,1)S(1)} %bitcast.75), channel_id=1, replica_groups=mesh['y'=4,'z'=16,'x'=4,'c'=2] {'y'}, dimensions={0}, use_global_device_ids=true | all-gather | bytes 40960 | tf_op jit(solution)/shard_map/all_gather | solution.py:186
  135.3 0.6 reshape.186.rows_ref
  136.0 7.3 %all-gather.6.cloned.1.call-done.v_ref = bf16[256,2048]{1,0:T(8,128)(2,1)} async-done(((bf16[64,2048]{1,0:T(8,128)(2,1)}), bf16[256,2048]{1,0:T(8,128)(2,1)}) %all-gather.6.cloned.1.call-update) | async-done | bytes 1048592 | tf_op jit(solution)/shard_map/all_gather | solution.py:118
  143.3 8.9 %shard_map.136 = (bf16[128,2048]{1,0:T(8,128)(2,1)}, bf16[128,2048]{1,0:T(8,128)(2,1)}, bf16[256,2048]{1,0:T(8,128)(2,1)}, bf16[256,2048]{1,0:T(8,128)(2,1)}) custom-call(s32[1]{0:T(128)} %bitcast.core_ref, bf16[128,8]{1,0:T(8,128)(2,1)} %copy.49.place_ref, bf16[8,2048]{1,0:T(8,128)(2,1)} %reshape.186.rows_ref, bf16[128,2048]{1,0:T(8,128)(2,1)} %up_ref.1, ...), custom_call_target="tpu_custom_call" | custom-call | flops 805306368 | bytes 4194304 | tf_op jit(solution)/shard_map/pallas_call | solution.py:84
  152.2 3.5 %collective-permute-start.2 = (bf16[256,2048]{1,0:T(8,128)(2,1)}, bf16[256,2048]{1,0:T(8,128)(2,1)S(1)}, u32[]{:S(2)}, u32[]{:S(2)}) collective-permute-start(bf16[256,2048]{1,0:T(8,128)(2,1)} %get-tuple-element.13), channel_id=1, source_target_pairs={{0,1},{1,0},{2,3},{3,2},{4,5},{5,4},{6,7},{7,6},{8,9},{9,8},{10,11... | collective-permute-start | bytes 3145736 | tf_op jit(solution)/shard_map/ppermute | solution.py:43
  155.7 2.5 collective-permute-done.2
  158.2 1.6 add_convert_fusion
  159.8 21.7 %all_to_all.78 = bf16[16,16,2048]{2,1,0:T(8,128)(2,1)S(1)} all-to-all(bf16[16,16,2048]{2,1,0:T(8,128)(2,1)S(1)} %bitcast.68), channel_id=1, replica_groups=mesh['y'=4,'z'=16,'x'=4,'c'=2] {'y','x'}, dimensions={0} | all-to-all | bytes 2097152 | tf_op jit(solution)/shard_map/all_to_all | solution.py:25
  181.5 0.1 reduce_sum.120
  181.7 0.5 broadcast.181
  182.2 0.7 reduce.12
  182.9 0.7 reshape.189
  183.5 11.9 %all-to-all-start.6 = ((bf16[16,2,1024]{2,1,0:T(2,128)(2,1)}), bf16[16,2,1024]{2,1,0:T(2,128)(2,1)S(1)}, u32[]{:S(2)}, u32[]{:S(2)}) async-start(bf16[16,2,1024]{2,1,0:T(2,128)(2,1)} %reshape.189), calls=%async_computation.6 | async-start | bytes 131072 | tf_op jit(solution)/shard_map/all_to_all | solution.py:25
  195.5 11.6 %all-to-all-done.6 = bf16[16,2,1024]{2,1,0:T(2,128)(2,1)S(1)} async-done(((bf16[16,2,1024]{2,1,0:T(2,128)(2,1)}), bf16[16,2,1024]{2,1,0:T(2,128)(2,1)S(1)}, u32[]{:S(2)}, u32[]{:S(2)}) %all-to-all-start.6) | async-done | bytes 65568 | tf_op jit(solution)/shard_map/all_to_all | solution.py:25
  207.1 0.1 reduce_sum.121
  207.3 1.0 reduce.13
  208.3 0.7 reshape.191
  209.0 3.5 %all-to-all-start.7 = ((bf16[16,2,1024]{2,1,0:T(2,128)(2,1)}), bf16[16,2,1024]{2,1,0:T(2,128)(2,1)S(1)}, u32[]{:S(2)}, u32[]{:S(2)}) async-start(bf16[16,2,1024]{2,1,0:T(2,128)(2,1)} %reshape.191), calls=%async_computation.7 | async-start | bytes 131072 | tf_op jit(solution)/shard_map/all_to_all | solution.py:25
  212.5 0.2 fusion.22
  212.7 11.3 %all-to-all-done.7 = bf16[16,2,1024]{2,1,0:T(2,128)(2,1)S(1)} async-done(((bf16[16,2,1024]{2,1,0:T(2,128)(2,1)}), bf16[16,2,1024]{2,1,0:T(2,128)(2,1)S(1)}, u32[]{:S(2)}, u32[]{:S(2)}) %all-to-all-start.7) | async-done | bytes 65568 | tf_op jit(solution)/shard_map/all_to_all | solution.py:25
  224.2 0.7 broadcast_in_dim.118
  224.9 3.4 %all-to-all-start.8 = ((bf16[4,16,2048]{2,1,0:T(8,128)(2,1)}), bf16[4,16,2048]{2,1,0:T(8,128)(2,1)S(1)}, u32[]{:S(2)}, u32[]{:S(2)}) async-start(bf16[4,16,2048]{2,1,0:T(8,128)(2,1)} %broadcast_in_dim.118), calls=%async_computation.8 | async-start | bytes 524288 | tf_op jit(solution)/shard_map/all_to_all | solution.py:25
  228.3 0.2 fusion.18
  228.6 5.2 %all-to-all-done.8 = bf16[4,16,2048]{2,1,0:T(8,128)(2,1)S(1)} async-done(((bf16[4,16,2048]{2,1,0:T(8,128)(2,1)}), bf16[4,16,2048]{2,1,0:T(8,128)(2,1)S(1)}, u32[]{:S(2)}, u32[]{:S(2)}) %all-to-all-start.8) | async-done | bytes 262176 | tf_op jit(solution)/shard_map/all_to_all | solution.py:25
  233.8 7.5 %collective-permute-start.3 = (bf16[64,2048]{1,0:T(8,128)(2,1)S(1)}, bf16[64,2048]{1,0:T(8,128)(2,1)S(1)}, u32[]{:S(2)}, u32[]{:S(2)}) collective-permute-start(bf16[64,2048]{1,0:T(8,128)(2,1)S(1)} %bitcast.70), channel_id=1, source_target_pairs={{0,1},{1,0},{2,3},{3,2},{4,5},{5,4},{6,7},{7,6},{8,9},{9,8},{10,11... | collective-permute-start | bytes 786440 | tf_op jit(solution)/shard_map/ppermute | solution.py:43
  241.3 2.0 fusion.4
  243.3 1.0 fusion.3
  244.2 0.8 broadcast_select_fusion
  (70 shorter events, 2.6 us)
Async XLA Ops:
  7.2 4.4 %copy-start = (bf16[128,2048]{1,0:T(8,128)(2,1)S(1)}, bf16[128,2048]{1,0:T(8,128)(2,1)}, u32[]{:S(2)}) copy-start(bf16[128,2048]{1,0:T(8,128)(2,1)} %param.9) | copy-start | bytes 1572868
  7.2 4.6 %copy-start.1 = (bf16[128,2048]{1,0:T(8,128)(2,1)S(1)}, bf16[128,2048]{1,0:T(8,128)(2,1)}, u32[]{:S(2)}) copy-start(bf16[128,2048]{1,0:T(8,128)(2,1)} %q_ref.1) | copy-start | bytes 1572868
  10.4 12.9 %copy-start.7 = (s32[128]{0:T(128)}, s32[128]{0:T(128)S(1)}, u32[]{:S(2)}) copy-start(s32[128]{0:T(128)S(1)} %compare_select_fusion) | copy-start | bytes 1540
  11.8 12.3 %copy-start.5 = (bf16[64,2048]{1,0:T(8,128)(2,1)S(1)}, bf16[64,2048]{1,0:T(8,128)(2,1)}, u32[]{:S(2)}) copy-start(bf16[64,2048]{1,0:T(8,128)(2,1)} %param.11) | copy-start | bytes 786436
  23.8 6.1 %copy-start.9 = (s32[32]{0:T(128)}, s32[32]{0:T(128)S(1)}, u32[]{:S(2)}) copy-start(s32[32]{0:T(128)S(1)} %select_n.62) | copy-start | bytes 388
  24.0 1.0 copy-start.6
  26.4 8.0 %all-to-all-start = ((f32[4,2,2176]{2,1,0:T(2,128)}), f32[4,2,2176]{2,1,0:T(2,128)S(1)}, u32[]{:S(2)}, u32[]{:S(2)}) async-start(f32[4,2,2176]{2,1,0:T(2,128)} %all_to_all.50), calls=%async_computation | async-start | bytes 139264 | tf_op jit(solution)/shard_map/all_to_all | solution.py:25
  29.9 106.1 %all-gather.4.cloned.1.call-start = ((), (), s32[]{:S(2)}) async-start(), calls=%async_computation.9 | async-start | bytes 1310720 | tf_op jit(solution)/shard_map/all_gather | solution.py:117
  63.7 28.0 %copy-start.2 = (bf16[1,80,2048]{2,1,0:T(8,128)(2,1)S(1)}, bf16[1,80,2048]{2,1,0:T(8,128)(2,1)}, u32[]{:S(2)}) copy-start(bf16[1,80,2048]{2,1,0:T(8,128)(2,1)} %param.15) | copy-start | bytes 983044
  77.4 14.6 %copy-start.11 = (bf16[1,80,2048]{2,1,0:T(8,128)(2,1)S(1)}, bf16[1,80,2048]{2,1,0:T(8,128)(2,1)}, u32[]{:S(2)}) copy-start(bf16[1,80,2048]{2,1,0:T(8,128)(2,1)} %param.16) | copy-start | bytes 983044
  77.4 14.3 %collective-permute-start = (bf16[128,4096]{1,0:T(8,128)(2,1)S(1)}, bf16[128,4096]{1,0:T(8,128)(2,1)S(1)}, u32[]{:S(2)}, u32[]{:S(2)}) collective-permute-start(bf16[128,4096]{1,0:T(8,128)(2,1)S(1)} %bitcast.63), channel_id=1, source_target_pairs={{0,1},{1,0},{2,3},{3,2},{4,5},{5,4},{6,7},{7,6},{8,9},{9,8},{10,11... | collective-permute-start | bytes 3145736 | tf_op jit(solution)/shard_map/ppermute | solution.py:43
  89.4 53.9 %all-gather.6.cloned.1.call-start = ((), (), s32[]{:S(2)}) async-start(), calls=%async_computation.10 | async-start | bytes 1310720 | tf_op jit(solution)/shard_map/all_gather | solution.py:118
  91.7 1.8 copy-start.3
  93.4 4.0 %collective-permute-start.1 = (bf16[128,2048]{1,0:T(8,128)(2,1)}, bf16[128,2048]{1,0:T(8,128)(2,1)S(1)}, u32[]{:S(2)}, u32[]{:S(2)}) collective-permute-start(bf16[128,2048]{1,0:T(8,128)(2,1)} %convolution_convert_fusion.1), channel_id=1, source_target_pairs={{0,1},{1,0},{2,3},{3,2},{4,5},{5,4},{6,7},{7,6},{8,9},{9,8},{10,11... | collective-permute-start | bytes 1572872 | tf_op jit(solution)/shard_map/ppermute | solution.py:43
  97.8 16.1 %copy-start.10 = (s32[32]{0:T(128)S(1)}, s32[32]{0:T(128)}, u32[]{:S(2)}) copy-start(s32[32]{0:T(128)} %copy-done.9) | copy-start | bytes 388
  97.8 16.2 %copy-start.8 = (s32[128]{0:T(128)S(1)}, s32[128]{0:T(128)}, u32[]{:S(2)}) copy-start(s32[128]{0:T(128)} %copy-done.7) | copy-start | bytes 1540
  110.3 15.6 %all-to-all-start.4 = ((bf16[16,2,2048]{2,1,0:T(2,128)(2,1)}), bf16[16,2,2048]{2,1,0:T(2,128)(2,1)S(1)}, u32[]{:S(2)}, u32[]{:S(2)}) async-start(bf16[16,2,2048]{2,1,0:T(2,128)(2,1)} %all_to_all.57), calls=%async_computation.4 | async-start | bytes 262144 | tf_op jit(solution)/shard_map/all_to_all | solution.py:25
  152.2 6.0 %collective-permute-start.2 = (bf16[256,2048]{1,0:T(8,128)(2,1)}, bf16[256,2048]{1,0:T(8,128)(2,1)S(1)}, u32[]{:S(2)}, u32[]{:S(2)}) collective-permute-start(bf16[256,2048]{1,0:T(8,128)(2,1)} %get-tuple-element.13), channel_id=1, source_target_pairs={{0,1},{1,0},{2,3},{3,2},{4,5},{5,4},{6,7},{7,6},{8,9},{9,8},{10,11... | collective-permute-start | bytes 3145736 | tf_op jit(solution)/shard_map/ppermute | solution.py:43
  183.5 23.5 %all-to-all-start.6 = ((bf16[16,2,1024]{2,1,0:T(2,128)(2,1)}), bf16[16,2,1024]{2,1,0:T(2,128)(2,1)S(1)}, u32[]{:S(2)}, u32[]{:S(2)}) async-start(bf16[16,2,1024]{2,1,0:T(2,128)(2,1)} %reshape.189), calls=%async_computation.6 | async-start | bytes 131072 | tf_op jit(solution)/shard_map/all_to_all | solution.py:25
  209.0 15.1 %all-to-all-start.7 = ((bf16[16,2,1024]{2,1,0:T(2,128)(2,1)}), bf16[16,2,1024]{2,1,0:T(2,128)(2,1)S(1)}, u32[]{:S(2)}, u32[]{:S(2)}) async-start(bf16[16,2,1024]{2,1,0:T(2,128)(2,1)} %reshape.191), calls=%async_computation.7 | async-start | bytes 131072 | tf_op jit(solution)/shard_map/all_to_all | solution.py:25
  224.9 8.9 %all-to-all-start.8 = ((bf16[4,16,2048]{2,1,0:T(8,128)(2,1)}), bf16[4,16,2048]{2,1,0:T(8,128)(2,1)S(1)}, u32[]{:S(2)}, u32[]{:S(2)}) async-start(bf16[4,16,2048]{2,1,0:T(8,128)(2,1)} %broadcast_in_dim.118), calls=%async_computation.8 | async-start | bytes 524288 | tf_op jit(solution)/shard_map/all_to_all | solution.py:25
  228.5 14.7 %copy-start.4 = (bf16[128,4096]{1,0:T(8,128)(2,1)S(1)}, bf16[128,4096]{1,0:T(8,128)(2,1)}, u32[]{:S(2)}) copy-start(bf16[128,4096]{1,0:T(8,128)(2,1)} %copy-done.3) | copy-start | bytes 3145732
  233.8 10.5 %collective-permute-start.3 = (bf16[64,2048]{1,0:T(8,128)(2,1)S(1)}, bf16[64,2048]{1,0:T(8,128)(2,1)S(1)}, u32[]{:S(2)}, u32[]{:S(2)}) collective-permute-start(bf16[64,2048]{1,0:T(8,128)(2,1)S(1)} %bitcast.70), channel_id=1, source_target_pairs={{0,1},{1,0},{2,3},{3,2},{4,5},{5,4},{6,7},{7,6},{8,9},{9,8},{10,11... | collective-permute-start | bytes 786440 | tf_op jit(solution)/shard_map/ppermute | solution.py:43
Sparse Core Ops, SparseCore 0:
  89.6 19.4 all-gather.3
  111.2 32.0 all-gather.5

commit v2 on v1

v2 whole, which is shorter than its diff:
```python
import jax
import jax.numpy as jnp
from jax import lax
from jax.experimental import pallas as pl
from jax.experimental.pallas import tpu as pltpu
from jax.sharding import Mesh, PartitionSpec as P

HEAD = 64
GCAP = 2
SCALE = HEAD ** (-0.5)
BF, F32 = jnp.bfloat16, jnp.float32
DEVICES = ("y", "z", "x", "c")
PLANE = ("z", "x", "c")


def dot(left, right, left_dim=1, right_dim=0):
    return lax.dot_general(
        left, right, (((left_dim,), (right_dim,)), ((), ())), preferred_element_type=F32
    )


def exchange(values, axes):
    return lax.all_to_all(values, axes, split_axis=0, concat_axis=0, tiled=True)


def spread(values, axes):
    n = lax.axis_size(axes)
    copies = jnp.broadcast_to(values[None], (n,) + values.shape).reshape(
        (n * values.shape[0],) + values.shape[1:]
    )
    return exchange(copies, axes)


def collect(values, axes):
    n = lax.axis_size(axes)
    got = exchange(values, axes)
    return jnp.sum(got.reshape((n, -1) + got.shape[1:]).astype(F32), axis=0)


def head_pairs(values):
    rows, width = values.shape
    return values.reshape(rows, width // (2 * HEAD), 2 * HEAD).transpose(1, 0, 2)


def rows_of(pairs):
    return pairs.transpose(1, 0, 2).reshape(pairs.shape[1], -1)


def after(values, *others):
    return lax.optimization_barrier((values,) + others)[0]


def shifts(pick):
    n = lax.axis_size("y")
    moves = [[(i, (i + d) % n) for i in range(n)] for d in range(n)]
    return [pick(0)] + [lax.ppermute(pick(d), "y", moves[d]) for d in range(1, n)]


def other_core(values):
    return lax.ppermute(values, "c", [(0, 1), (1, 0)])


def both_heads(block):
    low = lax.broadcasted_iota(jnp.int32, block.shape, 1) < HEAD
    none = jnp.zeros_like(block)
    return jnp.concatenate([jnp.where(low, block, none), jnp.where(low, none, block)], axis=0)


def pair_backward(first, queries, grads, own, across):
    tokens = queries.shape[0]
    keys, values = jnp.where(first, own, across), jnp.where(first, across, own)
    queries, grads = both_heads(queries * BF(SCALE)), both_heads(grads)
    scores = dot(keys, queries, 1, 1)
    exps = jnp.exp(scores - jnp.max(scores, axis=0, keepdims=True))
    probs = exps * (1.0 / jnp.sum(exps, axis=0, keepdims=True))
    d_probs = dot(values, grads, 1, 1)
    centre = jnp.sum(probs * d_probs, axis=0, keepdims=True)
    d_scores = (probs * (d_probs - centre)).astype(BF)
    g_keys = dot(d_scores, queries)
    g_values = dot(probs.astype(BF), grads)
    g_queries = dot(keys, d_scores, 0, 0)
    g_queries = jnp.concatenate([g_queries[:HEAD, :tokens], g_queries[HEAD:, tokens:]], axis=0)
    keep = jnp.where(first, g_keys, g_values).astype(BF)
    send = jnp.where(first, g_values, g_keys).astype(BF)
    return (g_queries.T * SCALE).astype(BF), keep, send


def bulk_kernel(core_ref, free_ref, up_ref, q_ref, own_ref, across_ref, gq_ref, keep_ref, send_ref):
    first = core_ref[0] == 0
    free = free_ref[...]
    for pair in range(q_ref.shape[1] // (2 * HEAD)):
        cols = slice(pair * 2 * HEAD, (pair + 1) * 2 * HEAD)
        gq_ref[:, cols], keep_ref[:, cols], send_ref[:, cols] = pair_backward(
            first, q_ref[:, cols], up_ref[:, cols] * free, own_ref[:, cols], across_ref[:, cols]
        )


def bulk_backward(core, free, upstream, queries, own, across):
    tokens, width = queries.shape
    mem = own.shape[0]
    block = 512
    column = lambda n: pl.BlockSpec((n, block), lambda i: (0, i))
    return pl.pallas_call(
        bulk_kernel,
        grid=(width // block,),
        in_specs=[
            pl.BlockSpec(memory_space=pltpu.SMEM),
            pl.BlockSpec(free.shape, lambda i: (0, 0)),
            column(tokens),
            column(tokens),
            column(mem),
            column(mem),
        ],
        out_specs=[column(tokens), column(mem), column(mem)],
        out_shape=[
            jax.ShapeDtypeStruct((tokens, width), BF),
            jax.ShapeDtypeStruct((mem, width), BF),
            jax.ShapeDtypeStruct((mem, width), BF),
        ],
        cost_estimate=pl.CostEstimate(
            flops=48 * tokens * mem * width, bytes_accessed=32 * mem * width, transcendentals=0
        ),
    )(core, free, upstream, queries, own, across)


def routed_kernel(
    spot_ref, sums_ref, up_ref, q_ref, own_ref, across_ref, ret_ref, keep_ref, send_ref, bulk_ref
):
    first = spot_ref[0] == 0
    tokens = q_ref.shape[0]
    sums = jnp.sum(sums_ref[...].astype(F32), axis=0)
    moe = sums[:tokens].astype(BF)
    bulk_ref[...] = sums[tokens:]
    grads = (up_ref[...].astype(F32) + moe.astype(F32)).astype(BF)
    g_queries, keep_ref[...], send_ref[...] = pair_backward(
        first, q_ref[...], grads, own_ref[...], across_ref[...]
    )
    ret_ref[:, : 2 * HEAD] = moe
    ret_ref[:, 2 * HEAD :] = g_queries


def routed_backward(spot, sums, gathered, queries, own, across):
    tokens, lanes = queries.shape
    mem, more = own.shape[0], sums.shape[1] - tokens
    skip = gathered.shape[1] // lanes // 2
    whole = lambda shape: pl.BlockSpec(shape, lambda i, spot: (0,) * len(shape))
    column = lambda n, base: pl.BlockSpec((n, lanes), lambda i, spot: (0, base + spot[1]))
    outs = [(tokens, 2 * lanes), (mem, lanes), (mem, lanes), (more, lanes)]
    return pl.pallas_call(
        routed_kernel,
        grid_spec=pltpu.PrefetchScalarGridSpec(
            num_scalar_prefetch=1,
            grid=(1,),
            in_specs=[
                whole(sums.shape),
                column(tokens, skip),
                whole(queries.shape),
                column(mem, 0),
                column(mem, 0),
            ],
            out_specs=[whole(shape) for shape in outs],
        ),
        out_shape=[
            jax.ShapeDtypeStruct(shape, dtype) for shape, dtype in zip(outs, (BF, BF, BF, F32))
        ],
    )(spot, sums, gathered, queries, own, across)


def per_device(
    states, queries, mem_keys, mem_values, expert_ids, send_counts, w_in, w_out, upstream
):
    tokens, width = states.shape
    heads = width // HEAD
    window = lax.axis_size("y")
    slots = window * GCAP
    mine, core, depth = lax.axis_index("y"), lax.axis_index("c"), lax.axis_index("z")
    first = core == 0
    own_memory = lax.all_gather(jnp.where(first, mem_keys, mem_values), "y", axis=0, tiled=True)
    across_memory = other_core(own_memory)

    experts = jnp.arange(window, dtype=jnp.int32)
    onehot = (expert_ids[:, None] == experts[None, :]).astype(jnp.int32)
    rank = jnp.sum((jnp.cumsum(onehot, axis=0) - 1) * onehot, axis=1)
    limit = jnp.sum(onehot * send_counts, axis=1)
    slot = jnp.where(rank < limit, expert_ids * GCAP + rank, -1)
    slot_ids = jnp.arange(slots, dtype=jnp.int32)
    place = (slot_ids[:, None] == slot[None, :]).astype(BF)
    payload = [dot(place, part).astype(BF) for part in (queries, states, upstream)]
    flags = jnp.broadcast_to(jnp.repeat(send_counts[0], GCAP).astype(BF)[:, None], (slots, 128))
    group = spread(jnp.concatenate(payload + [flags], axis=1), "y")

    counts = group[:, 3 * width].reshape(window, slots)[:, ::GCAP].astype(jnp.int32)
    offsets = jnp.cumsum(counts, axis=0).astype(jnp.int32) - counts
    order = jnp.arange(GCAP, dtype=jnp.int32)
    position = offsets[:, :, None] + order
    kept = (order < counts[:, :, None]) & (position < GCAP)
    target = jnp.where(kept, experts[None, :, None] * GCAP + position, -1).reshape(-1)
    pack = (slot_ids[:, None] == target[None, :]).astype(BF)
    filled = jnp.sum(pack.astype(F32), axis=1)
    routed = dot(pack, group[:, : 3 * width]).astype(BF)
    own_target = lax.dynamic_slice_in_dim(target, mine * slots, slots, 0)
    steps_back = (mine - slot_ids // GCAP + window) % window * GCAP + slot_ids % GCAP
    own = (own_target[:, None] == steps_back[None, :]).astype(BF)
    place_back = dot(place, own, 0, 0)
    taken = jnp.sum(place_back, axis=1, keepdims=True)
    place_back = place_back.astype(BF)

    in_head = jnp.arange(heads)[:, None] == (jnp.arange(width) // HEAD)[None, :]
    by_head = jnp.where(in_head[:, None, :], routed[None, :, :width], 0).reshape(-1, width)
    scores = dot(by_head, mem_keys, 1, 1) * SCALE
    top = jnp.max(scores, axis=1, keepdims=True)
    exps = jnp.exp(scores - top)
    total = jnp.sum(exps, axis=1)
    part = dot(exps.astype(BF), mem_values).reshape(heads, slots, width)
    part = jnp.sum(jnp.where(in_head[:, None, :], part, 0.0), axis=0)
    tops, totals = top.reshape(heads, slots).T, total.reshape(heads, slots).T
    pad = jnp.zeros((slots, 128 - 2 * heads), F32)
    parts = exchange(jnp.concatenate([part, tops, totals, pad], axis=1), "y")
    parts = parts.reshape(window, GCAP, -1)
    tops, totals = parts[:, :, width : width + heads], parts[:, :, width + heads : width + 2 * heads]
    share = jnp.exp(tops - jnp.max(tops, axis=0))
    share = share / jnp.sum(share * totals, axis=0)
    share = jnp.dot(
        share.reshape(-1, heads), in_head.astype(F32), precision=lax.Precision.HIGHEST
    ).reshape(window, GCAP, width)
    attended = jnp.sum(parts[:, :, :width] * share, axis=0)
    here = lax.dynamic_slice_in_dim(routed, mine * GCAP, GCAP, 0)
    here_filled = lax.dynamic_slice_in_dim(filled, mine * GCAP, GCAP, 0)
    row = (here[:, width : 2 * width].astype(F32) + attended) * here_filled[:, None]
    pair = jnp.concatenate([row.astype(BF), here[:, 2 * width :]], axis=1)

    copies = jnp.broadcast_to(pair[None], (lax.axis_size("z"),) + pair.shape)
    level = exchange(jnp.concatenate([copies, head_pairs(here[:, :width])], axis=2), "z")
    level = level.reshape(-1, level.shape[2])
    routed_queries = level[:, 2 * width :]
    level = level[:, : 2 * width]

    bulk_queries, keep, send = bulk_backward(
        core.reshape(1).astype(jnp.int32),
        (1.0 - taken).astype(BF),
        upstream,
        queries,
        own_memory,
        across_memory,
    )
    near = spread(after(level, send), "x")
    bulk = (keep.astype(F32) + other_core(send).astype(F32)).astype(BF)
    far = other_core(after(near, bulk))
    own_rows = mem_keys.shape[0]
    ahead = lambda d: lax.dynamic_slice_in_dim(bulk, (mine + d) % window * own_rows, own_rows, 0)
    bulk = sum(part.astype(F32) for part in shifts(ahead)).astype(BF)
    weight_in, weight_out = w_in[0], w_out[0]

    def expert(block):
        rows, grads = block[:, :width], block[:, width:]
        pre = dot(rows, weight_in, 1, 1)
        act, pullback = jax.vjp(jax.nn.gelu, pre)
        d_pre = pullback(dot(grads, weight_out, 1, 1))[0].astype(BF)
        return d_pre, dot(d_pre, rows, 0, 0), dot(act.astype(BF), grads, 0, 0), dot(d_pre, weight_in)

    _, far_in, far_out, far_back = expert(far)
    _, near_in, near_out, near_back = expert(near)
    grad_in, grad_out = (near_in + far_in).astype(BF), (near_out + far_out).astype(BF)

    back = (near_back + other_core(far_back.astype(BF)).astype(F32)).astype(BF)
    parts_of_x = lax.axis_size("x")
    joined = jnp.concatenate(
        [back.reshape(parts_of_x, -1, width), bulk.reshape(parts_of_x, -1, width)], axis=1
    )
    joined = collect(joined.reshape(-1, width), "x").astype(BF)
    joined = exchange(head_pairs(joined), "z")
    returned, keep, send, bulk = routed_backward(
        jnp.stack([core, depth]).astype(jnp.int32),
        joined,
        level,
        routed_queries,
        own_memory,
        across_memory,
    )

    memory = (keep.astype(F32) + other_core(send).astype(F32)).astype(BF)
    memory = (collect(memory, ("y", "x")) + bulk).astype(BF)
    copies = jnp.broadcast_to(memory[None], (lax.axis_size("z"),) + memory.shape)
    returned = returned.reshape(copies.shape[0], 2 * GCAP, 2 * HEAD)
    joined = exchange(jnp.concatenate([copies, returned], axis=1), "z")
    memory, returned = joined[:, : memory.shape[0]], joined[:, memory.shape[0] :]
    returned = rows_of(returned).reshape(GCAP, 2 * width)
    returned = jnp.concatenate(shifts(lambda d: returned), axis=0)
    memory = spread(rows_of(memory), ("x", "c")).reshape(parts_of_x, 2, -1, width)
    grad_keys = memory[:, 0].reshape(own_rows, width)
    grad_values = memory[:, 1].reshape(own_rows, width)
    moe_grad = dot(place_back, returned[:, :width])
    grad_states = (upstream.astype(F32) + moe_grad).astype(BF)
    grad_queries = jnp.where(taken > 0, dot(place_back, returned[:, width:]).astype(BF), bulk_queries)
    return grad_states, grad_queries, grad_keys, grad_values, grad_in[None], grad_out[None]


def solution(mesh):
    chips = Mesh(mesh.devices.reshape(4, 16, 4, 2), DEVICES)
    rows, memory, weights = P(DEVICES, None), P("y", None), P("y", PLANE, None)
    return jax.shard_map(
        per_device,
        mesh=chips,
        in_specs=(rows, rows, memory, memory, P(DEVICES), rows, weights, weights, rows),
        out_specs=(rows, rows, memory, memory, weights, weights),
        check_vma=False,
    )
```

time: 253 us -> 246 us (0.972)
  blocking collectives: 95.7 us -> 14.3 us
  starting transfers between devices: 51.2 us -> 89.7 us
  waiting for transfers between devices: 55.4 us -> 78.3 us
  local copies, waits for them, and re-layouts: 7.55 us -> 12.1 us
  matrix products: 10.4 us -> 14 us
  Pallas kernels: 8.91 us -> 11.6 us
    all_to_all x4 -> x1, blocking collectives: 75.3 us -> 14.3 us  [exchange(): return lax.all_to_all(values, axes, split_axis=0, concat_axis=0, tiled=True)]
    all_to_all x5 -> x8, starting transfers between devices: 25.9 us -> 49.4 us  [exchange(): return lax.all_to_all(values, axes, split_axis=0, concat_axis=0, tiled=True)]
    all_gather x2 -> x0, blocking collectives: 20.4 us -> none  [the longest x1 11 us: per_device(): lax.all_gather(jnp.concatenate(payload + [flags], axis=1), 'y', axis=0, t...]
    ppermute x0 -> x6, starting transfers between devices: none -> 16.4 us  [shifts(): lax.ppermute(pick(d), 'y', moves[d])]
    all_gather x2 -> x1, waiting for transfers between devices: 7.34 us -> 22 us  [per_device(): lax.all_gather(jnp.where(first, mem_keys, mem_values), 'y', axis=0, tiled...]
    ppermute x0 -> x6, waiting for transfers between devices: none -> 6.11 us  [shifts(): lax.ppermute(pick(d), 'y', moves[d])]
    all_to_all x5 -> x8, waiting for transfers between devices: 43.3 us -> 49.3 us  [exchange(): return lax.all_to_all(values, axes, split_axis=0, concat_axis=0, tiled=True)]
    ppermute x4 -> x5, waiting for transfers between devices: 4.74 us -> 0.83 us  [other_core(): return lax.ppermute(values, 'c', [(0, 1), (1, 0)])]
  transfers between devices with their start and end apart: 11 -> 20, of which waited for: 9 -> 11; matrix products, arithmetic and copies ran while one was open for 4% -> 9% of each run, Pallas kernels for 0% -> 4%
where the time goes in v2:
time: 246 us; the launch traced here: 245 us
  starting transfers between devices  89.7 us (36%)
  waiting for transfers between devices  78.3 us (32%)
  between operations  14.7 us (6%)
  blocking collectives  14.3 us (6%)
  matrix products  14 us (6%)
  local copies, waits for them, and re-layouts  12.1 us (5%)
  Pallas kernels  11.6 us (5%)
  other arithmetic  9.82 us (4%)
    all_to_all x8, starting transfers between devices, exchange(): return lax.all_to_all(values, axes, split_axis=0, concat_axis=0, tiled=True)  49.4 us
    all_to_all x8, waiting for transfers between devices, exchange(): return lax.all_to_all(values, axes, split_axis=0, concat_axis=0, tiled=True)  49.3 us
    ppermute x5, starting transfers between devices, other_core(): return lax.ppermute(values, 'c', [(0, 1), (1, 0)])  24 us
    all_gather x1, waiting for transfers between devices, per_device(): lax.all_gather(jnp.where(first, mem_keys, mem_values), 'y', axis=0, tiled...  22 us
    ppermute x6, starting transfers between devices, shifts(): lax.ppermute(pick(d), 'y', moves[d])  16.4 us
    all_to_all x1, blocking collectives, exchange(): return lax.all_to_all(values, axes, split_axis=0, concat_axis=0, tiled=True)  14.3 us
    dot_general x19, matrix products, dot(): lax.dot_general(left, right, (((left_dim,), (right_dim,)), ((), ())), pre...  13.8 us
    pallas_call x1, Pallas kernels, bulk_backward(): pl.pallas_call(bulk_kernel, grid=(width // block,), in_specs=[pl.BlockSpe...  8.79 us
  transfers between devices with their start and end apart: 20, of which 11 were waited for; matrix products, arithmetic and copies ran while one was open for 9% of the time, Pallas kernels for 4%

profile of v2, /device:TPU:1, one launch (start us, length us, event | category | flops | bytes accessed | tf_op | source)
XLA Modules:
  0.0 244.7 jit_solution(4478455348523309715)
XLA Ops:
  7.2 0.7 bitcast_convert_fusion
  8.1 0.7 fusion.39
  9.0 0.8 select_reduce_fusion
  9.9 0.7 compare_select_fusion.2
  10.5 1.2 convolution_convert_fusion.3
  12.2 0.8 broadcast_in_dim.70
  13.0 5.0 %all-to-all-start = ((bf16[4,8,6272]{2,1,0:T(8,128)(2,1)}), bf16[4,8,6272]{2,1,0:T(8,128)(2,1)S(1)}, u32[]{:S(2)}, u32[]{:S(2)}) async-start(bf16[4,8,6272]{2,1,0:T(8,128)(2,1)} %broadcast_in_dim.70), calls=%async_computation | async-start | bytes 802816 | tf_op jit(solution)/shard_map/all_to_all | solution.py:23
  18.0 0.7 broadcast_select_fusion
  18.9 5.4 %all-to-all-done = bf16[4,8,6272]{2,1,0:T(8,128)(2,1)S(1)} async-done(((bf16[4,8,6272]{2,1,0:T(8,128)(2,1)}), bf16[4,8,6272]{2,1,0:T(8,128)(2,1)S(1)}, u32[]{:S(2)}, u32[]{:S(2)}) %all-to-all-start) | async-done | bytes 401440 | tf_op jit(solution)/shard_map/all_to_all | solution.py:23
  25.0 0.5 fusion.112
  25.9 0.5 fusion.7
  26.5 0.7 all_to_all.43
  27.2 3.3 %all-to-all-start.1 = ((f32[4,2,2176]{2,1,0:T(2,128)}), f32[4,2,2176]{2,1,0:T(2,128)S(1)}, u32[]{:S(2)}, u32[]{:S(2)}) async-start(f32[4,2,2176]{2,1,0:T(2,128)} %all_to_all.43), calls=%async_computation.1 | async-start | bytes 139264 | tf_op jit(solution)/shard_map/all_to_all | solution.py:23
  31.0 0.7 copy.46.free_ref
  31.8 3.2 %all-to-all-done.1 = f32[4,2,2176]{2,1,0:T(2,128)S(1)} async-done(((f32[4,2,2176]{2,1,0:T(2,128)}), f32[4,2,2176]{2,1,0:T(2,128)S(1)}, u32[]{:S(2)}, u32[]{:S(2)}) %all-to-all-start.1) | async-done | bytes 69664 | tf_op jit(solution)/shard_map/all_to_all | solution.py:23
  35.4 22.0 %all-gather.2.cloned.1.call-done.own_ref = bf16[256,2048]{1,0:T(8,128)(2,1)} async-done(((bf16[64,2048]{1,0:T(8,128)(2,1)}), bf16[256,2048]{1,0:T(8,128)(2,1)}) %all-gather.2.cloned.1.call-update) | async-done | bytes 1048592 | tf_op jit(solution)/shard_map/all_gather | solution.py:178
  57.4 3.5 %collective-permute-start = (bf16[256,2048]{1,0:T(8,128)(2,1)}, bf16[256,2048]{1,0:T(8,128)(2,1)S(1)}, u32[]{:S(2)}, u32[]{:S(2)}) collective-permute-start(bf16[256,2048]{1,0:T(8,128)(2,1)} %all-gather.2.cloned.1.call-done.own_ref), channel_id=1, source_target_pairs={{0,1},{1,0},{2,3},{3,2},{4,5},{5,4},{6,7},{7,6},{8,9},{9,8},{10,11... | collective-permute-start | bytes 3145736 | tf_op jit(solution)/shard_map/ppermute | solution.py:60
  61.2 1.0 pad_maximum_fusion.1
  62.2 12.0 %all-to-all-start.2 = ((bf16[16,2,4224]{2,1,0:T(2,128)(2,1)}), bf16[16,2,4224]{2,1,0:T(2,128)(2,1)S(1)}, u32[]{:S(2)}, u32[]{:S(2)}) async-start(bf16[16,2,4224]{2,1,0:T(2,128)(2,1)} %pad_maximum_fusion.1), calls=%async_computation.2 | async-start | bytes 540672 | tf_op jit(solution)/shard_map/all_to_all | solution.py:23
  74.2 1.0 copy-done.6
  75.2 8.8 %shard_map.136 = (bf16[128,2048]{1,0:T(8,128)(2,1)}, bf16[256,2048]{1,0:T(8,128)(2,1)}, bf16[256,2048]{1,0:T(8,128)(2,1)}) custom-call(s32[1]{0:T(128)} %bitcast.2.core_ref, bf16[128,1]{1,0:T(8,128)(2,1)} %copy.46.free_ref, bf16[128,2048]{1,0:T(8,128)(2,1)} %up_ref.1, bf16[128,2048]{1,0:T(8,128)(2,1)} %q_ref.1, ...), custom_call_target="tpu_custom_call" | custom-call | flops 3221225472 | bytes 16777216 | tf_op jit(solution)/shard_map/pallas_call | solution.py:103
  84.0 2.2 collective-permute-start.1
  86.2 2.5 %all-to-all-done.2 = bf16[16,2,4224]{2,1,0:T(2,128)(2,1)S(1)} async-done(((bf16[16,2,4224]{2,1,0:T(2,128)(2,1)}), bf16[16,2,4224]{2,1,0:T(2,128)(2,1)S(1)}, u32[]{:S(2)}, u32[]{:S(2)}) %all-to-all-start.2) | async-done | bytes 270368 | tf_op jit(solution)/shard_map/all_to_all | solution.py:23
  88.8 0.7 copy-done.1
  89.6 1.1 broadcast_in_dim.130
  90.7 4.0 %all-to-all-start.3 = ((bf16[4,32,4096]{2,1,0:T(8,128)(2,1)}), bf16[4,32,4096]{2,1,0:T(8,128)(2,1)S(1)}, u32[]{:S(2)}, u32[]{:S(2)}) async-start(bf16[4,32,4096]{2,1,0:T(8,128)(2,1)} %broadcast_in_dim.130), calls=%async_computation.3 | async-start | bytes 2097152 | tf_op jit(solution)/shard_map/all_to_all | solution.py:23
  94.6 1.0 copy-done.5
  95.6 2.0 add_convert_fusion
  97.6 6.8 %all-to-all-done.3 = bf16[4,32,4096]{2,1,0:T(8,128)(2,1)S(1)} async-done(((bf16[4,32,4096]{2,1,0:T(8,128)(2,1)}), bf16[4,32,4096]{2,1,0:T(8,128)(2,1)S(1)}, u32[]{:S(2)}, u32[]{:S(2)}) %all-to-all-start.3) | async-done | bytes 1048608 | tf_op jit(solution)/shard_map/all_to_all | solution.py:23
  104.4 8.3 %collective-permute-start.2 = (bf16[128,4096]{1,0:T(8,128)(2,1)S(1)}, bf16[128,4096]{1,0:T(8,128)(2,1)}, u32[]{:S(2)}, u32[]{:S(2)}) collective-permute-start(bf16[128,4096]{1,0:T(8,128)(2,1)S(1)} %bitcast.84), channel_id=1, source_target_pairs={{0,1},{1,0},{2,3},{3,2},{4,5},{5,4},{6,7},{7,6},{8,9},{9,8},{10,11... | collective-permute-start | bytes 3145736 | tf_op jit(solution)/shard_map/ppermute | solution.py:60
  113.1 3.5 %collective-permute-start.6 = (bf16[64,2048]{1,0:T(8,128)(2,1)S(1)}, bf16[64,2048]{1,0:T(8,128)(2,1)S(1)}, u32[]{:S(2)}, u32[]{:S(2)}) collective-permute-start(bf16[64,2048]{1,0:T(8,128)(2,1)S(1)} %get-tuple-element.27), channel_id=1, source_target_pairs={{0,384},{128,0},{256,128},{384,256},{1,385},{129,1},{257,129},{385... | collective-permute-start | bytes 786440 | tf_op jit(solution)/shard_map/ppermute | solution.py:56
  116.7 2.5 %collective-permute-start.5 = (bf16[64,2048]{1,0:T(8,128)(2,1)S(1)}, bf16[64,2048]{1,0:T(8,128)(2,1)S(1)}, u32[]{:S(2)}, u32[]{:S(2)}) collective-permute-start(bf16[64,2048]{1,0:T(8,128)(2,1)S(1)} %get-tuple-element.28), channel_id=1, source_target_pairs={{0,256},{128,384},{256,0},{384,128},{1,257},{129,385},{257,1},{385... | collective-permute-start | bytes 786440 | tf_op jit(solution)/shard_map/ppermute | solution.py:56
  119.2 2.5 %collective-permute-start.4 = (bf16[64,2048]{1,0:T(8,128)(2,1)S(1)}, bf16[64,2048]{1,0:T(8,128)(2,1)S(1)}, u32[]{:S(2)}, u32[]{:S(2)}) collective-permute-start(bf16[64,2048]{1,0:T(8,128)(2,1)S(1)} %get-tuple-element.26), channel_id=1, source_target_pairs={{0,128},{128,256},{256,384},{384,0},{1,129},{129,257},{257,385},{3... | collective-permute-start | bytes 786440 | tf_op jit(solution)/shard_map/ppermute | solution.py:56
  121.7 1.4 fusion.15
  123.0 1.4 fusion.55
  124.7 2.8 %collective-permute-start.3 = (bf16[128,2048]{1,0:T(8,128)(2,1)S(1)}, bf16[128,2048]{1,0:T(8,128)(2,1)S(1)}, u32[]{:S(2)}, u32[]{:S(2)}) collective-permute-start(bf16[128,2048]{1,0:T(8,128)(2,1)S(1)} %convolution_convert_fusion.2), channel_id=1, source_target_pairs={{0,1},{1,0},{2,3},{3,2},{4,5},{5,4},{6,7},{7,6},{8,9},{9,8},{10,11... | collective-permute-start | bytes 1572872 | tf_op jit(solution)/shard_map/ppermute | solution.py:60
  127.8 6.1 %collective-permute-done.4 = bf16[64,2048]{1,0:T(8,128)(2,1)S(1)} collective-permute-done((bf16[64,2048]{1,0:T(8,128)(2,1)S(1)}, bf16[64,2048]{1,0:T(8,128)(2,1)S(1)}, u32[]{:S(2)}, u32[]{:S(2)}) %collective-permute-start.4) | collective-permute-done | bytes 262176 | tf_op jit(solution)/shard_map/ppermute | solution.py:56
  134.5 14.3 %all_to_all.63 = bf16[4,48,2048]{2,1,0:T(8,128)(2,1)S(1)} all-to-all(bf16[4,48,2048]{2,1,0:T(8,128)(2,1)S(1)} %pad_maximum_fusion), channel_id=1, replica_groups=mesh['y'=4,'z'=16,'x'=4,'c'=2] {'x'}, dimensions={0} | all-to-all | bytes 1572864 | tf_op jit(solution)/shard_map/all_to_all | solution.py:23
  148.9 0.7 bitcast_bitcast_fusion
  149.6 10.1 %all-to-all-start.5 = ((bf16[16,48,128]{2,1,0:T(8,128)(2,1)}), bf16[16,48,128]{2,1,0:T(8,128)(2,1)S(1)}, u32[]{:S(2)}, u32[]{:S(2)}) async-start(bf16[16,48,128]{2,1,0:T(8,128)(2,1)} %bitcast_bitcast_fusion), calls=%async_computation.5 | async-start | bytes 393216 | tf_op jit(solution)/shard_map/all_to_all | solution.py:23
  159.7 0.7 pad_add_fusion.spot_ref
  160.4 1.3 slice.99.q_ref
  161.7 10.4 %all-to-all-done.5.sums_ref = bf16[16,48,128]{2,1,0:T(8,128)(2,1)S(1)} async-done(((bf16[16,48,128]{2,1,0:T(8,128)(2,1)}), bf16[16,48,128]{2,1,0:T(8,128)(2,1)S(1)}, u32[]{:S(2)}, u32[]{:S(2)}) %all-to-all-start.5) | async-done | bytes 196640 | tf_op jit(solution)/shard_map/all_to_all | solution.py:23
  172.1 0.7 copy-done.7
  172.7 2.9 %shard_map.137 = (bf16[32,256]{1,0:T(8,128)(2,1)}, bf16[256,128]{1,0:T(8,128)(2,1)}, bf16[256,128]{1,0:T(8,128)(2,1)}, f32[16,128]{1,0:T(8,128)}) custom-call(s32[2]{0:T(128)} %pad_add_fusion.spot_ref, bf16[16,48,128]{2,1,0:T(8,128)(2,1)} %copy-done.7, bf16[32,4096]{1,0:T(8,128)(2,1)} %copy-done.1, bf16[32,128]{1,0:T(8,128)(2,1)} %slice.99.q_ref, ...), custom_call_target="tpu_custom_call" | custom-call | tf_op jit(solution)/shard_map/pallas_call | solution.py:149
  175.6 7.2 %collective-permute-start.7 = (bf16[256,128]{1,0:T(8,128)(2,1)}, bf16[256,128]{1,0:T(8,128)(2,1)S(1)}, u32[]{:S(2)}, u32[]{:S(2)}) collective-permute-start(bf16[256,128]{1,0:T(8,128)(2,1)} %get-tuple-element.20), channel_id=1, source_target_pairs={{0,1},{1,0},{2,3},{3,2},{4,5},{5,4},{6,7},{7,6},{8,9},{9,8},{10,11... | collective-permute-start | bytes 196616 | tf_op jit(solution)/shard_map/ppermute | solution.py:60
  183.1 0.8 collective-permute-done.7
  183.9 0.6 add_convert_fusion.3
  184.6 3.5 %all-to-all-start.6 = ((bf16[16,16,128]{2,1,0:T(8,128)(2,1)}), bf16[16,16,128]{2,1,0:T(8,128)(2,1)S(1)}, u32[]{:S(2)}, u32[]{:S(2)}) async-start(bf16[16,16,128]{2,1,0:T(8,128)(2,1)} %bitcast.18), calls=%async_computation.6 | async-start | bytes 131072 | tf_op jit(solution)/shard_map/all_to_all | solution.py:23
  188.3 6.2 %all-to-all-done.6 = bf16[16,16,128]{2,1,0:T(8,128)(2,1)S(1)} async-done(((bf16[16,16,128]{2,1,0:T(8,128)(2,1)}), bf16[16,16,128]{2,1,0:T(8,128)(2,1)S(1)}, u32[]{:S(2)}, u32[]{:S(2)}) %all-to-all-start.6) | async-done | bytes 65568 | tf_op jit(solution)/shard_map/all_to_all | solution.py:23
  194.6 0.7 pad_maximum_fusion.3
  195.2 4.5 %all-to-all-start.7 = ((bf16[16,20,128]{2,1,0:T(8,128)(2,1)}), bf16[16,20,128]{2,1,0:T(8,128)(2,1)S(1)}, u32[]{:S(2)}, u32[]{:S(2)}) async-start(bf16[16,20,128]{2,1,0:T(8,128)(2,1)} %pad_maximum_fusion.3), calls=%async_computation.7 | async-start | bytes 196608 | tf_op jit(solution)/shard_map/all_to_all | solution.py:23
  199.7 2.0 fusion.6
  201.7 2.0 fusion.5
  203.8 7.8 %all-to-all-done.7 = bf16[16,20,128]{2,1,0:T(8,128)(2,1)S(1)} async-done(((bf16[16,20,128]{2,1,0:T(8,128)(2,1)}), bf16[16,20,128]{2,1,0:T(8,128)(2,1)S(1)}, u32[]{:S(2)}, u32[]{:S(2)}) %all-to-all-start.7) | async-done | bytes 81952 | tf_op jit(solution)/shard_map/all_to_all | solution.py:23
  211.6 2.8 %collective-permute-start.10 = (bf16[2,4096]{1,0:T(2,128)(2,1)S(1)}, bf16[2,4096]{1,0:T(2,128)(2,1)S(1)}, u32[]{:S(2)}, u32[]{:S(2)}) collective-permute-start(bf16[2,4096]{1,0:T(2,128)(2,1)S(1)} %reshape_reshape.3), channel_id=1, source_target_pairs={{0,384},{128,0},{256,128},{384,256},{1,385},{129,1},{257,129},{385... | collective-permute-start | bytes 49160 | tf_op jit(solution)/shard_map/ppermute | solution.py:56
  214.5 3.1 %collective-permute-start.9 = (bf16[2,4096]{1,0:T(2,128)(2,1)S(1)}, bf16[2,4096]{1,0:T(2,128)(2,1)S(1)}, u32[]{:S(2)}, u32[]{:S(2)}) collective-permute-start(bf16[2,4096]{1,0:T(2,128)(2,1)S(1)} %reshape_reshape.3), channel_id=1, source_target_pairs={{0,256},{128,384},{256,0},{384,128},{1,257},{129,385},{257,1},{385... | collective-permute-start | bytes 49160 | tf_op jit(solution)/shard_map/ppermute | solution.py:56
  217.6 1.9 collective-permute-start.8
  219.6 0.8 broadcast_in_dim.134
  220.4 7.1 %all-to-all-start.8 = ((bf16[8,16,2048]{2,1,0:T(8,128)(2,1)}), bf16[8,16,2048]{2,1,0:T(8,128)(2,1)S(1)}, u32[]{:S(2)}, u32[]{:S(2)}) async-start(bf16[8,16,2048]{2,1,0:T(8,128)(2,1)} %broadcast_in_dim.134), calls=%async_computation.8 | async-start | bytes 1048576 | tf_op jit(solution)/shard_map/all_to_all | solution.py:23
  227.6 1.1 fusion.1
  228.7 1.1 fusion.2
  229.9 7.1 %all-to-all-done.8 = bf16[8,16,2048]{2,1,0:T(8,128)(2,1)S(1)} async-done(((bf16[8,16,2048]{2,1,0:T(8,128)(2,1)}), bf16[8,16,2048]{2,1,0:T(8,128)(2,1)S(1)}, u32[]{:S(2)}, u32[]{:S(2)}) %all-to-all-start.8) | async-done | bytes 524320 | tf_op jit(solution)/shard_map/all_to_all | solution.py:23
  237.0 0.8 fusion.109
  (103 shorter events, 5.8 us)
Async XLA Ops:
  7.2 4.6 %copy-start = (bf16[128,2048]{1,0:T(8,128)(2,1)S(1)}, bf16[128,2048]{1,0:T(8,128)(2,1)}, u32[]{:S(2)}) copy-start(bf16[128,2048]{1,0:T(8,128)(2,1)} %param.9) | copy-start | bytes 1572868
  7.2 4.8 %copy-start.8 = (bf16[128,2048]{1,0:T(8,128)(2,1)S(1)}, bf16[128,2048]{1,0:T(8,128)(2,1)}, u32[]{:S(2)}) copy-start(bf16[128,2048]{1,0:T(8,128)(2,1)} %q_ref.1) | copy-start | bytes 1572868
  11.9 6.1 %copy-start.10 = (bf16[64,2048]{1,0:T(8,128)(2,1)S(1)}, bf16[64,2048]{1,0:T(8,128)(2,1)}, u32[]{:S(2)}) copy-start(bf16[64,2048]{1,0:T(8,128)(2,1)} %param.11) | copy-start | bytes 786436
  11.9 6.1 %copy-start.11 = (bf16[64,2048]{1,0:T(8,128)(2,1)S(1)}, bf16[64,2048]{1,0:T(8,128)(2,1)}, u32[]{:S(2)}) copy-start(bf16[64,2048]{1,0:T(8,128)(2,1)} %param.12) | copy-start | bytes 786436
  13.0 11.3 %all-to-all-start = ((bf16[4,8,6272]{2,1,0:T(8,128)(2,1)}), bf16[4,8,6272]{2,1,0:T(8,128)(2,1)S(1)}, u32[]{:S(2)}, u32[]{:S(2)}) async-start(bf16[4,8,6272]{2,1,0:T(8,128)(2,1)} %broadcast_in_dim.70), calls=%async_computation | async-start | bytes 802816 | tf_op jit(solution)/shard_map/all_to_all | solution.py:23
  18.0 39.4 %all-gather.2.cloned.1.call-start = ((), (), s32[]{:S(2)}) async-start(), calls=%async_computation.9 | async-start | bytes 1310720 | tf_op jit(solution)/shard_map/all_gather | solution.py:178
  27.2 7.8 %all-to-all-start.1 = ((f32[4,2,2176]{2,1,0:T(2,128)}), f32[4,2,2176]{2,1,0:T(2,128)S(1)}, u32[]{:S(2)}, u32[]{:S(2)}) async-start(f32[4,2,2176]{2,1,0:T(2,128)} %all_to_all.43), calls=%async_computation.1 | async-start | bytes 139264 | tf_op jit(solution)/shard_map/all_to_all | solution.py:23
  57.4 16.8 %collective-permute-start = (bf16[256,2048]{1,0:T(8,128)(2,1)}, bf16[256,2048]{1,0:T(8,128)(2,1)S(1)}, u32[]{:S(2)}, u32[]{:S(2)}) collective-permute-start(bf16[256,2048]{1,0:T(8,128)(2,1)} %all-gather.2.cloned.1.call-done.own_ref), channel_id=1, source_target_pairs={{0,1},{1,0},{2,3},{3,2},{4,5},{5,4},{6,7},{7,6},{8,9},{9,8},{10,11... | collective-permute-start | bytes 3145736 | tf_op jit(solution)/shard_map/ppermute | solution.py:60
  62.2 26.5 %all-to-all-start.2 = ((bf16[16,2,4224]{2,1,0:T(2,128)(2,1)}), bf16[16,2,4224]{2,1,0:T(2,128)(2,1)S(1)}, u32[]{:S(2)}, u32[]{:S(2)}) async-start(bf16[16,2,4224]{2,1,0:T(2,128)(2,1)} %pad_maximum_fusion.1), calls=%async_computation.2 | async-start | bytes 540672 | tf_op jit(solution)/shard_map/all_to_all | solution.py:23
  74.2 1.0 copy-start.6
  84.0 10.6 %collective-permute-start.1 = (bf16[256,2048]{1,0:T(8,128)(2,1)}, bf16[256,2048]{1,0:T(8,128)(2,1)S(1)}, u32[]{:S(2)}, u32[]{:S(2)}) collective-permute-start(bf16[256,2048]{1,0:T(8,128)(2,1)} %get-tuple-element.15), channel_id=1, source_target_pairs={{0,1},{1,0},{2,3},{3,2},{4,5},{5,4},{6,7},{7,6},{8,9},{9,8},{10,11... | collective-permute-start | bytes 3145736 | tf_op jit(solution)/shard_map/ppermute | solution.py:60
  88.8 1.9 copy-start.4
  88.8 0.8 copy-start.1
  90.7 13.7 %all-to-all-start.3 = ((bf16[4,32,4096]{2,1,0:T(8,128)(2,1)}), bf16[4,32,4096]{2,1,0:T(8,128)(2,1)S(1)}, u32[]{:S(2)}, u32[]{:S(2)}) async-start(bf16[4,32,4096]{2,1,0:T(8,128)(2,1)} %broadcast_in_dim.130), calls=%async_computation.3 | async-start | bytes 2097152 | tf_op jit(solution)/shard_map/all_to_all | solution.py:23
  94.6 1.0 copy-start.5
  95.6 17.2 %copy-start.3 = (bf16[1,80,2048]{2,1,0:T(8,128)(2,1)S(1)}, bf16[1,80,2048]{2,1,0:T(8,128)(2,1)}, u32[]{:S(2)}) copy-start(bf16[1,80,2048]{2,1,0:T(8,128)(2,1)} %param.15) | copy-start | bytes 983044
  104.4 17.3 %collective-permute-start.2 = (bf16[128,4096]{1,0:T(8,128)(2,1)S(1)}, bf16[128,4096]{1,0:T(8,128)(2,1)}, u32[]{:S(2)}, u32[]{:S(2)}) collective-permute-start(bf16[128,4096]{1,0:T(8,128)(2,1)S(1)} %bitcast.84), channel_id=1, source_target_pairs={{0,1},{1,0},{2,3},{3,2},{4,5},{5,4},{6,7},{7,6},{8,9},{9,8},{10,11... | collective-permute-start | bytes 3145736 | tf_op jit(solution)/shard_map/ppermute | solution.py:60
  113.1 10.0 %copy-start.15 = (bf16[1,80,2048]{2,1,0:T(8,128)(2,1)S(1)}, bf16[1,80,2048]{2,1,0:T(8,128)(2,1)}, u32[]{:S(2)}) copy-start(bf16[1,80,2048]{2,1,0:T(8,128)(2,1)} %param.16) | copy-start | bytes 983044
  113.1 14.7 %collective-permute-start.6 = (bf16[64,2048]{1,0:T(8,128)(2,1)S(1)}, bf16[64,2048]{1,0:T(8,128)(2,1)S(1)}, u32[]{:S(2)}, u32[]{:S(2)}) collective-permute-start(bf16[64,2048]{1,0:T(8,128)(2,1)S(1)} %get-tuple-element.27), channel_id=1, source_target_pairs={{0,384},{128,0},{256,128},{384,256},{1,385},{129,1},{257,129},{385... | collective-permute-start | bytes 786440 | tf_op jit(solution)/shard_map/ppermute | solution.py:56
  116.7 11.1 %collective-permute-start.5 = (bf16[64,2048]{1,0:T(8,128)(2,1)S(1)}, bf16[64,2048]{1,0:T(8,128)(2,1)S(1)}, u32[]{:S(2)}, u32[]{:S(2)}) collective-permute-start(bf16[64,2048]{1,0:T(8,128)(2,1)S(1)} %get-tuple-element.28), channel_id=1, source_target_pairs={{0,256},{128,384},{256,0},{384,128},{1,257},{129,385},{257,1},{385... | collective-permute-start | bytes 786440 | tf_op jit(solution)/shard_map/ppermute | solution.py:56
  119.2 14.7 %collective-permute-start.4 = (bf16[64,2048]{1,0:T(8,128)(2,1)S(1)}, bf16[64,2048]{1,0:T(8,128)(2,1)S(1)}, u32[]{:S(2)}, u32[]{:S(2)}) collective-permute-start(bf16[64,2048]{1,0:T(8,128)(2,1)S(1)} %get-tuple-element.26), channel_id=1, source_target_pairs={{0,128},{128,256},{256,384},{384,0},{1,129},{129,257},{257,385},{3... | collective-permute-start | bytes 786440 | tf_op jit(solution)/shard_map/ppermute | solution.py:56
  124.7 9.3 %collective-permute-start.3 = (bf16[128,2048]{1,0:T(8,128)(2,1)S(1)}, bf16[128,2048]{1,0:T(8,128)(2,1)S(1)}, u32[]{:S(2)}, u32[]{:S(2)}) collective-permute-start(bf16[128,2048]{1,0:T(8,128)(2,1)S(1)} %convolution_convert_fusion.2), channel_id=1, source_target_pairs={{0,1},{1,0},{2,3},{3,2},{4,5},{5,4},{6,7},{7,6},{8,9},{9,8},{10,11... | collective-permute-start | bytes 1572872 | tf_op jit(solution)/shard_map/ppermute | solution.py:60
  149.6 22.4 %all-to-all-start.5 = ((bf16[16,48,128]{2,1,0:T(8,128)(2,1)}), bf16[16,48,128]{2,1,0:T(8,128)(2,1)S(1)}, u32[]{:S(2)}, u32[]{:S(2)}) async-start(bf16[16,48,128]{2,1,0:T(8,128)(2,1)} %bitcast_bitcast_fusion), calls=%async_computation.5 | async-start | bytes 393216 | tf_op jit(solution)/shard_map/all_to_all | solution.py:23
  172.1 0.7 copy-start.7
  175.6 8.3 %copy-start.12 = (bf16[256,128]{1,0:T(8,128)(2,1)S(1)}, bf16[256,128]{1,0:T(8,128)(2,1)}, u32[]{:S(2)}) copy-start(bf16[256,128]{1,0:T(8,128)(2,1)} %get-tuple-element.19) | copy-start | bytes 196612
  175.6 8.3 %collective-permute-start.7 = (bf16[256,128]{1,0:T(8,128)(2,1)}, bf16[256,128]{1,0:T(8,128)(2,1)S(1)}, u32[]{:S(2)}, u32[]{:S(2)}) collective-permute-start(bf16[256,128]{1,0:T(8,128)(2,1)} %get-tuple-element.20), channel_id=1, source_target_pairs={{0,1},{1,0},{2,3},{3,2},{4,5},{5,4},{6,7},{7,6},{8,9},{9,8},{10,11... | collective-permute-start | bytes 196616 | tf_op jit(solution)/shard_map/ppermute | solution.py:60
  183.1 5.3 %copy-start.13 = (bf16[32,256]{1,0:T(8,128)(2,1)S(1)}, bf16[32,256]{1,0:T(8,128)(2,1)}, u32[]{:S(2)}) copy-start(bf16[32,256]{1,0:T(8,128)(2,1)} %get-tuple-element.22) | copy-start | bytes 49156
  183.1 11.5 %copy-start.14 = (f32[16,128]{1,0:T(8,128)S(1)}, f32[16,128]{1,0:T(8,128)}, u32[]{:S(2)}) copy-start(f32[16,128]{1,0:T(8,128)} %get-tuple-element.21) | copy-start | bytes 24580
  184.6 10.0 %all-to-all-start.6 = ((bf16[16,16,128]{2,1,0:T(8,128)(2,1)}), bf16[16,16,128]{2,1,0:T(8,128)(2,1)S(1)}, u32[]{:S(2)}, u32[]{:S(2)}) async-start(bf16[16,16,128]{2,1,0:T(8,128)(2,1)} %bitcast.18), calls=%async_computation.6 | async-start | bytes 131072 | tf_op jit(solution)/shard_map/all_to_all | solution.py:23
  195.2 16.3 %all-to-all-start.7 = ((bf16[16,20,128]{2,1,0:T(8,128)(2,1)}), bf16[16,20,128]{2,1,0:T(8,128)(2,1)S(1)}, u32[]{:S(2)}, u32[]{:S(2)}) async-start(bf16[16,20,128]{2,1,0:T(8,128)(2,1)} %pad_maximum_fusion.3), calls=%async_computation.7 | async-start | bytes 196608 | tf_op jit(solution)/shard_map/all_to_all | solution.py:23
  203.8 23.8 %copy-start.2 = (bf16[128,2048]{1,0:T(8,128)(2,1)S(1)}, bf16[128,2048]{1,0:T(8,128)(2,1)}, u32[]{:S(2)}) copy-start(bf16[128,2048]{1,0:T(8,128)(2,1)} %up_ref.1) | copy-start | bytes 1572868
  211.6 15.9 %collective-permute-start.10 = (bf16[2,4096]{1,0:T(2,128)(2,1)S(1)}, bf16[2,4096]{1,0:T(2,128)(2,1)S(1)}, u32[]{:S(2)}, u32[]{:S(2)}) collective-permute-start(bf16[2,4096]{1,0:T(2,128)(2,1)S(1)} %reshape_reshape.3), channel_id=1, source_target_pairs={{0,384},{128,0},{256,128},{384,256},{1,385},{129,1},{257,129},{385... | collective-permute-start | bytes 49160 | tf_op jit(solution)/shard_map/ppermute | solution.py:56
  214.5 13.0 %collective-permute-start.9 = (bf16[2,4096]{1,0:T(2,128)(2,1)S(1)}, bf16[2,4096]{1,0:T(2,128)(2,1)S(1)}, u32[]{:S(2)}, u32[]{:S(2)}) collective-permute-start(bf16[2,4096]{1,0:T(2,128)(2,1)S(1)} %reshape_reshape.3), channel_id=1, source_target_pairs={{0,256},{128,384},{256,0},{384,128},{1,257},{129,385},{257,1},{385... | collective-permute-start | bytes 49160 | tf_op jit(solution)/shard_map/ppermute | solution.py:56
  217.6 9.9 %collective-permute-start.8 = (bf16[2,4096]{1,0:T(2,128)(2,1)S(1)}, bf16[2,4096]{1,0:T(2,128)(2,1)S(1)}, u32[]{:S(2)}, u32[]{:S(2)}) collective-permute-start(bf16[2,4096]{1,0:T(2,128)(2,1)S(1)} %reshape_reshape.3), channel_id=1, source_target_pairs={{0,128},{128,256},{256,384},{384,0},{1,129},{129,257},{257,385},{3... | collective-permute-start | bytes 49160 | tf_op jit(solution)/shard_map/ppermute | solution.py:56
  220.4 8.3 %copy-start.9 = (bf16[128,2048]{1,0:T(8,128)(2,1)S(1)}, bf16[128,2048]{1,0:T(8,128)(2,1)}, u32[]{:S(2)}) copy-start(bf16[128,2048]{1,0:T(8,128)(2,1)} %get-tuple-element.23) | copy-start | bytes 1572868
  220.4 16.6 %all-to-all-start.8 = ((bf16[8,16,2048]{2,1,0:T(8,128)(2,1)}), bf16[8,16,2048]{2,1,0:T(8,128)(2,1)S(1)}, u32[]{:S(2)}, u32[]{:S(2)}) async-start(bf16[8,16,2048]{2,1,0:T(8,128)(2,1)} %broadcast_in_dim.134), calls=%async_computation.8 | async-start | bytes 1048576 | tf_op jit(solution)/shard_map/all_to_all | solution.py:23
Sparse Core Ops, SparseCore 0:
  21.5 35.8 all-gather.1

commit v3 on v2

--- a/solution.py
+++ b/solution.py
@@ -118,7 +118,7 @@
             jax.ShapeDtypeStruct((mem, width), BF),
         ],
         cost_estimate=pl.CostEstimate(
-            flops=48 * tokens * mem * width, bytes_accessed=32 * mem * width, transcendentals=0
+            flops=12 * tokens * mem * width, bytes_accessed=8 * mem * width, transcendentals=0
         ),
     )(core, free, upstream, queries, own, across)
 
@@ -135,17 +135,16 @@
     g_queries, keep_ref[...], send_ref[...] = pair_backward(
         first, q_ref[...], grads, own_ref[...], across_ref[...]
     )
-    ret_ref[:, : 2 * HEAD] = moe
-    ret_ref[:, 2 * HEAD :] = g_queries
+    ret_ref[:tokens] = moe
+    ret_ref[tokens:] = g_queries
 
 
 def routed_backward(spot, sums, gathered, queries, own, across):
     tokens, lanes = queries.shape
     mem, more = own.shape[0], sums.shape[1] - tokens
-    skip = gathered.shape[1] // lanes // 2
     whole = lambda shape: pl.BlockSpec(shape, lambda i, spot: (0,) * len(shape))
-    column = lambda n, base: pl.BlockSpec((n, lanes), lambda i, spot: (0, base + spot[1]))
-    outs = [(tokens, 2 * lanes), (mem, lanes), (mem, lanes), (more, lanes)]
+    column = lambda n: pl.BlockSpec((n, lanes), lambda i, spot: (0, spot[1]))
+    outs = [(2 * tokens, lanes), (mem, lanes), (mem, lanes), (more, lanes)]
     return pl.pallas_call(
         routed_kernel,
         grid_spec=pltpu.PrefetchScalarGridSpec(
@@ -153,10 +152,10 @@
             grid=(1,),
             in_specs=[
                 whole(sums.shape),
-                column(tokens, skip),
+                column(tokens),
                 whole(queries.shape),
-                column(mem, 0),
-                column(mem, 0),
+                column(mem),
+                column(mem),
             ],
             out_specs=[whole(shape) for shape in outs],
         ),
@@ -164,6 +163,40 @@
             jax.ShapeDtypeStruct(shape, dtype) for shape, dtype in zip(outs, (BF, BF, BF, F32))
         ],
     )(spot, sums, gathered, queries, own, across)
+
+
+def pick_kernel(counts_ref, ids_ref, *refs):
+    parts, (rows_ref, place_ref) = refs[:-2], refs[-2:]
+    slots, tokens = place_ref.shape
+    slot = lax.broadcasted_iota(jnp.int32, (slots, tokens), 0)
+    expert, order = slot // GCAP, slot % GCAP
+    count = jnp.zeros((slots, tokens), jnp.int32)
+    for e in range(slots // GCAP):
+        count = jnp.where(expert == e, counts_ref[0, e], count)
+    named = ids_ref[...] == expert
+    earlier = lax.broadcasted_iota(jnp.int32, (tokens, tokens), 0)
+    earlier = (earlier < lax.broadcasted_iota(jnp.int32, (tokens, tokens), 1)).astype(BF)
+    rank = dot(named.astype(BF), earlier).astype(jnp.int32)
+    place = (named & (rank == order) & (rank < count)).astype(BF)
+    place_ref[...] = place
+    width = parts[0].shape[1]
+    for i, part in enumerate(parts):
+        rows_ref[:, i * width : (i + 1) * width] = dot(place, part[...]).astype(BF)
+    rows_ref[:, len(parts) * width :] = count.astype(F32).astype(BF)
+
+
+def pick_rows(counts, ids, parts, slots):
+    tokens, width = parts[0].shape
+    vmem = pl.BlockSpec(memory_space=pltpu.VMEM)
+    return pl.pallas_call(
+        pick_kernel,
+        in_specs=[pl.BlockSpec(memory_space=pltpu.SMEM)] + [vmem] * (1 + len(parts)),
+        out_specs=[vmem, vmem],
+        out_shape=[
+            jax.ShapeDtypeStruct((slots, len(parts) * width + tokens), BF),
+            jax.ShapeDtypeStruct((slots, tokens), BF),
+        ],
+    )(counts, ids, *parts)
 
 
 def per_device(
@@ -176,18 +209,13 @@
     mine, core, depth = lax.axis_index("y"), lax.axis_index("c"), lax.axis_index("z")
     first = core == 0
     own_memory = lax.all_gather(jnp.where(first, mem_keys, mem_values), "y", axis=0, tiled=True)
-    across_memory = other_core(own_memory)
 
     experts = jnp.arange(window, dtype=jnp.int32)
-    onehot = (expert_ids[:, None] == experts[None, :]).astype(jnp.int32)
-    rank = jnp.sum((jnp.cumsum(onehot, axis=0) - 1) * onehot, axis=1)
-    limit = jnp.sum(onehot * send_counts, axis=1)
-    slot = jnp.where(rank < limit, expert_ids * GCAP + rank, -1)
     slot_ids = jnp.arange(slots, dtype=jnp.int32)
-    place = (slot_ids[:, None] == slot[None, :]).astype(BF)
-    payload = [dot(place, part).astype(BF) for part in (queries, states, upstream)]
-    flags = jnp.broadcast_to(jnp.repeat(send_counts[0], GCAP).astype(BF)[:, None], (slots, 128))
-    group = spread(jnp.concatenate(payload + [flags], axis=1), "y")
+    picked, place = pick_rows(
+        send_counts, expert_ids.reshape(1, tokens), (queries, states, upstream), slots
+    )
+    group = spread(picked, "y")
 
     counts = group[:, 3 * width].reshape(window, slots)[:, ::GCAP].astype(jnp.int32)
     offsets = jnp.cumsum(counts, axis=0).astype(jnp.int32) - counts
@@ -199,11 +227,17 @@
     filled = jnp.sum(pack.astype(F32), axis=1)
     routed = dot(pack, group[:, : 3 * width]).astype(BF)
     own_target = lax.dynamic_slice_in_dim(target, mine * slots, slots, 0)
-    steps_back = (mine - slot_ids // GCAP + window) % window * GCAP + slot_ids % GCAP
-    own = (own_target[:, None] == steps_back[None, :]).astype(BF)
+    own = (own_target[:, None] == slot_ids[None, :]).astype(BF)
     place_back = dot(place, own, 0, 0)
     taken = jnp.sum(place_back, axis=1, keepdims=True)
     place_back = place_back.astype(BF)
+
+    here = lax.dynamic_slice_in_dim(routed, mine * GCAP, GCAP, 0)
+    depths = lax.axis_size("z")
+    copies = jnp.broadcast_to(here[None, :, 2 * width :], (depths, GCAP, width))
+    level = exchange(jnp.concatenate([copies, head_pairs(here[:, :width])], axis=2), "z")
+    level = level.reshape(-1, level.shape[2])
+    level_grads, routed_queries = level[:, :width], level[:, width:]
 
     in_head = jnp.arange(heads)[:, None] == (jnp.arange(width) // HEAD)[None, :]
     by_head = jnp.where(in_head[:, None, :], routed[None, :, :width], 0).reshape(-1, width)
@@ -215,7 +249,7 @@
     part = jnp.sum(jnp.where(in_head[:, None, :], part, 0.0), axis=0)
     tops, totals = top.reshape(heads, slots).T, total.reshape(heads, slots).T
     pad = jnp.zeros((slots, 128 - 2 * heads), F32)
-    parts = exchange(jnp.concatenate([part, tops, totals, pad], axis=1), "y")
+    parts = exchange(after(jnp.concatenate([part, tops, totals, pad], axis=1), level), "y")
     parts = parts.reshape(window, GCAP, -1)
     tops, totals = parts[:, :, width : width + heads], parts[:, :, width + heads : width + 2 * heads]
     share = jnp.exp(tops - jnp.max(tops, axis=0))
@@ -224,16 +258,12 @@
         share.reshape(-1, heads), in_head.astype(F32), precision=lax.Precision.HIGHEST
     ).reshape(window, GCAP, width)
     attended = jnp.sum(parts[:, :, :width] * share, axis=0)
-    here = lax.dynamic_slice_in_dim(routed, mine * GCAP, GCAP, 0)
     here_filled = lax.dynamic_slice_in_dim(filled, mine * GCAP, GCAP, 0)
     row = (here[:, width : 2 * width].astype(F32) + attended) * here_filled[:, None]
-    pair = jnp.concatenate([row.astype(BF), here[:, 2 * width :]], axis=1)
-
-    copies = jnp.broadcast_to(pair[None], (lax.axis_size("z"),) + pair.shape)
-    level = exchange(jnp.concatenate([copies, head_pairs(here[:, :width])], axis=2), "z")
-    level = level.reshape(-1, level.shape[2])
-    routed_queries = level[:, 2 * width :]
-    level = level[:, : 2 * width]
+    row = row.astype(BF)
+    across_memory = other_core(after(own_memory, row))
+
+    level_rows = spread(row, "z")
 
     bulk_queries, keep, send = bulk_backward(
         core.reshape(1).astype(jnp.int32),
@@ -243,12 +273,14 @@
         own_memory,
         across_memory,
     )
+    level = jnp.concatenate([level_rows, level_grads], axis=1)
     near = spread(after(level, send), "x")
-    bulk = (keep.astype(F32) + other_core(send).astype(F32)).astype(BF)
-    far = other_core(after(near, bulk))
+    sent = jnp.concatenate([other_core(part) for part in jnp.split(send, 2, axis=0)], axis=0)
+    bulk = (keep.astype(F32) + sent.astype(F32)).astype(BF)
     own_rows = mem_keys.shape[0]
     ahead = lambda d: lax.dynamic_slice_in_dim(bulk, (mine + d) % window * own_rows, own_rows, 0)
     bulk = sum(part.astype(F32) for part in shifts(ahead)).astype(BF)
+    far = other_core(after(near, bulk))
     weight_in, weight_out = w_in[0], w_out[0]
 
     def expert(block):
@@ -272,26 +304,36 @@
     returned, keep, send, bulk = routed_backward(
         jnp.stack([core, depth]).astype(jnp.int32),
         joined,
-        level,
+        level_grads,
         routed_queries,
         own_memory,
         across_memory,
     )
 
     memory = (keep.astype(F32) + other_core(send).astype(F32)).astype(BF)
-    memory = (collect(memory, ("y", "x")) + bulk).astype(BF)
-    copies = jnp.broadcast_to(memory[None], (lax.axis_size("z"),) + memory.shape)
-    returned = returned.reshape(copies.shape[0], 2 * GCAP, 2 * HEAD)
-    joined = exchange(jnp.concatenate([copies, returned], axis=1), "z")
-    memory, returned = joined[:, : memory.shape[0]], joined[:, memory.shape[0] :]
-    returned = rows_of(returned).reshape(GCAP, 2 * width)
-    returned = jnp.concatenate(shifts(lambda d: returned), axis=0)
+    blocks = window * parts_of_x
+    copies = jnp.broadcast_to(returned[None], (blocks,) + returned.shape)
+    joined = exchange(
+        jnp.concatenate([memory.reshape(blocks, -1, 2 * HEAD), copies], axis=1), ("y", "x")
+    )
+    rows_of_x = joined.shape[1] - returned.shape[0]
+    memory = (jnp.sum(joined[:, :rows_of_x].astype(F32), axis=0) + bulk).astype(BF)
+    returned = joined[:, rows_of_x:].reshape((window, parts_of_x) + returned.shape)
+    returned = lax.dynamic_index_in_dim(returned, lax.axis_index("x"), 1, False)
+    returned = returned.reshape(window, 2, depths, GCAP, 2 * HEAD).transpose(2, 0, 1, 3, 4)
+    copies = jnp.broadcast_to(memory[None], (depths,) + memory.shape)
+    joined = exchange(
+        jnp.concatenate([copies, returned.reshape(depths, -1, 2 * HEAD)], axis=1), "z"
+    )
+    memory, returned = joined[:, :rows_of_x], rows_of(joined[:, rows_of_x:])
+    returned = returned.reshape(window, 2, GCAP, width)
+    moe_rows, query_rows = returned[:, 0].reshape(slots, width), returned[:, 1].reshape(slots, width)
     memory = spread(rows_of(memory), ("x", "c")).reshape(parts_of_x, 2, -1, width)
     grad_keys = memory[:, 0].reshape(own_rows, width)
     grad_values = memory[:, 1].reshape(own_rows, width)
-    moe_grad = dot(place_back, returned[:, :width])
+    moe_grad = dot(place_back, moe_rows)
     grad_states = (upstream.astype(F32) + moe_grad).astype(BF)
-    grad_queries = jnp.where(taken > 0, dot(place_back, returned[:, width:]).astype(BF), bulk_queries)
+    grad_queries = jnp.where(taken > 0, dot(place_back, query_rows).astype(BF), bulk_queries)
     return grad_states, grad_queries, grad_keys, grad_values, grad_in[None], grad_out[None]
 
 

time: 246 us -> 244 us (level)
  matrix products: 14 us -> 8.47 us
  local copies, waits for them, and re-layouts: 12.1 us -> 16.9 us
  waiting for transfers between devices: 78.3 us -> 73.9 us
  Pallas kernels: 11.6 us -> 14.2 us
    all_gather x1, waiting for transfers between devices: 22 us -> 0.02 us  [per_device(): lax.all_gather(jnp.where(first, mem_keys, mem_values), 'y', axis=0, tiled...]
    all_to_all x8 -> x9, starting transfers between devices: 49.4 us -> 58 us  [exchange(): return lax.all_to_all(values, axes, split_axis=0, concat_axis=0, tiled=True)]
    all_to_all x8 -> x9, waiting for transfers between devices: 49.3 us -> 57.7 us  [exchange(): return lax.all_to_all(values, axes, split_axis=0, concat_axis=0, tiled=True)]
    ppermute x6 -> x3, starting transfers between devices: 16.4 us -> 8.3 us  [shifts(): lax.ppermute(pick(d), 'y', moves[d])]
    ppermute x6 -> x3, waiting for transfers between devices: 6.11 us -> 11.9 us  [shifts(): lax.ppermute(pick(d), 'y', moves[d])]
    dot_general x19 -> x16, matrix products: 13.8 us -> 8.21 us  [dot(): lax.dot_general(left, right, (((left_dim,), (right_dim,)), ((), ())), pre...]
    ppermute x5 -> x6, waiting for transfers between devices: 0.83 us -> 4.21 us  [other_core(): return lax.ppermute(values, 'c', [(0, 1), (1, 0)])]
    pallas_call x0 -> x1, Pallas kernels: none -> 2.51 us  [pick_rows(): pl.pallas_call(pick_kernel, in_specs=[pl.BlockSpec(memory_space=pltpu.SME...]
  transfers between devices with their start and end apart: 20 -> 19, of which waited for: 11 -> 13; matrix products, arithmetic and copies ran while one was open for 9% -> 8% of each run, Pallas kernels for 4% -> 4%
where the time goes in v3:
time: 244 us; the launch traced here: 242 us
  starting transfers between devices  89.9 us (37%)
  waiting for transfers between devices  73.9 us (30%)
  local copies, waits for them, and re-layouts  16.9 us (7%)
  blocking collectives  15.5 us (6%)
  between operations  14.7 us (6%)
  Pallas kernels  14.2 us (6%)
  other arithmetic  8.87 us (4%)
  matrix products  8.47 us (3%)
    all_to_all x9, starting transfers between devices, exchange(): return lax.all_to_all(values, axes, split_axis=0, concat_axis=0, tiled=True)  58 us
    all_to_all x9, waiting for transfers between devices, exchange(): return lax.all_to_all(values, axes, split_axis=0, concat_axis=0, tiled=True)  57.7 us
    ppermute x6, starting transfers between devices, other_core(): return lax.ppermute(values, 'c', [(0, 1), (1, 0)])  23.6 us
    all_to_all x1, blocking collectives, exchange(): return lax.all_to_all(values, axes, split_axis=0, concat_axis=0, tiled=True)  15.5 us
    ppermute x3, waiting for transfers between devices, shifts(): lax.ppermute(pick(d), 'y', moves[d])  11.9 us
    pallas_call x1, Pallas kernels, bulk_backward(): pl.pallas_call(bulk_kernel, grid=(width // block,), in_specs=[pl.BlockSpe...  8.81 us
    ppermute x3, starting transfers between devices, shifts(): lax.ppermute(pick(d), 'y', moves[d])  8.3 us
    dot_general x16, matrix products, dot(): lax.dot_general(left, right, (((left_dim,), (right_dim,)), ((), ())), pre...  8.21 us
  transfers between devices with their start and end apart: 19, of which 13 were waited for; matrix products, arithmetic and copies ran while one was open for 8% of the time, Pallas kernels for 4%

profile of v3, /device:TPU:1, one launch (start us, length us, event | category | flops | bytes accessed | tf_op | source)
XLA Modules:
  0.0 242.3 jit_solution(14763776787517081273)
XLA Ops:
  7.2 2.5 %shard_map.136 = (bf16[8,6272]{1,0:T(8,128)(2,1)}, bf16[8,128]{1,0:T(8,128)(2,1)}) custom-call(s32[1,4]{1,0:T(1,128)} %counts_ref.1, s32[1,128]{1,0:T(1,128)} %bitcast.107, bf16[128,2048]{1,0:T(8,128)(2,1)} %q_ref.1, bf16[128,2048]{1,0:T(8,128)(2,1)} %refs_1_.1, bf16[128,2048]{1,0:T(8,128)(2,1)} %up_ref.1), custom_call_target="tpu_custom_call" | custom-call | tf_op jit(solution)/shard_map/pallas_call | solution.py:191
  9.7 1.7 broadcast_in_dim.63
  11.4 5.0 %all-to-all-start = ((bf16[4,8,6272]{2,1,0:T(8,128)(2,1)}), bf16[4,8,6272]{2,1,0:T(8,128)(2,1)S(1)}, u32[]{:S(2)}, u32[]{:S(2)}) async-start(bf16[4,8,6272]{2,1,0:T(8,128)(2,1)} %broadcast_in_dim.63), calls=%async_computation | async-start | bytes 802816 | tf_op jit(solution)/shard_map/all_to_all | solution.py:23
  16.4 0.7 broadcast_select_fusion.1
  17.2 5.5 %all-to-all-done = bf16[4,8,6272]{2,1,0:T(8,128)(2,1)S(1)} async-done(((bf16[4,8,6272]{2,1,0:T(8,128)(2,1)}), bf16[4,8,6272]{2,1,0:T(8,128)(2,1)S(1)}, u32[]{:S(2)}, u32[]{:S(2)}) %all-to-all-start) | async-done | bytes 401440 | tf_op jit(solution)/shard_map/all_to_all | solution.py:23
  23.6 0.8 pad_maximum_fusion.3
  24.4 15.6 %all-to-all-start.1 = ((bf16[16,2,2176]{2,1,0:T(2,128)(2,1)}), bf16[16,2,2176]{2,1,0:T(2,128)(2,1)S(1)}, u32[]{:S(2)}, u32[]{:S(2)}) async-start(bf16[16,2,2176]{2,1,0:T(2,128)(2,1)} %pad_maximum_fusion.3), calls=%async_computation.1 | async-start | bytes 278528 | tf_op jit(solution)/shard_map/all_to_all | solution.py:23
  40.9 0.5 fusion.6
  41.5 10.5 %all-to-all-done.1 = bf16[16,2,2176]{2,1,0:T(2,128)(2,1)S(1)} async-done(((bf16[16,2,2176]{2,1,0:T(2,128)(2,1)}), bf16[16,2,2176]{2,1,0:T(2,128)(2,1)S(1)}, u32[]{:S(2)}, u32[]{:S(2)}) %all-to-all-start.1) | async-done | bytes 139296 | tf_op jit(solution)/shard_map/all_to_all | solution.py:23
  52.1 0.7 all_to_all.47
  52.8 3.3 %all-to-all-start.2 = ((f32[4,2,2176]{2,1,0:T(2,128)}), f32[4,2,2176]{2,1,0:T(2,128)S(1)}, u32[]{:S(2)}, u32[]{:S(2)}) async-start(f32[4,2,2176]{2,1,0:T(2,128)} %all_to_all.47), calls=%async_computation.2 | async-start | bytes 139264 | tf_op jit(solution)/shard_map/all_to_all | solution.py:23
  56.2 4.3 %all-to-all-done.2 = f32[4,2,2176]{2,1,0:T(2,128)S(1)} async-done(((f32[4,2,2176]{2,1,0:T(2,128)}), f32[4,2,2176]{2,1,0:T(2,128)S(1)}, u32[]{:S(2)}, u32[]{:S(2)}) %all-to-all-start.2) | async-done | bytes 69664 | tf_op jit(solution)/shard_map/all_to_all | solution.py:23
  61.0 7.4 %collective-permute-start = (bf16[256,2048]{1,0:T(8,128)(2,1)}, bf16[256,2048]{1,0:T(8,128)(2,1)S(1)}, u32[]{:S(2)}, u32[]{:S(2)}) collective-permute-start(bf16[256,2048]{1,0:T(8,128)(2,1)} %all-gather.2.cloned.1.call-done.own_ref), channel_id=1, source_target_pairs={{0,1},{1,0},{2,3},{3,2},{4,5},{5,4},{6,7},{7,6},{8,9},{9,8},{10,11... | collective-permute-start | bytes 3145736 | tf_op jit(solution)/shard_map/ppermute | solution.py:60
  68.8 0.7 copy.54.free_ref
  69.6 0.7 broadcast_in_dim.71
  70.3 3.5 %all-to-all-start.3 = ((bf16[16,2,2048]{2,1,0:T(2,128)(2,1)}), bf16[16,2,2048]{2,1,0:T(2,128)(2,1)S(1)}, u32[]{:S(2)}, u32[]{:S(2)}) async-start(bf16[16,2,2048]{2,1,0:T(2,128)(2,1)} %broadcast_in_dim.71), calls=%async_computation.3 | async-start | bytes 262144 | tf_op jit(solution)/shard_map/all_to_all | solution.py:23
  73.8 1.0 copy-done.2
  74.8 8.8 %shard_map.137 = (bf16[128,2048]{1,0:T(8,128)(2,1)}, bf16[256,2048]{1,0:T(8,128)(2,1)}, bf16[256,2048]{1,0:T(8,128)(2,1)}) custom-call(s32[1]{0:T(128)} %bitcast.2.core_ref, bf16[128,1]{1,0:T(8,128)(2,1)} %copy.54.free_ref, bf16[128,2048]{1,0:T(8,128)(2,1)} %up_ref.1, bf16[128,2048]{1,0:T(8,128)(2,1)} %q_ref.1, ...), custom_call_target="tpu_custom_call" | custom-call | flops 805306368 | bytes 4194304 | tf_op jit(solution)/shard_map/pallas_call | solution.py:103
  83.6 2.1 fusion.94
  85.7 2.1 collective-permute-start.2
  87.8 2.3 collective-permute-start.1
  90.2 1.1 broadcast_in_dim.72
  91.3 4.1 %all-to-all-start.4 = ((bf16[4,32,4096]{2,1,0:T(8,128)(2,1)}), bf16[4,32,4096]{2,1,0:T(8,128)(2,1)S(1)}, u32[]{:S(2)}, u32[]{:S(2)}) async-start(bf16[4,32,4096]{2,1,0:T(8,128)(2,1)} %broadcast_in_dim.72), calls=%async_computation.4 | async-start | bytes 2097152 | tf_op jit(solution)/shard_map/all_to_all | solution.py:23
  95.5 0.8 copy-done.9
  96.3 1.6 add_convert_fusion
  97.9 0.8 constant_dynamic-slice_fusion.3
  98.6 2.9 %collective-permute-start.5 = (bf16[64,2048]{1,0:T(8,128)(2,1)}, bf16[64,2048]{1,0:T(8,128)(2,1)S(1)}, u32[]{:S(2)}, u32[]{:S(2)}) collective-permute-start(bf16[64,2048]{1,0:T(8,128)(2,1)} %get-tuple-element.33), channel_id=1, source_target_pairs={{0,384},{128,0},{256,128},{384,256},{1,385},{129,1},{257,129},{385... | collective-permute-start | bytes 786440 | tf_op jit(solution)/shard_map/ppermute | solution.py:56
  101.5 3.0 %collective-permute-start.4 = (bf16[64,2048]{1,0:T(8,128)(2,1)S(1)}, bf16[64,2048]{1,0:T(8,128)(2,1)S(1)}, u32[]{:S(2)}, u32[]{:S(2)}) collective-permute-start(bf16[64,2048]{1,0:T(8,128)(2,1)S(1)} %get-tuple-element.34), channel_id=1, source_target_pairs={{0,256},{128,384},{256,0},{384,128},{1,257},{129,385},{257,1},{385... | collective-permute-start | bytes 786440 | tf_op jit(solution)/shard_map/ppermute | solution.py:56
  104.5 2.4 collective-permute-start.3
  107.0 1.2 collective-permute-done.5
  108.2 3.8 %collective-permute-done.4 = bf16[64,2048]{1,0:T(8,128)(2,1)S(1)} collective-permute-done((bf16[64,2048]{1,0:T(8,128)(2,1)S(1)}, bf16[64,2048]{1,0:T(8,128)(2,1)S(1)}, u32[]{:S(2)}, u32[]{:S(2)}) %collective-permute-start.4) | collective-permute-done | bytes 262176 | tf_op jit(solution)/shard_map/ppermute | solution.py:56
  111.9 7.0 %collective-permute-done.3 = bf16[64,2048]{1,0:T(8,128)(2,1)} collective-permute-done((bf16[64,2048]{1,0:T(8,128)(2,1)S(1)}, bf16[64,2048]{1,0:T(8,128)(2,1)}, u32[]{:S(2)}, u32[]{:S(2)}) %collective-permute-start.3) | collective-permute-done | bytes 262176 | tf_op jit(solution)/shard_map/ppermute | solution.py:56
  118.9 1.8 add_convert_fusion.2
  120.7 2.4 collective-permute-start.6
  123.1 2.3 collective-permute-done.6
  125.7 1.3 fusion.53
  127.3 2.3 collective-permute-start.7
  130.3 0.9 collective-permute-done.7
  131.5 15.5 %all_to_all.68 = bf16[4,48,2048]{2,1,0:T(8,128)(2,1)S(1)} all-to-all(bf16[4,48,2048]{2,1,0:T(8,128)(2,1)S(1)} %pad_maximum_fusion), channel_id=1, replica_groups=mesh['y'=4,'z'=16,'x'=4,'c'=2] {'x'}, dimensions={0} | all-to-all | bytes 1572864 | tf_op jit(solution)/shard_map/all_to_all | solution.py:23
  147.1 0.7 bitcast_bitcast_fusion
  147.9 11.5 %all-to-all-start.6 = ((bf16[16,48,128]{2,1,0:T(8,128)(2,1)}), bf16[16,48,128]{2,1,0:T(8,128)(2,1)S(1)}, u32[]{:S(2)}, u32[]{:S(2)}) async-start(bf16[16,48,128]{2,1,0:T(8,128)(2,1)} %bitcast_bitcast_fusion), calls=%async_computation.6 | async-start | bytes 393216 | tf_op jit(solution)/shard_map/all_to_all | solution.py:23
  159.4 0.6 pad_add_fusion.spot_ref
  160.0 1.3 slice.107.q_ref
  161.3 10.4 %all-to-all-done.6.sums_ref = bf16[16,48,128]{2,1,0:T(8,128)(2,1)S(1)} async-done(((bf16[16,48,128]{2,1,0:T(8,128)(2,1)}), bf16[16,48,128]{2,1,0:T(8,128)(2,1)S(1)}, u32[]{:S(2)}, u32[]{:S(2)}) %all-to-all-start.6) | async-done | bytes 196640 | tf_op jit(solution)/shard_map/all_to_all | solution.py:23
  171.7 0.7 copy-done.6
  172.4 2.9 %shard_map.138 = (bf16[64,128]{1,0:T(8,128)(2,1)}, bf16[256,128]{1,0:T(8,128)(2,1)}, bf16[256,128]{1,0:T(8,128)(2,1)}, f32[16,128]{1,0:T(8,128)}) custom-call(s32[2]{0:T(128)} %pad_add_fusion.spot_ref, bf16[16,48,128]{2,1,0:T(8,128)(2,1)} %copy-done.6, bf16[32,2048]{1,0:T(8,128)(2,1)} %copy-done.3, bf16[32,128]{1,0:T(8,128)(2,1)} %slice.107.q_ref, ...), custom_call_target="tpu_custom_call" | custom-call | tf_op jit(solution)/shard_map/pallas_call | solution.py:148
  175.2 7.2 %collective-permute-start.8 = (bf16[256,128]{1,0:T(8,128)(2,1)}, bf16[256,128]{1,0:T(8,128)(2,1)S(1)}, u32[]{:S(2)}, u32[]{:S(2)}) collective-permute-start(bf16[256,128]{1,0:T(8,128)(2,1)} %get-tuple-element.28), channel_id=1, source_target_pairs={{0,1},{1,0},{2,3},{3,2},{4,5},{5,4},{6,7},{7,6},{8,9},{9,8},{10,11... | collective-permute-start | bytes 196616 | tf_op jit(solution)/shard_map/ppermute | solution.py:60
  182.5 1.1 collective-permute-done.8
  183.6 0.9 add_convert_fusion.3
  184.4 0.8 broadcast_in_dim.76
  185.2 0.7 pad_maximum_fusion.1
  185.9 3.5 %all-to-all-start.7 = ((bf16[16,80,128]{2,1,0:T(8,128)(2,1)}), bf16[16,80,128]{2,1,0:T(8,128)(2,1)S(1)}, u32[]{:S(2)}, u32[]{:S(2)}) async-start(bf16[16,80,128]{2,1,0:T(8,128)(2,1)} %pad_maximum_fusion.1), calls=%async_computation.7 | async-start | bytes 655360 | tf_op jit(solution)/shard_map/all_to_all | solution.py:23
  189.8 8.7 %all-to-all-done.7 = bf16[16,80,128]{2,1,0:T(8,128)(2,1)S(1)} async-done(((bf16[16,80,128]{2,1,0:T(8,128)(2,1)}), bf16[16,80,128]{2,1,0:T(8,128)(2,1)S(1)}, u32[]{:S(2)}, u32[]{:S(2)}) %all-to-all-start.7) | async-done | bytes 327712 | tf_op jit(solution)/shard_map/all_to_all | solution.py:23
  198.6 0.7 copy.57
  199.3 4.4 %all-to-all-start.8 = ((bf16[16,32,128]{2,1,0:T(8,128)(2,1)}), bf16[16,32,128]{2,1,0:T(8,128)(2,1)S(1)}, u32[]{:S(2)}, u32[]{:S(2)}) async-start(bf16[16,32,128]{2,1,0:T(8,128)(2,1)} %copy.57), calls=%async_computation.8 | async-start | bytes 262144 | tf_op jit(solution)/shard_map/all_to_all | solution.py:23
  203.9 1.0 fusion.5
  204.9 1.0 fusion.4
  205.8 9.8 %all-to-all-done.8 = bf16[16,32,128]{2,1,0:T(8,128)(2,1)S(1)} async-done(((bf16[16,32,128]{2,1,0:T(8,128)(2,1)}), bf16[16,32,128]{2,1,0:T(8,128)(2,1)S(1)}, u32[]{:S(2)}, u32[]{:S(2)}) %all-to-all-start.8) | async-done | bytes 131104 | tf_op jit(solution)/shard_map/all_to_all | solution.py:23
  215.8 1.1 fusion.1
  217.3 0.8 broadcast_in_dim.128
  218.1 7.0 %all-to-all-start.9 = ((bf16[8,16,2048]{2,1,0:T(8,128)(2,1)}), bf16[8,16,2048]{2,1,0:T(8,128)(2,1)S(1)}, u32[]{:S(2)}, u32[]{:S(2)}) async-start(bf16[8,16,2048]{2,1,0:T(8,128)(2,1)} %broadcast_in_dim.128), calls=%async_computation.9 | async-start | bytes 1048576 | tf_op jit(solution)/shard_map/all_to_all | solution.py:23
  225.1 0.9 broadcast_select_fusion
  226.1 8.6 %all-to-all-done.9 = bf16[8,16,2048]{2,1,0:T(8,128)(2,1)S(1)} async-done(((bf16[8,16,2048]{2,1,0:T(8,128)(2,1)}), bf16[8,16,2048]{2,1,0:T(8,128)(2,1)S(1)}, u32[]{:S(2)}, u32[]{:S(2)}) %all-to-all-start.9) | async-done | bytes 524320 | tf_op jit(solution)/shard_map/all_to_all | solution.py:23
  234.6 0.8 fusion.95
  (98 shorter events, 6.0 us)
Async XLA Ops:
  7.2 118.2 %copy-start = (bf16[1,80,2048]{2,1,0:T(8,128)(2,1)S(1)}, bf16[1,80,2048]{2,1,0:T(8,128)(2,1)}, u32[]{:S(2)}) copy-start(bf16[1,80,2048]{2,1,0:T(8,128)(2,1)} %param.15) | copy-start | bytes 983044
  9.7 6.7 %copy-start.10 = (bf16[64,2048]{1,0:T(8,128)(2,1)S(1)}, bf16[64,2048]{1,0:T(8,128)(2,1)}, u32[]{:S(2)}) copy-start(bf16[64,2048]{1,0:T(8,128)(2,1)} %param.11) | copy-start | bytes 786436
  9.7 6.7 %copy-start.11 = (bf16[64,2048]{1,0:T(8,128)(2,1)S(1)}, bf16[64,2048]{1,0:T(8,128)(2,1)}, u32[]{:S(2)}) copy-start(bf16[64,2048]{1,0:T(8,128)(2,1)} %param.12) | copy-start | bytes 786436
  11.4 11.3 %all-to-all-start = ((bf16[4,8,6272]{2,1,0:T(8,128)(2,1)}), bf16[4,8,6272]{2,1,0:T(8,128)(2,1)S(1)}, u32[]{:S(2)}, u32[]{:S(2)}) async-start(bf16[4,8,6272]{2,1,0:T(8,128)(2,1)} %broadcast_in_dim.63), calls=%async_computation | async-start | bytes 802816 | tf_op jit(solution)/shard_map/all_to_all | solution.py:23
  16.4 44.6 %all-gather.2.cloned.1.call-start = ((), (), s32[]{:S(2)}) async-start(), calls=%async_computation.10 | async-start | bytes 1310720 | tf_op jit(solution)/shard_map/all_gather | solution.py:211
  24.4 27.6 %all-to-all-start.1 = ((bf16[16,2,2176]{2,1,0:T(2,128)(2,1)}), bf16[16,2,2176]{2,1,0:T(2,128)(2,1)S(1)}, u32[]{:S(2)}, u32[]{:S(2)}) async-start(bf16[16,2,2176]{2,1,0:T(2,128)(2,1)} %pad_maximum_fusion.3), calls=%async_computation.1 | async-start | bytes 278528 | tf_op jit(solution)/shard_map/all_to_all | solution.py:23
  40.9 27.7 %copy-start.14 = (bf16[8,128]{1,0:T(8,128)(2,1)S(1)}, bf16[8,128]{1,0:T(8,128)(2,1)}, u32[]{:S(2)}) copy-start(bf16[8,128]{1,0:T(8,128)(2,1)} %get-tuple-element.19) | copy-start | bytes 6148
  52.1 38.0 %copy-start.7 = (bf16[32,2176]{1,0:T(8,128)(2,1)}, bf16[32,2176]{1,0:T(8,128)(2,1)S(1)}, u32[]{:S(2)}) copy-start(bf16[32,2176]{1,0:T(8,128)(2,1)S(1)} %reshape.212) | copy-start | bytes 417796
  52.8 7.8 %all-to-all-start.2 = ((f32[4,2,2176]{2,1,0:T(2,128)}), f32[4,2,2176]{2,1,0:T(2,128)S(1)}, u32[]{:S(2)}, u32[]{:S(2)}) async-start(f32[4,2,2176]{2,1,0:T(2,128)} %all_to_all.47), calls=%async_computation.2 | async-start | bytes 139264 | tf_op jit(solution)/shard_map/all_to_all | solution.py:23
  61.0 12.8 %collective-permute-start = (bf16[256,2048]{1,0:T(8,128)(2,1)}, bf16[256,2048]{1,0:T(8,128)(2,1)S(1)}, u32[]{:S(2)}, u32[]{:S(2)}) collective-permute-start(bf16[256,2048]{1,0:T(8,128)(2,1)} %all-gather.2.cloned.1.call-done.own_ref), channel_id=1, source_target_pairs={{0,1},{1,0},{2,3},{3,2},{4,5},{5,4},{6,7},{7,6},{8,9},{9,8},{10,11... | collective-permute-start | bytes 3145736 | tf_op jit(solution)/shard_map/ppermute | solution.py:60
  70.3 19.8 %all-to-all-start.3 = ((bf16[16,2,2048]{2,1,0:T(2,128)(2,1)}), bf16[16,2,2048]{2,1,0:T(2,128)(2,1)S(1)}, u32[]{:S(2)}, u32[]{:S(2)}) async-start(bf16[16,2,2048]{2,1,0:T(2,128)(2,1)} %broadcast_in_dim.71), calls=%async_computation.3 | async-start | bytes 262144 | tf_op jit(solution)/shard_map/all_to_all | solution.py:23
  73.8 1.0 copy-start.2
  85.7 9.8 %collective-permute-start.2 = (bf16[128,2048]{1,0:T(8,128)(2,1)}, bf16[128,2048]{1,0:T(8,128)(2,1)S(1)}, u32[]{:S(2)}, u32[]{:S(2)}) collective-permute-start(bf16[128,2048]{1,0:T(8,128)(2,1)} %get-tuple-element.36), channel_id=1, source_target_pairs={{0,1},{1,0},{2,3},{3,2},{4,5},{5,4},{6,7},{7,6},{8,9},{9,8},{10,11... | collective-permute-start | bytes 1572872 | tf_op jit(solution)/shard_map/ppermute | solution.py:60
  87.8 7.7 %collective-permute-start.1 = (bf16[128,2048]{1,0:T(8,128)(2,1)S(1)}, bf16[128,2048]{1,0:T(8,128)(2,1)}, u32[]{:S(2)}, u32[]{:S(2)}) collective-permute-start(bf16[128,2048]{1,0:T(8,128)(2,1)S(1)} %get-tuple-element.35), channel_id=1, source_target_pairs={{0,1},{1,0},{2,3},{3,2},{4,5},{5,4},{6,7},{7,6},{8,9},{9,8},{10,11... | collective-permute-start | bytes 1572872 | tf_op jit(solution)/shard_map/ppermute | solution.py:60
  90.1 1.2 copy-start.3
  91.3 4.9 %copy-start.4 = (bf16[256,2048]{1,0:T(8,128)(2,1)S(1)}, bf16[256,2048]{1,0:T(8,128)(2,1)}, u32[]{:S(2)}) copy-start(bf16[256,2048]{1,0:T(8,128)(2,1)} %get-tuple-element.25) | copy-start | bytes 3145732
  91.3 29.4 %all-to-all-start.4 = ((bf16[4,32,4096]{2,1,0:T(8,128)(2,1)}), bf16[4,32,4096]{2,1,0:T(8,128)(2,1)S(1)}, u32[]{:S(2)}, u32[]{:S(2)}) async-start(bf16[4,32,4096]{2,1,0:T(8,128)(2,1)} %broadcast_in_dim.72), calls=%async_computation.4 | async-start | bytes 2097152 | tf_op jit(solution)/shard_map/all_to_all | solution.py:23
  95.5 0.8 copy-start.9
  98.6 9.5 %collective-permute-start.5 = (bf16[64,2048]{1,0:T(8,128)(2,1)}, bf16[64,2048]{1,0:T(8,128)(2,1)S(1)}, u32[]{:S(2)}, u32[]{:S(2)}) collective-permute-start(bf16[64,2048]{1,0:T(8,128)(2,1)} %get-tuple-element.33), channel_id=1, source_target_pairs={{0,384},{128,0},{256,128},{384,256},{1,385},{129,1},{257,129},{385... | collective-permute-start | bytes 786440 | tf_op jit(solution)/shard_map/ppermute | solution.py:56
  101.5 10.4 %collective-permute-start.4 = (bf16[64,2048]{1,0:T(8,128)(2,1)S(1)}, bf16[64,2048]{1,0:T(8,128)(2,1)S(1)}, u32[]{:S(2)}, u32[]{:S(2)}) collective-permute-start(bf16[64,2048]{1,0:T(8,128)(2,1)S(1)} %get-tuple-element.34), channel_id=1, source_target_pairs={{0,256},{128,384},{256,0},{384,128},{1,257},{129,385},{257,1},{385... | collective-permute-start | bytes 786440 | tf_op jit(solution)/shard_map/ppermute | solution.py:56
  104.5 14.3 %collective-permute-start.3 = (bf16[64,2048]{1,0:T(8,128)(2,1)S(1)}, bf16[64,2048]{1,0:T(8,128)(2,1)}, u32[]{:S(2)}, u32[]{:S(2)}) collective-permute-start(bf16[64,2048]{1,0:T(8,128)(2,1)S(1)} %get-tuple-element.32), channel_id=1, source_target_pairs={{0,128},{128,256},{256,384},{384,0},{1,129},{129,257},{257,385},{3... | collective-permute-start | bytes 786440 | tf_op jit(solution)/shard_map/ppermute | solution.py:56
  120.7 4.7 %collective-permute-start.6 = (bf16[128,4096]{1,0:T(8,128)(2,1)S(1)}, bf16[128,4096]{1,0:T(8,128)(2,1)S(1)}, u32[]{:S(2)}, u32[]{:S(2)}) collective-permute-start(bf16[128,4096]{1,0:T(8,128)(2,1)S(1)} %bitcast.88), channel_id=1, source_target_pairs={{0,1},{1,0},{2,3},{3,2},{4,5},{5,4},{6,7},{7,6},{8,9},{9,8},{10,11... | collective-permute-start | bytes 3145736 | tf_op jit(solution)/shard_map/ppermute | solution.py:60
  127.0 2.9 %copy-start.13 = (bf16[1,80,2048]{2,1,0:T(8,128)(2,1)S(1)}, bf16[1,80,2048]{2,1,0:T(8,128)(2,1)}, u32[]{:S(2)}) copy-start(bf16[1,80,2048]{2,1,0:T(8,128)(2,1)} %param.16) | copy-start | bytes 983044
  127.3 3.8 %collective-permute-start.7 = (bf16[128,2048]{1,0:T(8,128)(2,1)S(1)}, bf16[128,2048]{1,0:T(8,128)(2,1)S(1)}, u32[]{:S(2)}, u32[]{:S(2)}) collective-permute-start(bf16[128,2048]{1,0:T(8,128)(2,1)S(1)} %convolution_convert_fusion.2), channel_id=1, source_target_pairs={{0,1},{1,0},{2,3},{3,2},{4,5},{5,4},{6,7},{7,6},{8,9},{9,8},{10,11... | collective-permute-start | bytes 1572872 | tf_op jit(solution)/shard_map/ppermute | solution.py:60
  129.9 1.5 copy-start.5
  147.9 23.9 %all-to-all-start.6 = ((bf16[16,48,128]{2,1,0:T(8,128)(2,1)}), bf16[16,48,128]{2,1,0:T(8,128)(2,1)S(1)}, u32[]{:S(2)}, u32[]{:S(2)}) async-start(bf16[16,48,128]{2,1,0:T(8,128)(2,1)} %bitcast_bitcast_fusion), calls=%async_computation.6 | async-start | bytes 393216 | tf_op jit(solution)/shard_map/all_to_all | solution.py:23
  171.7 0.7 copy-start.6
  175.2 8.3 %collective-permute-start.8 = (bf16[256,128]{1,0:T(8,128)(2,1)}, bf16[256,128]{1,0:T(8,128)(2,1)S(1)}, u32[]{:S(2)}, u32[]{:S(2)}) collective-permute-start(bf16[256,128]{1,0:T(8,128)(2,1)} %get-tuple-element.28), channel_id=1, source_target_pairs={{0,1},{1,0},{2,3},{3,2},{4,5},{5,4},{6,7},{7,6},{8,9},{9,8},{10,11... | collective-permute-start | bytes 196616 | tf_op jit(solution)/shard_map/ppermute | solution.py:60
  185.9 12.5 %all-to-all-start.7 = ((bf16[16,80,128]{2,1,0:T(8,128)(2,1)}), bf16[16,80,128]{2,1,0:T(8,128)(2,1)S(1)}, u32[]{:S(2)}, u32[]{:S(2)}) async-start(bf16[16,80,128]{2,1,0:T(8,128)(2,1)} %pad_maximum_fusion.1), calls=%async_computation.7 | async-start | bytes 655360 | tf_op jit(solution)/shard_map/all_to_all | solution.py:23
  189.5 9.0 %copy-start.12 = (f32[16,128]{1,0:T(8,128)S(1)}, f32[16,128]{1,0:T(8,128)}, u32[]{:S(2)}) copy-start(f32[16,128]{1,0:T(8,128)} %get-tuple-element.30) | copy-start | bytes 24580
  199.3 16.4 %all-to-all-start.8 = ((bf16[16,32,128]{2,1,0:T(8,128)(2,1)}), bf16[16,32,128]{2,1,0:T(8,128)(2,1)S(1)}, u32[]{:S(2)}, u32[]{:S(2)}) async-start(bf16[16,32,128]{2,1,0:T(8,128)(2,1)} %copy.57), calls=%async_computation.8 | async-start | bytes 262144 | tf_op jit(solution)/shard_map/all_to_all | solution.py:23
  204.8 10.9 %copy-start.1 = (bf16[128,2048]{1,0:T(8,128)(2,1)S(1)}, bf16[128,2048]{1,0:T(8,128)(2,1)}, u32[]{:S(2)}) copy-start(bf16[128,2048]{1,0:T(8,128)(2,1)} %up_ref.1) | copy-start | bytes 1572868
  216.9 8.2 %copy-start.8 = (bf16[128,2048]{1,0:T(8,128)(2,1)S(1)}, bf16[128,2048]{1,0:T(8,128)(2,1)}, u32[]{:S(2)}) copy-start(bf16[128,2048]{1,0:T(8,128)(2,1)} %get-tuple-element.31) | copy-start | bytes 1572868
  218.1 16.5 %all-to-all-start.9 = ((bf16[8,16,2048]{2,1,0:T(8,128)(2,1)}), bf16[8,16,2048]{2,1,0:T(8,128)(2,1)S(1)}, u32[]{:S(2)}, u32[]{:S(2)}) async-start(bf16[8,16,2048]{2,1,0:T(8,128)(2,1)} %broadcast_in_dim.128), calls=%async_computation.9 | async-start | bytes 1048576 | tf_op jit(solution)/shard_map/all_to_all | solution.py:23
Sparse Core Ops, SparseCore 0:
  19.9 35.8 all-gather.1

commit v4 on v3

--- a/solution.py
+++ b/solution.py
@@ -7,6 +7,7 @@
 
 HEAD = 64
 GCAP = 2
+PIECES = 2
 SCALE = HEAD ** (-0.5)
 BF, F32 = jnp.bfloat16, jnp.float32
 DEVICES = ("y", "z", "x", "c")
@@ -48,12 +49,6 @@
 
 def after(values, *others):
     return lax.optimization_barrier((values,) + others)[0]
-
-
-def shifts(pick):
-    n = lax.axis_size("y")
-    moves = [[(i, (i + d) % n) for i in range(n)] for d in range(n)]
-    return [pick(0)] + [lax.ppermute(pick(d), "y", moves[d]) for d in range(1, n)]
 
 
 def other_core(values):
@@ -85,14 +80,22 @@
     return (g_queries.T * SCALE).astype(BF), keep, send
 
 
-def bulk_kernel(core_ref, free_ref, up_ref, q_ref, own_ref, across_ref, gq_ref, keep_ref, send_ref):
+def bulk_kernel(core_ref, free_ref, up_ref, q_ref, own_ref, *refs):
+    across, (gq_ref, keep_ref), sends = refs[:PIECES], refs[PIECES : PIECES + 2], refs[PIECES + 2 :]
     first = core_ref[0] == 0
     free = free_ref[...]
+    rows = own_ref.shape[0] // PIECES
     for pair in range(q_ref.shape[1] // (2 * HEAD)):
         cols = slice(pair * 2 * HEAD, (pair + 1) * 2 * HEAD)
-        gq_ref[:, cols], keep_ref[:, cols], send_ref[:, cols] = pair_backward(
-            first, q_ref[:, cols], up_ref[:, cols] * free, own_ref[:, cols], across_ref[:, cols]
+        gq_ref[:, cols], keep_ref[:, cols], send = pair_backward(
+            first,
+            q_ref[:, cols],
+            up_ref[:, cols] * free,
+            own_ref[:, cols],
+            jnp.concatenate([ref[:, cols] for ref in across], axis=0),
         )
+        for i, ref in enumerate(sends):
+            ref[:, cols] = send[i * rows : (i + 1) * rows]
 
 
 def bulk_backward(core, free, upstream, queries, own, across):
@@ -100,7 +103,8 @@
     mem = own.shape[0]
     block = 512
     column = lambda n: pl.BlockSpec((n, block), lambda i: (0, i))
-    return pl.pallas_call(
+    outs = [tokens, mem] + [mem // PIECES] * PIECES
+    got = pl.pallas_call(
         bulk_kernel,
         grid=(width // block,),
         in_specs=[
@@ -109,18 +113,15 @@
             column(tokens),
             column(tokens),
             column(mem),
-            column(mem),
-        ],
-        out_specs=[column(tokens), column(mem), column(mem)],
-        out_shape=[
-            jax.ShapeDtypeStruct((tokens, width), BF),
-            jax.ShapeDtypeStruct((mem, width), BF),
-            jax.ShapeDtypeStruct((mem, width), BF),
-        ],
+        ]
+        + [column(mem // PIECES)] * PIECES,
+        out_specs=[column(n) for n in outs],
+        out_shape=[jax.ShapeDtypeStruct((n, width), BF) for n in outs],
         cost_estimate=pl.CostEstimate(
             flops=12 * tokens * mem * width, bytes_accessed=8 * mem * width, transcendentals=0
         ),
-    )(core, free, upstream, queries, own, across)
+    )(core, free, upstream, queries, own, *across)
+    return got[0], got[1], got[2:]
 
 
 def routed_kernel(
@@ -143,7 +144,8 @@
     tokens, lanes = queries.shape
     mem, more = own.shape[0], sums.shape[1] - tokens
     whole = lambda shape: pl.BlockSpec(shape, lambda i, spot: (0,) * len(shape))
-    column = lambda n: pl.BlockSpec((n, lanes), lambda i, spot: (0, spot[1]))
+    skip = gathered.shape[1] // lanes // 2
+    column = lambda n, base: pl.BlockSpec((n, lanes), lambda i, spot: (0, base + spot[1]))
     outs = [(2 * tokens, lanes), (mem, lanes), (mem, lanes), (more, lanes)]
     return pl.pallas_call(
         routed_kernel,
@@ -152,10 +154,10 @@
             grid=(1,),
             in_specs=[
                 whole(sums.shape),
-                column(tokens),
+                column(tokens, skip),
                 whole(queries.shape),
-                column(mem),
-                column(mem),
+                column(mem, 0),
+                column(mem, 0),
             ],
             out_specs=[whole(shape) for shape in outs],
         ),
@@ -181,11 +183,14 @@
     place_ref[...] = place
     width = parts[0].shape[1]
     for i, part in enumerate(parts):
-        rows_ref[:, i * width : (i + 1) * width] = dot(place, part[...]).astype(BF)
-    rows_ref[:, len(parts) * width :] = count.astype(F32).astype(BF)
-
-
-def pick_rows(counts, ids, parts, slots):
+        rows = dot(place, part[...]).astype(BF)
+        for copy in range(rows_ref.shape[0]):
+            rows_ref[copy, :, i * width : (i + 1) * width] = rows
+    for copy in range(rows_ref.shape[0]):
+        rows_ref[copy, :, len(parts) * width :] = count.astype(F32).astype(BF)
+
+
+def pick_rows(counts, ids, parts, slots, copies):
     tokens, width = parts[0].shape
     vmem = pl.BlockSpec(memory_space=pltpu.VMEM)
     return pl.pallas_call(
@@ -193,7 +198,7 @@
         in_specs=[pl.BlockSpec(memory_space=pltpu.SMEM)] + [vmem] * (1 + len(parts)),
         out_specs=[vmem, vmem],
         out_shape=[
-            jax.ShapeDtypeStruct((slots, len(parts) * width + tokens), BF),
+            jax.ShapeDtypeStruct((copies, slots, len(parts) * width + tokens), BF),
             jax.ShapeDtypeStruct((slots, tokens), BF),
         ],
     )(counts, ids, *parts)
@@ -213,9 +218,9 @@
     experts = jnp.arange(window, dtype=jnp.int32)
     slot_ids = jnp.arange(slots, dtype=jnp.int32)
     picked, place = pick_rows(
-        send_counts, expert_ids.reshape(1, tokens), (queries, states, upstream), slots
-    )
-    group = spread(picked, "y")
+        send_counts, expert_ids.reshape(1, tokens), (queries, states, upstream), slots, window
+    )
+    group = exchange(picked, "y").reshape(window * slots, -1)
 
     counts = group[:, 3 * width].reshape(window, slots)[:, ::GCAP].astype(jnp.int32)
     offsets = jnp.cumsum(counts, axis=0).astype(jnp.int32) - counts
@@ -232,13 +237,6 @@
     taken = jnp.sum(place_back, axis=1, keepdims=True)
     place_back = place_back.astype(BF)
 
-    here = lax.dynamic_slice_in_dim(routed, mine * GCAP, GCAP, 0)
-    depths = lax.axis_size("z")
-    copies = jnp.broadcast_to(here[None, :, 2 * width :], (depths, GCAP, width))
-    level = exchange(jnp.concatenate([copies, head_pairs(here[:, :width])], axis=2), "z")
-    level = level.reshape(-1, level.shape[2])
-    level_grads, routed_queries = level[:, :width], level[:, width:]
-
     in_head = jnp.arange(heads)[:, None] == (jnp.arange(width) // HEAD)[None, :]
     by_head = jnp.where(in_head[:, None, :], routed[None, :, :width], 0).reshape(-1, width)
     scores = dot(by_head, mem_keys, 1, 1) * SCALE
@@ -249,7 +247,7 @@
     part = jnp.sum(jnp.where(in_head[:, None, :], part, 0.0), axis=0)
     tops, totals = top.reshape(heads, slots).T, total.reshape(heads, slots).T
     pad = jnp.zeros((slots, 128 - 2 * heads), F32)
-    parts = exchange(after(jnp.concatenate([part, tops, totals, pad], axis=1), level), "y")
+    parts = exchange(jnp.concatenate([part, tops, totals, pad], axis=1), "y")
     parts = parts.reshape(window, GCAP, -1)
     tops, totals = parts[:, :, width : width + heads], parts[:, :, width + heads : width + 2 * heads]
     share = jnp.exp(tops - jnp.max(tops, axis=0))
@@ -258,12 +256,20 @@
         share.reshape(-1, heads), in_head.astype(F32), precision=lax.Precision.HIGHEST
     ).reshape(window, GCAP, width)
     attended = jnp.sum(parts[:, :, :width] * share, axis=0)
+    here = lax.dynamic_slice_in_dim(routed, mine * GCAP, GCAP, 0)
     here_filled = lax.dynamic_slice_in_dim(filled, mine * GCAP, GCAP, 0)
     row = (here[:, width : 2 * width].astype(F32) + attended) * here_filled[:, None]
-    row = row.astype(BF)
-    across_memory = other_core(after(own_memory, row))
-
-    level_rows = spread(row, "z")
+    pair = jnp.concatenate([row.astype(BF), here[:, 2 * width :]], axis=1)
+
+    depths = lax.axis_size("z")
+    copies = jnp.broadcast_to(pair[None], (depths,) + pair.shape)
+    level = exchange(jnp.concatenate([copies, head_pairs(here[:, :width])], axis=2), "z")
+    level = level.reshape(-1, level.shape[2])
+    routed_queries = level[:, 2 * width :]
+    level = level[:, : 2 * width]
+    across_memory = [
+        other_core(piece) for piece in jnp.split(after(own_memory, pair), PIECES, axis=0)
+    ]
 
     bulk_queries, keep, send = bulk_backward(
         core.reshape(1).astype(jnp.int32),
@@ -273,15 +279,12 @@
         own_memory,
         across_memory,
     )
-    level = jnp.concatenate([level_rows, level_grads], axis=1)
-    near = spread(after(level, send), "x")
-    sent = jnp.concatenate([other_core(part) for part in jnp.split(send, 2, axis=0)], axis=0)
+    near = spread(after(level, *send), "x")
+    sent = jnp.concatenate([other_core(piece) for piece in send], axis=0)
     bulk = (keep.astype(F32) + sent.astype(F32)).astype(BF)
-    own_rows = mem_keys.shape[0]
-    ahead = lambda d: lax.dynamic_slice_in_dim(bulk, (mine + d) % window * own_rows, own_rows, 0)
-    bulk = sum(part.astype(F32) for part in shifts(ahead)).astype(BF)
     far = other_core(after(near, bulk))
     weight_in, weight_out = w_in[0], w_out[0]
+    parts_of_x = lax.axis_size("x")
 
     def expert(block):
         rows, grads = block[:, :width], block[:, width:]
@@ -295,29 +298,40 @@
     grad_in, grad_out = (near_in + far_in).astype(BF), (near_out + far_out).astype(BF)
 
     back = (near_back + other_core(far_back.astype(BF)).astype(F32)).astype(BF)
-    parts_of_x = lax.axis_size("x")
-    joined = jnp.concatenate(
-        [back.reshape(parts_of_x, -1, width), bulk.reshape(parts_of_x, -1, width)], axis=1
-    )
-    joined = collect(joined.reshape(-1, width), "x").astype(BF)
-    joined = exchange(head_pairs(joined), "z")
+    half = width // 2
+    over_y = lax.psum_scatter(bulk[:, :half], "y", scatter_dimension=0, tiled=True)
+    over_x = bulk[:, half:].reshape(window, parts_of_x, -1, half).transpose(1, 0, 2, 3)
+    over_x = over_x.reshape(parts_of_x, -1, half)
+    over_x = jnp.concatenate(jnp.split(over_x, 2, axis=1), axis=2)
+    rows = back.shape[0] // parts_of_x
+    back = jnp.concatenate([back.reshape(parts_of_x, rows, width), over_x], axis=1)
+    back = collect(back.reshape(-1, width), "x").astype(BF)
+    over_x = jnp.concatenate([back[rows:, :half], back[rows:, half:]], axis=0)
+    bulk = jnp.concatenate([head_pairs(over_y), head_pairs(over_x)], axis=0)
+    joined = exchange(jnp.concatenate([head_pairs(back[:rows]), bulk], axis=1), "z")
     returned, keep, send, bulk = routed_backward(
         jnp.stack([core, depth]).astype(jnp.int32),
         joined,
-        level_grads,
+        level,
         routed_queries,
         own_memory,
-        across_memory,
-    )
-
-    memory = (keep.astype(F32) + other_core(send).astype(F32)).astype(BF)
+        jnp.concatenate(across_memory, axis=0),
+    )
+
+    memory = keep.astype(F32) + other_core(send).astype(F32)
+    memory = memory.reshape(window, parts_of_x, -1, 2 * HEAD)
+    bulk = bulk.reshape(window, -1, 2 * HEAD)
+    of_y = (depth < depths // 2) & (experts == mine)
+    of_x = (depth >= depths // 2) & (jnp.arange(parts_of_x) == lax.axis_index("x"))
+    memory = memory + jnp.where(of_y[:, None, None, None], bulk[None], 0.0)
+    memory = (memory + jnp.where(of_x[None, :, None, None], bulk[:, None], 0.0)).astype(BF)
     blocks = window * parts_of_x
     copies = jnp.broadcast_to(returned[None], (blocks,) + returned.shape)
     joined = exchange(
         jnp.concatenate([memory.reshape(blocks, -1, 2 * HEAD), copies], axis=1), ("y", "x")
     )
     rows_of_x = joined.shape[1] - returned.shape[0]
-    memory = (jnp.sum(joined[:, :rows_of_x].astype(F32), axis=0) + bulk).astype(BF)
+    memory = jnp.sum(joined[:, :rows_of_x].astype(F32), axis=0).astype(BF)
     returned = joined[:, rows_of_x:].reshape((window, parts_of_x) + returned.shape)
     returned = lax.dynamic_index_in_dim(returned, lax.axis_index("x"), 1, False)
     returned = returned.reshape(window, 2, depths, GCAP, 2 * HEAD).transpose(2, 0, 1, 3, 4)
@@ -329,8 +343,7 @@
     returned = returned.reshape(window, 2, GCAP, width)
     moe_rows, query_rows = returned[:, 0].reshape(slots, width), returned[:, 1].reshape(slots, width)
     memory = spread(rows_of(memory), ("x", "c")).reshape(parts_of_x, 2, -1, width)
-    grad_keys = memory[:, 0].reshape(own_rows, width)
-    grad_values = memory[:, 1].reshape(own_rows, width)
+    grad_keys, grad_values = memory[:, 0].reshape(-1, width), memory[:, 1].reshape(-1, width)
     moe_grad = dot(place_back, moe_rows)
     grad_states = (upstream.astype(F32) + moe_grad).astype(BF)
     grad_queries = jnp.where(taken > 0, dot(place_back, query_rows).astype(BF), bulk_queries)

time: 244 us -> 238 us (0.975)
  blocking collectives: 15.5 us -> 0 us
  waiting for transfers between devices: 73.9 us -> 84.5 us
  other arithmetic: 8.87 us -> 12.1 us
  local copies, waits for them, and re-layouts: 16.9 us -> 13.9 us
    reduce_scatter x0 -> x1, waiting for transfers between devices: none -> 17.8 us  [per_device(): lax.psum_scatter(bulk[:, :half], 'y', scatter_dimension=0, tiled=True)]
    all_to_all x1 -> x0, blocking collectives: 15.5 us -> none  [exchange(): return lax.all_to_all(values, axes, split_axis=0, concat_axis=0, tiled=True)]
    ppermute x3 -> x0, waiting for transfers between devices: 11.9 us -> none  [shifts(): lax.ppermute(pick(d), 'y', moves[d])]
    ppermute x3 -> x0, starting transfers between devices: 8.3 us -> none  [shifts(): lax.ppermute(pick(d), 'y', moves[d])]
    all_to_all x9, waiting for transfers between devices: 57.7 us -> 63.5 us  [exchange(): return lax.all_to_all(values, axes, split_axis=0, concat_axis=0, tiled=True)]
    all_to_all x9, starting transfers between devices: 58 us -> 62 us  [exchange(): return lax.all_to_all(values, axes, split_axis=0, concat_axis=0, tiled=True)]
    concatenate x2 -> x4, other arithmetic: 0.09 us -> 2.88 us  [the longest x1 1.05 us: per_device(): jnp.concatenate(across_memory, axis=0)]
    ppermute x6 -> x7, starting transfers between devices: 23.6 us -> 26.4 us  [other_core(): return lax.ppermute(values, 'c', [(0, 1), (1, 0)])]
  transfers between devices with their start and end apart: 19 -> 18, of which waited for: 13 -> 11; matrix products, arithmetic and copies ran while one was open for 8% -> 9% of each run, Pallas kernels for 4% -> 5%
where the time goes in v4:
time: 238 us; the launch traced here: 236 us
  starting transfers between devices  88.4 us (37%)
  waiting for transfers between devices  84.5 us (36%)
  between operations  14.7 us (6%)
  Pallas kernels  14.4 us (6%)
  local copies, waits for them, and re-layouts  13.9 us (6%)
  other arithmetic  12.1 us (5%)
  matrix products  8.41 us (4%)
    all_to_all x9, waiting for transfers between devices, exchange(): return lax.all_to_all(values, axes, split_axis=0, concat_axis=0, tiled=True)  63.5 us
    all_to_all x9, starting transfers between devices, exchange(): return lax.all_to_all(values, axes, split_axis=0, concat_axis=0, tiled=True)  62 us
    ppermute x7, starting transfers between devices, other_core(): return lax.ppermute(values, 'c', [(0, 1), (1, 0)])  26.4 us
    reduce_scatter x1, waiting for transfers between devices, per_device(): lax.psum_scatter(bulk[:, :half], 'y', scatter_dimension=0, tiled=True)  17.8 us
    pallas_call x1, Pallas kernels, bulk_backward(): pl.pallas_call(bulk_kernel, grid=(width // block,), in_specs=[pl.BlockSpe...  8.86 us
    dot_general x16, matrix products, dot(): lax.dot_general(left, right, (((left_dim,), (right_dim,)), ((), ())), pre...  8.14 us
  transfers between devices with their start and end apart: 18, of which 11 were waited for; matrix products, arithmetic and copies ran while one was open for 9% of the time, Pallas kernels for 5%

profile of v4, /device:TPU:1, one launch (start us, length us, event | category | flops | bytes accessed | tf_op | source)
XLA Modules:
  0.0 236.4 jit_solution(2818272618168822967)
XLA Ops:
  7.2 1.7 broadcast_select_fusion.1
  9.0 2.6 %shard_map.136 = (bf16[4,8,6272]{2,1,0:T(8,128)(2,1)}, bf16[8,128]{1,0:T(8,128)(2,1)}) custom-call(s32[1,4]{1,0:T(1,128)} %counts_ref.1, s32[1,128]{1,0:T(1,128)} %bitcast.139, bf16[128,2048]{1,0:T(8,128)(2,1)} %q_ref.1, bf16[128,2048]{1,0:T(8,128)(2,1)} %refs_1_.1, bf16[128,2048]{1,0:T(8,128)(2,1)} %up_ref.1), custom_call_target="tpu_custom_call" | custom-call | tf_op jit(solution)/shard_map/pallas_call | solution.py:196
  11.6 5.1 %all-to-all-start = ((bf16[4,8,6272]{2,1,0:T(8,128)(2,1)}), bf16[4,8,6272]{2,1,0:T(8,128)(2,1)S(1)}, u32[]{:S(2)}, u32[]{:S(2)}) async-start(bf16[4,8,6272]{2,1,0:T(8,128)(2,1)} %get-tuple-element.20), calls=%async_computation | async-start | bytes 802816 | tf_op jit(solution)/shard_map/all_to_all | solution.py:24
  16.8 6.2 %all-to-all-done = bf16[4,8,6272]{2,1,0:T(8,128)(2,1)S(1)} async-done(((bf16[4,8,6272]{2,1,0:T(8,128)(2,1)}), bf16[4,8,6272]{2,1,0:T(8,128)(2,1)S(1)}, u32[]{:S(2)}, u32[]{:S(2)}) %all-to-all-start) | async-done | bytes 401440 | tf_op jit(solution)/shard_map/all_to_all | solution.py:24
  23.7 0.5 fusion.104
  24.5 0.5 fusion.6
  25.4 0.7 all_to_all.36
  26.1 3.3 %all-to-all-start.1 = ((f32[4,2,2176]{2,1,0:T(2,128)}), f32[4,2,2176]{2,1,0:T(2,128)S(1)}, u32[]{:S(2)}, u32[]{:S(2)}) async-start(f32[4,2,2176]{2,1,0:T(2,128)} %all_to_all.36), calls=%async_computation.1 | async-start | bytes 139264 | tf_op jit(solution)/shard_map/all_to_all | solution.py:24
  29.7 4.2 %all-to-all-done.1 = f32[4,2,2176]{2,1,0:T(2,128)S(1)} async-done(((f32[4,2,2176]{2,1,0:T(2,128)}), f32[4,2,2176]{2,1,0:T(2,128)S(1)}, u32[]{:S(2)}, u32[]{:S(2)}) %all-to-all-start.1) | async-done | bytes 69664 | tf_op jit(solution)/shard_map/all_to_all | solution.py:24
  34.6 1.0 pad_maximum_fusion.2
  35.5 15.9 %all-to-all-start.2 = ((bf16[16,2,4224]{2,1,0:T(2,128)(2,1)}), bf16[16,2,4224]{2,1,0:T(2,128)(2,1)S(1)}, u32[]{:S(2)}, u32[]{:S(2)}) async-start(bf16[16,2,4224]{2,1,0:T(2,128)(2,1)} %pad_maximum_fusion.2), calls=%async_computation.2 | async-start | bytes 540672 | tf_op jit(solution)/shard_map/all_to_all | solution.py:24
  51.5 1.3 fusion.98
  52.8 5.9 %collective-permute-start.1 = (bf16[128,2048]{1,0:T(8,128)(2,1)S(1)}, bf16[128,2048]{1,0:T(8,128)(2,1)S(1)}, u32[]{:S(2)}, u32[]{:S(2)}) collective-permute-start(bf16[128,2048]{1,0:T(8,128)(2,1)S(1)} %get-tuple-element.34), channel_id=1, source_target_pairs={{0,1},{1,0},{2,3},{3,2},{4,5},{5,4},{6,7},{7,6},{8,9},{9,8},{10,11... | collective-permute-start | bytes 1572872 | tf_op jit(solution)/shard_map/ppermute | solution.py:55
  58.7 1.9 collective-permute-start
  61.0 0.7 copy.71.free_ref
  61.7 0.8 collective-permute-done.refs_0_
  62.5 0.8 copy-done.5
  63.3 8.9 %shard_map.137 = (bf16[128,2048]{1,0:T(8,128)(2,1)}, bf16[256,2048]{1,0:T(8,128)(2,1)}, bf16[128,2048]{1,0:T(8,128)(2,1)}, bf16[128,2048]{1,0:T(8,128)(2,1)}) custom-call(s32[1]{0:T(128)} %bitcast.2.core_ref, bf16[128,1]{1,0:T(8,128)(2,1)} %copy.71.free_ref, bf16[128,2048]{1,0:T(8,128)(2,1)} %up_ref.1, bf16[128,2048]{1,0:T(8,128)(2,1)} %q_ref.1, ...), custom_call_target="tpu_custom_call" | custom-call | flops 805306368 | bytes 4194304 | tf_op jit(solution)/shard_map/pallas_call | solution.py:107
  72.1 2.0 collective-permute-start.2
  74.2 2.3 collective-permute-start.3
  76.6 1.1 broadcast_in_dim.163
  77.7 4.0 %all-to-all-start.3 = ((bf16[4,32,4096]{2,1,0:T(8,128)(2,1)}), bf16[4,32,4096]{2,1,0:T(8,128)(2,1)S(1)}, u32[]{:S(2)}, u32[]{:S(2)}) async-start(bf16[4,32,4096]{2,1,0:T(8,128)(2,1)} %broadcast_in_dim.163), calls=%async_computation.3 | async-start | bytes 2097152 | tf_op jit(solution)/shard_map/all_to_all | solution.py:24
  81.8 0.8 copy-done.11
  82.5 1.7 add_convert_fusion
  84.3 12.2 %all-to-all-done.3 = bf16[4,32,4096]{2,1,0:T(8,128)(2,1)S(1)} async-done(((bf16[4,32,4096]{2,1,0:T(8,128)(2,1)}), bf16[4,32,4096]{2,1,0:T(8,128)(2,1)S(1)}, u32[]{:S(2)}, u32[]{:S(2)}) %all-to-all-start.3) | async-done | bytes 1048608 | tf_op jit(solution)/shard_map/all_to_all | solution.py:24
  96.5 3.2 %collective-permute-start.4 = (bf16[128,4096]{1,0:T(8,128)(2,1)S(1)}, bf16[128,4096]{1,0:T(8,128)(2,1)S(1)}, u32[]{:S(2)}, u32[]{:S(2)}) collective-permute-start(bf16[128,4096]{1,0:T(8,128)(2,1)S(1)} %bitcast.118), channel_id=1, source_target_pairs={{0,1},{1,0},{2,3},{3,2},{4,5},{5,4},{6,7},{7,6},{8,9},{9,8},{10,11... | collective-permute-start | bytes 3145736 | tf_op jit(solution)/shard_map/ppermute | solution.py:55
  99.7 0.9 fusion.97
  100.6 1.4 collective-permute-done.4
  102.3 0.3 fusion.56
  102.9 2.3 collective-permute-start.5
  105.6 1.3 fusion.49
  106.9 0.3 add_convert_fusion.1
  107.2 1.0 maximum_maximum_fusion
  108.3 3.5 %all-to-all-start.4 = ((bf16[4,64,2048]{2,1,0:T(8,128)(2,1)}), bf16[4,64,2048]{2,1,0:T(8,128)(2,1)S(1)}, u32[]{:S(2)}, u32[]{:S(2)}) async-start(bf16[4,64,2048]{2,1,0:T(8,128)(2,1)} %maximum_maximum_fusion), calls=%async_computation.4 | async-start | bytes 2097152 | tf_op jit(solution)/shard_map/all_to_all | solution.py:24
  111.8 17.8 %reduce-scatter.2.cloned.1.call-done = bf16[64,1024]{1,0:T(8,128)(2,1)} async-done(((bf16[256,1024]{1,0:T(8,128)(2,1)}), bf16[64,1024]{1,0:T(8,128)(2,1)}) %reduce-scatter.2.cloned.1.call-update) | async-done | bytes 131088 | tf_op jit(solution)/shard_map/reduce_scatter | solution.py:302
  129.6 0.9 bitcast_bitcast_fusion.1
  130.9 0.8 maximum_maximum_fusion.1
  131.6 12.0 %all-to-all-start.5 = ((bf16[16,96,128]{2,1,0:T(8,128)(2,1)}), bf16[16,96,128]{2,1,0:T(8,128)(2,1)S(1)}, u32[]{:S(2)}, u32[]{:S(2)}) async-start(bf16[16,96,128]{2,1,0:T(8,128)(2,1)} %maximum_maximum_fusion.1), calls=%async_computation.6 | async-start | bytes 786432 | tf_op jit(solution)/shard_map/all_to_all | solution.py:24
  143.9 0.6 pad_add_fusion.spot_ref
  144.4 0.6 slice.132.q_ref
  145.0 1.0 pad_maximum_fusion.across_ref
  146.1 15.4 %all-to-all-done.5.sums_ref = bf16[16,96,128]{2,1,0:T(8,128)(2,1)S(1)} async-done(((bf16[16,96,128]{2,1,0:T(8,128)(2,1)}), bf16[16,96,128]{2,1,0:T(8,128)(2,1)S(1)}, u32[]{:S(2)}, u32[]{:S(2)}) %all-to-all-start.5) | async-done | bytes 393248 | tf_op jit(solution)/shard_map/all_to_all | solution.py:24
  161.4 0.7 copy-done.7
  162.2 2.9 %shard_map.138 = (bf16[64,128]{1,0:T(8,128)(2,1)}, bf16[256,128]{1,0:T(8,128)(2,1)}, bf16[256,128]{1,0:T(8,128)(2,1)}, f32[64,128]{1,0:T(8,128)}) custom-call(s32[2]{0:T(128)} %pad_add_fusion.spot_ref, bf16[16,96,128]{2,1,0:T(8,128)(2,1)} %copy-done.7, bf16[32,4096]{1,0:T(8,128)(2,1)} %copy-done.2, bf16[32,128]{1,0:T(8,128)(2,1)} %slice.132.q_ref, ...), custom_call_target="tpu_custom_call" | custom-call | tf_op jit(solution)/shard_map/pallas_call | solution.py:150
  165.1 8.8 %collective-permute-start.6 = (bf16[256,128]{1,0:T(8,128)(2,1)}, bf16[256,128]{1,0:T(8,128)(2,1)S(1)}, u32[]{:S(2)}, u32[]{:S(2)}) collective-permute-start(bf16[256,128]{1,0:T(8,128)(2,1)} %get-tuple-element.28), channel_id=1, source_target_pairs={{0,1},{1,0},{2,3},{3,2},{4,5},{5,4},{6,7},{7,6},{8,9},{9,8},{10,11... | collective-permute-start | bytes 196616 | tf_op jit(solution)/shard_map/ppermute | solution.py:55
  174.0 1.0 collective-permute-done.6
  175.0 0.9 convert_add_fusion
  175.9 0.9 fusion.39
  176.8 0.8 broadcast_in_dim.176
  177.6 0.7 pad_maximum_fusion.1
  178.3 5.3 %all-to-all-start.6 = ((bf16[16,80,128]{2,1,0:T(8,128)(2,1)}), bf16[16,80,128]{2,1,0:T(8,128)(2,1)S(1)}, u32[]{:S(2)}, u32[]{:S(2)}) async-start(bf16[16,80,128]{2,1,0:T(8,128)(2,1)} %pad_maximum_fusion.1), calls=%async_computation.7 | async-start | bytes 655360 | tf_op jit(solution)/shard_map/all_to_all | solution.py:24
  183.9 8.6 %all-to-all-done.6 = bf16[16,80,128]{2,1,0:T(8,128)(2,1)S(1)} async-done(((bf16[16,80,128]{2,1,0:T(8,128)(2,1)}), bf16[16,80,128]{2,1,0:T(8,128)(2,1)S(1)}, u32[]{:S(2)}, u32[]{:S(2)}) %all-to-all-start.6) | async-done | bytes 327712 | tf_op jit(solution)/shard_map/all_to_all | solution.py:24
  192.6 0.7 copy.77
  193.3 5.7 %all-to-all-start.7 = ((bf16[16,32,128]{2,1,0:T(8,128)(2,1)}), bf16[16,32,128]{2,1,0:T(8,128)(2,1)S(1)}, u32[]{:S(2)}, u32[]{:S(2)}) async-start(bf16[16,32,128]{2,1,0:T(8,128)(2,1)} %copy.77), calls=%async_computation.8 | async-start | bytes 262144 | tf_op jit(solution)/shard_map/all_to_all | solution.py:24
  199.3 1.0 fusion.5
  200.2 1.0 fusion.4
  201.2 9.8 %all-to-all-done.7 = bf16[16,32,128]{2,1,0:T(8,128)(2,1)S(1)} async-done(((bf16[16,32,128]{2,1,0:T(8,128)(2,1)}), bf16[16,32,128]{2,1,0:T(8,128)(2,1)S(1)}, u32[]{:S(2)}, u32[]{:S(2)}) %all-to-all-start.7) | async-done | bytes 131104 | tf_op jit(solution)/shard_map/all_to_all | solution.py:24
  211.2 0.9 broadcast_in_dim.180
  212.1 7.1 %all-to-all-start.8 = ((bf16[8,16,2048]{2,1,0:T(8,128)(2,1)}), bf16[8,16,2048]{2,1,0:T(8,128)(2,1)S(1)}, u32[]{:S(2)}, u32[]{:S(2)}) async-start(bf16[8,16,2048]{2,1,0:T(8,128)(2,1)} %broadcast_in_dim.180), calls=%async_computation.9 | async-start | bytes 1048576 | tf_op jit(solution)/shard_map/all_to_all | solution.py:24
  219.2 1.1 fusion.1
  220.3 0.3 convolution_convert_fusion.1
  220.7 0.9 broadcast_select_fusion
  221.6 7.1 %all-to-all-done.8 = bf16[8,16,2048]{2,1,0:T(8,128)(2,1)S(1)} async-done(((bf16[8,16,2048]{2,1,0:T(8,128)(2,1)}), bf16[8,16,2048]{2,1,0:T(8,128)(2,1)S(1)}, u32[]{:S(2)}, u32[]{:S(2)}) %all-to-all-start.8) | async-done | bytes 524320 | tf_op jit(solution)/shard_map/all_to_all | solution.py:24
  228.7 0.8 fusion.99
  (107 shorter events, 5.3 us)
Async XLA Ops:
  7.2 94.8 %copy-start = (bf16[1,80,2048]{2,1,0:T(8,128)(2,1)S(1)}, bf16[1,80,2048]{2,1,0:T(8,128)(2,1)}, u32[]{:S(2)}) copy-start(bf16[1,80,2048]{2,1,0:T(8,128)(2,1)} %param.15) | copy-start | bytes 983044
  7.2 44.3 %all-gather.2.cloned.1.call-start = ((), (), s32[]{:S(2)}) async-start(), calls=%async_computation.10 | async-start | bytes 1310720 | tf_op jit(solution)/shard_map/all_gather | solution.py:216
  11.6 12.2 %copy-start.12 = (bf16[64,2048]{1,0:T(8,128)(2,1)S(1)}, bf16[64,2048]{1,0:T(8,128)(2,1)}, u32[]{:S(2)}) copy-start(bf16[64,2048]{1,0:T(8,128)(2,1)} %param.11) | copy-start | bytes 786436
  11.6 11.4 %all-to-all-start = ((bf16[4,8,6272]{2,1,0:T(8,128)(2,1)}), bf16[4,8,6272]{2,1,0:T(8,128)(2,1)S(1)}, u32[]{:S(2)}, u32[]{:S(2)}) async-start(bf16[4,8,6272]{2,1,0:T(8,128)(2,1)} %get-tuple-element.20), calls=%async_computation | async-start | bytes 802816 | tf_op jit(solution)/shard_map/all_to_all | solution.py:24
  23.5 1.0 copy-start.13
  26.1 7.8 %all-to-all-start.1 = ((f32[4,2,2176]{2,1,0:T(2,128)}), f32[4,2,2176]{2,1,0:T(2,128)S(1)}, u32[]{:S(2)}, u32[]{:S(2)}) async-start(f32[4,2,2176]{2,1,0:T(2,128)} %all_to_all.36), calls=%async_computation.1 | async-start | bytes 139264 | tf_op jit(solution)/shard_map/all_to_all | solution.py:24
  35.5 40.9 %all-to-all-start.2 = ((bf16[16,2,4224]{2,1,0:T(2,128)(2,1)}), bf16[16,2,4224]{2,1,0:T(2,128)(2,1)S(1)}, u32[]{:S(2)}, u32[]{:S(2)}) async-start(bf16[16,2,4224]{2,1,0:T(2,128)(2,1)} %pad_maximum_fusion.2), calls=%async_computation.2 | async-start | bytes 540672 | tf_op jit(solution)/shard_map/all_to_all | solution.py:24
  51.4 9.2 %copy-start.15 = (bf16[8,128]{1,0:T(8,128)(2,1)S(1)}, bf16[8,128]{1,0:T(8,128)(2,1)}, u32[]{:S(2)}) copy-start(bf16[8,128]{1,0:T(8,128)(2,1)} %get-tuple-element.19) | copy-start | bytes 6148
  52.8 8.9 %collective-permute-start.1 = (bf16[128,2048]{1,0:T(8,128)(2,1)S(1)}, bf16[128,2048]{1,0:T(8,128)(2,1)S(1)}, u32[]{:S(2)}, u32[]{:S(2)}) collective-permute-start(bf16[128,2048]{1,0:T(8,128)(2,1)S(1)} %get-tuple-element.34), channel_id=1, source_target_pairs={{0,1},{1,0},{2,3},{3,2},{4,5},{5,4},{6,7},{7,6},{8,9},{9,8},{10,11... | collective-permute-start | bytes 1572872 | tf_op jit(solution)/shard_map/ppermute | solution.py:55
  58.7 3.8 %collective-permute-start = (bf16[128,2048]{1,0:T(8,128)(2,1)S(1)}, bf16[128,2048]{1,0:T(8,128)(2,1)S(1)}, u32[]{:S(2)}, u32[]{:S(2)}) collective-permute-start(bf16[128,2048]{1,0:T(8,128)(2,1)S(1)} %get-tuple-element.35), channel_id=1, source_target_pairs={{0,1},{1,0},{2,3},{3,2},{4,5},{5,4},{6,7},{7,6},{8,9},{9,8},{10,11... | collective-permute-start | bytes 1572872 | tf_op jit(solution)/shard_map/ppermute | solution.py:55
  61.7 0.8 copy-start.3
  62.5 0.8 copy-start.5
  72.1 9.6 %collective-permute-start.2 = (bf16[128,2048]{1,0:T(8,128)(2,1)}, bf16[128,2048]{1,0:T(8,128)(2,1)S(1)}, u32[]{:S(2)}, u32[]{:S(2)}) collective-permute-start(bf16[128,2048]{1,0:T(8,128)(2,1)} %get-tuple-element.22), channel_id=1, source_target_pairs={{0,1},{1,0},{2,3},{3,2},{4,5},{5,4},{6,7},{7,6},{8,9},{9,8},{10,11... | collective-permute-start | bytes 1572872 | tf_op jit(solution)/shard_map/ppermute | solution.py:55
  74.2 7.6 %collective-permute-start.3 = (bf16[128,2048]{1,0:T(8,128)(2,1)}, bf16[128,2048]{1,0:T(8,128)(2,1)S(1)}, u32[]{:S(2)}, u32[]{:S(2)}) collective-permute-start(bf16[128,2048]{1,0:T(8,128)(2,1)} %get-tuple-element.23), channel_id=1, source_target_pairs={{0,1},{1,0},{2,3},{3,2},{4,5},{5,4},{6,7},{7,6},{8,9},{9,8},{10,11... | collective-permute-start | bytes 1572872 | tf_op jit(solution)/shard_map/ppermute | solution.py:55
  76.6 1.1 copy-start.2
  77.7 18.8 %all-to-all-start.3 = ((bf16[4,32,4096]{2,1,0:T(8,128)(2,1)}), bf16[4,32,4096]{2,1,0:T(8,128)(2,1)S(1)}, u32[]{:S(2)}, u32[]{:S(2)}) async-start(bf16[4,32,4096]{2,1,0:T(8,128)(2,1)} %broadcast_in_dim.163), calls=%async_computation.3 | async-start | bytes 2097152 | tf_op jit(solution)/shard_map/all_to_all | solution.py:24
  81.7 47.9 %reduce-scatter.2.cloned.1.call-start = ((), (), s32[]{:S(2)}) async-start(), calls=%async_computation.11 | async-start | bytes 655360 | tf_op jit(solution)/shard_map/reduce_scatter | solution.py:302
  81.8 0.8 copy-start.11
  96.5 5.4 %collective-permute-start.4 = (bf16[128,4096]{1,0:T(8,128)(2,1)S(1)}, bf16[128,4096]{1,0:T(8,128)(2,1)S(1)}, u32[]{:S(2)}, u32[]{:S(2)}) collective-permute-start(bf16[128,4096]{1,0:T(8,128)(2,1)S(1)} %bitcast.118), channel_id=1, source_target_pairs={{0,1},{1,0},{2,3},{3,2},{4,5},{5,4},{6,7},{7,6},{8,9},{9,8},{10,11... | collective-permute-start | bytes 3145736 | tf_op jit(solution)/shard_map/ppermute | solution.py:55
  100.6 1.7 copy-start.14
  102.0 1.0 copy-start.8
  102.9 4.0 %collective-permute-start.5 = (bf16[128,2048]{1,0:T(8,128)(2,1)S(1)}, bf16[128,2048]{1,0:T(8,128)(2,1)S(1)}, u32[]{:S(2)}, u32[]{:S(2)}) collective-permute-start(bf16[128,2048]{1,0:T(8,128)(2,1)S(1)} %convolution_convert_fusion.2), channel_id=1, source_target_pairs={{0,1},{1,0},{2,3},{3,2},{4,5},{5,4},{6,7},{7,6},{8,9},{9,8},{10,11... | collective-permute-start | bytes 1572872 | tf_op jit(solution)/shard_map/ppermute | solution.py:55
  108.3 22.3 %all-to-all-start.4 = ((bf16[4,64,2048]{2,1,0:T(8,128)(2,1)}), bf16[4,64,2048]{2,1,0:T(8,128)(2,1)S(1)}, u32[]{:S(2)}, u32[]{:S(2)}) async-start(bf16[4,64,2048]{2,1,0:T(8,128)(2,1)} %maximum_maximum_fusion), calls=%async_computation.4 | async-start | bytes 2097152 | tf_op jit(solution)/shard_map/all_to_all | solution.py:24
  130.8 14.2 %copy-start.4 = (bf16[128,2048]{1,0:T(8,128)(2,1)S(1)}, bf16[128,2048]{1,0:T(8,128)(2,1)}, u32[]{:S(2)}) copy-start(bf16[128,2048]{1,0:T(8,128)(2,1)} %copy-done.3) | copy-start | bytes 1572868
  130.8 14.2 %copy-start.6 = (bf16[128,2048]{1,0:T(8,128)(2,1)S(1)}, bf16[128,2048]{1,0:T(8,128)(2,1)}, u32[]{:S(2)}) copy-start(bf16[128,2048]{1,0:T(8,128)(2,1)} %copy-done.5) | copy-start | bytes 1572868
  131.6 29.8 %all-to-all-start.5 = ((bf16[16,96,128]{2,1,0:T(8,128)(2,1)}), bf16[16,96,128]{2,1,0:T(8,128)(2,1)S(1)}, u32[]{:S(2)}, u32[]{:S(2)}) async-start(bf16[16,96,128]{2,1,0:T(8,128)(2,1)} %maximum_maximum_fusion.1), calls=%async_computation.6 | async-start | bytes 786432 | tf_op jit(solution)/shard_map/all_to_all | solution.py:24
  161.4 0.7 copy-start.7
  165.1 9.9 %collective-permute-start.6 = (bf16[256,128]{1,0:T(8,128)(2,1)}, bf16[256,128]{1,0:T(8,128)(2,1)S(1)}, u32[]{:S(2)}, u32[]{:S(2)}) collective-permute-start(bf16[256,128]{1,0:T(8,128)(2,1)} %get-tuple-element.28), channel_id=1, source_target_pairs={{0,1},{1,0},{2,3},{3,2},{4,5},{5,4},{6,7},{7,6},{8,9},{9,8},{10,11... | collective-permute-start | bytes 196616 | tf_op jit(solution)/shard_map/ppermute | solution.py:55
  178.3 14.1 %all-to-all-start.6 = ((bf16[16,80,128]{2,1,0:T(8,128)(2,1)}), bf16[16,80,128]{2,1,0:T(8,128)(2,1)S(1)}, u32[]{:S(2)}, u32[]{:S(2)}) async-start(bf16[16,80,128]{2,1,0:T(8,128)(2,1)} %pad_maximum_fusion.1), calls=%async_computation.7 | async-start | bytes 655360 | tf_op jit(solution)/shard_map/all_to_all | solution.py:24
  192.5 6.7 %copy-start.9 = (bf16[128,4096]{1,0:T(8,128)(2,1)S(1)}, bf16[128,4096]{1,0:T(8,128)(2,1)}, u32[]{:S(2)}) copy-start(bf16[128,4096]{1,0:T(8,128)(2,1)} %copy-done.8) | copy-start | bytes 3145732
  193.3 17.7 %all-to-all-start.7 = ((bf16[16,32,128]{2,1,0:T(8,128)(2,1)}), bf16[16,32,128]{2,1,0:T(8,128)(2,1)S(1)}, u32[]{:S(2)}, u32[]{:S(2)}) async-start(bf16[16,32,128]{2,1,0:T(8,128)(2,1)} %copy.77), calls=%async_computation.8 | async-start | bytes 262144 | tf_op jit(solution)/shard_map/all_to_all | solution.py:24
  211.1 8.1 %copy-start.1 = (bf16[128,2048]{1,0:T(8,128)(2,1)S(1)}, bf16[128,2048]{1,0:T(8,128)(2,1)}, u32[]{:S(2)}) copy-start(bf16[128,2048]{1,0:T(8,128)(2,1)} %up_ref.1) | copy-start | bytes 1572868
  212.1 16.6 %all-to-all-start.8 = ((bf16[8,16,2048]{2,1,0:T(8,128)(2,1)}), bf16[8,16,2048]{2,1,0:T(8,128)(2,1)S(1)}, u32[]{:S(2)}, u32[]{:S(2)}) async-start(bf16[8,16,2048]{2,1,0:T(8,128)(2,1)} %broadcast_in_dim.180), calls=%async_computation.9 | async-start | bytes 1048576 | tf_op jit(solution)/shard_map/all_to_all | solution.py:24
  219.2 1.5 copy-start.10
Sparse Core Ops, SparseCore 0:
  10.7 36.0 all-gather.1
  105.4 24.1 reduce-scatter.1

commit v5 on v4

--- a/solution.py
+++ b/solution.py
@@ -7,7 +7,7 @@
 
 HEAD = 64
 GCAP = 2
-PIECES = 2
+PIECES = 4
 SCALE = HEAD ** (-0.5)
 BF, F32 = jnp.bfloat16, jnp.float32
 DEVICES = ("y", "z", "x", "c")
@@ -36,6 +36,27 @@
     n = lax.axis_size(axes)
     got = exchange(values, axes)
     return jnp.sum(got.reshape((n, -1) + got.shape[1:]).astype(F32), axis=0)
+
+
+def join_kernel(spot_ref, keep_ref, got_ref, more_ref, ret_ref, out_ref):
+    blocks, rows = out_ref.shape[0], more_ref.shape[0]
+    for block in range(blocks):
+        part = pl.ds(block * rows, rows)
+        memory = keep_ref[part].astype(F32) + got_ref[part].astype(F32)
+        memory = memory + jnp.where(spot_ref[0] == block, more_ref[...], 0.0)
+        out_ref[block, :rows] = memory.astype(BF)
+        out_ref[block, rows:] = ret_ref[...]
+
+
+def join_blocks(spot, keep, got, more, returned, blocks):
+    vmem = pl.BlockSpec(memory_space=pltpu.VMEM)
+    shape = (blocks, more.shape[0] + returned.shape[0], more.shape[1])
+    return pl.pallas_call(
+        join_kernel,
+        in_specs=[pl.BlockSpec(memory_space=pltpu.SMEM)] + [vmem] * 4,
+        out_specs=vmem,
+        out_shape=jax.ShapeDtypeStruct(shape, BF),
+    )(spot, keep, got, more, returned)
 
 
 def head_pairs(values):
@@ -84,7 +105,7 @@
     across, (gq_ref, keep_ref), sends = refs[:PIECES], refs[PIECES : PIECES + 2], refs[PIECES + 2 :]
     first = core_ref[0] == 0
     free = free_ref[...]
-    rows = own_ref.shape[0] // PIECES
+    rows = sends[0].shape[0]
     for pair in range(q_ref.shape[1] // (2 * HEAD)):
         cols = slice(pair * 2 * HEAD, (pair + 1) * 2 * HEAD)
         gq_ref[:, cols], keep_ref[:, cols], send = pair_backward(
@@ -103,7 +124,7 @@
     mem = own.shape[0]
     block = 512
     column = lambda n: pl.BlockSpec((n, block), lambda i: (0, i))
-    outs = [tokens, mem] + [mem // PIECES] * PIECES
+    outs = [tokens, mem] + [mem // 2] * 2
     got = pl.pallas_call(
         bulk_kernel,
         grid=(width // block,),
@@ -282,7 +303,14 @@
     near = spread(after(level, *send), "x")
     sent = jnp.concatenate([other_core(piece) for piece in send], axis=0)
     bulk = (keep.astype(F32) + sent.astype(F32)).astype(BF)
-    far = other_core(after(near, bulk))
+    own_rows = mem_keys.shape[0]
+    blocks = [
+        lax.dynamic_slice_in_dim(bulk, (mine + d) % window * own_rows, own_rows, 0)
+        for d in range(window)
+    ]
+    moves = [[(i, (i + d) % window) for i in range(window)] for d in range(window)]
+    got = [lax.ppermute(blocks[d], "y", moves[d]) for d in (1, 3)]
+    far = other_core(after(near, *blocks))
     weight_in, weight_out = w_in[0], w_out[0]
     parts_of_x = lax.axis_size("x")
 
@@ -295,20 +323,15 @@
 
     _, far_in, far_out, far_back = expert(far)
     _, near_in, near_out, near_back = expert(near)
+    bulk = sum(part.astype(F32) for part in blocks[:1] + [after(part, far_back) for part in got])
+    bulk = jnp.stack([bulk.astype(BF), blocks[2]])
     grad_in, grad_out = (near_in + far_in).astype(BF), (near_out + far_out).astype(BF)
 
     back = (near_back + other_core(far_back.astype(BF)).astype(F32)).astype(BF)
-    half = width // 2
-    over_y = lax.psum_scatter(bulk[:, :half], "y", scatter_dimension=0, tiled=True)
-    over_x = bulk[:, half:].reshape(window, parts_of_x, -1, half).transpose(1, 0, 2, 3)
-    over_x = over_x.reshape(parts_of_x, -1, half)
-    over_x = jnp.concatenate(jnp.split(over_x, 2, axis=1), axis=2)
     rows = back.shape[0] // parts_of_x
-    back = jnp.concatenate([back.reshape(parts_of_x, rows, width), over_x], axis=1)
-    back = collect(back.reshape(-1, width), "x").astype(BF)
-    over_x = jnp.concatenate([back[rows:, :half], back[rows:, half:]], axis=0)
-    bulk = jnp.concatenate([head_pairs(over_y), head_pairs(over_x)], axis=0)
-    joined = exchange(jnp.concatenate([head_pairs(back[:rows]), bulk], axis=1), "z")
+    back = [back.reshape(parts_of_x, rows, width), bulk.reshape(2, parts_of_x, -1, width).transpose(1, 0, 2, 3).reshape(parts_of_x, -1, width)]
+    back = collect(jnp.concatenate(back, axis=1).reshape(-1, width), "x").astype(BF)
+    joined = exchange(head_pairs(back), "z")
     returned, keep, send, bulk = routed_backward(
         jnp.stack([core, depth]).astype(jnp.int32),
         joined,
@@ -318,20 +341,15 @@
         jnp.concatenate(across_memory, axis=0),
     )
 
-    memory = keep.astype(F32) + other_core(send).astype(F32)
-    memory = memory.reshape(window, parts_of_x, -1, 2 * HEAD)
-    bulk = bulk.reshape(window, -1, 2 * HEAD)
-    of_y = (depth < depths // 2) & (experts == mine)
-    of_x = (depth >= depths // 2) & (jnp.arange(parts_of_x) == lax.axis_index("x"))
-    memory = memory + jnp.where(of_y[:, None, None, None], bulk[None], 0.0)
-    memory = (memory + jnp.where(of_x[None, :, None, None], bulk[:, None], 0.0)).astype(BF)
     blocks = window * parts_of_x
-    copies = jnp.broadcast_to(returned[None], (blocks,) + returned.shape)
-    joined = exchange(
-        jnp.concatenate([memory.reshape(blocks, -1, 2 * HEAD), copies], axis=1), ("y", "x")
-    )
+    spot = (mine + 2) % window * parts_of_x + lax.axis_index("x")
+    bulk, opposite = jnp.split(bulk, 2, axis=0)
+    joined = join_blocks(
+        spot.reshape(1).astype(jnp.int32), keep, other_core(send), opposite, returned, blocks
+    )
+    joined = exchange(joined, ("y", "x"))
     rows_of_x = joined.shape[1] - returned.shape[0]
-    memory = jnp.sum(joined[:, :rows_of_x].astype(F32), axis=0).astype(BF)
+    memory = (jnp.sum(joined[:, :rows_of_x].astype(F32), axis=0) + bulk).astype(BF)
     returned = joined[:, rows_of_x:].reshape((window, parts_of_x) + returned.shape)
     returned = lax.dynamic_index_in_dim(returned, lax.axis_index("x"), 1, False)
     returned = returned.reshape(window, 2, depths, GCAP, 2 * HEAD).transpose(2, 0, 1, 3, 4)

time: 238 us -> 234 us (0.983)
  waiting for transfers between devices: 84.5 us -> 61.3 us
  blocking collectives: 0 us -> 16.5 us
  starting transfers between devices: 88.4 us -> 95.2 us
  other arithmetic: 12.1 us -> 7.82 us
    reduce_scatter x1 -> x0, waiting for transfers between devices: 17.8 us -> none  [per_device(): lax.psum_scatter(bulk[:, :half], 'y', scatter_dimension=0, tiled=True)]
    all_to_all x0 -> x1, blocking collectives: none -> 16.5 us  [exchange(): return lax.all_to_all(values, axes, split_axis=0, concat_axis=0, tiled=True)]
    ppermute x0 -> x2, starting transfers between devices: none -> 6.49 us  [per_device(): got = [lax.ppermute(blocks[d], 'y', moves[d]) for d in (1, 3)]]
    ppermute x7 -> x9, starting transfers between devices: 26.4 us -> 31.2 us  [other_core(): return lax.ppermute(values, 'c', [(0, 1), (1, 0)])]
    all_to_all x9 -> x8, starting transfers between devices: 62 us -> 57.4 us  [exchange(): return lax.all_to_all(values, axes, split_axis=0, concat_axis=0, tiled=True)]
    all_to_all x9 -> x8, waiting for transfers between devices: 63.5 us -> 59.5 us  [exchange(): return lax.all_to_all(values, axes, split_axis=0, concat_axis=0, tiled=True)]
    concatenate x3 -> x1, other arithmetic: 2.56 us -> 0.1 us  [per_device(): jnp.concatenate(back, axis=1).reshape(-1, width)]
  transfers between devices with their start and end apart: 18 -> 20, of which waited for: 11 -> 10; matrix products, arithmetic and copies ran while one was open for 9% -> 8% of each run, Pallas kernels for 5% -> 5%
where the time goes in v5:
time: 234 us; the launch traced here: 232 us
  starting transfers between devices  95.2 us (41%)
  waiting for transfers between devices  61.3 us (26%)
  blocking collectives  16.5 us (7%)
  Pallas kernels  15.9 us (7%)
  between operations  14.7 us (6%)
  local copies, waits for them, and re-layouts  13.1 us (6%)
  other arithmetic  7.82 us (3%)
  matrix products  7.44 us (3%)
    all_to_all x8, waiting for transfers between devices, exchange(): return lax.all_to_all(values, axes, split_axis=0, concat_axis=0, tiled=True)  59.5 us
    all_to_all x8, starting transfers between devices, exchange(): return lax.all_to_all(values, axes, split_axis=0, concat_axis=0, tiled=True)  57.4 us
    ppermute x9, starting transfers between devices, other_core(): return lax.ppermute(values, 'c', [(0, 1), (1, 0)])  31.2 us
    all_to_all x1, blocking collectives, exchange(): return lax.all_to_all(values, axes, split_axis=0, concat_axis=0, tiled=True)  16.5 us
    pallas_call x1, Pallas kernels, bulk_backward(): pl.pallas_call(bulk_kernel, grid=(width // block,), in_specs=[pl.BlockSpe...  8.83 us
    dot_general x16, matrix products, dot(): lax.dot_general(left, right, (((left_dim,), (right_dim,)), ((), ())), pre...  7.18 us
    ppermute x2, starting transfers between devices, per_device(): got = [lax.ppermute(blocks[d], 'y', moves[d]) for d in (1, 3)]  6.49 us
  transfers between devices with their start and end apart: 20, of which 10 were waited for; matrix products, arithmetic and copies ran while one was open for 8% of the time, Pallas kernels for 5%

profile of v5, /device:TPU:1, one launch (start us, length us, event | category | flops | bytes accessed | tf_op | source)
XLA Modules:
  0.0 232.1 jit_solution(17008549699785140782)
XLA Ops:
  7.2 1.7 broadcast_select_fusion.1
  9.0 2.6 %shard_map.136 = (bf16[4,8,6272]{2,1,0:T(8,128)(2,1)}, bf16[8,128]{1,0:T(8,128)(2,1)}) custom-call(s32[1,4]{1,0:T(1,128)} %counts_ref.1, s32[1,128]{1,0:T(1,128)} %bitcast.116, bf16[128,2048]{1,0:T(8,128)(2,1)} %q_ref.1, bf16[128,2048]{1,0:T(8,128)(2,1)} %refs_1_.1, bf16[128,2048]{1,0:T(8,128)(2,1)} %up_ref.1), custom_call_target="tpu_custom_call" | custom-call | tf_op jit(solution)/shard_map/pallas_call | solution.py:217
  11.6 5.1 %all-to-all-start = ((bf16[4,8,6272]{2,1,0:T(8,128)(2,1)}), bf16[4,8,6272]{2,1,0:T(8,128)(2,1)S(1)}, u32[]{:S(2)}, u32[]{:S(2)}) async-start(bf16[4,8,6272]{2,1,0:T(8,128)(2,1)} %get-tuple-element.22), calls=%async_computation | async-start | bytes 802816 | tf_op jit(solution)/shard_map/all_to_all | solution.py:24
  16.8 6.2 %all-to-all-done = bf16[4,8,6272]{2,1,0:T(8,128)(2,1)S(1)} async-done(((bf16[4,8,6272]{2,1,0:T(8,128)(2,1)}), bf16[4,8,6272]{2,1,0:T(8,128)(2,1)S(1)}, u32[]{:S(2)}, u32[]{:S(2)}) %all-to-all-start) | async-done | bytes 401440 | tf_op jit(solution)/shard_map/all_to_all | solution.py:24
  23.7 0.5 fusion.99
  24.5 0.5 fusion.6
  25.4 0.7 all_to_all.36
  26.1 3.3 %all-to-all-start.1 = ((f32[4,2,2176]{2,1,0:T(2,128)}), f32[4,2,2176]{2,1,0:T(2,128)S(1)}, u32[]{:S(2)}, u32[]{:S(2)}) async-start(f32[4,2,2176]{2,1,0:T(2,128)} %all_to_all.36), calls=%async_computation.1 | async-start | bytes 139264 | tf_op jit(solution)/shard_map/all_to_all | solution.py:24
  29.8 4.1 %all-to-all-done.1 = f32[4,2,2176]{2,1,0:T(2,128)S(1)} async-done(((f32[4,2,2176]{2,1,0:T(2,128)}), f32[4,2,2176]{2,1,0:T(2,128)S(1)}, u32[]{:S(2)}, u32[]{:S(2)}) %all-to-all-start.1) | async-done | bytes 69664 | tf_op jit(solution)/shard_map/all_to_all | solution.py:24
  34.6 1.0 pad_maximum_fusion.3
  35.5 15.9 %all-to-all-start.2 = ((bf16[16,2,4224]{2,1,0:T(2,128)(2,1)}), bf16[16,2,4224]{2,1,0:T(2,128)(2,1)S(1)}, u32[]{:S(2)}, u32[]{:S(2)}) async-start(bf16[16,2,4224]{2,1,0:T(2,128)(2,1)} %pad_maximum_fusion.3), calls=%async_computation.2 | async-start | bytes 540672 | tf_op jit(solution)/shard_map/all_to_all | solution.py:24
  51.5 1.3 fusion.95
  52.7 5.9 %collective-permute-start.3 = (bf16[64,2048]{1,0:T(8,128)(2,1)S(1)}, bf16[64,2048]{1,0:T(8,128)(2,1)S(1)}, u32[]{:S(2)}, u32[]{:S(2)}) collective-permute-start(bf16[64,2048]{1,0:T(8,128)(2,1)S(1)} %get-tuple-element.40), channel_id=1, source_target_pairs={{0,1},{1,0},{2,3},{3,2},{4,5},{5,4},{6,7},{7,6},{8,9},{9,8},{10,11... | collective-permute-start | bytes 786440 | tf_op jit(solution)/shard_map/ppermute | solution.py:76
  58.7 1.9 collective-permute-start.2
  60.6 2.4 %collective-permute-start.1 = (bf16[64,2048]{1,0:T(8,128)(2,1)S(1)}, bf16[64,2048]{1,0:T(8,128)(2,1)S(1)}, u32[]{:S(2)}, u32[]{:S(2)}) collective-permute-start(bf16[64,2048]{1,0:T(8,128)(2,1)S(1)} %get-tuple-element.42), channel_id=1, source_target_pairs={{0,1},{1,0},{2,3},{3,2},{4,5},{5,4},{6,7},{7,6},{8,9},{9,8},{10,11... | collective-permute-start | bytes 786440 | tf_op jit(solution)/shard_map/ppermute | solution.py:76
  63.0 1.9 collective-permute-start
  65.2 0.7 copy.56.free_ref
  66.0 0.4 collective-permute-done.refs_0_
  66.8 0.3 copy-done.13
  67.1 8.8 %shard_map.137 = (bf16[128,2048]{1,0:T(8,128)(2,1)}, bf16[256,2048]{1,0:T(8,128)(2,1)}, bf16[128,2048]{1,0:T(8,128)(2,1)}, bf16[128,2048]{1,0:T(8,128)(2,1)}) custom-call(s32[1]{0:T(128)} %bitcast.3.core_ref, bf16[128,1]{1,0:T(8,128)(2,1)} %copy.56.free_ref, bf16[128,2048]{1,0:T(8,128)(2,1)} %up_ref.1, bf16[128,2048]{1,0:T(8,128)(2,1)} %q_ref.1, ...), custom_call_target="tpu_custom_call" | custom-call | flops 805306368 | bytes 4194304 | tf_op jit(solution)/shard_map/pallas_call | solution.py:128
  76.0 2.2 collective-permute-start.4
  78.2 2.1 collective-permute-start.5
  80.5 1.1 broadcast_in_dim.103
  81.6 4.1 %all-to-all-start.3 = ((bf16[4,32,4096]{2,1,0:T(8,128)(2,1)}), bf16[4,32,4096]{2,1,0:T(8,128)(2,1)S(1)}, u32[]{:S(2)}, u32[]{:S(2)}) async-start(bf16[4,32,4096]{2,1,0:T(8,128)(2,1)} %broadcast_in_dim.103), calls=%async_computation.3 | async-start | bytes 2097152 | tf_op jit(solution)/shard_map/all_to_all | solution.py:24
  85.7 1.4 add_convert_fusion
  87.3 13.1 %all-to-all-done.3 = bf16[4,32,4096]{2,1,0:T(8,128)(2,1)S(1)} async-done(((bf16[4,32,4096]{2,1,0:T(8,128)(2,1)}), bf16[4,32,4096]{2,1,0:T(8,128)(2,1)S(1)}, u32[]{:S(2)}, u32[]{:S(2)}) %all-to-all-start.3) | async-done | bytes 1048608 | tf_op jit(solution)/shard_map/all_to_all | solution.py:24
  100.4 3.3 %collective-permute-start.6 = (bf16[128,4096]{1,0:T(8,128)(2,1)S(1)}, bf16[128,4096]{1,0:T(8,128)(2,1)S(1)}, u32[]{:S(2)}, u32[]{:S(2)}) collective-permute-start(bf16[128,4096]{1,0:T(8,128)(2,1)S(1)} %bitcast.96), channel_id=1, source_target_pairs={{0,1},{1,0},{2,3},{3,2},{4,5},{5,4},{6,7},{7,6},{8,9},{9,8},{10,11... | collective-permute-start | bytes 3145736 | tf_op jit(solution)/shard_map/ppermute | solution.py:76
  103.7 2.2 collective-permute-start.8
  105.9 4.3 %collective-permute-start.9 = (bf16[64,2048]{1,0:T(8,128)(2,1)S(1)}, bf16[64,2048]{1,0:T(8,128)(2,1)S(1)}, u32[]{:S(2)}, u32[]{:S(2)}) collective-permute-start(bf16[64,2048]{1,0:T(8,128)(2,1)S(1)} %get-tuple-element.37), channel_id=1, source_target_pairs={{0,384},{128,0},{256,128},{384,256},{1,385},{129,1},{257,129},{385... | collective-permute-start | bytes 786440 | tf_op jit(solution)/shard_map/ppermute | solution.py:312
  110.5 0.3 fusion.47
  111.1 0.3 fusion.14
  111.5 0.3 fusion.54
  111.8 0.3 fusion.28
  112.1 2.5 %collective-permute-start.7 = (bf16[128,2048]{1,0:T(8,128)(2,1)S(1)}, bf16[128,2048]{1,0:T(8,128)(2,1)S(1)}, u32[]{:S(2)}, u32[]{:S(2)}) collective-permute-start(bf16[128,2048]{1,0:T(8,128)(2,1)S(1)} %fusion.28), channel_id=1, source_target_pairs={{0,1},{1,0},{2,3},{3,2},{4,5},{5,4},{6,7},{7,6},{8,9},{9,8},{10,11... | collective-permute-start | bytes 1572872 | tf_op jit(solution)/shard_map/ppermute | solution.py:76
  114.6 1.0 collective-permute-done.9
  115.8 0.4 collective-permute-done.7
  116.1 0.3 add_convert_fusion.1
  116.5 16.5 %all_to_all.55 = bf16[4,64,2048]{2,1,0:T(8,128)(2,1)S(1)} all-to-all(bf16[4,64,2048]{2,1,0:T(8,128)(2,1)S(1)} %pad_maximum_fusion), channel_id=1, replica_groups=mesh['y'=4,'z'=16,'x'=4,'c'=2] {'x'}, dimensions={0} | all-to-all | bytes 2097152 | tf_op jit(solution)/shard_map/all_to_all | solution.py:24
  133.3 0.8 bitcast_bitcast_fusion
  134.1 11.7 %all-to-all-start.5 = ((bf16[16,64,128]{2,1,0:T(8,128)(2,1)}), bf16[16,64,128]{2,1,0:T(8,128)(2,1)S(1)}, u32[]{:S(2)}, u32[]{:S(2)}) async-start(bf16[16,64,128]{2,1,0:T(8,128)(2,1)} %bitcast_bitcast_fusion), calls=%async_computation.5 | async-start | bytes 524288 | tf_op jit(solution)/shard_map/all_to_all | solution.py:24
  145.8 0.7 pad_add_fusion.spot_ref
  146.5 0.6 slice.107.q_ref
  147.1 1.1 pad_maximum_fusion.1.across_ref
  148.2 10.4 %all-to-all-done.5.sums_ref = bf16[16,64,128]{2,1,0:T(8,128)(2,1)S(1)} async-done(((bf16[16,64,128]{2,1,0:T(8,128)(2,1)}), bf16[16,64,128]{2,1,0:T(8,128)(2,1)S(1)}, u32[]{:S(2)}, u32[]{:S(2)}) %all-to-all-start.5) | async-done | bytes 262176 | tf_op jit(solution)/shard_map/all_to_all | solution.py:24
  158.6 0.7 copy-done.6
  159.3 2.9 %shard_map.138 = (bf16[64,128]{1,0:T(8,128)(2,1)}, bf16[256,128]{1,0:T(8,128)(2,1)}, bf16[256,128]{1,0:T(8,128)(2,1)}, f32[32,128]{1,0:T(8,128)}) custom-call(s32[2]{0:T(128)} %pad_add_fusion.spot_ref, bf16[16,64,128]{2,1,0:T(8,128)(2,1)} %copy-done.6, bf16[32,4096]{1,0:T(8,128)(2,1)} %copy-done.2, bf16[32,128]{1,0:T(8,128)(2,1)} %slice.107.q_ref, ...), custom_call_target="tpu_custom_call" | custom-call | tf_op jit(solution)/shard_map/pallas_call | solution.py:171
  162.2 9.0 %collective-permute-start.10 = (bf16[256,128]{1,0:T(8,128)(2,1)}, bf16[256,128]{1,0:T(8,128)(2,1)S(1)}, u32[]{:S(2)}, u32[]{:S(2)}) collective-permute-start(bf16[256,128]{1,0:T(8,128)(2,1)} %get-tuple-element.32), channel_id=1, source_target_pairs={{0,1},{1,0},{2,3},{3,2},{4,5},{5,4},{6,7},{7,6},{8,9},{9,8},{10,11... | collective-permute-start | bytes 196616 | tf_op jit(solution)/shard_map/ppermute | solution.py:76
  171.2 1.3 split.22.more_ref
  172.5 0.6 copy-done.18
  173.1 1.6 shard_map.139
  174.8 5.1 %all-to-all-start.6 = ((bf16[16,80,128]{2,1,0:T(8,128)(2,1)}), bf16[16,80,128]{2,1,0:T(8,128)(2,1)S(1)}, u32[]{:S(2)}, u32[]{:S(2)}) async-start(bf16[16,80,128]{2,1,0:T(8,128)(2,1)} %shard_map.139), calls=%async_computation.6 | async-start | bytes 655360 | tf_op jit(solution)/shard_map/all_to_all | solution.py:24
  180.1 8.8 %all-to-all-done.6 = bf16[16,80,128]{2,1,0:T(8,128)(2,1)S(1)} async-done(((bf16[16,80,128]{2,1,0:T(8,128)(2,1)}), bf16[16,80,128]{2,1,0:T(8,128)(2,1)S(1)}, u32[]{:S(2)}, u32[]{:S(2)}) %all-to-all-start.6) | async-done | bytes 327712 | tf_op jit(solution)/shard_map/all_to_all | solution.py:24
  189.0 0.7 copy.61
  189.7 5.1 %all-to-all-start.7 = ((bf16[16,32,128]{2,1,0:T(8,128)(2,1)}), bf16[16,32,128]{2,1,0:T(8,128)(2,1)S(1)}, u32[]{:S(2)}, u32[]{:S(2)}) async-start(bf16[16,32,128]{2,1,0:T(8,128)(2,1)} %copy.61), calls=%async_computation.7 | async-start | bytes 262144 | tf_op jit(solution)/shard_map/all_to_all | solution.py:24
  195.1 1.0 fusion.5
  196.1 1.0 fusion.4
  197.1 9.8 %all-to-all-done.7 = bf16[16,32,128]{2,1,0:T(8,128)(2,1)S(1)} async-done(((bf16[16,32,128]{2,1,0:T(8,128)(2,1)}), bf16[16,32,128]{2,1,0:T(8,128)(2,1)S(1)}, u32[]{:S(2)}, u32[]{:S(2)}) %all-to-all-start.7) | async-done | bytes 131104 | tf_op jit(solution)/shard_map/all_to_all | solution.py:24
  207.1 0.9 broadcast_in_dim.107
  207.9 7.0 %all-to-all-start.8 = ((bf16[8,16,2048]{2,1,0:T(8,128)(2,1)}), bf16[8,16,2048]{2,1,0:T(8,128)(2,1)S(1)}, u32[]{:S(2)}, u32[]{:S(2)}) async-start(bf16[8,16,2048]{2,1,0:T(8,128)(2,1)} %broadcast_in_dim.107), calls=%async_computation.8 | async-start | bytes 1048576 | tf_op jit(solution)/shard_map/all_to_all | solution.py:24
  214.9 1.1 fusion.1
  216.1 0.3 convolution_convert_fusion.1
  216.4 0.9 broadcast_select_fusion
  217.3 7.1 %all-to-all-done.8 = bf16[8,16,2048]{2,1,0:T(8,128)(2,1)S(1)} async-done(((bf16[8,16,2048]{2,1,0:T(8,128)(2,1)}), bf16[8,16,2048]{2,1,0:T(8,128)(2,1)S(1)}, u32[]{:S(2)}, u32[]{:S(2)}) %all-to-all-start.8) | async-done | bytes 524320 | tf_op jit(solution)/shard_map/all_to_all | solution.py:24
  224.4 0.8 fusion.96
  (120 shorter events, 5.3 us)
Async XLA Ops:
  7.2 103.0 %copy-start = (bf16[1,80,2048]{2,1,0:T(8,128)(2,1)S(1)}, bf16[1,80,2048]{2,1,0:T(8,128)(2,1)}, u32[]{:S(2)}) copy-start(bf16[1,80,2048]{2,1,0:T(8,128)(2,1)} %param.15) | copy-start | bytes 983044
  7.2 44.3 %all-gather.2.cloned.1.call-start = ((), (), s32[]{:S(2)}) async-start(), calls=%async_computation.9 | async-start | bytes 1310720 | tf_op jit(solution)/shard_map/all_gather | solution.py:237
  11.6 12.2 %copy-start.16 = (bf16[64,2048]{1,0:T(8,128)(2,1)S(1)}, bf16[64,2048]{1,0:T(8,128)(2,1)}, u32[]{:S(2)}) copy-start(bf16[64,2048]{1,0:T(8,128)(2,1)} %param.11) | copy-start | bytes 786436
  11.6 11.4 %all-to-all-start = ((bf16[4,8,6272]{2,1,0:T(8,128)(2,1)}), bf16[4,8,6272]{2,1,0:T(8,128)(2,1)S(1)}, u32[]{:S(2)}, u32[]{:S(2)}) async-start(bf16[4,8,6272]{2,1,0:T(8,128)(2,1)} %get-tuple-element.22), calls=%async_computation | async-start | bytes 802816 | tf_op jit(solution)/shard_map/all_to_all | solution.py:24
  23.5 1.0 copy-start.17
  26.1 7.8 %all-to-all-start.1 = ((f32[4,2,2176]{2,1,0:T(2,128)}), f32[4,2,2176]{2,1,0:T(2,128)S(1)}, u32[]{:S(2)}, u32[]{:S(2)}) async-start(f32[4,2,2176]{2,1,0:T(2,128)} %all_to_all.36), calls=%async_computation.1 | async-start | bytes 139264 | tf_op jit(solution)/shard_map/all_to_all | solution.py:24
  35.5 44.8 %all-to-all-start.2 = ((bf16[16,2,4224]{2,1,0:T(2,128)(2,1)}), bf16[16,2,4224]{2,1,0:T(2,128)(2,1)S(1)}, u32[]{:S(2)}, u32[]{:S(2)}) async-start(bf16[16,2,4224]{2,1,0:T(2,128)(2,1)} %pad_maximum_fusion.3), calls=%async_computation.2 | async-start | bytes 540672 | tf_op jit(solution)/shard_map/all_to_all | solution.py:24
  51.4 13.5 %copy-start.25 = (bf16[8,128]{1,0:T(8,128)(2,1)S(1)}, bf16[8,128]{1,0:T(8,128)(2,1)}, u32[]{:S(2)}) copy-start(bf16[8,128]{1,0:T(8,128)(2,1)} %get-tuple-element.21) | copy-start | bytes 6148
  52.7 13.2 %collective-permute-start.3 = (bf16[64,2048]{1,0:T(8,128)(2,1)S(1)}, bf16[64,2048]{1,0:T(8,128)(2,1)S(1)}, u32[]{:S(2)}, u32[]{:S(2)}) collective-permute-start(bf16[64,2048]{1,0:T(8,128)(2,1)S(1)} %get-tuple-element.40), channel_id=1, source_target_pairs={{0,1},{1,0},{2,3},{3,2},{4,5},{5,4},{6,7},{7,6},{8,9},{9,8},{10,11... | collective-permute-start | bytes 786440 | tf_op jit(solution)/shard_map/ppermute | solution.py:76
  58.7 7.3 %collective-permute-start.2 = (bf16[64,2048]{1,0:T(8,128)(2,1)S(1)}, bf16[64,2048]{1,0:T(8,128)(2,1)S(1)}, u32[]{:S(2)}, u32[]{:S(2)}) collective-permute-start(bf16[64,2048]{1,0:T(8,128)(2,1)S(1)} %get-tuple-element.41), channel_id=1, source_target_pairs={{0,1},{1,0},{2,3},{3,2},{4,5},{5,4},{6,7},{7,6},{8,9},{9,8},{10,11... | collective-permute-start | bytes 786440 | tf_op jit(solution)/shard_map/ppermute | solution.py:76
  60.6 5.4 %collective-permute-start.1 = (bf16[64,2048]{1,0:T(8,128)(2,1)S(1)}, bf16[64,2048]{1,0:T(8,128)(2,1)S(1)}, u32[]{:S(2)}, u32[]{:S(2)}) collective-permute-start(bf16[64,2048]{1,0:T(8,128)(2,1)S(1)} %get-tuple-element.42), channel_id=1, source_target_pairs={{0,1},{1,0},{2,3},{3,2},{4,5},{5,4},{6,7},{7,6},{8,9},{9,8},{10,11... | collective-permute-start | bytes 786440 | tf_op jit(solution)/shard_map/ppermute | solution.py:76
  63.0 3.4 %collective-permute-start = (bf16[64,2048]{1,0:T(8,128)(2,1)S(1)}, bf16[64,2048]{1,0:T(8,128)(2,1)S(1)}, u32[]{:S(2)}, u32[]{:S(2)}) collective-permute-start(bf16[64,2048]{1,0:T(8,128)(2,1)S(1)} %get-tuple-element.43), channel_id=1, source_target_pairs={{0,1},{1,0},{2,3},{3,2},{4,5},{5,4},{6,7},{7,6},{8,9},{9,8},{10,11... | collective-permute-start | bytes 786440 | tf_op jit(solution)/shard_map/ppermute | solution.py:76
  65.9 0.7 copy-start.7
  66.0 0.8 copy-start.9
  66.0 0.8 copy-start.11
  66.4 0.7 copy-start.13
  76.0 9.8 %collective-permute-start.4 = (bf16[128,2048]{1,0:T(8,128)(2,1)}, bf16[128,2048]{1,0:T(8,128)(2,1)S(1)}, u32[]{:S(2)}, u32[]{:S(2)}) collective-permute-start(bf16[128,2048]{1,0:T(8,128)(2,1)} %get-tuple-element.24), channel_id=1, source_target_pairs={{0,1},{1,0},{2,3},{3,2},{4,5},{5,4},{6,7},{7,6},{8,9},{9,8},{10,11... | collective-permute-start | bytes 1572872 | tf_op jit(solution)/shard_map/ppermute | solution.py:76
  78.2 7.6 %collective-permute-start.5 = (bf16[128,2048]{1,0:T(8,128)(2,1)}, bf16[128,2048]{1,0:T(8,128)(2,1)}, u32[]{:S(2)}, u32[]{:S(2)}) collective-permute-start(bf16[128,2048]{1,0:T(8,128)(2,1)} %get-tuple-element.25), channel_id=1, source_target_pairs={{0,1},{1,0},{2,3},{3,2},{4,5},{5,4},{6,7},{7,6},{8,9},{9,8},{10,11... | collective-permute-start | bytes 1572872 | tf_op jit(solution)/shard_map/ppermute | solution.py:76
  80.5 1.1 copy-start.2
  81.6 4.2 %copy-start.5 = (bf16[256,2048]{1,0:T(8,128)(2,1)S(1)}, bf16[256,2048]{1,0:T(8,128)(2,1)}, u32[]{:S(2)}) copy-start(bf16[256,2048]{1,0:T(8,128)(2,1)} %get-tuple-element.27) | copy-start | bytes 3145732
  81.6 18.8 %all-to-all-start.3 = ((bf16[4,32,4096]{2,1,0:T(8,128)(2,1)}), bf16[4,32,4096]{2,1,0:T(8,128)(2,1)S(1)}, u32[]{:S(2)}, u32[]{:S(2)}) async-start(bf16[4,32,4096]{2,1,0:T(8,128)(2,1)} %broadcast_in_dim.103), calls=%async_computation.3 | async-start | bytes 2097152 | tf_op jit(solution)/shard_map/all_to_all | solution.py:24
  87.2 23.3 %copy-start.24 = (bf16[1,80,2048]{2,1,0:T(8,128)(2,1)S(1)}, bf16[1,80,2048]{2,1,0:T(8,128)(2,1)}, u32[]{:S(2)}) copy-start(bf16[1,80,2048]{2,1,0:T(8,128)(2,1)} %param.16) | copy-start | bytes 983044
  100.4 10.8 %collective-permute-start.6 = (bf16[128,4096]{1,0:T(8,128)(2,1)S(1)}, bf16[128,4096]{1,0:T(8,128)(2,1)S(1)}, u32[]{:S(2)}, u32[]{:S(2)}) collective-permute-start(bf16[128,4096]{1,0:T(8,128)(2,1)S(1)} %bitcast.96), channel_id=1, source_target_pairs={{0,1},{1,0},{2,3},{3,2},{4,5},{5,4},{6,7},{7,6},{8,9},{9,8},{10,11... | collective-permute-start | bytes 3145736 | tf_op jit(solution)/shard_map/ppermute | solution.py:76
  103.7 11.9 %collective-permute-start.8 = (bf16[64,2048]{1,0:T(8,128)(2,1)S(1)}, bf16[64,2048]{1,0:T(8,128)(2,1)S(1)}, u32[]{:S(2)}, u32[]{:S(2)}) collective-permute-start(bf16[64,2048]{1,0:T(8,128)(2,1)S(1)} %get-tuple-element.36), channel_id=1, source_target_pairs={{0,128},{128,256},{256,384},{384,0},{1,129},{129,257},{257,385},{3... | collective-permute-start | bytes 786440 | tf_op jit(solution)/shard_map/ppermute | solution.py:312
  105.9 9.7 %collective-permute-start.9 = (bf16[64,2048]{1,0:T(8,128)(2,1)S(1)}, bf16[64,2048]{1,0:T(8,128)(2,1)S(1)}, u32[]{:S(2)}, u32[]{:S(2)}) collective-permute-start(bf16[64,2048]{1,0:T(8,128)(2,1)S(1)} %get-tuple-element.37), channel_id=1, source_target_pairs={{0,384},{128,0},{256,128},{384,256},{1,385},{129,1},{257,129},{385... | collective-permute-start | bytes 786440 | tf_op jit(solution)/shard_map/ppermute | solution.py:312
  110.5 0.6 copy-start.21
  111.1 1.0 copy-start.3
  111.5 4.2 %copy-start.19 = (f32[128,80]{0,1:T(8,128)}, f32[128,80]{0,1:T(8,128)S(1)}, u32[]{:S(2)}) copy-start(f32[128,80]{0,1:T(8,128)S(1)} %fusion.14) | copy-start | bytes 122884
  112.1 4.0 %collective-permute-start.7 = (bf16[128,2048]{1,0:T(8,128)(2,1)S(1)}, bf16[128,2048]{1,0:T(8,128)(2,1)S(1)}, u32[]{:S(2)}, u32[]{:S(2)}) collective-permute-start(bf16[128,2048]{1,0:T(8,128)(2,1)S(1)} %fusion.28), channel_id=1, source_target_pairs={{0,1},{1,0},{2,3},{3,2},{4,5},{5,4},{6,7},{7,6},{8,9},{9,8},{10,11... | collective-permute-start | bytes 1572872 | tf_op jit(solution)/shard_map/ppermute | solution.py:76
  133.1 14.0 %copy-start.8 = (bf16[64,2048]{1,0:T(8,128)(2,1)S(1)}, bf16[64,2048]{1,0:T(8,128)(2,1)}, u32[]{:S(2)}) copy-start(bf16[64,2048]{1,0:T(8,128)(2,1)} %copy-done.7) | copy-start | bytes 786436
  133.1 14.0 %copy-start.10 = (bf16[64,2048]{1,0:T(8,128)(2,1)S(1)}, bf16[64,2048]{1,0:T(8,128)(2,1)}, u32[]{:S(2)}) copy-start(bf16[64,2048]{1,0:T(8,128)(2,1)} %copy-done.9) | copy-start | bytes 786436
  133.3 13.8 %copy-start.12 = (bf16[64,2048]{1,0:T(8,128)(2,1)S(1)}, bf16[64,2048]{1,0:T(8,128)(2,1)}, u32[]{:S(2)}) copy-start(bf16[64,2048]{1,0:T(8,128)(2,1)} %copy-done.11) | copy-start | bytes 786436
  133.3 13.8 %copy-start.14 = (bf16[64,2048]{1,0:T(8,128)(2,1)S(1)}, bf16[64,2048]{1,0:T(8,128)(2,1)}, u32[]{:S(2)}) copy-start(bf16[64,2048]{1,0:T(8,128)(2,1)} %copy-done.13) | copy-start | bytes 786436
  134.1 24.5 %all-to-all-start.5 = ((bf16[16,64,128]{2,1,0:T(8,128)(2,1)}), bf16[16,64,128]{2,1,0:T(8,128)(2,1)S(1)}, u32[]{:S(2)}, u32[]{:S(2)}) async-start(bf16[16,64,128]{2,1,0:T(8,128)(2,1)} %bitcast_bitcast_fusion), calls=%async_computation.5 | async-start | bytes 524288 | tf_op jit(solution)/shard_map/all_to_all | solution.py:24
  158.6 0.7 copy-start.6
  162.2 17.6 %copy-start.22 = (f32[128,80]{0,1:T(8,128)S(1)}, f32[128,80]{0,1:T(8,128)}, u32[]{:S(2)}) copy-start(f32[128,80]{0,1:T(8,128)} %copy-done.21) | copy-start | bytes 122884
  162.2 10.3 %collective-permute-start.10 = (bf16[256,128]{1,0:T(8,128)(2,1)}, bf16[256,128]{1,0:T(8,128)(2,1)S(1)}, u32[]{:S(2)}, u32[]{:S(2)}) collective-permute-start(bf16[256,128]{1,0:T(8,128)(2,1)} %get-tuple-element.32), channel_id=1, source_target_pairs={{0,1},{1,0},{2,3},{3,2},{4,5},{5,4},{6,7},{7,6},{8,9},{9,8},{10,11... | collective-permute-start | bytes 196616 | tf_op jit(solution)/shard_map/ppermute | solution.py:76
  172.5 0.6 copy-start.18
  174.7 14.2 %copy-start.23 = (f32[32,128]{1,0:T(8,128)S(1)}, f32[32,128]{1,0:T(8,128)}, u32[]{:S(2)}) copy-start(f32[32,128]{1,0:T(8,128)} %get-tuple-element.33) | copy-start | bytes 49156
  174.8 14.1 %all-to-all-start.6 = ((bf16[16,80,128]{2,1,0:T(8,128)(2,1)}), bf16[16,80,128]{2,1,0:T(8,128)(2,1)S(1)}, u32[]{:S(2)}, u32[]{:S(2)}) async-start(bf16[16,80,128]{2,1,0:T(8,128)(2,1)} %shard_map.139), calls=%async_computation.6 | async-start | bytes 655360 | tf_op jit(solution)/shard_map/all_to_all | solution.py:24
  189.0 6.1 %copy-start.4 = (bf16[128,4096]{1,0:T(8,128)(2,1)S(1)}, bf16[128,4096]{1,0:T(8,128)(2,1)}, u32[]{:S(2)}) copy-start(bf16[128,4096]{1,0:T(8,128)(2,1)} %copy-done.3) | copy-start | bytes 3145732
  189.7 17.1 %all-to-all-start.7 = ((bf16[16,32,128]{2,1,0:T(8,128)(2,1)}), bf16[16,32,128]{2,1,0:T(8,128)(2,1)S(1)}, u32[]{:S(2)}, u32[]{:S(2)}) async-start(bf16[16,32,128]{2,1,0:T(8,128)(2,1)} %copy.61), calls=%async_computation.7 | async-start | bytes 262144 | tf_op jit(solution)/shard_map/all_to_all | solution.py:24
  195.1 1.0 copy-start.20
  206.9 8.0 %copy-start.1 = (bf16[128,2048]{1,0:T(8,128)(2,1)S(1)}, bf16[128,2048]{1,0:T(8,128)(2,1)}, u32[]{:S(2)}) copy-start(bf16[128,2048]{1,0:T(8,128)(2,1)} %up_ref.1) | copy-start | bytes 1572868
  207.9 16.5 %all-to-all-start.8 = ((bf16[8,16,2048]{2,1,0:T(8,128)(2,1)}), bf16[8,16,2048]{2,1,0:T(8,128)(2,1)S(1)}, u32[]{:S(2)}, u32[]{:S(2)}) async-start(bf16[8,16,2048]{2,1,0:T(8,128)(2,1)} %broadcast_in_dim.107), calls=%async_computation.8 | async-start | bytes 1048576 | tf_op jit(solution)/shard_map/all_to_all | solution.py:24
  214.9 1.5 copy-start.15
Sparse Core Ops, SparseCore 0:
  10.7 36.0 all-gather.1

commit v6 on v5

--- a/solution.py
+++ b/solution.py
@@ -7,7 +7,7 @@
 
 HEAD = 64
 GCAP = 2
-PIECES = 4
+PIECES = 2
 SCALE = HEAD ** (-0.5)
 BF, F32 = jnp.bfloat16, jnp.float32
 DEVICES = ("y", "z", "x", "c")
@@ -101,48 +101,42 @@
     return (g_queries.T * SCALE).astype(BF), keep, send
 
 
-def bulk_kernel(core_ref, free_ref, up_ref, q_ref, own_ref, *refs):
-    across, (gq_ref, keep_ref), sends = refs[:PIECES], refs[PIECES : PIECES + 2], refs[PIECES + 2 :]
+def bulk_kernel(
+    core_ref, free_ref, up_ref, q_ref, own_ref, across_ref, gq_ref, keep_ref, send_ref
+):
     first = core_ref[0] == 0
     free = free_ref[...]
-    rows = sends[0].shape[0]
     for pair in range(q_ref.shape[1] // (2 * HEAD)):
         cols = slice(pair * 2 * HEAD, (pair + 1) * 2 * HEAD)
-        gq_ref[:, cols], keep_ref[:, cols], send = pair_backward(
-            first,
-            q_ref[:, cols],
-            up_ref[:, cols] * free,
-            own_ref[:, cols],
-            jnp.concatenate([ref[:, cols] for ref in across], axis=0),
+        gq_ref[:, cols], keep_ref[:, cols], send_ref[:, cols] = pair_backward(
+            first, q_ref[:, cols], up_ref[:, cols] * free, own_ref[:, cols], across_ref[:, cols]
         )
-        for i, ref in enumerate(sends):
-            ref[:, cols] = send[i * rows : (i + 1) * rows]
-
-
-def bulk_backward(core, free, upstream, queries, own, across):
-    tokens, width = queries.shape
-    mem = own.shape[0]
+
+
+def bulk_backward(core, free, upstream, queries, own, across, piece):
+    tokens = queries.shape[0]
+    mem, width = across.shape
     block = 512
+    skip = piece * (width // block)
+    part = lambda n: pl.BlockSpec((n, block), lambda i: (0, skip + i))
     column = lambda n: pl.BlockSpec((n, block), lambda i: (0, i))
-    outs = [tokens, mem] + [mem // 2] * 2
-    got = pl.pallas_call(
+    return pl.pallas_call(
         bulk_kernel,
         grid=(width // block,),
         in_specs=[
             pl.BlockSpec(memory_space=pltpu.SMEM),
             pl.BlockSpec(free.shape, lambda i: (0, 0)),
-            column(tokens),
-            column(tokens),
+            part(tokens),
+            part(tokens),
+            part(mem),
             column(mem),
-        ]
-        + [column(mem // PIECES)] * PIECES,
-        out_specs=[column(n) for n in outs],
-        out_shape=[jax.ShapeDtypeStruct((n, width), BF) for n in outs],
+        ],
+        out_specs=[column(tokens), column(mem), column(mem)],
+        out_shape=[jax.ShapeDtypeStruct((n, width), BF) for n in (tokens, mem, mem)],
         cost_estimate=pl.CostEstimate(
             flops=12 * tokens * mem * width, bytes_accessed=8 * mem * width, transcendentals=0
         ),
-    )(core, free, upstream, queries, own, *across)
-    return got[0], got[1], got[2:]
+    )(core, free, upstream, queries, own, across)
 
 
 def routed_kernel(
@@ -234,13 +228,14 @@
     slots = window * GCAP
     mine, core, depth = lax.axis_index("y"), lax.axis_index("c"), lax.axis_index("z")
     first = core == 0
-    own_memory = lax.all_gather(jnp.where(first, mem_keys, mem_values), "y", axis=0, tiled=True)
 
     experts = jnp.arange(window, dtype=jnp.int32)
     slot_ids = jnp.arange(slots, dtype=jnp.int32)
     picked, place = pick_rows(
         send_counts, expert_ids.reshape(1, tokens), (queries, states, upstream), slots, window
     )
+    own_memory = jnp.where(first, after(mem_keys, picked), mem_values)
+    own_memory = lax.all_gather(own_memory, "y", axis=0, tiled=True)
     group = exchange(picked, "y").reshape(window * slots, -1)
 
     counts = group[:, 3 * width].reshape(window, slots)[:, ::GCAP].astype(jnp.int32)
@@ -289,20 +284,27 @@
     routed_queries = level[:, 2 * width :]
     level = level[:, : 2 * width]
     across_memory = [
-        other_core(piece) for piece in jnp.split(after(own_memory, pair), PIECES, axis=0)
+        other_core(piece) for piece in jnp.split(after(own_memory, pair), PIECES, axis=1)
     ]
 
-    bulk_queries, keep, send = bulk_backward(
-        core.reshape(1).astype(jnp.int32),
-        (1.0 - taken).astype(BF),
-        upstream,
-        queries,
-        own_memory,
-        across_memory,
-    )
-    near = spread(after(level, *send), "x")
-    sent = jnp.concatenate([other_core(piece) for piece in send], axis=0)
-    bulk = (keep.astype(F32) + sent.astype(F32)).astype(BF)
+    bulk = [
+        bulk_backward(
+            core.reshape(1).astype(jnp.int32),
+            (1.0 - taken).astype(BF),
+            upstream,
+            queries,
+            own_memory,
+            across_memory[piece],
+            piece,
+        )
+        for piece in range(PIECES)
+    ]
+    near = spread(after(level, *across_memory), "x")
+    bulk_queries = jnp.concatenate([part[0] for part in bulk], axis=1)
+    bulk = jnp.concatenate(
+        [(keep.astype(F32) + other_core(send).astype(F32)).astype(BF) for _, keep, send in bulk],
+        axis=1,
+    )
     own_rows = mem_keys.shape[0]
     blocks = [
         lax.dynamic_slice_in_dim(bulk, (mine + d) % window * own_rows, own_rows, 0)
@@ -310,7 +312,7 @@
     ]
     moves = [[(i, (i + d) % window) for i in range(window)] for d in range(window)]
     got = [lax.ppermute(blocks[d], "y", moves[d]) for d in (1, 3)]
-    far = other_core(after(near, *blocks))
+    far = other_core(near)
     weight_in, weight_out = w_in[0], w_out[0]
     parts_of_x = lax.axis_size("x")
 
@@ -338,7 +340,7 @@
         level,
         routed_queries,
         own_memory,
-        jnp.concatenate(across_memory, axis=0),
+        jnp.concatenate(across_memory, axis=1),
     )
 
     blocks = window * parts_of_x

time: 234 us -> 222 us (0.949)
  waiting for transfers between devices: 61.3 us -> 53.3 us
  starting transfers between devices: 95.2 us -> 87.9 us
    all_to_all x8, waiting for transfers between devices: 59.5 us -> 45.2 us  [exchange(): return lax.all_to_all(values, axes, split_axis=0, concat_axis=0, tiled=True)]
    all_to_all x8, starting transfers between devices: 57.4 us -> 51.5 us  [exchange(): return lax.all_to_all(values, axes, split_axis=0, concat_axis=0, tiled=True)]
    all_gather x1, waiting for transfers between devices: 0.02 us -> 5.23 us  [per_device(): own_memory = lax.all_gather(own_memory, 'y', axis=0, tiled=True)]
    pallas_call x1 -> x2, Pallas kernels: 8.83 us -> 10.7 us  [bulk_backward(): pl.pallas_call(bulk_kernel, grid=(width // block,), in_specs=[pl.BlockSpe...]
    ppermute x9 -> x7, starting transfers between devices: 31.2 us -> 29.7 us  [other_core(): return lax.ppermute(values, 'c', [(0, 1), (1, 0)])]
  transfers between devices with their start and end apart: 20 -> 18, of which waited for: 10 -> 12; matrix products, arithmetic and copies ran while one was open for 8% -> 9% of each run, Pallas kernels for 5% -> 5%
where the time goes in v6:
time: 222 us; the launch traced here: 221 us
  starting transfers between devices  87.9 us (40%)
  waiting for transfers between devices  53.3 us (24%)
  Pallas kernels  17.8 us (8%)
  blocking collectives  17.8 us (8%)
  between operations  14.8 us (7%)
  local copies, waits for them, and re-layouts  14.3 us (6%)
  matrix products  8.82 us (4%)
  other arithmetic  5.64 us (3%)
    all_to_all x8, starting transfers between devices, exchange(): return lax.all_to_all(values, axes, split_axis=0, concat_axis=0, tiled=True)  51.5 us
    all_to_all x8, waiting for transfers between devices, exchange(): return lax.all_to_all(values, axes, split_axis=0, concat_axis=0, tiled=True)  45.2 us
    ppermute x7, starting transfers between devices, other_core(): return lax.ppermute(values, 'c', [(0, 1), (1, 0)])  29.7 us
    all_to_all x1, blocking collectives, exchange(): return lax.all_to_all(values, axes, split_axis=0, concat_axis=0, tiled=True)  17.8 us
    pallas_call x2, Pallas kernels, bulk_backward(): pl.pallas_call(bulk_kernel, grid=(width // block,), in_specs=[pl.BlockSpe...  10.7 us
    dot_general x16, matrix products, dot(): lax.dot_general(left, right, (((left_dim,), (right_dim,)), ((), ())), pre...  8.55 us
    ppermute x2, starting transfers between devices, per_device(): got = [lax.ppermute(blocks[d], 'y', moves[d]) for d in (1, 3)]  6.62 us
    all_gather x1, waiting for transfers between devices, per_device(): own_memory = lax.all_gather(own_memory, 'y', axis=0, tiled=True)  5.23 us
  transfers between devices with their start and end apart: 18, of which 12 were waited for; matrix products, arithmetic and copies ran while one was open for 9% of the time, Pallas kernels for 5%

profile of v6, /device:TPU:1, one launch (start us, length us, event | category | flops | bytes accessed | tf_op | source)
XLA Modules:
  0.0 220.5 jit_solution(225285937193904061)
XLA Ops:
  7.2 2.6 %shard_map.136 = (bf16[4,8,6272]{2,1,0:T(8,128)(2,1)}, bf16[8,128]{1,0:T(8,128)(2,1)}) custom-call(s32[1,4]{1,0:T(1,128)} %counts_ref.1, s32[1,128]{1,0:T(1,128)} %bitcast.116, bf16[128,2048]{1,0:T(8,128)(2,1)} %q_ref.3, bf16[128,2048]{1,0:T(8,128)(2,1)} %refs_1_.1, bf16[128,2048]{1,0:T(8,128)(2,1)} %up_ref.3), custom_call_target="tpu_custom_call" | custom-call | tf_op jit(solution)/shard_map/pallas_call | solution.py:211
  9.9 5.0 %all-to-all-start = ((bf16[4,8,6272]{2,1,0:T(8,128)(2,1)}), bf16[4,8,6272]{2,1,0:T(8,128)(2,1)S(1)}, u32[]{:S(2)}, u32[]{:S(2)}) async-start(bf16[4,8,6272]{2,1,0:T(8,128)(2,1)} %get-tuple-element.24), calls=%async_computation | async-start | bytes 802816 | tf_op jit(solution)/shard_map/all_to_all | solution.py:24
  14.9 0.7 broadcast_select_fusion
  15.7 5.4 %all-to-all-done = bf16[4,8,6272]{2,1,0:T(8,128)(2,1)S(1)} async-done(((bf16[4,8,6272]{2,1,0:T(8,128)(2,1)}), bf16[4,8,6272]{2,1,0:T(8,128)(2,1)S(1)}, u32[]{:S(2)}, u32[]{:S(2)}) %all-to-all-start) | async-done | bytes 401440 | tf_op jit(solution)/shard_map/all_to_all | solution.py:24
  21.9 0.5 fusion.105
  22.4 0.5 fusion.6
  23.3 0.7 all_to_all.36
  24.0 3.3 %all-to-all-start.1 = ((f32[4,2,2176]{2,1,0:T(2,128)}), f32[4,2,2176]{2,1,0:T(2,128)S(1)}, u32[]{:S(2)}, u32[]{:S(2)}) async-start(f32[4,2,2176]{2,1,0:T(2,128)} %all_to_all.36), calls=%async_computation.1 | async-start | bytes 139264 | tf_op jit(solution)/shard_map/all_to_all | solution.py:24
  27.6 4.2 %all-to-all-done.1 = f32[4,2,2176]{2,1,0:T(2,128)S(1)} async-done(((f32[4,2,2176]{2,1,0:T(2,128)}), f32[4,2,2176]{2,1,0:T(2,128)S(1)}, u32[]{:S(2)}, u32[]{:S(2)}) %all-to-all-start.1) | async-done | bytes 69664 | tf_op jit(solution)/shard_map/all_to_all | solution.py:24
  31.9 0.3 fusion.7
  32.5 1.0 pad_maximum_fusion.3
  33.4 15.6 %all-to-all-start.2 = ((bf16[16,2,4224]{2,1,0:T(2,128)(2,1)}), bf16[16,2,4224]{2,1,0:T(2,128)(2,1)S(1)}, u32[]{:S(2)}, u32[]{:S(2)}) async-start(bf16[16,2,4224]{2,1,0:T(2,128)(2,1)} %pad_maximum_fusion.3), calls=%async_computation.2 | async-start | bytes 540672 | tf_op jit(solution)/shard_map/all_to_all | solution.py:24
  49.0 5.2 %all-gather.2.cloned.1.call-done.own_ref = bf16[256,2048]{1,0:T(8,128)(2,1)} async-done(((bf16[64,2048]{1,0:T(8,128)(2,1)}), bf16[256,2048]{1,0:T(8,128)(2,1)}) %all-gather.2.cloned.1.call-update) | async-done | bytes 1048592 | tf_op jit(solution)/shard_map/all_gather | solution.py:238
  54.2 2.1 fusion.101
  56.3 3.5 %collective-permute-start = (bf16[256,1024]{1,0:T(8,128)(2,1)}, bf16[256,1024]{1,0:T(8,128)(2,1)S(1)}, u32[]{:S(2)}, u32[]{:S(2)}) collective-permute-start(bf16[256,1024]{1,0:T(8,128)(2,1)} %get-tuple-element.44), channel_id=1, source_target_pairs={{0,1},{1,0},{2,3},{3,2},{4,5},{5,4},{6,7},{7,6},{8,9},{9,8},{10,11... | collective-permute-start | bytes 1572872 | tf_op jit(solution)/shard_map/ppermute | solution.py:76
  59.8 1.9 collective-permute-start.1
  62.0 1.6 collective-permute-done.1.across_ref
  63.6 1.1 broadcast_in_dim.103
  64.8 4.0 %all-to-all-start.3 = ((bf16[4,32,4096]{2,1,0:T(8,128)(2,1)}), bf16[4,32,4096]{2,1,0:T(8,128)(2,1)S(1)}, u32[]{:S(2)}, u32[]{:S(2)}) async-start(bf16[4,32,4096]{2,1,0:T(8,128)(2,1)} %broadcast_in_dim.103), calls=%async_computation.3 | async-start | bytes 2097152 | tf_op jit(solution)/shard_map/all_to_all | solution.py:24
  68.7 0.8 fusion.104
  69.6 0.7 copy.60.free_ref
  70.3 5.3 %shard_map.138 = (bf16[128,1024]{1,0:T(8,128)(2,1)}, bf16[256,1024]{1,0:T(8,128)(2,1)}, bf16[256,1024]{1,0:T(8,128)(2,1)}) custom-call(s32[1]{0:T(128)} %bitcast.3.core_ref, bf16[128,1]{1,0:T(8,128)(2,1)} %copy.60.free_ref, bf16[128,2048]{1,0:T(8,128)(2,1)} %up_ref.3, bf16[128,2048]{1,0:T(8,128)(2,1)} %q_ref.3, ...), custom_call_target="tpu_custom_call" | custom-call | flops 402653184 | bytes 2097152 | tf_op jit(solution)/shard_map/pallas_call | solution.py:123
  75.7 8.4 %collective-permute-start.5 = (bf16[256,1024]{1,0:T(8,128)(2,1)}, bf16[256,1024]{1,0:T(8,128)(2,1)S(1)}, u32[]{:S(2)}, u32[]{:S(2)}) collective-permute-start(bf16[256,1024]{1,0:T(8,128)(2,1)} %get-tuple-element.31), channel_id=1, source_target_pairs={{0,1},{1,0},{2,3},{3,2},{4,5},{5,4},{6,7},{7,6},{8,9},{9,8},{10,11... | collective-permute-start | bytes 1572872 | tf_op jit(solution)/shard_map/ppermute | solution.py:76
  84.1 5.3 %shard_map.137 = (bf16[128,1024]{1,0:T(8,128)(2,1)}, bf16[256,1024]{1,0:T(8,128)(2,1)}, bf16[256,1024]{1,0:T(8,128)(2,1)}) custom-call(s32[1]{0:T(128)} %bitcast.3.core_ref, bf16[128,1]{1,0:T(8,128)(2,1)} %copy.60.free_ref, bf16[128,2048]{1,0:T(8,128)(2,1)} %up_ref.3, bf16[128,2048]{1,0:T(8,128)(2,1)} %q_ref.3, ...), custom_call_target="tpu_custom_call" | custom-call | flops 402653184 | bytes 2097152 | tf_op jit(solution)/shard_map/pallas_call | solution.py:123
  89.4 2.1 collective-permute-start.4
  91.5 2.4 %collective-permute-start.2 = (bf16[128,4096]{1,0:T(8,128)(2,1)S(1)}, bf16[128,4096]{1,0:T(8,128)(2,1)S(1)}, u32[]{:S(2)}, u32[]{:S(2)}) collective-permute-start(bf16[128,4096]{1,0:T(8,128)(2,1)S(1)} %bitcast.96), channel_id=1, source_target_pairs={{0,1},{1,0},{2,3},{3,2},{4,5},{5,4},{6,7},{7,6},{8,9},{9,8},{10,11... | collective-permute-start | bytes 3145736 | tf_op jit(solution)/shard_map/ppermute | solution.py:76
  94.5 2.3 %collective-permute-start.6 = (bf16[64,2048]{1,0:T(8,128)(2,1)S(1)}, bf16[64,2048]{1,0:T(8,128)(2,1)S(1)}, u32[]{:S(2)}, u32[]{:S(2)}) collective-permute-start(bf16[64,2048]{1,0:T(8,128)(2,1)S(1)} %get-tuple-element.40), channel_id=1, source_target_pairs={{0,128},{128,256},{256,384},{384,0},{1,129},{129,257},{257,385},{3... | collective-permute-start | bytes 786440 | tf_op jit(solution)/shard_map/ppermute | solution.py:314
  96.8 4.3 %collective-permute-start.7 = (bf16[64,2048]{1,0:T(8,128)(2,1)S(1)}, bf16[64,2048]{1,0:T(8,128)(2,1)S(1)}, u32[]{:S(2)}, u32[]{:S(2)}) collective-permute-start(bf16[64,2048]{1,0:T(8,128)(2,1)S(1)} %get-tuple-element.41), channel_id=1, source_target_pairs={{0,384},{128,0},{256,128},{384,256},{1,385},{129,1},{257,129},{385... | collective-permute-start | bytes 786440 | tf_op jit(solution)/shard_map/ppermute | solution.py:314
  101.1 0.3 fusion.21
  101.5 0.3 fusion.51
  101.8 0.3 fusion.14
  102.1 0.3 fusion.58
  102.4 0.3 fusion.28
  102.8 2.5 %collective-permute-start.3 = (bf16[128,2048]{1,0:T(8,128)(2,1)S(1)}, bf16[128,2048]{1,0:T(8,128)(2,1)S(1)}, u32[]{:S(2)}, u32[]{:S(2)}) collective-permute-start(bf16[128,2048]{1,0:T(8,128)(2,1)S(1)} %fusion.28), channel_id=1, source_target_pairs={{0,1},{1,0},{2,3},{3,2},{4,5},{5,4},{6,7},{7,6},{8,9},{9,8},{10,11... | collective-permute-start | bytes 1572872 | tf_op jit(solution)/shard_map/ppermute | solution.py:76
  105.3 0.4 collective-permute-done.6
  105.6 0.9 collective-permute-done.7
  106.8 0.3 add_convert_fusion.2
  107.2 17.8 %all_to_all.55 = bf16[4,64,2048]{2,1,0:T(8,128)(2,1)S(1)} all-to-all(bf16[4,64,2048]{2,1,0:T(8,128)(2,1)S(1)} %pad_maximum_fusion), channel_id=1, replica_groups=mesh['y'=4,'z'=16,'x'=4,'c'=2] {'x'}, dimensions={0} | all-to-all | bytes 2097152 | tf_op jit(solution)/shard_map/all_to_all | solution.py:24
  125.0 0.9 reduce_sum.81
  126.0 1.7 bitcast_bitcast_fusion
  127.7 6.1 %all-to-all-start.5 = ((bf16[16,64,128]{2,1,0:T(8,128)(2,1)}), bf16[16,64,128]{2,1,0:T(8,128)(2,1)S(1)}, u32[]{:S(2)}, u32[]{:S(2)}) async-start(bf16[16,64,128]{2,1,0:T(8,128)(2,1)} %bitcast_bitcast_fusion), calls=%async_computation.5 | async-start | bytes 524288 | tf_op jit(solution)/shard_map/all_to_all | solution.py:24
  133.8 0.7 pad_add_fusion.spot_ref
  134.5 1.3 slice.107.q_ref
  135.8 1.1 pad_maximum_fusion.1.across_ref
  136.8 9.7 %all-to-all-done.5.sums_ref = bf16[16,64,128]{2,1,0:T(8,128)(2,1)S(1)} async-done(((bf16[16,64,128]{2,1,0:T(8,128)(2,1)}), bf16[16,64,128]{2,1,0:T(8,128)(2,1)S(1)}, u32[]{:S(2)}, u32[]{:S(2)}) %all-to-all-start.5) | async-done | bytes 262176 | tf_op jit(solution)/shard_map/all_to_all | solution.py:24
  146.6 0.7 copy-done.10
  147.3 2.9 %shard_map.139 = (bf16[64,128]{1,0:T(8,128)(2,1)}, bf16[256,128]{1,0:T(8,128)(2,1)}, bf16[256,128]{1,0:T(8,128)(2,1)}, f32[32,128]{1,0:T(8,128)}) custom-call(s32[2]{0:T(128)} %pad_add_fusion.spot_ref, bf16[16,64,128]{2,1,0:T(8,128)(2,1)} %copy-done.10, bf16[32,4096]{1,0:T(8,128)(2,1)} %copy-done.2, bf16[32,128]{1,0:T(8,128)(2,1)} %slice.107.q_ref, ...), custom_call_target="tpu_custom_call" | custom-call | tf_op jit(solution)/shard_map/pallas_call | solution.py:165
  150.1 9.0 %collective-permute-start.8 = (bf16[256,128]{1,0:T(8,128)(2,1)}, bf16[256,128]{1,0:T(8,128)(2,1)S(1)}, u32[]{:S(2)}, u32[]{:S(2)}) collective-permute-start(bf16[256,128]{1,0:T(8,128)(2,1)} %get-tuple-element.35), channel_id=1, source_target_pairs={{0,1},{1,0},{2,3},{3,2},{4,5},{5,4},{6,7},{7,6},{8,9},{9,8},{10,11... | collective-permute-start | bytes 196616 | tf_op jit(solution)/shard_map/ppermute | solution.py:76
  159.2 1.3 split.14.more_ref
  160.5 0.6 copy-done.15
  161.1 1.6 shard_map.140
  162.8 5.2 %all-to-all-start.6 = ((bf16[16,80,128]{2,1,0:T(8,128)(2,1)}), bf16[16,80,128]{2,1,0:T(8,128)(2,1)S(1)}, u32[]{:S(2)}, u32[]{:S(2)}) async-start(bf16[16,80,128]{2,1,0:T(8,128)(2,1)} %shard_map.140), calls=%async_computation.6 | async-start | bytes 655360 | tf_op jit(solution)/shard_map/all_to_all | solution.py:24
  168.2 8.8 %all-to-all-done.6 = bf16[16,80,128]{2,1,0:T(8,128)(2,1)S(1)} async-done(((bf16[16,80,128]{2,1,0:T(8,128)(2,1)}), bf16[16,80,128]{2,1,0:T(8,128)(2,1)S(1)}, u32[]{:S(2)}, u32[]{:S(2)}) %all-to-all-start.6) | async-done | bytes 327712 | tf_op jit(solution)/shard_map/all_to_all | solution.py:24
  177.2 0.7 copy.66
  177.9 5.2 %all-to-all-start.7 = ((bf16[16,32,128]{2,1,0:T(8,128)(2,1)}), bf16[16,32,128]{2,1,0:T(8,128)(2,1)S(1)}, u32[]{:S(2)}, u32[]{:S(2)}) async-start(bf16[16,32,128]{2,1,0:T(8,128)(2,1)} %copy.66), calls=%async_computation.7 | async-start | bytes 262144 | tf_op jit(solution)/shard_map/all_to_all | solution.py:24
  183.4 1.0 fusion.5
  184.3 1.0 fusion.4
  185.3 9.8 %all-to-all-done.7 = bf16[16,32,128]{2,1,0:T(8,128)(2,1)S(1)} async-done(((bf16[16,32,128]{2,1,0:T(8,128)(2,1)}), bf16[16,32,128]{2,1,0:T(8,128)(2,1)S(1)}, u32[]{:S(2)}, u32[]{:S(2)}) %all-to-all-start.7) | async-done | bytes 131104 | tf_op jit(solution)/shard_map/all_to_all | solution.py:24
  195.3 0.9 broadcast_in_dim.107
  196.2 7.1 %all-to-all-start.8 = ((bf16[8,16,2048]{2,1,0:T(8,128)(2,1)}), bf16[8,16,2048]{2,1,0:T(8,128)(2,1)S(1)}, u32[]{:S(2)}, u32[]{:S(2)}) async-start(bf16[8,16,2048]{2,1,0:T(8,128)(2,1)} %broadcast_in_dim.107), calls=%async_computation.8 | async-start | bytes 1048576 | tf_op jit(solution)/shard_map/all_to_all | solution.py:24
  203.4 1.1 maximum_select_fusion
  204.5 1.1 fusion.1
  205.6 7.2 %all-to-all-done.8 = bf16[8,16,2048]{2,1,0:T(8,128)(2,1)S(1)} async-done(((bf16[8,16,2048]{2,1,0:T(8,128)(2,1)}), bf16[8,16,2048]{2,1,0:T(8,128)(2,1)S(1)}, u32[]{:S(2)}, u32[]{:S(2)}) %all-to-all-start.8) | async-done | bytes 524320 | tf_op jit(solution)/shard_map/all_to_all | solution.py:24
  212.8 0.8 fusion.102
  (117 shorter events, 3.8 us)
Async XLA Ops:
  7.2 94.0 %copy-start = (bf16[1,80,2048]{2,1,0:T(8,128)(2,1)S(1)}, bf16[1,80,2048]{2,1,0:T(8,128)(2,1)}, u32[]{:S(2)}) copy-start(bf16[1,80,2048]{2,1,0:T(8,128)(2,1)} %param.15) | copy-start | bytes 983044
  7.2 7.7 %copy-start.13 = (bf16[64,2048]{1,0:T(8,128)(2,1)S(1)}, bf16[64,2048]{1,0:T(8,128)(2,1)}, u32[]{:S(2)}) copy-start(bf16[64,2048]{1,0:T(8,128)(2,1)} %param.11) | copy-start | bytes 786436
  7.2 7.7 %copy-start.14 = (bf16[64,2048]{1,0:T(8,128)(2,1)S(1)}, bf16[64,2048]{1,0:T(8,128)(2,1)}, u32[]{:S(2)}) copy-start(bf16[64,2048]{1,0:T(8,128)(2,1)} %param.12) | copy-start | bytes 786436
  9.9 11.3 %all-to-all-start = ((bf16[4,8,6272]{2,1,0:T(8,128)(2,1)}), bf16[4,8,6272]{2,1,0:T(8,128)(2,1)S(1)}, u32[]{:S(2)}, u32[]{:S(2)}) async-start(bf16[4,8,6272]{2,1,0:T(8,128)(2,1)} %get-tuple-element.24), calls=%async_computation | async-start | bytes 802816 | tf_op jit(solution)/shard_map/all_to_all | solution.py:24
  14.9 39.4 %all-gather.2.cloned.1.call-start = ((), (), s32[]{:S(2)}) async-start(), calls=%async_computation.9 | async-start | bytes 1310720 | tf_op jit(solution)/shard_map/all_gather | solution.py:238
  24.0 7.8 %all-to-all-start.1 = ((f32[4,2,2176]{2,1,0:T(2,128)}), f32[4,2,2176]{2,1,0:T(2,128)S(1)}, u32[]{:S(2)}, u32[]{:S(2)}) async-start(f32[4,2,2176]{2,1,0:T(2,128)} %all_to_all.36), calls=%async_computation.1 | async-start | bytes 139264 | tf_op jit(solution)/shard_map/all_to_all | solution.py:24
  33.4 28.5 %all-to-all-start.2 = ((bf16[16,2,4224]{2,1,0:T(2,128)(2,1)}), bf16[16,2,4224]{2,1,0:T(2,128)(2,1)S(1)}, u32[]{:S(2)}, u32[]{:S(2)}) async-start(bf16[16,2,4224]{2,1,0:T(2,128)(2,1)} %pad_maximum_fusion.3), calls=%async_computation.2 | async-start | bytes 540672 | tf_op jit(solution)/shard_map/all_to_all | solution.py:24
  56.3 5.7 %collective-permute-start = (bf16[256,1024]{1,0:T(8,128)(2,1)}, bf16[256,1024]{1,0:T(8,128)(2,1)S(1)}, u32[]{:S(2)}, u32[]{:S(2)}) collective-permute-start(bf16[256,1024]{1,0:T(8,128)(2,1)} %get-tuple-element.44), channel_id=1, source_target_pairs={{0,1},{1,0},{2,3},{3,2},{4,5},{5,4},{6,7},{7,6},{8,9},{9,8},{10,11... | collective-permute-start | bytes 1572872 | tf_op jit(solution)/shard_map/ppermute | solution.py:76
  59.8 3.8 %collective-permute-start.1 = (bf16[256,1024]{1,0:T(8,128)(2,1)S(1)}, bf16[256,1024]{1,0:T(8,128)(2,1)S(1)}, u32[]{:S(2)}, u32[]{:S(2)}) collective-permute-start(bf16[256,1024]{1,0:T(8,128)(2,1)S(1)} %get-tuple-element.43), channel_id=1, source_target_pairs={{0,1},{1,0},{2,3},{3,2},{4,5},{5,4},{6,7},{7,6},{8,9},{9,8},{10,11... | collective-permute-start | bytes 1572872 | tf_op jit(solution)/shard_map/ppermute | solution.py:76
  62.0 2.8 %copy-start.7 = (bf16[32,4224]{1,0:T(8,128)(2,1)}, bf16[32,4224]{1,0:T(8,128)(2,1)S(1)}, u32[]{:S(2)}) copy-start(bf16[32,4224]{1,0:T(8,128)(2,1)S(1)} %reshape.212) | copy-start | bytes 811012
  62.0 2.7 %copy-start.2 = (bf16[32,4096]{1,0:T(8,128)(2,1)}, bf16[32,4096]{1,0:T(8,128)(2,1)S(1)}, u32[]{:S(2)}) copy-start(bf16[32,4096]{1,0:T(8,128)(2,1)S(1)} %slice.102.up_ref) | copy-start | bytes 786436
  62.0 2.7 %copy-start.3 = (bf16[256,1024]{1,0:T(8,128)(2,1)}, bf16[256,1024]{1,0:T(8,128)(2,1)S(1)}, u32[]{:S(2)}) copy-start(bf16[256,1024]{1,0:T(8,128)(2,1)S(1)} %collective-permute-done.across_ref) | copy-start | bytes 1572868
  63.6 1.2 copy-start.5
  64.7 4.0 %copy-start.23 = (bf16[8,128]{1,0:T(8,128)(2,1)S(1)}, bf16[8,128]{1,0:T(8,128)(2,1)}, u32[]{:S(2)}) copy-start(bf16[8,128]{1,0:T(8,128)(2,1)} %get-tuple-element.23) | copy-start | bytes 6148
  64.8 26.8 %all-to-all-start.3 = ((bf16[4,32,4096]{2,1,0:T(8,128)(2,1)}), bf16[4,32,4096]{2,1,0:T(8,128)(2,1)S(1)}, u32[]{:S(2)}, u32[]{:S(2)}) async-start(bf16[4,32,4096]{2,1,0:T(8,128)(2,1)} %broadcast_in_dim.103), calls=%async_computation.3 | async-start | bytes 2097152 | tf_op jit(solution)/shard_map/all_to_all | solution.py:24
  69.6 6.1 %copy-start.24 = (f32[128]{0:T(128)}, f32[128]{0:T(128)S(1)}, u32[]{:S(2)}) copy-start(f32[128]{0:T(128)S(1)} %get-tuple-element.53) | copy-start | bytes 1540
  75.7 18.3 %copy-start.11 = (bf16[256,1024]{1,0:T(8,128)(2,1)S(1)}, bf16[256,1024]{1,0:T(8,128)(2,1)}, u32[]{:S(2)}) copy-start(bf16[256,1024]{1,0:T(8,128)(2,1)} %get-tuple-element.30) | copy-start | bytes 1572868
  75.7 18.3 %collective-permute-start.5 = (bf16[256,1024]{1,0:T(8,128)(2,1)}, bf16[256,1024]{1,0:T(8,128)(2,1)S(1)}, u32[]{:S(2)}, u32[]{:S(2)}) collective-permute-start(bf16[256,1024]{1,0:T(8,128)(2,1)} %get-tuple-element.31), channel_id=1, source_target_pairs={{0,1},{1,0},{2,3},{3,2},{4,5},{5,4},{6,7},{7,6},{8,9},{9,8},{10,11... | collective-permute-start | bytes 1572872 | tf_op jit(solution)/shard_map/ppermute | solution.py:76
  89.4 4.8 %copy-start.12 = (bf16[256,1024]{1,0:T(8,128)(2,1)S(1)}, bf16[256,1024]{1,0:T(8,128)(2,1)}, u32[]{:S(2)}) copy-start(bf16[256,1024]{1,0:T(8,128)(2,1)} %get-tuple-element.28) | copy-start | bytes 1572868
  89.4 4.8 %collective-permute-start.4 = (bf16[256,1024]{1,0:T(8,128)(2,1)}, bf16[256,1024]{1,0:T(8,128)(2,1)S(1)}, u32[]{:S(2)}, u32[]{:S(2)}) collective-permute-start(bf16[256,1024]{1,0:T(8,128)(2,1)} %get-tuple-element.29), channel_id=1, source_target_pairs={{0,1},{1,0},{2,3},{3,2},{4,5},{5,4},{6,7},{7,6},{8,9},{9,8},{10,11... | collective-permute-start | bytes 1572872 | tf_op jit(solution)/shard_map/ppermute | solution.py:76
  91.5 10.2 %collective-permute-start.2 = (bf16[128,4096]{1,0:T(8,128)(2,1)S(1)}, bf16[128,4096]{1,0:T(8,128)(2,1)S(1)}, u32[]{:S(2)}, u32[]{:S(2)}) collective-permute-start(bf16[128,4096]{1,0:T(8,128)(2,1)S(1)} %bitcast.96), channel_id=1, source_target_pairs={{0,1},{1,0},{2,3},{3,2},{4,5},{5,4},{6,7},{7,6},{8,9},{9,8},{10,11... | collective-permute-start | bytes 3145736 | tf_op jit(solution)/shard_map/ppermute | solution.py:76
  94.4 7.0 %copy-start.20 = (bf16[1,80,2048]{2,1,0:T(8,128)(2,1)S(1)}, bf16[1,80,2048]{2,1,0:T(8,128)(2,1)}, u32[]{:S(2)}) copy-start(bf16[1,80,2048]{2,1,0:T(8,128)(2,1)} %param.16) | copy-start | bytes 983044
  94.5 11.2 %collective-permute-start.6 = (bf16[64,2048]{1,0:T(8,128)(2,1)S(1)}, bf16[64,2048]{1,0:T(8,128)(2,1)S(1)}, u32[]{:S(2)}, u32[]{:S(2)}) collective-permute-start(bf16[64,2048]{1,0:T(8,128)(2,1)S(1)} %get-tuple-element.40), channel_id=1, source_target_pairs={{0,128},{128,256},{256,384},{384,0},{1,129},{129,257},{257,385},{3... | collective-permute-start | bytes 786440 | tf_op jit(solution)/shard_map/ppermute | solution.py:314
  96.8 9.7 %collective-permute-start.7 = (bf16[64,2048]{1,0:T(8,128)(2,1)S(1)}, bf16[64,2048]{1,0:T(8,128)(2,1)S(1)}, u32[]{:S(2)}, u32[]{:S(2)}) collective-permute-start(bf16[64,2048]{1,0:T(8,128)(2,1)S(1)} %get-tuple-element.41), channel_id=1, source_target_pairs={{0,384},{128,0},{256,128},{384,256},{1,385},{129,1},{257,129},{385... | collective-permute-start | bytes 786440 | tf_op jit(solution)/shard_map/ppermute | solution.py:314
  101.4 1.0 copy-start.16
  101.8 1.0 copy-start.8
  102.8 4.0 %collective-permute-start.3 = (bf16[128,2048]{1,0:T(8,128)(2,1)S(1)}, bf16[128,2048]{1,0:T(8,128)(2,1)S(1)}, u32[]{:S(2)}, u32[]{:S(2)}) collective-permute-start(bf16[128,2048]{1,0:T(8,128)(2,1)S(1)} %fusion.28), channel_id=1, source_target_pairs={{0,1},{1,0},{2,3},{3,2},{4,5},{5,4},{6,7},{7,6},{8,9},{9,8},{10,11... | collective-permute-start | bytes 1572872 | tf_op jit(solution)/shard_map/ppermute | solution.py:76
  125.0 10.7 %copy-start.4 = (bf16[256,1024]{1,0:T(8,128)(2,1)S(1)}, bf16[256,1024]{1,0:T(8,128)(2,1)}, u32[]{:S(2)}) copy-start(bf16[256,1024]{1,0:T(8,128)(2,1)} %copy-done.3) | copy-start | bytes 1572868
  125.0 10.7 %copy-start.6 = (bf16[256,1024]{1,0:T(8,128)(2,1)S(1)}, bf16[256,1024]{1,0:T(8,128)(2,1)}, u32[]{:S(2)}) copy-start(bf16[256,1024]{1,0:T(8,128)(2,1)} %copy-done.5) | copy-start | bytes 1572868
  127.7 18.9 %all-to-all-start.5 = ((bf16[16,64,128]{2,1,0:T(8,128)(2,1)}), bf16[16,64,128]{2,1,0:T(8,128)(2,1)S(1)}, u32[]{:S(2)}, u32[]{:S(2)}) async-start(bf16[16,64,128]{2,1,0:T(8,128)(2,1)} %bitcast_bitcast_fusion), calls=%async_computation.5 | async-start | bytes 524288 | tf_op jit(solution)/shard_map/all_to_all | solution.py:24
  146.6 0.7 copy-start.10
  150.1 17.8 %copy-start.25 = (f32[128]{0:T(128)S(1)}, f32[128]{0:T(128)}, u32[]{:S(2)}) copy-start(f32[128]{0:T(128)} %copy-done.24) | copy-start | bytes 1540
  150.1 17.8 %copy-start.17 = (f32[128,80]{0,1:T(8,128)S(1)}, f32[128,80]{0,1:T(8,128)}, u32[]{:S(2)}) copy-start(f32[128,80]{0,1:T(8,128)} %copy-done.16) | copy-start | bytes 122884
  150.1 10.3 %collective-permute-start.8 = (bf16[256,128]{1,0:T(8,128)(2,1)}, bf16[256,128]{1,0:T(8,128)(2,1)S(1)}, u32[]{:S(2)}, u32[]{:S(2)}) collective-permute-start(bf16[256,128]{1,0:T(8,128)(2,1)} %get-tuple-element.35), channel_id=1, source_target_pairs={{0,1},{1,0},{2,3},{3,2},{4,5},{5,4},{6,7},{7,6},{8,9},{9,8},{10,11... | collective-permute-start | bytes 196616 | tf_op jit(solution)/shard_map/ppermute | solution.py:76
  160.5 0.6 copy-start.15
  162.8 14.3 %copy-start.18 = (f32[32,128]{1,0:T(8,128)S(1)}, f32[32,128]{1,0:T(8,128)}, u32[]{:S(2)}) copy-start(f32[32,128]{1,0:T(8,128)} %get-tuple-element.36) | copy-start | bytes 49156
  162.8 14.3 %all-to-all-start.6 = ((bf16[16,80,128]{2,1,0:T(8,128)(2,1)}), bf16[16,80,128]{2,1,0:T(8,128)(2,1)S(1)}, u32[]{:S(2)}, u32[]{:S(2)}) async-start(bf16[16,80,128]{2,1,0:T(8,128)(2,1)} %shard_map.140), calls=%async_computation.6 | async-start | bytes 655360 | tf_op jit(solution)/shard_map/all_to_all | solution.py:24
  177.1 6.2 %copy-start.9 = (bf16[128,4096]{1,0:T(8,128)(2,1)S(1)}, bf16[128,4096]{1,0:T(8,128)(2,1)}, u32[]{:S(2)}) copy-start(bf16[128,4096]{1,0:T(8,128)(2,1)} %copy-done.8) | copy-start | bytes 3145732
  177.9 17.2 %all-to-all-start.7 = ((bf16[16,32,128]{2,1,0:T(8,128)(2,1)}), bf16[16,32,128]{2,1,0:T(8,128)(2,1)S(1)}, u32[]{:S(2)}, u32[]{:S(2)}) async-start(bf16[16,32,128]{2,1,0:T(8,128)(2,1)} %copy.66), calls=%async_computation.7 | async-start | bytes 262144 | tf_op jit(solution)/shard_map/all_to_all | solution.py:24
  195.2 8.2 %copy-start.19 = (bf16[128,8]{0,1:T(8,128)(2,1)S(1)}, bf16[128,8]{0,1:T(8,128)(2,1)}, u32[]{:S(2)}) copy-start(bf16[128,8]{0,1:T(8,128)(2,1)} %get-tuple-element.54) | copy-start | bytes 6148
  195.2 8.2 %copy-start.21 = (bf16[128,1024]{1,0:T(8,128)(2,1)S(1)}, bf16[128,1024]{1,0:T(8,128)(2,1)}, u32[]{:S(2)}) copy-start(bf16[128,1024]{1,0:T(8,128)(2,1)} %get-tuple-element.39) | copy-start | bytes 786436
  195.2 8.2 %copy-start.22 = (bf16[128,1024]{1,0:T(8,128)(2,1)S(1)}, bf16[128,1024]{1,0:T(8,128)(2,1)}, u32[]{:S(2)}) copy-start(bf16[128,1024]{1,0:T(8,128)(2,1)} %get-tuple-element.38) | copy-start | bytes 786436
  196.2 8.3 %copy-start.1 = (bf16[128,2048]{1,0:T(8,128)(2,1)S(1)}, bf16[128,2048]{1,0:T(8,128)(2,1)}, u32[]{:S(2)}) copy-start(bf16[128,2048]{1,0:T(8,128)(2,1)} %up_ref.3) | copy-start | bytes 1572868
  196.2 16.6 %all-to-all-start.8 = ((bf16[8,16,2048]{2,1,0:T(8,128)(2,1)}), bf16[8,16,2048]{2,1,0:T(8,128)(2,1)S(1)}, u32[]{:S(2)}, u32[]{:S(2)}) async-start(bf16[8,16,2048]{2,1,0:T(8,128)(2,1)} %broadcast_in_dim.107), calls=%async_computation.8 | async-start | bytes 1048576 | tf_op jit(solution)/shard_map/all_to_all | solution.py:24
Sparse Core Ops, SparseCore 0:
  18.4 35.8 all-gather.1

commit v7 on v6

--- a/solution.py
+++ b/solution.py
@@ -38,25 +38,42 @@
     return jnp.sum(got.reshape((n, -1) + got.shape[1:]).astype(F32), axis=0)
 
 
-def join_kernel(spot_ref, keep_ref, got_ref, more_ref, ret_ref, out_ref):
-    blocks, rows = out_ref.shape[0], more_ref.shape[0]
+def join_kernel(keep_ref, got_ref, ret_ref, out_ref):
+    blocks = out_ref.shape[0]
+    rows = keep_ref.shape[0] // blocks
     for block in range(blocks):
         part = pl.ds(block * rows, rows)
         memory = keep_ref[part].astype(F32) + got_ref[part].astype(F32)
-        memory = memory + jnp.where(spot_ref[0] == block, more_ref[...], 0.0)
         out_ref[block, :rows] = memory.astype(BF)
         out_ref[block, rows:] = ret_ref[...]
 
 
-def join_blocks(spot, keep, got, more, returned, blocks):
+def join_blocks(keep, got, returned, blocks):
     vmem = pl.BlockSpec(memory_space=pltpu.VMEM)
-    shape = (blocks, more.shape[0] + returned.shape[0], more.shape[1])
+    shape = (blocks, keep.shape[0] // blocks + returned.shape[0], keep.shape[1])
     return pl.pallas_call(
         join_kernel,
-        in_specs=[pl.BlockSpec(memory_space=pltpu.SMEM)] + [vmem] * 4,
+        in_specs=[vmem] * 3,
         out_specs=vmem,
         out_shape=jax.ShapeDtypeStruct(shape, BF),
-    )(spot, keep, got, more, returned)
+    )(keep, got, returned)
+
+
+def sum_kernel(parts_ref, out_ref):
+    for pair in range(out_ref.shape[0]):
+        cols = slice(pair * 2 * HEAD, (pair + 1) * 2 * HEAD)
+        total = parts_ref[0, :, cols].astype(F32)
+        for part in range(1, parts_ref.shape[0]):
+            total = total + parts_ref[part, :, cols].astype(F32)
+        out_ref[pair] = total.astype(BF)
+
+
+def sum_by_pairs(parts):
+    vmem = pl.BlockSpec(memory_space=pltpu.VMEM)
+    shape = (parts.shape[2] // (2 * HEAD), parts.shape[1], 2 * HEAD)
+    return pl.pallas_call(
+        sum_kernel, in_specs=[vmem], out_specs=vmem, out_shape=jax.ShapeDtypeStruct(shape, BF)
+    )(parts)
 
 
 def head_pairs(values):
@@ -182,8 +199,9 @@
     )(spot, sums, gathered, queries, own, across)
 
 
-def pick_kernel(counts_ref, ids_ref, *refs):
-    parts, (rows_ref, place_ref) = refs[:-2], refs[-2:]
+def pick_kernel(core_ref, counts_ref, ids_ref, keys_ref, values_ref, *refs):
+    parts, (rows_ref, place_ref, own_ref) = refs[:-3], refs[-3:]
+    own_ref[...] = jnp.where(core_ref[0] == 0, keys_ref[...], values_ref[...])
     slots, tokens = place_ref.shape
     slot = lax.broadcasted_iota(jnp.int32, (slots, tokens), 0)
     expert, order = slot // GCAP, slot % GCAP
@@ -205,18 +223,19 @@
         rows_ref[copy, :, len(parts) * width :] = count.astype(F32).astype(BF)
 
 
-def pick_rows(counts, ids, parts, slots, copies):
+def pick_rows(core, counts, ids, keys, values, parts, slots, copies):
     tokens, width = parts[0].shape
     vmem = pl.BlockSpec(memory_space=pltpu.VMEM)
     return pl.pallas_call(
         pick_kernel,
-        in_specs=[pl.BlockSpec(memory_space=pltpu.SMEM)] + [vmem] * (1 + len(parts)),
-        out_specs=[vmem, vmem],
+        in_specs=[pl.BlockSpec(memory_space=pltpu.SMEM)] * 2 + [vmem] * (3 + len(parts)),
+        out_specs=[vmem] * 3,
         out_shape=[
             jax.ShapeDtypeStruct((copies, slots, len(parts) * width + tokens), BF),
             jax.ShapeDtypeStruct((slots, tokens), BF),
+            jax.ShapeDtypeStruct(keys.shape, BF),
         ],
-    )(counts, ids, *parts)
+    )(core, counts, ids, keys, values, *parts)
 
 
 def per_device(
@@ -231,10 +250,17 @@
 
     experts = jnp.arange(window, dtype=jnp.int32)
     slot_ids = jnp.arange(slots, dtype=jnp.int32)
-    picked, place = pick_rows(
-        send_counts, expert_ids.reshape(1, tokens), (queries, states, upstream), slots, window
-    )
-    own_memory = jnp.where(first, after(mem_keys, picked), mem_values)
+    core_id = core.reshape(1).astype(jnp.int32)
+    picked, place, own_memory = pick_rows(
+        core_id,
+        send_counts,
+        expert_ids.reshape(1, tokens),
+        mem_keys,
+        mem_values,
+        (queries, states, upstream),
+        slots,
+        window,
+    )
     own_memory = lax.all_gather(own_memory, "y", axis=0, tiled=True)
     group = exchange(picked, "y").reshape(window * slots, -1)
 
@@ -251,6 +277,7 @@
     own = (own_target[:, None] == slot_ids[None, :]).astype(BF)
     place_back = dot(place, own, 0, 0)
     taken = jnp.sum(place_back, axis=1, keepdims=True)
+    free = (1.0 - taken).astype(BF)
     place_back = place_back.astype(BF)
 
     in_head = jnp.arange(heads)[:, None] == (jnp.arange(width) // HEAD)[None, :]
@@ -289,8 +316,8 @@
 
     bulk = [
         bulk_backward(
-            core.reshape(1).astype(jnp.int32),
-            (1.0 - taken).astype(BF),
+            core_id,
+            free,
             upstream,
             queries,
             own_memory,
@@ -299,19 +326,14 @@
         )
         for piece in range(PIECES)
     ]
-    near = spread(after(level, *across_memory), "x")
+    near = spread(after(level, free, *across_memory), "x")
     bulk_queries = jnp.concatenate([part[0] for part in bulk], axis=1)
+    got = [other_core(part[2]) for part in bulk]
+    near = after(near, *got)
     bulk = jnp.concatenate(
-        [(keep.astype(F32) + other_core(send).astype(F32)).astype(BF) for _, keep, send in bulk],
-        axis=1,
-    )
-    own_rows = mem_keys.shape[0]
-    blocks = [
-        lax.dynamic_slice_in_dim(bulk, (mine + d) % window * own_rows, own_rows, 0)
-        for d in range(window)
-    ]
-    moves = [[(i, (i + d) % window) for i in range(window)] for d in range(window)]
-    got = [lax.ppermute(blocks[d], "y", moves[d]) for d in (1, 3)]
+        [(part[1].astype(F32) + more.astype(F32)).astype(BF) for part, more in zip(bulk, got)], axis=1
+    )
+    bulk = collect(bulk, "y").astype(BF)
     far = other_core(near)
     weight_in, weight_out = w_in[0], w_out[0]
     parts_of_x = lax.axis_size("x")
@@ -325,15 +347,13 @@
 
     _, far_in, far_out, far_back = expert(far)
     _, near_in, near_out, near_back = expert(near)
-    bulk = sum(part.astype(F32) for part in blocks[:1] + [after(part, far_back) for part in got])
-    bulk = jnp.stack([bulk.astype(BF), blocks[2]])
     grad_in, grad_out = (near_in + far_in).astype(BF), (near_out + far_out).astype(BF)
 
     back = (near_back + other_core(far_back.astype(BF)).astype(F32)).astype(BF)
     rows = back.shape[0] // parts_of_x
-    back = [back.reshape(parts_of_x, rows, width), bulk.reshape(2, parts_of_x, -1, width).transpose(1, 0, 2, 3).reshape(parts_of_x, -1, width)]
-    back = collect(jnp.concatenate(back, axis=1).reshape(-1, width), "x").astype(BF)
-    joined = exchange(head_pairs(back), "z")
+    back = [back.reshape(parts_of_x, rows, width), bulk.reshape(parts_of_x, -1, width)]
+    back = exchange(jnp.concatenate(back, axis=1), "x")
+    joined = exchange(sum_by_pairs(back), "z")
     returned, keep, send, bulk = routed_backward(
         jnp.stack([core, depth]).astype(jnp.int32),
         joined,
@@ -344,11 +364,7 @@
     )
 
     blocks = window * parts_of_x
-    spot = (mine + 2) % window * parts_of_x + lax.axis_index("x")
-    bulk, opposite = jnp.split(bulk, 2, axis=0)
-    joined = join_blocks(
-        spot.reshape(1).astype(jnp.int32), keep, other_core(send), opposite, returned, blocks
-    )
+    joined = join_blocks(keep, other_core(send), returned, blocks)
     joined = exchange(joined, ("y", "x"))
     rows_of_x = joined.shape[1] - returned.shape[0]
     memory = (jnp.sum(joined[:, :rows_of_x].astype(F32), axis=0) + bulk).astype(BF)

time: 222 us -> 222 us (level)
  waiting for transfers between devices: 53.3 us -> 61.3 us
  starting transfers between devices: 87.9 us -> 80.2 us
  matrix products: 8.82 us -> 13.2 us
  local copies, waits for them, and re-layouts: 14.3 us -> 10.2 us
  blocking collectives: 17.8 us -> 15.1 us
    ppermute x2 -> x0, starting transfers between devices: 6.62 us -> none  [per_device(): got = [lax.ppermute(blocks[d], 'y', moves[d]) for d in (1, 3)]]
    all_to_all x8 -> x9, waiting for transfers between devices: 45.2 us -> 51.7 us  [exchange(): return lax.all_to_all(values, axes, split_axis=0, concat_axis=0, tiled=True)]
    dot_general x16, matrix products: 8.55 us -> 13 us  [dot(): lax.dot_general(left, right, (((left_dim,), (right_dim,)), ((), ())), pre...]
    all_to_all x1, blocking collectives: 17.8 us -> 15.1 us  [exchange(): return lax.all_to_all(values, axes, split_axis=0, concat_axis=0, tiled=True)]
    ppermute x7, waiting for transfers between devices: 1.67 us -> 3.91 us  [other_core(): return lax.ppermute(values, 'c', [(0, 1), (1, 0)])]
    all_to_all x8 -> x9, starting transfers between devices: 51.5 us -> 51.7 us  [exchange(): return lax.all_to_all(values, axes, split_axis=0, concat_axis=0, tiled=True)]
  transfers between devices with their start and end apart: 18 -> 17, of which waited for: 12 -> 12; matrix products, arithmetic and copies ran while one was open for 9% -> 10% of each run, Pallas kernels for 5% -> 5%
where the time goes in v7:
time: 222 us; the launch traced here: 221 us
  starting transfers between devices  80.2 us (36%)
  waiting for transfers between devices  61.3 us (28%)
  Pallas kernels  20 us (9%)
  blocking collectives  15.1 us (7%)
  between operations  14.7 us (7%)
  matrix products  13.2 us (6%)
  local copies, waits for them, and re-layouts  10.2 us (5%)
  other arithmetic  6.04 us (3%)
    all_to_all x9, waiting for transfers between devices, exchange(): return lax.all_to_all(values, axes, split_axis=0, concat_axis=0, tiled=True)  51.7 us
    all_to_all x9, starting transfers between devices, exchange(): return lax.all_to_all(values, axes, split_axis=0, concat_axis=0, tiled=True)  51.7 us
    ppermute x7, starting transfers between devices, other_core(): return lax.ppermute(values, 'c', [(0, 1), (1, 0)])  28.5 us
    all_to_all x1, blocking collectives, exchange(): return lax.all_to_all(values, axes, split_axis=0, concat_axis=0, tiled=True)  15.1 us
    dot_general x16, matrix products, dot(): lax.dot_general(left, right, (((left_dim,), (right_dim,)), ((), ())), pre...  13 us
    pallas_call x2, Pallas kernels, bulk_backward(): pl.pallas_call(bulk_kernel, grid=(width // block,), in_specs=[pl.BlockSpe...  10.7 us
    all_gather x1, waiting for transfers between devices, per_device(): own_memory = lax.all_gather(own_memory, 'y', axis=0, tiled=True)  5.04 us
  transfers between devices with their start and end apart: 17, of which 12 were waited for; matrix products, arithmetic and copies ran while one was open for 10% of the time, Pallas kernels for 5%

profile of v7, /device:TPU:1, one launch (start us, length us, event | category | flops | bytes accessed | tf_op | source)
XLA Modules:
  0.0 220.7 jit_solution(15075379605696586796)
XLA Ops:
  7.2 2.8 %shard_map.136 = (bf16[4,8,6272]{2,1,0:T(8,128)(2,1)}, bf16[8,128]{1,0:T(8,128)(2,1)}, bf16[64,2048]{1,0:T(8,128)(2,1)}) custom-call(s32[1]{0:T(128)} %bitcast.core_ref, s32[1,4]{1,0:T(1,128)} %counts_ref.1, s32[1,128]{1,0:T(1,128)} %bitcast.101, bf16[64,2048]{1,0:T(8,128)(2,1)} %keys_ref.1, bf16[64,2048]{1,0:T(8,128)(2,1)} %values_ref.1, ...), custom_call_target="tpu_custom_call" | custom-call | tf_op jit(solution)/shard_map/pallas_call | solution.py:229
  10.0 5.1 %all-to-all-start = ((bf16[4,8,6272]{2,1,0:T(8,128)(2,1)}), bf16[4,8,6272]{2,1,0:T(8,128)(2,1)S(1)}, u32[]{:S(2)}, u32[]{:S(2)}) async-start(bf16[4,8,6272]{2,1,0:T(8,128)(2,1)} %get-tuple-element.23), calls=%async_computation | async-start | bytes 802816 | tf_op jit(solution)/shard_map/all_to_all | solution.py:24
  15.2 0.7 all-gather.2.cloned.1.call-update
  15.9 5.5 %all-to-all-done = bf16[4,8,6272]{2,1,0:T(8,128)(2,1)S(1)} async-done(((bf16[4,8,6272]{2,1,0:T(8,128)(2,1)}), bf16[4,8,6272]{2,1,0:T(8,128)(2,1)S(1)}, u32[]{:S(2)}, u32[]{:S(2)}) %all-to-all-start) | async-done | bytes 401440 | tf_op jit(solution)/shard_map/all_to_all | solution.py:24
  22.2 0.5 fusion.100
  22.9 0.5 fusion.6
  23.8 0.7 all_to_all.41
  24.5 3.3 %all-to-all-start.1 = ((f32[4,2,2176]{2,1,0:T(2,128)}), f32[4,2,2176]{2,1,0:T(2,128)S(1)}, u32[]{:S(2)}, u32[]{:S(2)}) async-start(f32[4,2,2176]{2,1,0:T(2,128)} %all_to_all.41), calls=%async_computation.1 | async-start | bytes 139264 | tf_op jit(solution)/shard_map/all_to_all | solution.py:24
  28.0 4.2 %all-to-all-done.1 = f32[4,2,2176]{2,1,0:T(2,128)S(1)} async-done(((f32[4,2,2176]{2,1,0:T(2,128)}), f32[4,2,2176]{2,1,0:T(2,128)S(1)}, u32[]{:S(2)}, u32[]{:S(2)}) %all-to-all-start.1) | async-done | bytes 69664 | tf_op jit(solution)/shard_map/all_to_all | solution.py:24
  32.9 1.0 pad_maximum_fusion.3
  33.9 15.6 %all-to-all-start.2 = ((bf16[16,2,4224]{2,1,0:T(2,128)(2,1)}), bf16[16,2,4224]{2,1,0:T(2,128)(2,1)S(1)}, u32[]{:S(2)}, u32[]{:S(2)}) async-start(bf16[16,2,4224]{2,1,0:T(2,128)(2,1)} %pad_maximum_fusion.3), calls=%async_computation.2 | async-start | bytes 540672 | tf_op jit(solution)/shard_map/all_to_all | solution.py:24
  49.5 5.0 %all-gather.2.cloned.1.call-done.own_ref = bf16[256,2048]{1,0:T(8,128)(2,1)} async-done(((bf16[64,2048]{1,0:T(8,128)(2,1)}), bf16[256,2048]{1,0:T(8,128)(2,1)}) %all-gather.2.cloned.1.call-update) | async-done | bytes 1048592 | tf_op jit(solution)/shard_map/all_gather | solution.py:264
  54.5 1.3 fusion.96
  55.8 3.5 %collective-permute-start.1 = (bf16[256,1024]{1,0:T(8,128)(2,1)S(1)}, bf16[256,1024]{1,0:T(8,128)(2,1)S(1)}, u32[]{:S(2)}, u32[]{:S(2)}) collective-permute-start(bf16[256,1024]{1,0:T(8,128)(2,1)S(1)} %get-tuple-element.39), channel_id=1, source_target_pairs={{0,1},{1,0},{2,3},{3,2},{4,5},{5,4},{6,7},{7,6},{8,9},{9,8},{10,11... | collective-permute-start | bytes 1572872 | tf_op jit(solution)/shard_map/ppermute | solution.py:93
  59.3 1.9 collective-permute-start
  61.6 0.7 all-to-all-done.2
  62.5 0.6 collective-permute-done.across_ref
  63.1 1.1 broadcast_in_dim.103
  64.3 4.0 %all-to-all-start.3 = ((bf16[4,32,4096]{2,1,0:T(8,128)(2,1)}), bf16[4,32,4096]{2,1,0:T(8,128)(2,1)S(1)}, u32[]{:S(2)}, u32[]{:S(2)}) async-start(bf16[4,32,4096]{2,1,0:T(8,128)(2,1)} %broadcast_in_dim.103), calls=%async_computation.3 | async-start | bytes 2097152 | tf_op jit(solution)/shard_map/all_to_all | solution.py:24
  68.2 0.7 copy.54.free_ref
  69.0 5.3 %shard_map.138 = (bf16[128,1024]{1,0:T(8,128)(2,1)}, bf16[256,1024]{1,0:T(8,128)(2,1)}, bf16[256,1024]{1,0:T(8,128)(2,1)}) custom-call(s32[1]{0:T(128)} %bitcast.core_ref, bf16[128,1]{1,0:T(8,128)(2,1)} %copy.54.free_ref, bf16[128,2048]{1,0:T(8,128)(2,1)} %up_ref.3, bf16[128,2048]{1,0:T(8,128)(2,1)} %q_ref.3, ...), custom_call_target="tpu_custom_call" | custom-call | flops 402653184 | bytes 2097152 | tf_op jit(solution)/shard_map/pallas_call | solution.py:140
  74.3 9.3 %collective-permute-start.3 = (bf16[256,1024]{1,0:T(8,128)(2,1)}, bf16[256,1024]{1,0:T(8,128)(2,1)S(1)}, u32[]{:S(2)}, u32[]{:S(2)}) collective-permute-start(bf16[256,1024]{1,0:T(8,128)(2,1)} %get-tuple-element.28), channel_id=1, source_target_pairs={{0,1},{1,0},{2,3},{3,2},{4,5},{5,4},{6,7},{7,6},{8,9},{9,8},{10,11... | collective-permute-start | bytes 1572872 | tf_op jit(solution)/shard_map/ppermute | solution.py:93
  83.6 5.3 %shard_map.137 = (bf16[128,1024]{1,0:T(8,128)(2,1)}, bf16[256,1024]{1,0:T(8,128)(2,1)}, bf16[256,1024]{1,0:T(8,128)(2,1)}) custom-call(s32[1]{0:T(128)} %bitcast.core_ref, bf16[128,1]{1,0:T(8,128)(2,1)} %copy.54.free_ref, bf16[128,2048]{1,0:T(8,128)(2,1)} %up_ref.3, bf16[128,2048]{1,0:T(8,128)(2,1)} %q_ref.3, ...), custom_call_target="tpu_custom_call" | custom-call | flops 402653184 | bytes 2097152 | tf_op jit(solution)/shard_map/pallas_call | solution.py:140
  88.9 2.1 collective-permute-start.2
  91.0 2.2 %collective-permute-done.2 = bf16[256,1024]{1,0:T(8,128)(2,1)} collective-permute-done((bf16[256,1024]{1,0:T(8,128)(2,1)}, bf16[256,1024]{1,0:T(8,128)(2,1)}, u32[]{:S(2)}, u32[]{:S(2)}) %collective-permute-start.2) | collective-permute-done | bytes 524320 | tf_op jit(solution)/shard_map/ppermute | solution.py:93
  93.2 2.0 collective-permute-start.4
  95.5 1.2 add_convert_fusion.1
  96.7 1.1 pad_maximum_fusion
  97.8 3.6 %all-to-all-start.4 = ((bf16[4,64,2048]{2,1,0:T(8,128)(2,1)}), bf16[4,64,2048]{2,1,0:T(8,128)(2,1)S(1)}, u32[]{:S(2)}, u32[]{:S(2)}) async-start(bf16[4,64,2048]{2,1,0:T(8,128)(2,1)} %bitcast.16), calls=%async_computation.4 | async-start | bytes 2097152 | tf_op jit(solution)/shard_map/all_to_all | solution.py:24
  101.5 1.3 fusion.15
  102.8 1.4 fusion.53
  104.2 1.1 convolution_convert_fusion.2
  105.4 2.3 %collective-permute-start.5 = (bf16[128,2048]{1,0:T(8,128)(2,1)}, bf16[128,2048]{1,0:T(8,128)(2,1)S(1)}, u32[]{:S(2)}, u32[]{:S(2)}) collective-permute-start(bf16[128,2048]{1,0:T(8,128)(2,1)} %convolution_convert_fusion.2), channel_id=1, source_target_pairs={{0,1},{1,0},{2,3},{3,2},{4,5},{5,4},{6,7},{7,6},{8,9},{9,8},{10,11... | collective-permute-start | bytes 1572872 | tf_op jit(solution)/shard_map/ppermute | solution.py:93
  108.0 0.3 fusion.46
  108.6 7.7 %all-to-all-done.4 = bf16[4,64,2048]{2,1,0:T(8,128)(2,1)S(1)} async-done(((bf16[4,64,2048]{2,1,0:T(8,128)(2,1)}), bf16[4,64,2048]{2,1,0:T(8,128)(2,1)S(1)}, u32[]{:S(2)}, u32[]{:S(2)}) %all-to-all-start.4) | async-done | bytes 1048608 | tf_op jit(solution)/shard_map/all_to_all | solution.py:24
  116.5 0.3 add_convert_fusion.2
  116.9 15.1 %all_to_all.63.parts_ref = bf16[4,48,2048]{2,1,0:T(8,128)(2,1)} all-to-all(bf16[4,48,2048]{2,1,0:T(8,128)(2,1)S(1)} %pad_maximum_fusion.2), channel_id=1, replica_groups=mesh['y'=4,'z'=16,'x'=4,'c'=2] {'x'}, dimensions={0} | all-to-all | bytes 1572864 | tf_op jit(solution)/shard_map/all_to_all | solution.py:24
  131.9 2.0 shard_map.139
  133.9 5.2 %all-to-all-start.6 = ((bf16[16,48,128]{2,1,0:T(8,128)(2,1)}), bf16[16,48,128]{2,1,0:T(8,128)(2,1)S(1)}, u32[]{:S(2)}, u32[]{:S(2)}) async-start(bf16[16,48,128]{2,1,0:T(8,128)(2,1)} %shard_map.139), calls=%async_computation.6 | async-start | bytes 393216 | tf_op jit(solution)/shard_map/all_to_all | solution.py:24
  139.2 0.7 pad_add_fusion.spot_ref
  139.8 0.6 slice.105.q_ref
  140.4 1.1 pad_maximum_fusion.1.across_ref
  141.5 10.0 %all-to-all-done.6.sums_ref = bf16[16,48,128]{2,1,0:T(8,128)(2,1)S(1)} async-done(((bf16[16,48,128]{2,1,0:T(8,128)(2,1)}), bf16[16,48,128]{2,1,0:T(8,128)(2,1)S(1)}, u32[]{:S(2)}, u32[]{:S(2)}) %all-to-all-start.6) | async-done | bytes 196640 | tf_op jit(solution)/shard_map/all_to_all | solution.py:24
  151.5 0.7 copy-done.7
  152.2 2.8 %shard_map.140 = (bf16[64,128]{1,0:T(8,128)(2,1)}, bf16[256,128]{1,0:T(8,128)(2,1)}, bf16[256,128]{1,0:T(8,128)(2,1)}, f32[16,128]{1,0:T(8,128)}) custom-call(s32[2]{0:T(128)} %pad_add_fusion.spot_ref, bf16[16,48,128]{2,1,0:T(8,128)(2,1)} %copy-done.7, bf16[32,4096]{1,0:T(8,128)(2,1)} %copy-done.2, bf16[32,128]{1,0:T(8,128)(2,1)} %slice.105.q_ref, ...), custom_call_target="tpu_custom_call" | custom-call | tf_op jit(solution)/shard_map/pallas_call | solution.py:182
  155.0 7.5 %collective-permute-start.6 = (bf16[256,128]{1,0:T(8,128)(2,1)}, bf16[256,128]{1,0:T(8,128)(2,1)S(1)}, u32[]{:S(2)}, u32[]{:S(2)}) collective-permute-start(bf16[256,128]{1,0:T(8,128)(2,1)} %get-tuple-element.33), channel_id=1, source_target_pairs={{0,1},{1,0},{2,3},{3,2},{4,5},{5,4},{6,7},{7,6},{8,9},{9,8},{10,11... | collective-permute-start | bytes 196616 | tf_op jit(solution)/shard_map/ppermute | solution.py:93
  162.5 1.1 collective-permute-done.6.got_ref
  163.6 0.6 copy-done.12
  164.2 1.6 shard_map.141
  165.9 3.5 %all-to-all-start.7 = ((bf16[16,80,128]{2,1,0:T(8,128)(2,1)}), bf16[16,80,128]{2,1,0:T(8,128)(2,1)S(1)}, u32[]{:S(2)}, u32[]{:S(2)}) async-start(bf16[16,80,128]{2,1,0:T(8,128)(2,1)} %shard_map.141), calls=%async_computation.7 | async-start | bytes 655360 | tf_op jit(solution)/shard_map/all_to_all | solution.py:24
  169.4 1.3 fusion.13
  170.7 7.6 %all-to-all-done.7 = bf16[16,80,128]{2,1,0:T(8,128)(2,1)S(1)} async-done(((bf16[16,80,128]{2,1,0:T(8,128)(2,1)}), bf16[16,80,128]{2,1,0:T(8,128)(2,1)S(1)}, u32[]{:S(2)}, u32[]{:S(2)}) %all-to-all-start.7) | async-done | bytes 327712 | tf_op jit(solution)/shard_map/all_to_all | solution.py:24
  178.5 0.7 copy.58
  179.2 4.1 %all-to-all-start.8 = ((bf16[16,32,128]{2,1,0:T(8,128)(2,1)}), bf16[16,32,128]{2,1,0:T(8,128)(2,1)S(1)}, u32[]{:S(2)}, u32[]{:S(2)}) async-start(bf16[16,32,128]{2,1,0:T(8,128)(2,1)} %copy.58), calls=%async_computation.8 | async-start | bytes 262144 | tf_op jit(solution)/shard_map/all_to_all | solution.py:24
  183.3 1.0 fusion.5
  184.3 1.3 fusion.17
  185.6 1.0 fusion.4
  186.6 8.7 %all-to-all-done.8 = bf16[16,32,128]{2,1,0:T(8,128)(2,1)S(1)} async-done(((bf16[16,32,128]{2,1,0:T(8,128)(2,1)}), bf16[16,32,128]{2,1,0:T(8,128)(2,1)S(1)}, u32[]{:S(2)}, u32[]{:S(2)}) %all-to-all-start.8) | async-done | bytes 131104 | tf_op jit(solution)/shard_map/all_to_all | solution.py:24
  195.5 0.9 broadcast_in_dim.107
  196.4 7.1 %all-to-all-start.9 = ((bf16[8,16,2048]{2,1,0:T(8,128)(2,1)}), bf16[8,16,2048]{2,1,0:T(8,128)(2,1)S(1)}, u32[]{:S(2)}, u32[]{:S(2)}) async-start(bf16[8,16,2048]{2,1,0:T(8,128)(2,1)} %broadcast_in_dim.107), calls=%async_computation.9 | async-start | bytes 1048576 | tf_op jit(solution)/shard_map/all_to_all | solution.py:24
  203.5 1.1 maximum_select_fusion
  204.6 1.1 fusion.1
  205.8 7.2 %all-to-all-done.9 = bf16[8,16,2048]{2,1,0:T(8,128)(2,1)S(1)} async-done(((bf16[8,16,2048]{2,1,0:T(8,128)(2,1)}), bf16[8,16,2048]{2,1,0:T(8,128)(2,1)S(1)}, u32[]{:S(2)}, u32[]{:S(2)}) %all-to-all-start.9) | async-done | bytes 524320 | tf_op jit(solution)/shard_map/all_to_all | solution.py:24
  213.0 0.8 fusion.97
  (105 shorter events, 4.2 us)
Async XLA Ops:
  7.2 94.3 %copy-start = (bf16[1,80,2048]{2,1,0:T(8,128)(2,1)S(1)}, bf16[1,80,2048]{2,1,0:T(8,128)(2,1)}, u32[]{:S(2)}) copy-start(bf16[1,80,2048]{2,1,0:T(8,128)(2,1)} %param.15) | copy-start | bytes 983044
  10.0 12.2 %copy-start.10 = (bf16[64,2048]{1,0:T(8,128)(2,1)S(1)}, bf16[64,2048]{1,0:T(8,128)(2,1)}, u32[]{:S(2)}) copy-start(bf16[64,2048]{1,0:T(8,128)(2,1)} %keys_ref.1) | copy-start | bytes 786436
  10.0 11.4 %all-to-all-start = ((bf16[4,8,6272]{2,1,0:T(8,128)(2,1)}), bf16[4,8,6272]{2,1,0:T(8,128)(2,1)S(1)}, u32[]{:S(2)}, u32[]{:S(2)}) async-start(bf16[4,8,6272]{2,1,0:T(8,128)(2,1)} %get-tuple-element.23), calls=%async_computation | async-start | bytes 802816 | tf_op jit(solution)/shard_map/all_to_all | solution.py:24
  15.2 39.4 %all-gather.2.cloned.1.call-start = ((), (), s32[]{:S(2)}) async-start(), calls=%async_computation.10 | async-start | bytes 1310720 | tf_op jit(solution)/shard_map/all_gather | solution.py:264
  22.0 1.0 copy-start.11
  24.5 7.8 %all-to-all-start.1 = ((f32[4,2,2176]{2,1,0:T(2,128)}), f32[4,2,2176]{2,1,0:T(2,128)S(1)}, u32[]{:S(2)}, u32[]{:S(2)}) async-start(f32[4,2,2176]{2,1,0:T(2,128)} %all_to_all.41), calls=%async_computation.1 | async-start | bytes 139264 | tf_op jit(solution)/shard_map/all_to_all | solution.py:24
  33.9 28.4 %all-to-all-start.2 = ((bf16[16,2,4224]{2,1,0:T(2,128)(2,1)}), bf16[16,2,4224]{2,1,0:T(2,128)(2,1)S(1)}, u32[]{:S(2)}, u32[]{:S(2)}) async-start(bf16[16,2,4224]{2,1,0:T(2,128)(2,1)} %pad_maximum_fusion.3), calls=%async_computation.2 | async-start | bytes 540672 | tf_op jit(solution)/shard_map/all_to_all | solution.py:24
  49.5 11.8 %copy-start.22 = (bf16[8,128]{1,0:T(8,128)(2,1)S(1)}, bf16[8,128]{1,0:T(8,128)(2,1)}, u32[]{:S(2)}) copy-start(bf16[8,128]{1,0:T(8,128)(2,1)} %get-tuple-element.22) | copy-start | bytes 6148
  55.8 6.7 %collective-permute-start.1 = (bf16[256,1024]{1,0:T(8,128)(2,1)S(1)}, bf16[256,1024]{1,0:T(8,128)(2,1)S(1)}, u32[]{:S(2)}, u32[]{:S(2)}) collective-permute-start(bf16[256,1024]{1,0:T(8,128)(2,1)S(1)} %get-tuple-element.39), channel_id=1, source_target_pairs={{0,1},{1,0},{2,3},{3,2},{4,5},{5,4},{6,7},{7,6},{8,9},{9,8},{10,11... | collective-permute-start | bytes 1572872 | tf_op jit(solution)/shard_map/ppermute | solution.py:93
  59.3 3.8 %collective-permute-start = (bf16[256,1024]{1,0:T(8,128)(2,1)S(1)}, bf16[256,1024]{1,0:T(8,128)(2,1)S(1)}, u32[]{:S(2)}, u32[]{:S(2)}) collective-permute-start(bf16[256,1024]{1,0:T(8,128)(2,1)S(1)} %get-tuple-element.38), channel_id=1, source_target_pairs={{0,1},{1,0},{2,3},{3,2},{4,5},{5,4},{6,7},{7,6},{8,9},{9,8},{10,11... | collective-permute-start | bytes 1572872 | tf_op jit(solution)/shard_map/ppermute | solution.py:93
  62.5 1.8 copy-start.2
  62.5 1.8 copy-start.3
  63.1 1.1 copy-start.5
  64.3 29.0 %all-to-all-start.3 = ((bf16[4,32,4096]{2,1,0:T(8,128)(2,1)}), bf16[4,32,4096]{2,1,0:T(8,128)(2,1)S(1)}, u32[]{:S(2)}, u32[]{:S(2)}) async-start(bf16[4,32,4096]{2,1,0:T(8,128)(2,1)} %broadcast_in_dim.103), calls=%async_computation.3 | async-start | bytes 2097152 | tf_op jit(solution)/shard_map/all_to_all | solution.py:24
  74.3 21.0 %copy-start.8 = (bf16[256,1024]{1,0:T(8,128)(2,1)S(1)}, bf16[256,1024]{1,0:T(8,128)(2,1)}, u32[]{:S(2)}) copy-start(bf16[256,1024]{1,0:T(8,128)(2,1)} %get-tuple-element.31) | copy-start | bytes 1572868
  74.3 16.7 %collective-permute-start.3 = (bf16[256,1024]{1,0:T(8,128)(2,1)}, bf16[256,1024]{1,0:T(8,128)(2,1)S(1)}, u32[]{:S(2)}, u32[]{:S(2)}) collective-permute-start(bf16[256,1024]{1,0:T(8,128)(2,1)} %get-tuple-element.28), channel_id=1, source_target_pairs={{0,1},{1,0},{2,3},{3,2},{4,5},{5,4},{6,7},{7,6},{8,9},{9,8},{10,11... | collective-permute-start | bytes 1572872 | tf_op jit(solution)/shard_map/ppermute | solution.py:93
  88.9 6.5 %copy-start.9 = (bf16[256,1024]{1,0:T(8,128)(2,1)S(1)}, bf16[256,1024]{1,0:T(8,128)(2,1)}, u32[]{:S(2)}) copy-start(bf16[256,1024]{1,0:T(8,128)(2,1)} %get-tuple-element.30) | copy-start | bytes 1572868
  88.9 4.3 %collective-permute-start.2 = (bf16[256,1024]{1,0:T(8,128)(2,1)}, bf16[256,1024]{1,0:T(8,128)(2,1)}, u32[]{:S(2)}, u32[]{:S(2)}) collective-permute-start(bf16[256,1024]{1,0:T(8,128)(2,1)} %get-tuple-element.27), channel_id=1, source_target_pairs={{0,1},{1,0},{2,3},{3,2},{4,5},{5,4},{6,7},{7,6},{8,9},{9,8},{10,11... | collective-permute-start | bytes 1572872 | tf_op jit(solution)/shard_map/ppermute | solution.py:93
  93.2 8.2 %collective-permute-start.4 = (bf16[128,4096]{1,0:T(8,128)(2,1)S(1)}, bf16[128,4096]{1,0:T(8,128)(2,1)}, u32[]{:S(2)}, u32[]{:S(2)}) collective-permute-start(bf16[128,4096]{1,0:T(8,128)(2,1)S(1)} %bitcast.83), channel_id=1, source_target_pairs={{0,1},{1,0},{2,3},{3,2},{4,5},{5,4},{6,7},{7,6},{8,9},{9,8},{10,11... | collective-permute-start | bytes 3145736 | tf_op jit(solution)/shard_map/ppermute | solution.py:93
  97.8 5.0 %copy-start.18 = (bf16[1,80,2048]{2,1,0:T(8,128)(2,1)S(1)}, bf16[1,80,2048]{2,1,0:T(8,128)(2,1)}, u32[]{:S(2)}) copy-start(bf16[1,80,2048]{2,1,0:T(8,128)(2,1)} %param.16) | copy-start | bytes 983044
  97.8 18.5 %all-to-all-start.4 = ((bf16[4,64,2048]{2,1,0:T(8,128)(2,1)}), bf16[4,64,2048]{2,1,0:T(8,128)(2,1)S(1)}, u32[]{:S(2)}, u32[]{:S(2)}) async-start(bf16[4,64,2048]{2,1,0:T(8,128)(2,1)} %bitcast.16), calls=%async_computation.4 | async-start | bytes 2097152 | tf_op jit(solution)/shard_map/all_to_all | solution.py:24
  102.8 1.4 copy-start.13
  104.2 3.7 %copy-start.19 = (bf16[1,80,2048]{2,1,0:T(8,128)(2,1)S(1)}, bf16[1,80,2048]{2,1,0:T(8,128)(2,1)}, u32[]{:S(2)}) copy-start(bf16[1,80,2048]{2,1,0:T(8,128)(2,1)} %param.16) | copy-start | bytes 983044
  105.4 11.1 %collective-permute-start.5 = (bf16[128,2048]{1,0:T(8,128)(2,1)}, bf16[128,2048]{1,0:T(8,128)(2,1)S(1)}, u32[]{:S(2)}, u32[]{:S(2)}) collective-permute-start(bf16[128,2048]{1,0:T(8,128)(2,1)} %convolution_convert_fusion.2), channel_id=1, source_target_pairs={{0,1},{1,0},{2,3},{3,2},{4,5},{5,4},{6,7},{7,6},{8,9},{9,8},{10,11... | collective-permute-start | bytes 1572872 | tf_op jit(solution)/shard_map/ppermute | solution.py:93
  107.9 0.6 copy-start.15
  131.9 8.5 %copy-start.4 = (bf16[256,1024]{1,0:T(8,128)(2,1)S(1)}, bf16[256,1024]{1,0:T(8,128)(2,1)}, u32[]{:S(2)}) copy-start(bf16[256,1024]{1,0:T(8,128)(2,1)} %copy-done.3) | copy-start | bytes 1572868
  131.9 8.5 %copy-start.6 = (bf16[256,1024]{1,0:T(8,128)(2,1)S(1)}, bf16[256,1024]{1,0:T(8,128)(2,1)}, u32[]{:S(2)}) copy-start(bf16[256,1024]{1,0:T(8,128)(2,1)} %copy-done.5) | copy-start | bytes 1572868
  133.9 17.6 %all-to-all-start.6 = ((bf16[16,48,128]{2,1,0:T(8,128)(2,1)}), bf16[16,48,128]{2,1,0:T(8,128)(2,1)S(1)}, u32[]{:S(2)}, u32[]{:S(2)}) async-start(bf16[16,48,128]{2,1,0:T(8,128)(2,1)} %shard_map.139), calls=%async_computation.6 | async-start | bytes 393216 | tf_op jit(solution)/shard_map/all_to_all | solution.py:24
  151.5 0.7 copy-start.7
  155.0 8.6 %collective-permute-start.6 = (bf16[256,128]{1,0:T(8,128)(2,1)}, bf16[256,128]{1,0:T(8,128)(2,1)S(1)}, u32[]{:S(2)}, u32[]{:S(2)}) collective-permute-start(bf16[256,128]{1,0:T(8,128)(2,1)} %get-tuple-element.33), channel_id=1, source_target_pairs={{0,1},{1,0},{2,3},{3,2},{4,5},{5,4},{6,7},{7,6},{8,9},{9,8},{10,11... | collective-permute-start | bytes 196616 | tf_op jit(solution)/shard_map/ppermute | solution.py:93
  163.6 0.6 copy-start.12
  165.9 12.5 %all-to-all-start.7 = ((bf16[16,80,128]{2,1,0:T(8,128)(2,1)}), bf16[16,80,128]{2,1,0:T(8,128)(2,1)S(1)}, u32[]{:S(2)}, u32[]{:S(2)}) async-start(bf16[16,80,128]{2,1,0:T(8,128)(2,1)} %shard_map.141), calls=%async_computation.7 | async-start | bytes 655360 | tf_op jit(solution)/shard_map/all_to_all | solution.py:24
  169.4 9.0 %copy-start.17 = (f32[16,128]{1,0:T(8,128)S(1)}, f32[16,128]{1,0:T(8,128)}, u32[]{:S(2)}) copy-start(f32[16,128]{1,0:T(8,128)} %get-tuple-element.35) | copy-start | bytes 24580
  178.5 5.8 %copy-start.14 = (f32[128,80]{0,1:T(8,128)S(1)}, f32[128,80]{0,1:T(8,128)}, u32[]{:S(2)}) copy-start(f32[128,80]{0,1:T(8,128)} %copy-done.13) | copy-start | bytes 122884
  179.2 16.1 %all-to-all-start.8 = ((bf16[16,32,128]{2,1,0:T(8,128)(2,1)}), bf16[16,32,128]{2,1,0:T(8,128)(2,1)S(1)}, u32[]{:S(2)}, u32[]{:S(2)}) async-start(bf16[16,32,128]{2,1,0:T(8,128)(2,1)} %copy.58), calls=%async_computation.8 | async-start | bytes 262144 | tf_op jit(solution)/shard_map/all_to_all | solution.py:24
  183.3 2.3 %copy-start.16 = (f32[128,80]{0,1:T(8,128)S(1)}, f32[128,80]{0,1:T(8,128)}, u32[]{:S(2)}) copy-start(f32[128,80]{0,1:T(8,128)} %copy-done.15) | copy-start | bytes 122884
  195.4 8.1 %copy-start.20 = (bf16[128,1024]{1,0:T(8,128)(2,1)S(1)}, bf16[128,1024]{1,0:T(8,128)(2,1)}, u32[]{:S(2)}) copy-start(bf16[128,1024]{1,0:T(8,128)(2,1)} %get-tuple-element.37) | copy-start | bytes 786436
  195.4 8.1 %copy-start.21 = (bf16[128,1024]{1,0:T(8,128)(2,1)S(1)}, bf16[128,1024]{1,0:T(8,128)(2,1)}, u32[]{:S(2)}) copy-start(bf16[128,1024]{1,0:T(8,128)(2,1)} %get-tuple-element.36) | copy-start | bytes 786436
  196.4 8.3 %copy-start.1 = (bf16[128,2048]{1,0:T(8,128)(2,1)S(1)}, bf16[128,2048]{1,0:T(8,128)(2,1)}, u32[]{:S(2)}) copy-start(bf16[128,2048]{1,0:T(8,128)(2,1)} %up_ref.3) | copy-start | bytes 1572868
  196.4 16.6 %all-to-all-start.9 = ((bf16[8,16,2048]{2,1,0:T(8,128)(2,1)}), bf16[8,16,2048]{2,1,0:T(8,128)(2,1)S(1)}, u32[]{:S(2)}, u32[]{:S(2)}) async-start(bf16[8,16,2048]{2,1,0:T(8,128)(2,1)} %broadcast_in_dim.107), calls=%async_computation.9 | async-start | bytes 1048576 | tf_op jit(solution)/shard_map/all_to_all | solution.py:24
Sparse Core Ops, SparseCore 0:
  18.6 35.8 all-gather.1

commit v8 on v5

--- a/solution.py
+++ b/solution.py
@@ -7,7 +7,8 @@
 
 HEAD = 64
 GCAP = 2
-PIECES = 4
+PIECES = 2
+SENDS = 1
 SCALE = HEAD ** (-0.5)
 BF, F32 = jnp.bfloat16, jnp.float32
 DEVICES = ("y", "z", "x", "c")
@@ -39,24 +40,42 @@
 
 
 def join_kernel(spot_ref, keep_ref, got_ref, more_ref, ret_ref, out_ref):
-    blocks, rows = out_ref.shape[0], more_ref.shape[0]
+    blocks = out_ref.shape[0]
+    rows = keep_ref.shape[0] // blocks
     for block in range(blocks):
         part = pl.ds(block * rows, rows)
         memory = keep_ref[part].astype(F32) + got_ref[part].astype(F32)
-        memory = memory + jnp.where(spot_ref[0] == block, more_ref[...], 0.0)
+        memory = memory + jnp.where(spot_ref[0] == block, more_ref[rows:], 0.0)
         out_ref[block, :rows] = memory.astype(BF)
         out_ref[block, rows:] = ret_ref[...]
 
 
 def join_blocks(spot, keep, got, more, returned, blocks):
     vmem = pl.BlockSpec(memory_space=pltpu.VMEM)
-    shape = (blocks, more.shape[0] + returned.shape[0], more.shape[1])
+    shape = (blocks, keep.shape[0] // blocks + returned.shape[0], keep.shape[1])
     return pl.pallas_call(
         join_kernel,
         in_specs=[pl.BlockSpec(memory_space=pltpu.SMEM)] + [vmem] * 4,
         out_specs=vmem,
         out_shape=jax.ShapeDtypeStruct(shape, BF),
     )(spot, keep, got, more, returned)
+
+
+def sum_kernel(parts_ref, out_ref):
+    for pair in range(out_ref.shape[0]):
+        cols = slice(pair * 2 * HEAD, (pair + 1) * 2 * HEAD)
+        total = parts_ref[0, :, cols].astype(F32)
+        for part in range(1, parts_ref.shape[0]):
+            total = total + parts_ref[part, :, cols].astype(F32)
+        out_ref[pair] = total.astype(BF)
+
+
+def sum_by_pairs(parts):
+    vmem = pl.BlockSpec(memory_space=pltpu.VMEM)
+    shape = (parts.shape[2] // (2 * HEAD), parts.shape[1], 2 * HEAD)
+    return pl.pallas_call(
+        sum_kernel, in_specs=[vmem], out_specs=vmem, out_shape=jax.ShapeDtypeStruct(shape, BF)
+    )(parts)
 
 
 def head_pairs(values):
@@ -124,7 +143,7 @@
     mem = own.shape[0]
     block = 512
     column = lambda n: pl.BlockSpec((n, block), lambda i: (0, i))
-    outs = [tokens, mem] + [mem // 2] * 2
+    outs = [tokens, mem] + [mem // SENDS] * SENDS
     got = pl.pallas_call(
         bulk_kernel,
         grid=(width // block,),
@@ -188,8 +207,9 @@
     )(spot, sums, gathered, queries, own, across)
 
 
-def pick_kernel(counts_ref, ids_ref, *refs):
-    parts, (rows_ref, place_ref) = refs[:-2], refs[-2:]
+def pick_kernel(core_ref, counts_ref, ids_ref, keys_ref, values_ref, *refs):
+    parts, (rows_ref, place_ref, own_ref) = refs[:-3], refs[-3:]
+    own_ref[...] = jnp.where(core_ref[0] == 0, keys_ref[...], values_ref[...])
     slots, tokens = place_ref.shape
     slot = lax.broadcasted_iota(jnp.int32, (slots, tokens), 0)
     expert, order = slot // GCAP, slot % GCAP
@@ -211,18 +231,19 @@
         rows_ref[copy, :, len(parts) * width :] = count.astype(F32).astype(BF)
 
 
-def pick_rows(counts, ids, parts, slots, copies):
+def pick_rows(core, counts, ids, keys, values, parts, slots, copies):
     tokens, width = parts[0].shape
     vmem = pl.BlockSpec(memory_space=pltpu.VMEM)
     return pl.pallas_call(
         pick_kernel,
-        in_specs=[pl.BlockSpec(memory_space=pltpu.SMEM)] + [vmem] * (1 + len(parts)),
-        out_specs=[vmem, vmem],
+        in_specs=[pl.BlockSpec(memory_space=pltpu.SMEM)] * 2 + [vmem] * (3 + len(parts)),
+        out_specs=[vmem] * 3,
         out_shape=[
             jax.ShapeDtypeStruct((copies, slots, len(parts) * width + tokens), BF),
             jax.ShapeDtypeStruct((slots, tokens), BF),
+            jax.ShapeDtypeStruct(keys.shape, BF),
         ],
-    )(counts, ids, *parts)
+    )(core, counts, ids, keys, values, *parts)
 
 
 def per_device(
@@ -234,13 +255,21 @@
     slots = window * GCAP
     mine, core, depth = lax.axis_index("y"), lax.axis_index("c"), lax.axis_index("z")
     first = core == 0
-    own_memory = lax.all_gather(jnp.where(first, mem_keys, mem_values), "y", axis=0, tiled=True)
 
     experts = jnp.arange(window, dtype=jnp.int32)
     slot_ids = jnp.arange(slots, dtype=jnp.int32)
-    picked, place = pick_rows(
-        send_counts, expert_ids.reshape(1, tokens), (queries, states, upstream), slots, window
-    )
+    core_id = core.reshape(1).astype(jnp.int32)
+    picked, place, own_memory = pick_rows(
+        core_id,
+        send_counts,
+        expert_ids.reshape(1, tokens),
+        mem_keys,
+        mem_values,
+        (queries, states, upstream),
+        slots,
+        window,
+    )
+    own_memory = lax.all_gather(own_memory, "y", axis=0, tiled=True)
     group = exchange(picked, "y").reshape(window * slots, -1)
 
     counts = group[:, 3 * width].reshape(window, slots)[:, ::GCAP].astype(jnp.int32)
@@ -256,6 +285,7 @@
     own = (own_target[:, None] == slot_ids[None, :]).astype(BF)
     place_back = dot(place, own, 0, 0)
     taken = jnp.sum(place_back, axis=1, keepdims=True)
+    free = (1.0 - taken).astype(BF)
     place_back = place_back.astype(BF)
 
     in_head = jnp.arange(heads)[:, None] == (jnp.arange(width) // HEAD)[None, :]
@@ -293,16 +323,11 @@
     ]
 
     bulk_queries, keep, send = bulk_backward(
-        core.reshape(1).astype(jnp.int32),
-        (1.0 - taken).astype(BF),
-        upstream,
-        queries,
-        own_memory,
-        across_memory,
-    )
-    near = spread(after(level, *send), "x")
-    sent = jnp.concatenate([other_core(piece) for piece in send], axis=0)
-    bulk = (keep.astype(F32) + sent.astype(F32)).astype(BF)
+        core_id, free, upstream, queries, own_memory, across_memory
+    )
+    near = spread(after(level, free, *across_memory), "x")
+    got = [other_core(piece) for piece in send]
+    bulk = (keep.astype(F32) + jnp.concatenate(got, axis=0).astype(F32)).astype(BF)
     own_rows = mem_keys.shape[0]
     blocks = [
         lax.dynamic_slice_in_dim(bulk, (mine + d) % window * own_rows, own_rows, 0)
@@ -310,7 +335,7 @@
     ]
     moves = [[(i, (i + d) % window) for i in range(window)] for d in range(window)]
     got = [lax.ppermute(blocks[d], "y", moves[d]) for d in (1, 3)]
-    far = other_core(after(near, *blocks))
+    far = other_core(near)
     weight_in, weight_out = w_in[0], w_out[0]
     parts_of_x = lax.axis_size("x")
 
@@ -329,9 +354,10 @@
 
     back = (near_back + other_core(far_back.astype(BF)).astype(F32)).astype(BF)
     rows = back.shape[0] // parts_of_x
-    back = [back.reshape(parts_of_x, rows, width), bulk.reshape(2, parts_of_x, -1, width).transpose(1, 0, 2, 3).reshape(parts_of_x, -1, width)]
-    back = collect(jnp.concatenate(back, axis=1).reshape(-1, width), "x").astype(BF)
-    joined = exchange(head_pairs(back), "z")
+    bulk = bulk.reshape(2, parts_of_x, -1, width).transpose(1, 0, 2, 3)
+    back = [back.reshape(parts_of_x, rows, width), bulk.reshape(parts_of_x, -1, width)]
+    back = exchange(jnp.concatenate(back, axis=1), "x")
+    joined = exchange(sum_by_pairs(back), "z")
     returned, keep, send, bulk = routed_backward(
         jnp.stack([core, depth]).astype(jnp.int32),
         joined,
@@ -342,14 +368,11 @@
     )
 
     blocks = window * parts_of_x
-    spot = (mine + 2) % window * parts_of_x + lax.axis_index("x")
-    bulk, opposite = jnp.split(bulk, 2, axis=0)
-    joined = join_blocks(
-        spot.reshape(1).astype(jnp.int32), keep, other_core(send), opposite, returned, blocks
-    )
+    spot = ((mine + 2) % window * parts_of_x + lax.axis_index("x")).reshape(1).astype(jnp.int32)
+    joined = join_blocks(spot, keep, other_core(send), bulk, returned, blocks)
     joined = exchange(joined, ("y", "x"))
     rows_of_x = joined.shape[1] - returned.shape[0]
-    memory = (jnp.sum(joined[:, :rows_of_x].astype(F32), axis=0) + bulk).astype(BF)
+    memory = (jnp.sum(joined[:, :rows_of_x].astype(F32), axis=0) + bulk[:rows_of_x]).astype(BF)
     returned = joined[:, rows_of_x:].reshape((window, parts_of_x) + returned.shape)
     returned = lax.dynamic_index_in_dim(returned, lax.axis_index("x"), 1, False)
     returned = returned.reshape(window, 2, depths, GCAP, 2 * HEAD).transpose(2, 0, 1, 3, 4)

time: 234 us -> 218 us (0.932)
  waiting for transfers between devices: 61.3 us -> 52.3 us
  starting transfers between devices: 95.2 us -> 88.6 us
  local copies, waits for them, and re-layouts: 13.1 us -> 10.3 us
  Pallas kernels: 15.9 us -> 18.4 us
    all_to_all x8, waiting for transfers between devices: 59.5 us -> 49.8 us  [exchange(): return lax.all_to_all(values, axes, split_axis=0, concat_axis=0, tiled=True)]
    all_to_all x8, starting transfers between devices: 57.4 us -> 50.8 us  [exchange(): return lax.all_to_all(values, axes, split_axis=0, concat_axis=0, tiled=True)]
    ppermute x9 -> x6, starting transfers between devices: 31.2 us -> 31.1 us  [other_core(): return lax.ppermute(values, 'c', [(0, 1), (1, 0)])]
  transfers between devices with their start and end apart: 20 -> 17, of which waited for: 10 -> 10; matrix products, arithmetic and copies ran while one was open for 8% -> 8% of each run, Pallas kernels for 5% -> 4%
where the time goes in v8:
time: 218 us; the launch traced here: 217 us
  starting transfers between devices  88.6 us (41%)
  waiting for transfers between devices  52.3 us (24%)
  Pallas kernels  18.4 us (8%)
  blocking collectives  17.8 us (8%)
  between operations  14.7 us (7%)
  local copies, waits for them, and re-layouts  10.3 us (5%)
  matrix products  8.44 us (4%)
  other arithmetic  5.95 us (3%)
    all_to_all x8, starting transfers between devices, exchange(): return lax.all_to_all(values, axes, split_axis=0, concat_axis=0, tiled=True)  50.8 us
    all_to_all x8, waiting for transfers between devices, exchange(): return lax.all_to_all(values, axes, split_axis=0, concat_axis=0, tiled=True)  49.8 us
    ppermute x6, starting transfers between devices, other_core(): return lax.ppermute(values, 'c', [(0, 1), (1, 0)])  31.1 us
    all_to_all x1, blocking collectives, exchange(): return lax.all_to_all(values, axes, split_axis=0, concat_axis=0, tiled=True)  17.8 us
    pallas_call x1, Pallas kernels, bulk_backward(): pl.pallas_call(bulk_kernel, grid=(width // block,), in_specs=[pl.BlockSpe...  8.92 us
    dot_general x16, matrix products, dot(): lax.dot_general(left, right, (((left_dim,), (right_dim,)), ((), ())), pre...  8.18 us
    ppermute x2, starting transfers between devices, per_device(): got = [lax.ppermute(blocks[d], 'y', moves[d]) for d in (1, 3)]  6.62 us
  transfers between devices with their start and end apart: 17, of which 10 were waited for; matrix products, arithmetic and copies ran while one was open for 8% of the time, Pallas kernels for 4%

profile of v8, /device:TPU:1, one launch (start us, length us, event | category | flops | bytes accessed | tf_op | source)
XLA Modules:
  0.0 216.5 jit_solution(10395236872960923308)
XLA Ops:
  7.2 2.8 %shard_map.136 = (bf16[4,8,6272]{2,1,0:T(8,128)(2,1)}, bf16[8,128]{1,0:T(8,128)(2,1)}, bf16[64,2048]{1,0:T(8,128)(2,1)}) custom-call(s32[1]{0:T(128)} %bitcast.core_ref, s32[1,4]{1,0:T(1,128)} %counts_ref.1, s32[1,128]{1,0:T(1,128)} %bitcast.109, bf16[64,2048]{1,0:T(8,128)(2,1)} %keys_ref.1, bf16[64,2048]{1,0:T(8,128)(2,1)} %values_ref.1, ...), custom_call_target="tpu_custom_call" | custom-call | tf_op jit(solution)/shard_map/pallas_call | solution.py:237
  10.1 5.2 %all-to-all-start = ((bf16[4,8,6272]{2,1,0:T(8,128)(2,1)}), bf16[4,8,6272]{2,1,0:T(8,128)(2,1)S(1)}, u32[]{:S(2)}, u32[]{:S(2)}) async-start(bf16[4,8,6272]{2,1,0:T(8,128)(2,1)} %get-tuple-element.21), calls=%async_computation | async-start | bytes 802816 | tf_op jit(solution)/shard_map/all_to_all | solution.py:25
  15.3 6.2 %all-to-all-done = bf16[4,8,6272]{2,1,0:T(8,128)(2,1)S(1)} async-done(((bf16[4,8,6272]{2,1,0:T(8,128)(2,1)}), bf16[4,8,6272]{2,1,0:T(8,128)(2,1)S(1)}, u32[]{:S(2)}, u32[]{:S(2)}) %all-to-all-start) | async-done | bytes 401440 | tf_op jit(solution)/shard_map/all_to_all | solution.py:25
  22.2 0.5 fusion.99
  22.7 0.3 copy-done.13
  23.0 0.5 fusion.6
  23.9 0.7 all_to_all.35
  24.6 3.3 %all-to-all-start.1 = ((f32[4,2,2176]{2,1,0:T(2,128)}), f32[4,2,2176]{2,1,0:T(2,128)S(1)}, u32[]{:S(2)}, u32[]{:S(2)}) async-start(f32[4,2,2176]{2,1,0:T(2,128)} %all_to_all.35), calls=%async_computation.1 | async-start | bytes 139264 | tf_op jit(solution)/shard_map/all_to_all | solution.py:25
  28.2 4.2 %all-to-all-done.1 = f32[4,2,2176]{2,1,0:T(2,128)S(1)} async-done(((f32[4,2,2176]{2,1,0:T(2,128)}), f32[4,2,2176]{2,1,0:T(2,128)S(1)}, u32[]{:S(2)}, u32[]{:S(2)}) %all-to-all-start.1) | async-done | bytes 69664 | tf_op jit(solution)/shard_map/all_to_all | solution.py:25
  32.5 0.3 fusion.7
  33.1 1.0 pad_maximum_fusion.3
  34.1 15.6 %all-to-all-start.2 = ((bf16[16,2,4224]{2,1,0:T(2,128)(2,1)}), bf16[16,2,4224]{2,1,0:T(2,128)(2,1)S(1)}, u32[]{:S(2)}, u32[]{:S(2)}) async-start(bf16[16,2,4224]{2,1,0:T(2,128)(2,1)} %pad_maximum_fusion.3), calls=%async_computation.2 | async-start | bytes 540672 | tf_op jit(solution)/shard_map/all_to_all | solution.py:25
  49.7 1.3 fusion.95
  51.0 5.9 %collective-permute-start.1 = (bf16[128,2048]{1,0:T(8,128)(2,1)S(1)}, bf16[128,2048]{1,0:T(8,128)(2,1)S(1)}, u32[]{:S(2)}, u32[]{:S(2)}) collective-permute-start(bf16[128,2048]{1,0:T(8,128)(2,1)S(1)} %get-tuple-element.37), channel_id=1, source_target_pairs={{0,1},{1,0},{2,3},{3,2},{4,5},{5,4},{6,7},{7,6},{8,9},{9,8},{10,11... | collective-permute-start | bytes 1572872 | tf_op jit(solution)/shard_map/ppermute | solution.py:95
  56.9 1.9 collective-permute-start
  58.9 0.3 fusion.98
  59.1 3.4 %all-to-all-done.2 = bf16[16,2,4224]{2,1,0:T(2,128)(2,1)S(1)} async-done(((bf16[16,2,4224]{2,1,0:T(2,128)(2,1)}), bf16[16,2,4224]{2,1,0:T(2,128)(2,1)S(1)}, u32[]{:S(2)}, u32[]{:S(2)}) %all-to-all-start.2) | async-done | bytes 270368 | tf_op jit(solution)/shard_map/all_to_all | solution.py:25
  62.7 1.2 broadcast_in_dim.103
  64.0 4.0 %all-to-all-start.3 = ((bf16[4,32,4096]{2,1,0:T(8,128)(2,1)}), bf16[4,32,4096]{2,1,0:T(8,128)(2,1)S(1)}, u32[]{:S(2)}, u32[]{:S(2)}) async-start(bf16[4,32,4096]{2,1,0:T(8,128)(2,1)} %broadcast_in_dim.103), calls=%async_computation.3 | async-start | bytes 2097152 | tf_op jit(solution)/shard_map/all_to_all | solution.py:25
  68.0 0.7 copy.54.free_ref
  68.8 8.9 %shard_map.137 = (bf16[128,2048]{1,0:T(8,128)(2,1)}, bf16[256,2048]{1,0:T(8,128)(2,1)}, bf16[256,2048]{1,0:T(8,128)(2,1)}) custom-call(s32[1]{0:T(128)} %bitcast.core_ref, bf16[128,1]{1,0:T(8,128)(2,1)} %copy.54.free_ref, bf16[128,2048]{1,0:T(8,128)(2,1)} %up_ref.1, bf16[128,2048]{1,0:T(8,128)(2,1)} %q_ref.1, ...), custom_call_target="tpu_custom_call" | custom-call | flops 805306368 | bytes 4194304 | tf_op jit(solution)/shard_map/pallas_call | solution.py:147
  77.7 9.6 %collective-permute-start.4 = (bf16[256,2048]{1,0:T(8,128)(2,1)}, bf16[256,2048]{1,0:T(8,128)(2,1)}, u32[]{:S(2)}, u32[]{:S(2)}) collective-permute-start(bf16[256,2048]{1,0:T(8,128)(2,1)} %get-tuple-element.26), channel_id=1, source_target_pairs={{0,1},{1,0},{2,3},{3,2},{4,5},{5,4},{6,7},{7,6},{8,9},{9,8},{10,11... | collective-permute-start | bytes 3145736 | tf_op jit(solution)/shard_map/ppermute | solution.py:95
  87.4 2.1 collective-permute-start.2
  89.5 0.3 fusion.21
  89.8 1.3 fusion.47
  91.1 1.6 add_convert_fusion
  92.8 2.4 %collective-permute-start.5 = (bf16[64,2048]{1,0:T(8,128)(2,1)S(1)}, bf16[64,2048]{1,0:T(8,128)(2,1)S(1)}, u32[]{:S(2)}, u32[]{:S(2)}) collective-permute-start(bf16[64,2048]{1,0:T(8,128)(2,1)S(1)} %get-tuple-element.34), channel_id=1, source_target_pairs={{0,128},{128,256},{256,384},{384,0},{1,129},{129,257},{257,385},{3... | collective-permute-start | bytes 786440 | tf_op jit(solution)/shard_map/ppermute | solution.py:337
  95.2 4.3 %collective-permute-start.6 = (bf16[64,2048]{1,0:T(8,128)(2,1)S(1)}, bf16[64,2048]{1,0:T(8,128)(2,1)S(1)}, u32[]{:S(2)}, u32[]{:S(2)}) collective-permute-start(bf16[64,2048]{1,0:T(8,128)(2,1)S(1)} %get-tuple-element.36), channel_id=1, source_target_pairs={{0,384},{128,0},{256,128},{384,256},{1,385},{129,1},{257,129},{385... | collective-permute-start | bytes 786440 | tf_op jit(solution)/shard_map/ppermute | solution.py:337
  99.4 0.3 fusion.14
  99.8 0.3 fusion.54
  100.1 0.3 fusion.28
  100.4 3.0 %collective-permute-start.3 = (bf16[128,2048]{1,0:T(8,128)(2,1)S(1)}, bf16[128,2048]{1,0:T(8,128)(2,1)S(1)}, u32[]{:S(2)}, u32[]{:S(2)}) collective-permute-start(bf16[128,2048]{1,0:T(8,128)(2,1)S(1)} %fusion.28), channel_id=1, source_target_pairs={{0,1},{1,0},{2,3},{3,2},{4,5},{5,4},{6,7},{7,6},{8,9},{9,8},{10,11... | collective-permute-start | bytes 1572872 | tf_op jit(solution)/shard_map/ppermute | solution.py:95
  103.4 0.8 collective-permute-done.6
  104.4 0.5 collective-permute-done.3
  104.9 0.3 add_convert_fusion.1
  105.4 17.8 %all_to_all.54.parts_ref = bf16[4,64,2048]{2,1,0:T(8,128)(2,1)} all-to-all(bf16[4,64,2048]{2,1,0:T(8,128)(2,1)S(1)} %pad_maximum_fusion), channel_id=1, replica_groups=mesh['y'=4,'z'=16,'x'=4,'c'=2] {'x'}, dimensions={0} | all-to-all | bytes 2097152 | tf_op jit(solution)/shard_map/all_to_all | solution.py:25
  123.2 2.1 shard_map.138
  125.4 4.9 %all-to-all-start.5 = ((bf16[16,64,128]{2,1,0:T(8,128)(2,1)}), bf16[16,64,128]{2,1,0:T(8,128)(2,1)S(1)}, u32[]{:S(2)}, u32[]{:S(2)}) async-start(bf16[16,64,128]{2,1,0:T(8,128)(2,1)} %shard_map.138), calls=%async_computation.5 | async-start | bytes 524288 | tf_op jit(solution)/shard_map/all_to_all | solution.py:25
  130.3 0.6 pad_add_fusion.spot_ref
  130.8 0.6 slice.111.q_ref
  131.4 1.1 pad_maximum_fusion.1.across_ref
  132.5 10.6 %all-to-all-done.5.sums_ref = bf16[16,64,128]{2,1,0:T(8,128)(2,1)S(1)} async-done(((bf16[16,64,128]{2,1,0:T(8,128)(2,1)}), bf16[16,64,128]{2,1,0:T(8,128)(2,1)S(1)}, u32[]{:S(2)}, u32[]{:S(2)}) %all-to-all-start.5) | async-done | bytes 262176 | tf_op jit(solution)/shard_map/all_to_all | solution.py:25
  143.0 0.7 copy-done.10
  143.7 2.9 %shard_map.139 = (bf16[64,128]{1,0:T(8,128)(2,1)}, bf16[256,128]{1,0:T(8,128)(2,1)}, bf16[256,128]{1,0:T(8,128)(2,1)}, f32[32,128]{1,0:T(8,128)}) custom-call(s32[2]{0:T(128)} %pad_add_fusion.spot_ref, bf16[16,64,128]{2,1,0:T(8,128)(2,1)} %copy-done.10, bf16[32,4096]{1,0:T(8,128)(2,1)} %copy-done.2, bf16[32,128]{1,0:T(8,128)(2,1)} %slice.111.q_ref, ...), custom_call_target="tpu_custom_call" | custom-call | tf_op jit(solution)/shard_map/pallas_call | solution.py:190
  146.6 8.7 %collective-permute-start.7 = (bf16[256,128]{1,0:T(8,128)(2,1)}, bf16[256,128]{1,0:T(8,128)(2,1)S(1)}, u32[]{:S(2)}, u32[]{:S(2)}) collective-permute-start(bf16[256,128]{1,0:T(8,128)(2,1)} %get-tuple-element.30), channel_id=1, source_target_pairs={{0,1},{1,0},{2,3},{3,2},{4,5},{5,4},{6,7},{7,6},{8,9},{9,8},{10,11... | collective-permute-start | bytes 196616 | tf_op jit(solution)/shard_map/ppermute | solution.py:95
  155.3 1.1 collective-permute-done.7.got_ref
  156.4 0.6 copy-done.14
  157.0 1.6 shard_map.140
  158.7 5.5 %all-to-all-start.6 = ((bf16[16,80,128]{2,1,0:T(8,128)(2,1)}), bf16[16,80,128]{2,1,0:T(8,128)(2,1)S(1)}, u32[]{:S(2)}, u32[]{:S(2)}) async-start(bf16[16,80,128]{2,1,0:T(8,128)(2,1)} %shard_map.140), calls=%async_computation.6 | async-start | bytes 655360 | tf_op jit(solution)/shard_map/all_to_all | solution.py:25
  164.2 0.2 fusion.23
  164.5 8.6 %all-to-all-done.6 = bf16[16,80,128]{2,1,0:T(8,128)(2,1)S(1)} async-done(((bf16[16,80,128]{2,1,0:T(8,128)(2,1)}), bf16[16,80,128]{2,1,0:T(8,128)(2,1)S(1)}, u32[]{:S(2)}, u32[]{:S(2)}) %all-to-all-start.6) | async-done | bytes 327712 | tf_op jit(solution)/shard_map/all_to_all | solution.py:25
  173.2 0.7 copy.58
  173.9 5.3 %all-to-all-start.7 = ((bf16[16,32,128]{2,1,0:T(8,128)(2,1)}), bf16[16,32,128]{2,1,0:T(8,128)(2,1)S(1)}, u32[]{:S(2)}, u32[]{:S(2)}) async-start(bf16[16,32,128]{2,1,0:T(8,128)(2,1)} %copy.58), calls=%async_computation.7 | async-start | bytes 262144 | tf_op jit(solution)/shard_map/all_to_all | solution.py:25
  179.2 0.2 fusion.19
  179.4 1.0 fusion.5
  180.4 1.0 fusion.4
  181.4 9.8 %all-to-all-done.7 = bf16[16,32,128]{2,1,0:T(8,128)(2,1)S(1)} async-done(((bf16[16,32,128]{2,1,0:T(8,128)(2,1)}), bf16[16,32,128]{2,1,0:T(8,128)(2,1)S(1)}, u32[]{:S(2)}, u32[]{:S(2)}) %all-to-all-start.7) | async-done | bytes 131104 | tf_op jit(solution)/shard_map/all_to_all | solution.py:25
  191.4 0.9 broadcast_in_dim.107
  192.2 7.1 %all-to-all-start.8 = ((bf16[8,16,2048]{2,1,0:T(8,128)(2,1)}), bf16[8,16,2048]{2,1,0:T(8,128)(2,1)S(1)}, u32[]{:S(2)}, u32[]{:S(2)}) async-start(bf16[8,16,2048]{2,1,0:T(8,128)(2,1)} %broadcast_in_dim.107), calls=%async_computation.8 | async-start | bytes 1048576 | tf_op jit(solution)/shard_map/all_to_all | solution.py:25
  199.4 1.1 fusion.1
  200.5 0.3 convolution_convert_fusion.1
  200.8 0.9 broadcast_select_fusion
  201.8 7.1 %all-to-all-done.8 = bf16[8,16,2048]{2,1,0:T(8,128)(2,1)S(1)} async-done(((bf16[8,16,2048]{2,1,0:T(8,128)(2,1)}), bf16[8,16,2048]{2,1,0:T(8,128)(2,1)S(1)}, u32[]{:S(2)}, u32[]{:S(2)}) %all-to-all-start.8) | async-done | bytes 524320 | tf_op jit(solution)/shard_map/all_to_all | solution.py:25
  208.9 0.8 fusion.96
  (95 shorter events, 2.9 us)
Async XLA Ops:
  7.2 82.3 %copy-start = (bf16[1,80,2048]{2,1,0:T(8,128)(2,1)S(1)}, bf16[1,80,2048]{2,1,0:T(8,128)(2,1)}, u32[]{:S(2)}) copy-start(bf16[1,80,2048]{2,1,0:T(8,128)(2,1)} %param.15) | copy-start | bytes 983044
  7.2 42.5 %all-gather.2.cloned.1.call-start = ((), (), s32[]{:S(2)}) async-start(), calls=%async_computation.9 | async-start | bytes 1310720 | tf_op jit(solution)/shard_map/all_gather | solution.py:272
  10.0 12.2 %copy-start.12 = (bf16[64,2048]{1,0:T(8,128)(2,1)S(1)}, bf16[64,2048]{1,0:T(8,128)(2,1)}, u32[]{:S(2)}) copy-start(bf16[64,2048]{1,0:T(8,128)(2,1)} %keys_ref.1) | copy-start | bytes 786436
  10.1 11.4 %all-to-all-start = ((bf16[4,8,6272]{2,1,0:T(8,128)(2,1)}), bf16[4,8,6272]{2,1,0:T(8,128)(2,1)S(1)}, u32[]{:S(2)}, u32[]{:S(2)}) async-start(bf16[4,8,6272]{2,1,0:T(8,128)(2,1)} %get-tuple-element.21), calls=%async_computation | async-start | bytes 802816 | tf_op jit(solution)/shard_map/all_to_all | solution.py:25
  22.0 1.0 copy-start.13
  24.6 7.8 %all-to-all-start.1 = ((f32[4,2,2176]{2,1,0:T(2,128)}), f32[4,2,2176]{2,1,0:T(2,128)S(1)}, u32[]{:S(2)}, u32[]{:S(2)}) async-start(f32[4,2,2176]{2,1,0:T(2,128)} %all_to_all.35), calls=%async_computation.1 | async-start | bytes 139264 | tf_op jit(solution)/shard_map/all_to_all | solution.py:25
  34.1 28.5 %all-to-all-start.2 = ((bf16[16,2,4224]{2,1,0:T(2,128)(2,1)}), bf16[16,2,4224]{2,1,0:T(2,128)(2,1)S(1)}, u32[]{:S(2)}, u32[]{:S(2)}) async-start(bf16[16,2,4224]{2,1,0:T(2,128)(2,1)} %pad_maximum_fusion.3), calls=%async_computation.2 | async-start | bytes 540672 | tf_op jit(solution)/shard_map/all_to_all | solution.py:25
  49.7 9.2 %copy-start.17 = (bf16[8,128]{1,0:T(8,128)(2,1)S(1)}, bf16[8,128]{1,0:T(8,128)(2,1)}, u32[]{:S(2)}) copy-start(bf16[8,128]{1,0:T(8,128)(2,1)} %get-tuple-element.20) | copy-start | bytes 6148
  51.0 11.7 %collective-permute-start.1 = (bf16[128,2048]{1,0:T(8,128)(2,1)S(1)}, bf16[128,2048]{1,0:T(8,128)(2,1)S(1)}, u32[]{:S(2)}, u32[]{:S(2)}) collective-permute-start(bf16[128,2048]{1,0:T(8,128)(2,1)S(1)} %get-tuple-element.37), channel_id=1, source_target_pairs={{0,1},{1,0},{2,3},{3,2},{4,5},{5,4},{6,7},{7,6},{8,9},{9,8},{10,11... | collective-permute-start | bytes 1572872 | tf_op jit(solution)/shard_map/ppermute | solution.py:95
  56.9 5.8 %collective-permute-start = (bf16[128,2048]{1,0:T(8,128)(2,1)S(1)}, bf16[128,2048]{1,0:T(8,128)(2,1)S(1)}, u32[]{:S(2)}, u32[]{:S(2)}) collective-permute-start(bf16[128,2048]{1,0:T(8,128)(2,1)S(1)} %get-tuple-element.38), channel_id=1, source_target_pairs={{0,1},{1,0},{2,3},{3,2},{4,5},{5,4},{6,7},{7,6},{8,9},{9,8},{10,11... | collective-permute-start | bytes 1572872 | tf_op jit(solution)/shard_map/ppermute | solution.py:95
  62.6 1.3 copy-start.2
  62.7 1.3 copy-start.3
  62.7 1.4 copy-start.5
  64.0 23.4 %all-to-all-start.3 = ((bf16[4,32,4096]{2,1,0:T(8,128)(2,1)}), bf16[4,32,4096]{2,1,0:T(8,128)(2,1)S(1)}, u32[]{:S(2)}, u32[]{:S(2)}) async-start(bf16[4,32,4096]{2,1,0:T(8,128)(2,1)} %broadcast_in_dim.103), calls=%async_computation.3 | async-start | bytes 2097152 | tf_op jit(solution)/shard_map/all_to_all | solution.py:25
  77.7 13.4 %collective-permute-start.4 = (bf16[256,2048]{1,0:T(8,128)(2,1)}, bf16[256,2048]{1,0:T(8,128)(2,1)}, u32[]{:S(2)}, u32[]{:S(2)}) collective-permute-start(bf16[256,2048]{1,0:T(8,128)(2,1)} %get-tuple-element.26), channel_id=1, source_target_pairs={{0,1},{1,0},{2,3},{3,2},{4,5},{5,4},{6,7},{7,6},{8,9},{9,8},{10,11... | collective-permute-start | bytes 3145736 | tf_op jit(solution)/shard_map/ppermute | solution.py:95
  87.3 3.7 %copy-start.9 = (bf16[256,2048]{1,0:T(8,128)(2,1)S(1)}, bf16[256,2048]{1,0:T(8,128)(2,1)}, u32[]{:S(2)}) copy-start(bf16[256,2048]{1,0:T(8,128)(2,1)} %get-tuple-element.25) | copy-start | bytes 3145732
  87.4 12.0 %collective-permute-start.2 = (bf16[128,4096]{1,0:T(8,128)(2,1)S(1)}, bf16[128,4096]{1,0:T(8,128)(2,1)S(1)}, u32[]{:S(2)}, u32[]{:S(2)}) collective-permute-start(bf16[128,4096]{1,0:T(8,128)(2,1)S(1)} %bitcast.89), channel_id=1, source_target_pairs={{0,1},{1,0},{2,3},{3,2},{4,5},{5,4},{6,7},{7,6},{8,9},{9,8},{10,11... | collective-permute-start | bytes 3145736 | tf_op jit(solution)/shard_map/ppermute | solution.py:95
  92.7 7.1 %copy-start.16 = (bf16[1,80,2048]{2,1,0:T(8,128)(2,1)S(1)}, bf16[1,80,2048]{2,1,0:T(8,128)(2,1)}, u32[]{:S(2)}) copy-start(bf16[1,80,2048]{2,1,0:T(8,128)(2,1)} %param.16) | copy-start | bytes 983044
  92.8 10.6 %collective-permute-start.5 = (bf16[64,2048]{1,0:T(8,128)(2,1)S(1)}, bf16[64,2048]{1,0:T(8,128)(2,1)S(1)}, u32[]{:S(2)}, u32[]{:S(2)}) collective-permute-start(bf16[64,2048]{1,0:T(8,128)(2,1)S(1)} %get-tuple-element.34), channel_id=1, source_target_pairs={{0,128},{128,256},{256,384},{384,0},{1,129},{129,257},{257,385},{3... | collective-permute-start | bytes 786440 | tf_op jit(solution)/shard_map/ppermute | solution.py:337
  95.2 9.1 %collective-permute-start.6 = (bf16[64,2048]{1,0:T(8,128)(2,1)S(1)}, bf16[64,2048]{1,0:T(8,128)(2,1)S(1)}, u32[]{:S(2)}, u32[]{:S(2)}) collective-permute-start(bf16[64,2048]{1,0:T(8,128)(2,1)S(1)} %get-tuple-element.36), channel_id=1, source_target_pairs={{0,384},{128,0},{256,128},{384,256},{1,385},{129,1},{257,129},{385... | collective-permute-start | bytes 786440 | tf_op jit(solution)/shard_map/ppermute | solution.py:337
  99.4 1.0 copy-start.7
  100.4 4.5 %collective-permute-start.3 = (bf16[128,2048]{1,0:T(8,128)(2,1)S(1)}, bf16[128,2048]{1,0:T(8,128)(2,1)S(1)}, u32[]{:S(2)}, u32[]{:S(2)}) collective-permute-start(bf16[128,2048]{1,0:T(8,128)(2,1)S(1)} %fusion.28), channel_id=1, source_target_pairs={{0,1},{1,0},{2,3},{3,2},{4,5},{5,4},{6,7},{7,6},{8,9},{9,8},{10,11... | collective-permute-start | bytes 1572872 | tf_op jit(solution)/shard_map/ppermute | solution.py:95
  123.2 8.2 %copy-start.4 = (bf16[128,2048]{1,0:T(8,128)(2,1)S(1)}, bf16[128,2048]{1,0:T(8,128)(2,1)}, u32[]{:S(2)}) copy-start(bf16[128,2048]{1,0:T(8,128)(2,1)} %copy-done.3) | copy-start | bytes 1572868
  123.2 8.2 %copy-start.6 = (bf16[128,2048]{1,0:T(8,128)(2,1)S(1)}, bf16[128,2048]{1,0:T(8,128)(2,1)}, u32[]{:S(2)}) copy-start(bf16[128,2048]{1,0:T(8,128)(2,1)} %copy-done.5) | copy-start | bytes 1572868
  125.4 17.7 %all-to-all-start.5 = ((bf16[16,64,128]{2,1,0:T(8,128)(2,1)}), bf16[16,64,128]{2,1,0:T(8,128)(2,1)S(1)}, u32[]{:S(2)}, u32[]{:S(2)}) async-start(bf16[16,64,128]{2,1,0:T(8,128)(2,1)} %shard_map.138), calls=%async_computation.5 | async-start | bytes 524288 | tf_op jit(solution)/shard_map/all_to_all | solution.py:25
  143.0 0.7 copy-start.10
  146.6 9.8 %collective-permute-start.7 = (bf16[256,128]{1,0:T(8,128)(2,1)}, bf16[256,128]{1,0:T(8,128)(2,1)S(1)}, u32[]{:S(2)}, u32[]{:S(2)}) collective-permute-start(bf16[256,128]{1,0:T(8,128)(2,1)} %get-tuple-element.30), channel_id=1, source_target_pairs={{0,1},{1,0},{2,3},{3,2},{4,5},{5,4},{6,7},{7,6},{8,9},{9,8},{10,11... | collective-permute-start | bytes 196616 | tf_op jit(solution)/shard_map/ppermute | solution.py:95
  156.4 0.6 copy-start.14
  158.7 14.4 %copy-start.15 = (f32[32,128]{1,0:T(8,128)S(1)}, f32[32,128]{1,0:T(8,128)}, u32[]{:S(2)}) copy-start(f32[32,128]{1,0:T(8,128)} %get-tuple-element.31.more_ref) | copy-start | bytes 49156
  158.7 14.4 %all-to-all-start.6 = ((bf16[16,80,128]{2,1,0:T(8,128)(2,1)}), bf16[16,80,128]{2,1,0:T(8,128)(2,1)S(1)}, u32[]{:S(2)}, u32[]{:S(2)}) async-start(bf16[16,80,128]{2,1,0:T(8,128)(2,1)} %shard_map.140), calls=%async_computation.6 | async-start | bytes 655360 | tf_op jit(solution)/shard_map/all_to_all | solution.py:25
  173.2 6.3 %copy-start.8 = (bf16[128,4096]{1,0:T(8,128)(2,1)S(1)}, bf16[128,4096]{1,0:T(8,128)(2,1)}, u32[]{:S(2)}) copy-start(bf16[128,4096]{1,0:T(8,128)(2,1)} %copy-done.7) | copy-start | bytes 3145732
  173.9 17.3 %all-to-all-start.7 = ((bf16[16,32,128]{2,1,0:T(8,128)(2,1)}), bf16[16,32,128]{2,1,0:T(8,128)(2,1)S(1)}, u32[]{:S(2)}, u32[]{:S(2)}) async-start(bf16[16,32,128]{2,1,0:T(8,128)(2,1)} %copy.58), calls=%async_computation.7 | async-start | bytes 262144 | tf_op jit(solution)/shard_map/all_to_all | solution.py:25
  191.3 8.1 %copy-start.1 = (bf16[128,2048]{1,0:T(8,128)(2,1)S(1)}, bf16[128,2048]{1,0:T(8,128)(2,1)}, u32[]{:S(2)}) copy-start(bf16[128,2048]{1,0:T(8,128)(2,1)} %up_ref.1) | copy-start | bytes 1572868
  192.2 16.6 %all-to-all-start.8 = ((bf16[8,16,2048]{2,1,0:T(8,128)(2,1)}), bf16[8,16,2048]{2,1,0:T(8,128)(2,1)S(1)}, u32[]{:S(2)}, u32[]{:S(2)}) async-start(bf16[8,16,2048]{2,1,0:T(8,128)(2,1)} %broadcast_in_dim.107), calls=%async_computation.8 | async-start | bytes 1048576 | tf_op jit(solution)/shard_map/all_to_all | solution.py:25
  199.4 1.5 copy-start.11
Sparse Core Ops, SparseCore 0:
  10.7 35.9 all-gather.1

commit v9 on v8

--- a/solution.py
+++ b/solution.py
@@ -165,9 +165,9 @@
 
 
 def routed_kernel(
-    spot_ref, sums_ref, up_ref, q_ref, own_ref, across_ref, ret_ref, keep_ref, send_ref, bulk_ref
+    core_ref, sums_ref, up_ref, q_ref, own_ref, across_ref, ret_ref, keep_ref, send_ref, bulk_ref
 ):
-    first = spot_ref[0] == 0
+    first = core_ref[0] == 0
     tokens = q_ref.shape[0]
     sums = jnp.sum(sums_ref[...].astype(F32), axis=0)
     moe = sums[:tokens].astype(BF)
@@ -180,31 +180,19 @@
     ret_ref[tokens:] = g_queries
 
 
-def routed_backward(spot, sums, gathered, queries, own, across):
+def routed_backward(core, sums, upstream, queries, own, across):
     tokens, lanes = queries.shape
     mem, more = own.shape[0], sums.shape[1] - tokens
-    whole = lambda shape: pl.BlockSpec(shape, lambda i, spot: (0,) * len(shape))
-    skip = gathered.shape[1] // lanes // 2
-    column = lambda n, base: pl.BlockSpec((n, lanes), lambda i, spot: (0, base + spot[1]))
+    vmem = pl.BlockSpec(memory_space=pltpu.VMEM)
     outs = [(2 * tokens, lanes), (mem, lanes), (mem, lanes), (more, lanes)]
     return pl.pallas_call(
         routed_kernel,
-        grid_spec=pltpu.PrefetchScalarGridSpec(
-            num_scalar_prefetch=1,
-            grid=(1,),
-            in_specs=[
-                whole(sums.shape),
-                column(tokens, skip),
-                whole(queries.shape),
-                column(mem, 0),
-                column(mem, 0),
-            ],
-            out_specs=[whole(shape) for shape in outs],
-        ),
+        in_specs=[pl.BlockSpec(memory_space=pltpu.SMEM)] + [vmem] * 5,
+        out_specs=[vmem] * 4,
         out_shape=[
             jax.ShapeDtypeStruct(shape, dtype) for shape, dtype in zip(outs, (BF, BF, BF, F32))
         ],
-    )(spot, sums, gathered, queries, own, across)
+    )(core, sums, upstream, queries, own, across)
 
 
 def pick_kernel(core_ref, counts_ref, ids_ref, keys_ref, values_ref, *refs):
@@ -330,11 +318,12 @@
     bulk = (keep.astype(F32) + jnp.concatenate(got, axis=0).astype(F32)).astype(BF)
     own_rows = mem_keys.shape[0]
     blocks = [
-        lax.dynamic_slice_in_dim(bulk, (mine + d) % window * own_rows, own_rows, 0)
+        lax.dynamic_slice_in_dim(bulk, jnp.bitwise_xor(mine, d) * own_rows, own_rows, 0)
         for d in range(window)
     ]
-    moves = [[(i, (i + d) % window) for i in range(window)] for d in range(window)]
-    got = [lax.ppermute(blocks[d], "y", moves[d]) for d in (1, 3)]
+    got = [
+        lax.ppermute(blocks[d], "y", [(i, i ^ d) for i in range(window)]) for d in (1, 3)
+    ]
     far = other_core(near)
     weight_in, weight_out = w_in[0], w_out[0]
     parts_of_x = lax.axis_size("x")
@@ -358,13 +347,16 @@
     back = [back.reshape(parts_of_x, rows, width), bulk.reshape(parts_of_x, -1, width)]
     back = exchange(jnp.concatenate(back, axis=1), "x")
     joined = exchange(sum_by_pairs(back), "z")
+    column = lambda values, skip: lax.dynamic_slice_in_dim(
+        values, skip + depth * 2 * HEAD, 2 * HEAD, 1
+    )
     returned, keep, send, bulk = routed_backward(
-        jnp.stack([core, depth]).astype(jnp.int32),
+        core_id,
         joined,
-        level,
+        column(level, width),
         routed_queries,
-        own_memory,
-        jnp.concatenate(across_memory, axis=0),
+        column(own_memory, 0),
+        jnp.concatenate([column(piece, 0) for piece in across_memory], axis=0),
     )
 
     blocks = window * parts_of_x

time: 218 us -> 215 us (0.986)
  local copies, waits for them, and re-layouts: 10.3 us -> 13.8 us
  starting transfers between devices: 88.6 us -> 86 us
    dynamic_slice x1 -> x5, local copies, waits for them, and re-layouts: 0.06 us -> 3.65 us  [the longest x4 3.58 us: per_device(): lax.dynamic_slice_in_dim(values, skip + depth * 2 * HEAD, 2 * HEAD, 1)]
    all_to_all x8, waiting for transfers between devices: 49.8 us -> 46.7 us  [exchange(): return lax.all_to_all(values, axes, split_axis=0, concat_axis=0, tiled=True)]
    ppermute x2, waiting for transfers between devices: 0.83 us -> 3.75 us  [per_device(): lax.ppermute(blocks[d], 'y', [(i, i ^ d) for i in range(window)])]
  transfers between devices with their start and end apart: 17 -> 17, of which waited for: 10 -> 10; matrix products, arithmetic and copies ran while one was open for 8% -> 9% of each run, Pallas kernels for 4% -> 4%
where the time goes in v9:
time: 215 us; the launch traced here: 214 us
  starting transfers between devices  86 us (40%)
  waiting for transfers between devices  51.5 us (24%)
  Pallas kernels  17.7 us (8%)
  blocking collectives  17.3 us (8%)
  between operations  14.6 us (7%)
  local copies, waits for them, and re-layouts  13.8 us (6%)
  matrix products  7.43 us (3%)
  other arithmetic  5.59 us (3%)
    all_to_all x8, starting transfers between devices, exchange(): return lax.all_to_all(values, axes, split_axis=0, concat_axis=0, tiled=True)  49.9 us
    all_to_all x8, waiting for transfers between devices, exchange(): return lax.all_to_all(values, axes, split_axis=0, concat_axis=0, tiled=True)  46.7 us
    ppermute x6, starting transfers between devices, other_core(): return lax.ppermute(values, 'c', [(0, 1), (1, 0)])  31.3 us
    all_to_all x1, blocking collectives, exchange(): return lax.all_to_all(values, axes, split_axis=0, concat_axis=0, tiled=True)  17.3 us
    pallas_call x1, Pallas kernels, bulk_backward(): pl.pallas_call(bulk_kernel, grid=(width // block,), in_specs=[pl.BlockSpe...  8.97 us
    dot_general x16, matrix products, dot(): lax.dot_general(left, right, (((left_dim,), (right_dim,)), ((), ())), pre...  7.17 us
    ppermute x2, starting transfers between devices, per_device(): lax.ppermute(blocks[d], 'y', [(i, i ^ d) for i in range(window)])  4.74 us
  transfers between devices with their start and end apart: 17, of which 10 were waited for; matrix products, arithmetic and copies ran while one was open for 9% of the time, Pallas kernels for 4%

profile of v9, /device:TPU:1, one launch (start us, length us, event | category | flops | bytes accessed | tf_op | source)
XLA Modules:
  0.0 214.0 jit_solution(5231763802975065055)
XLA Ops:
  7.2 2.8 %shard_map.136 = (bf16[4,8,6272]{2,1,0:T(8,128)(2,1)}, bf16[8,128]{1,0:T(8,128)(2,1)}, bf16[64,2048]{1,0:T(8,128)(2,1)}) custom-call(s32[1]{0:T(128)} %bitcast.core_ref, s32[1,4]{1,0:T(1,128)} %counts_ref.1, s32[1,128]{1,0:T(1,128)} %bitcast.108, bf16[64,2048]{1,0:T(8,128)(2,1)} %keys_ref.1, bf16[64,2048]{1,0:T(8,128)(2,1)} %values_ref.1, ...), custom_call_target="tpu_custom_call" | custom-call | tf_op jit(solution)/shard_map/pallas_call | solution.py:225
  10.1 5.2 %all-to-all-start = ((bf16[4,8,6272]{2,1,0:T(8,128)(2,1)}), bf16[4,8,6272]{2,1,0:T(8,128)(2,1)S(1)}, u32[]{:S(2)}, u32[]{:S(2)}) async-start(bf16[4,8,6272]{2,1,0:T(8,128)(2,1)} %get-tuple-element.21), calls=%async_computation | async-start | bytes 802816 | tf_op jit(solution)/shard_map/all_to_all | solution.py:25
  15.3 6.2 %all-to-all-done = bf16[4,8,6272]{2,1,0:T(8,128)(2,1)S(1)} async-done(((bf16[4,8,6272]{2,1,0:T(8,128)(2,1)}), bf16[4,8,6272]{2,1,0:T(8,128)(2,1)S(1)}, u32[]{:S(2)}, u32[]{:S(2)}) %all-to-all-start) | async-done | bytes 401440 | tf_op jit(solution)/shard_map/all_to_all | solution.py:25
  22.2 0.5 fusion.99
  23.0 0.5 fusion.6
  23.9 0.7 all_to_all.35
  24.6 3.3 %all-to-all-start.1 = ((f32[4,2,2176]{2,1,0:T(2,128)}), f32[4,2,2176]{2,1,0:T(2,128)S(1)}, u32[]{:S(2)}, u32[]{:S(2)}) async-start(f32[4,2,2176]{2,1,0:T(2,128)} %all_to_all.35), calls=%async_computation.1 | async-start | bytes 139264 | tf_op jit(solution)/shard_map/all_to_all | solution.py:25
  28.2 4.2 %all-to-all-done.1 = f32[4,2,2176]{2,1,0:T(2,128)S(1)} async-done(((f32[4,2,2176]{2,1,0:T(2,128)}), f32[4,2,2176]{2,1,0:T(2,128)S(1)}, u32[]{:S(2)}, u32[]{:S(2)}) %all-to-all-start.1) | async-done | bytes 69664 | tf_op jit(solution)/shard_map/all_to_all | solution.py:25
  33.1 1.0 pad_maximum_fusion.2
  34.1 15.6 %all-to-all-start.2 = ((bf16[16,2,4224]{2,1,0:T(2,128)(2,1)}), bf16[16,2,4224]{2,1,0:T(2,128)(2,1)S(1)}, u32[]{:S(2)}, u32[]{:S(2)}) async-start(bf16[16,2,4224]{2,1,0:T(2,128)(2,1)} %pad_maximum_fusion.2), calls=%async_computation.2 | async-start | bytes 540672 | tf_op jit(solution)/shard_map/all_to_all | solution.py:25
  49.7 1.3 fusion.95
  51.0 5.9 %collective-permute-start.1 = (bf16[128,2048]{1,0:T(8,128)(2,1)S(1)}, bf16[128,2048]{1,0:T(8,128)(2,1)S(1)}, u32[]{:S(2)}, u32[]{:S(2)}) collective-permute-start(bf16[128,2048]{1,0:T(8,128)(2,1)S(1)} %get-tuple-element.37), channel_id=1, source_target_pairs={{0,1},{1,0},{2,3},{3,2},{4,5},{5,4},{6,7},{7,6},{8,9},{9,8},{10,11... | collective-permute-start | bytes 1572872 | tf_op jit(solution)/shard_map/ppermute | solution.py:95
  56.9 1.9 collective-permute-start
  58.9 0.3 fusion.98
  59.1 3.4 %all-to-all-done.2 = bf16[16,2,4224]{2,1,0:T(2,128)(2,1)S(1)} async-done(((bf16[16,2,4224]{2,1,0:T(2,128)(2,1)}), bf16[16,2,4224]{2,1,0:T(2,128)(2,1)S(1)}, u32[]{:S(2)}, u32[]{:S(2)}) %all-to-all-start.2) | async-done | bytes 270368 | tf_op jit(solution)/shard_map/all_to_all | solution.py:25
  62.7 1.2 broadcast_in_dim.103
  64.0 4.0 %all-to-all-start.3 = ((bf16[4,32,4096]{2,1,0:T(8,128)(2,1)}), bf16[4,32,4096]{2,1,0:T(8,128)(2,1)S(1)}, u32[]{:S(2)}, u32[]{:S(2)}) async-start(bf16[4,32,4096]{2,1,0:T(8,128)(2,1)} %broadcast_in_dim.103), calls=%async_computation.3 | async-start | bytes 2097152 | tf_op jit(solution)/shard_map/all_to_all | solution.py:25
  68.0 0.7 copy.54.free_ref
  68.7 9.0 %shard_map.137 = (bf16[128,2048]{1,0:T(8,128)(2,1)}, bf16[256,2048]{1,0:T(8,128)(2,1)}, bf16[256,2048]{1,0:T(8,128)(2,1)}) custom-call(s32[1]{0:T(128)} %bitcast.core_ref, bf16[128,1]{1,0:T(8,128)(2,1)} %copy.54.free_ref, bf16[128,2048]{1,0:T(8,128)(2,1)} %up_ref.1, bf16[128,2048]{1,0:T(8,128)(2,1)} %q_ref.1, ...), custom_call_target="tpu_custom_call" | custom-call | flops 805306368 | bytes 4194304 | tf_op jit(solution)/shard_map/pallas_call | solution.py:147
  77.7 9.6 %collective-permute-start.4 = (bf16[256,2048]{1,0:T(8,128)(2,1)}, bf16[256,2048]{1,0:T(8,128)(2,1)}, u32[]{:S(2)}, u32[]{:S(2)}) collective-permute-start(bf16[256,2048]{1,0:T(8,128)(2,1)} %get-tuple-element.26), channel_id=1, source_target_pairs={{0,1},{1,0},{2,3},{3,2},{4,5},{5,4},{6,7},{7,6},{8,9},{9,8},{10,11... | collective-permute-start | bytes 3145736 | tf_op jit(solution)/shard_map/ppermute | solution.py:95
  87.3 2.1 collective-permute-start.2
  89.4 0.3 fusion.21
  89.7 0.3 fusion.47
  90.1 1.6 add_convert_fusion
  91.7 2.2 %collective-permute-start.5 = (bf16[64,2048]{1,0:T(8,128)(2,1)S(1)}, bf16[64,2048]{1,0:T(8,128)(2,1)S(1)}, u32[]{:S(2)}, u32[]{:S(2)}) collective-permute-start(bf16[64,2048]{1,0:T(8,128)(2,1)S(1)} %get-tuple-element.34), channel_id=1, source_target_pairs={{0,128},{128,0},{256,384},{384,256},{1,129},{129,1},{257,385},{385... | collective-permute-start | bytes 786440 | tf_op jit(solution)/shard_map/ppermute | solution.py:325
  94.0 2.5 %collective-permute-start.6 = (bf16[64,2048]{1,0:T(8,128)(2,1)S(1)}, bf16[64,2048]{1,0:T(8,128)(2,1)S(1)}, u32[]{:S(2)}, u32[]{:S(2)}) collective-permute-start(bf16[64,2048]{1,0:T(8,128)(2,1)S(1)} %get-tuple-element.36), channel_id=1, source_target_pairs={{0,384},{128,256},{256,128},{384,0},{1,385},{129,257},{257,129},{3... | collective-permute-start | bytes 786440 | tf_op jit(solution)/shard_map/ppermute | solution.py:325
  96.5 0.3 fusion.14
  96.8 0.3 fusion.54
  97.1 0.3 fusion.28
  97.5 2.9 %collective-permute-start.3 = (bf16[128,2048]{1,0:T(8,128)(2,1)S(1)}, bf16[128,2048]{1,0:T(8,128)(2,1)S(1)}, u32[]{:S(2)}, u32[]{:S(2)}) collective-permute-start(bf16[128,2048]{1,0:T(8,128)(2,1)S(1)} %fusion.28), channel_id=1, source_target_pairs={{0,1},{1,0},{2,3},{3,2},{4,5},{5,4},{6,7},{7,6},{8,9},{9,8},{10,11... | collective-permute-start | bytes 1572872 | tf_op jit(solution)/shard_map/ppermute | solution.py:95
  100.4 0.6 collective-permute-done.5
  101.0 3.1 %collective-permute-done.6 = bf16[64,2048]{1,0:T(8,128)(2,1)S(1)} collective-permute-done((bf16[64,2048]{1,0:T(8,128)(2,1)S(1)}, bf16[64,2048]{1,0:T(8,128)(2,1)S(1)}, u32[]{:S(2)}, u32[]{:S(2)}) %collective-permute-start.6) | collective-permute-done | bytes 262176 | tf_op jit(solution)/shard_map/ppermute | solution.py:325
  104.3 0.3 add_convert_fusion.1
  104.7 17.3 %all_to_all.54.parts_ref = bf16[4,64,2048]{2,1,0:T(8,128)(2,1)} all-to-all(bf16[4,64,2048]{2,1,0:T(8,128)(2,1)S(1)} %pad_maximum_fusion), channel_id=1, replica_groups=mesh['y'=4,'z'=16,'x'=4,'c'=2] {'x'}, dimensions={0} | all-to-all | bytes 2097152 | tf_op jit(solution)/shard_map/all_to_all | solution.py:25
  122.1 2.1 shard_map.138
  124.1 6.2 %all-to-all-start.5 = ((bf16[16,64,128]{2,1,0:T(8,128)(2,1)}), bf16[16,64,128]{2,1,0:T(8,128)(2,1)S(1)}, u32[]{:S(2)}, u32[]{:S(2)}) async-start(bf16[16,64,128]{2,1,0:T(8,128)(2,1)} %shard_map.138), calls=%async_computation.5 | async-start | bytes 524288 | tf_op jit(solution)/shard_map/all_to_all | solution.py:25
  130.3 0.6 slice.111.q_ref
  130.9 0.6 constant_dynamic-slice_fusion.4.up_ref
  131.5 1.5 constant_dynamic-slice_fusion.3.own_ref
  133.0 0.8 constant_dynamic-slice_fusion.1
  133.8 0.8 constant_dynamic-slice_fusion.2
  134.5 0.6 pad_maximum_fusion.4.across_ref
  135.2 8.0 %all-to-all-done.5.sums_ref = bf16[16,64,128]{2,1,0:T(8,128)(2,1)S(1)} async-done(((bf16[16,64,128]{2,1,0:T(8,128)(2,1)}), bf16[16,64,128]{2,1,0:T(8,128)(2,1)S(1)}, u32[]{:S(2)}, u32[]{:S(2)}) %all-to-all-start.5) | async-done | bytes 262176 | tf_op jit(solution)/shard_map/all_to_all | solution.py:25
  143.1 0.7 copy-done.3
  143.8 2.2 %shard_map.139 = (bf16[64,128]{1,0:T(8,128)(2,1)}, bf16[256,128]{1,0:T(8,128)(2,1)}, bf16[256,128]{1,0:T(8,128)(2,1)}, f32[32,128]{1,0:T(8,128)}) custom-call(s32[1]{0:T(128)} %bitcast.core_ref, bf16[16,64,128]{2,1,0:T(8,128)(2,1)} %copy-done.3, bf16[32,128]{1,0:T(8,128)(2,1)} %constant_dynamic-slice_fusion.4.up_ref, bf16[32,128]{1,0:T(8,128)(2,1)} %slice.111.q_ref, ...), custom_call_target="tpu_custom_call" | custom-call | tf_op jit(solution)/shard_map/pallas_call | solution.py:188
  146.0 8.9 %collective-permute-start.7 = (bf16[256,128]{1,0:T(8,128)(2,1)}, bf16[256,128]{1,0:T(8,128)(2,1)S(1)}, u32[]{:S(2)}, u32[]{:S(2)}) collective-permute-start(bf16[256,128]{1,0:T(8,128)(2,1)} %get-tuple-element.30), channel_id=1, source_target_pairs={{0,1},{1,0},{2,3},{3,2},{4,5},{5,4},{6,7},{7,6},{8,9},{9,8},{10,11... | collective-permute-start | bytes 196616 | tf_op jit(solution)/shard_map/ppermute | solution.py:95
  155.0 1.1 collective-permute-done.7.got_ref
  156.0 0.6 copy-done.9
  156.7 1.6 shard_map.140
  158.3 3.7 %all-to-all-start.6 = ((bf16[16,80,128]{2,1,0:T(8,128)(2,1)}), bf16[16,80,128]{2,1,0:T(8,128)(2,1)S(1)}, u32[]{:S(2)}, u32[]{:S(2)}) async-start(bf16[16,80,128]{2,1,0:T(8,128)(2,1)} %shard_map.140), calls=%async_computation.6 | async-start | bytes 655360 | tf_op jit(solution)/shard_map/all_to_all | solution.py:25
  162.0 0.6 broadcast_compare_fusion
  162.9 8.1 %all-to-all-done.6 = bf16[16,80,128]{2,1,0:T(8,128)(2,1)S(1)} async-done(((bf16[16,80,128]{2,1,0:T(8,128)(2,1)}), bf16[16,80,128]{2,1,0:T(8,128)(2,1)S(1)}, u32[]{:S(2)}, u32[]{:S(2)}) %all-to-all-start.6) | async-done | bytes 327712 | tf_op jit(solution)/shard_map/all_to_all | solution.py:25
  171.1 0.7 copy.58
  171.8 5.0 %all-to-all-start.7 = ((bf16[16,32,128]{2,1,0:T(8,128)(2,1)}), bf16[16,32,128]{2,1,0:T(8,128)(2,1)S(1)}, u32[]{:S(2)}, u32[]{:S(2)}) async-start(bf16[16,32,128]{2,1,0:T(8,128)(2,1)} %copy.58), calls=%async_computation.7 | async-start | bytes 262144 | tf_op jit(solution)/shard_map/all_to_all | solution.py:25
  177.0 1.0 fusion.5
  178.0 1.0 fusion.4
  178.9 9.8 %all-to-all-done.7 = bf16[16,32,128]{2,1,0:T(8,128)(2,1)S(1)} async-done(((bf16[16,32,128]{2,1,0:T(8,128)(2,1)}), bf16[16,32,128]{2,1,0:T(8,128)(2,1)S(1)}, u32[]{:S(2)}, u32[]{:S(2)}) %all-to-all-start.7) | async-done | bytes 131104 | tf_op jit(solution)/shard_map/all_to_all | solution.py:25
  188.9 0.9 broadcast_in_dim.107
  189.8 7.0 %all-to-all-start.8 = ((bf16[8,16,2048]{2,1,0:T(8,128)(2,1)}), bf16[8,16,2048]{2,1,0:T(8,128)(2,1)S(1)}, u32[]{:S(2)}, u32[]{:S(2)}) async-start(bf16[8,16,2048]{2,1,0:T(8,128)(2,1)} %broadcast_in_dim.107), calls=%async_computation.8 | async-start | bytes 1048576 | tf_op jit(solution)/shard_map/all_to_all | solution.py:25
  196.8 1.1 fusion.1
  197.9 0.3 convolution_convert_fusion.1
  198.3 0.9 broadcast_select_fusion
  199.2 7.1 %all-to-all-done.8 = bf16[8,16,2048]{2,1,0:T(8,128)(2,1)S(1)} async-done(((bf16[8,16,2048]{2,1,0:T(8,128)(2,1)}), bf16[8,16,2048]{2,1,0:T(8,128)(2,1)S(1)}, u32[]{:S(2)}, u32[]{:S(2)}) %all-to-all-start.8) | async-done | bytes 524320 | tf_op jit(solution)/shard_map/all_to_all | solution.py:25
  206.3 0.8 fusion.96
  (90 shorter events, 3.9 us)
Async XLA Ops:
  7.2 82.2 %copy-start = (bf16[1,80,2048]{2,1,0:T(8,128)(2,1)S(1)}, bf16[1,80,2048]{2,1,0:T(8,128)(2,1)}, u32[]{:S(2)}) copy-start(bf16[1,80,2048]{2,1,0:T(8,128)(2,1)} %param.15) | copy-start | bytes 983044
  7.2 42.5 %all-gather.2.cloned.1.call-start = ((), (), s32[]{:S(2)}) async-start(), calls=%async_computation.9 | async-start | bytes 1310720 | tf_op jit(solution)/shard_map/all_gather | solution.py:260
  10.0 12.2 %copy-start.7 = (bf16[64,2048]{1,0:T(8,128)(2,1)S(1)}, bf16[64,2048]{1,0:T(8,128)(2,1)}, u32[]{:S(2)}) copy-start(bf16[64,2048]{1,0:T(8,128)(2,1)} %keys_ref.1) | copy-start | bytes 786436
  10.1 11.4 %all-to-all-start = ((bf16[4,8,6272]{2,1,0:T(8,128)(2,1)}), bf16[4,8,6272]{2,1,0:T(8,128)(2,1)S(1)}, u32[]{:S(2)}, u32[]{:S(2)}) async-start(bf16[4,8,6272]{2,1,0:T(8,128)(2,1)} %get-tuple-element.21), calls=%async_computation | async-start | bytes 802816 | tf_op jit(solution)/shard_map/all_to_all | solution.py:25
  22.0 1.0 copy-start.8
  24.6 7.8 %all-to-all-start.1 = ((f32[4,2,2176]{2,1,0:T(2,128)}), f32[4,2,2176]{2,1,0:T(2,128)S(1)}, u32[]{:S(2)}, u32[]{:S(2)}) async-start(f32[4,2,2176]{2,1,0:T(2,128)} %all_to_all.35), calls=%async_computation.1 | async-start | bytes 139264 | tf_op jit(solution)/shard_map/all_to_all | solution.py:25
  34.1 28.5 %all-to-all-start.2 = ((bf16[16,2,4224]{2,1,0:T(2,128)(2,1)}), bf16[16,2,4224]{2,1,0:T(2,128)(2,1)S(1)}, u32[]{:S(2)}, u32[]{:S(2)}) async-start(bf16[16,2,4224]{2,1,0:T(2,128)(2,1)} %pad_maximum_fusion.2), calls=%async_computation.2 | async-start | bytes 540672 | tf_op jit(solution)/shard_map/all_to_all | solution.py:25
  49.7 9.2 %copy-start.12 = (bf16[8,128]{1,0:T(8,128)(2,1)S(1)}, bf16[8,128]{1,0:T(8,128)(2,1)}, u32[]{:S(2)}) copy-start(bf16[8,128]{1,0:T(8,128)(2,1)} %get-tuple-element.20) | copy-start | bytes 6148
  51.0 11.7 %collective-permute-start.1 = (bf16[128,2048]{1,0:T(8,128)(2,1)S(1)}, bf16[128,2048]{1,0:T(8,128)(2,1)S(1)}, u32[]{:S(2)}, u32[]{:S(2)}) collective-permute-start(bf16[128,2048]{1,0:T(8,128)(2,1)S(1)} %get-tuple-element.37), channel_id=1, source_target_pairs={{0,1},{1,0},{2,3},{3,2},{4,5},{5,4},{6,7},{7,6},{8,9},{9,8},{10,11... | collective-permute-start | bytes 1572872 | tf_op jit(solution)/shard_map/ppermute | solution.py:95
  56.9 5.8 %collective-permute-start = (bf16[128,2048]{1,0:T(8,128)(2,1)S(1)}, bf16[128,2048]{1,0:T(8,128)(2,1)S(1)}, u32[]{:S(2)}, u32[]{:S(2)}) collective-permute-start(bf16[128,2048]{1,0:T(8,128)(2,1)S(1)} %get-tuple-element.38), channel_id=1, source_target_pairs={{0,1},{1,0},{2,3},{3,2},{4,5},{5,4},{6,7},{7,6},{8,9},{9,8},{10,11... | collective-permute-start | bytes 1572872 | tf_op jit(solution)/shard_map/ppermute | solution.py:95
  59.1 4.8 %copy-start.13 = (f32[128]{0:T(128)}, f32[128]{0:T(128)S(1)}, u32[]{:S(2)}) copy-start(f32[128]{0:T(128)S(1)} %get-tuple-element.47) | copy-start | bytes 1540
  62.6 1.3 copy-start.4
  62.7 1.3 copy-start.5
  64.0 23.4 %all-to-all-start.3 = ((bf16[4,32,4096]{2,1,0:T(8,128)(2,1)}), bf16[4,32,4096]{2,1,0:T(8,128)(2,1)S(1)}, u32[]{:S(2)}, u32[]{:S(2)}) async-start(bf16[4,32,4096]{2,1,0:T(8,128)(2,1)} %broadcast_in_dim.103), calls=%async_computation.3 | async-start | bytes 2097152 | tf_op jit(solution)/shard_map/all_to_all | solution.py:25
  68.7 21.0 %copy-start.11 = (bf16[1,80,2048]{2,1,0:T(8,128)(2,1)S(1)}, bf16[1,80,2048]{2,1,0:T(8,128)(2,1)}, u32[]{:S(2)}) copy-start(bf16[1,80,2048]{2,1,0:T(8,128)(2,1)} %param.16) | copy-start | bytes 983044
  77.7 12.4 %collective-permute-start.4 = (bf16[256,2048]{1,0:T(8,128)(2,1)}, bf16[256,2048]{1,0:T(8,128)(2,1)}, u32[]{:S(2)}, u32[]{:S(2)}) collective-permute-start(bf16[256,2048]{1,0:T(8,128)(2,1)} %get-tuple-element.26), channel_id=1, source_target_pairs={{0,1},{1,0},{2,3},{3,2},{4,5},{5,4},{6,7},{7,6},{8,9},{9,8},{10,11... | collective-permute-start | bytes 3145736 | tf_op jit(solution)/shard_map/ppermute | solution.py:95
  87.3 2.7 %copy-start.2 = (bf16[256,2048]{1,0:T(8,128)(2,1)S(1)}, bf16[256,2048]{1,0:T(8,128)(2,1)}, u32[]{:S(2)}) copy-start(bf16[256,2048]{1,0:T(8,128)(2,1)} %get-tuple-element.25) | copy-start | bytes 3145732
  87.3 9.2 %collective-permute-start.2 = (bf16[128,4096]{1,0:T(8,128)(2,1)S(1)}, bf16[128,4096]{1,0:T(8,128)(2,1)S(1)}, u32[]{:S(2)}, u32[]{:S(2)}) collective-permute-start(bf16[128,4096]{1,0:T(8,128)(2,1)S(1)} %bitcast.88), channel_id=1, source_target_pairs={{0,1},{1,0},{2,3},{3,2},{4,5},{5,4},{6,7},{7,6},{8,9},{9,8},{10,11... | collective-permute-start | bytes 3145736 | tf_op jit(solution)/shard_map/ppermute | solution.py:95
  91.7 9.3 %collective-permute-start.5 = (bf16[64,2048]{1,0:T(8,128)(2,1)S(1)}, bf16[64,2048]{1,0:T(8,128)(2,1)S(1)}, u32[]{:S(2)}, u32[]{:S(2)}) collective-permute-start(bf16[64,2048]{1,0:T(8,128)(2,1)S(1)} %get-tuple-element.34), channel_id=1, source_target_pairs={{0,128},{128,0},{256,384},{384,256},{1,129},{129,1},{257,385},{385... | collective-permute-start | bytes 786440 | tf_op jit(solution)/shard_map/ppermute | solution.py:325
  94.0 10.2 %collective-permute-start.6 = (bf16[64,2048]{1,0:T(8,128)(2,1)S(1)}, bf16[64,2048]{1,0:T(8,128)(2,1)S(1)}, u32[]{:S(2)}, u32[]{:S(2)}) collective-permute-start(bf16[64,2048]{1,0:T(8,128)(2,1)S(1)} %get-tuple-element.36), channel_id=1, source_target_pairs={{0,384},{128,256},{256,128},{384,0},{1,385},{129,257},{257,129},{3... | collective-permute-start | bytes 786440 | tf_op jit(solution)/shard_map/ppermute | solution.py:325
  97.5 6.8 %collective-permute-start.3 = (bf16[128,2048]{1,0:T(8,128)(2,1)S(1)}, bf16[128,2048]{1,0:T(8,128)(2,1)S(1)}, u32[]{:S(2)}, u32[]{:S(2)}) collective-permute-start(bf16[128,2048]{1,0:T(8,128)(2,1)S(1)} %fusion.28), channel_id=1, source_target_pairs={{0,1},{1,0},{2,3},{3,2},{4,5},{5,4},{6,7},{7,6},{8,9},{9,8},{10,11... | collective-permute-start | bytes 1572872 | tf_op jit(solution)/shard_map/ppermute | solution.py:95
  124.1 19.0 %all-to-all-start.5 = ((bf16[16,64,128]{2,1,0:T(8,128)(2,1)}), bf16[16,64,128]{2,1,0:T(8,128)(2,1)S(1)}, u32[]{:S(2)}, u32[]{:S(2)}) async-start(bf16[16,64,128]{2,1,0:T(8,128)(2,1)} %shard_map.138), calls=%async_computation.5 | async-start | bytes 524288 | tf_op jit(solution)/shard_map/all_to_all | solution.py:25
  143.1 0.7 copy-start.3
  146.0 10.0 %collective-permute-start.7 = (bf16[256,128]{1,0:T(8,128)(2,1)}, bf16[256,128]{1,0:T(8,128)(2,1)S(1)}, u32[]{:S(2)}, u32[]{:S(2)}) collective-permute-start(bf16[256,128]{1,0:T(8,128)(2,1)} %get-tuple-element.30), channel_id=1, source_target_pairs={{0,1},{1,0},{2,3},{3,2},{4,5},{5,4},{6,7},{7,6},{8,9},{9,8},{10,11... | collective-permute-start | bytes 196616 | tf_op jit(solution)/shard_map/ppermute | solution.py:95
  156.0 0.6 copy-start.9
  158.3 12.7 %copy-start.10 = (f32[32,128]{1,0:T(8,128)S(1)}, f32[32,128]{1,0:T(8,128)}, u32[]{:S(2)}) copy-start(f32[32,128]{1,0:T(8,128)} %get-tuple-element.31.more_ref) | copy-start | bytes 49156
  158.3 12.6 %all-to-all-start.6 = ((bf16[16,80,128]{2,1,0:T(8,128)(2,1)}), bf16[16,80,128]{2,1,0:T(8,128)(2,1)S(1)}, u32[]{:S(2)}, u32[]{:S(2)}) async-start(bf16[16,80,128]{2,1,0:T(8,128)(2,1)} %shard_map.140), calls=%async_computation.6 | async-start | bytes 655360 | tf_op jit(solution)/shard_map/all_to_all | solution.py:25
  171.8 17.0 %all-to-all-start.7 = ((bf16[16,32,128]{2,1,0:T(8,128)(2,1)}), bf16[16,32,128]{2,1,0:T(8,128)(2,1)S(1)}, u32[]{:S(2)}, u32[]{:S(2)}) async-start(bf16[16,32,128]{2,1,0:T(8,128)(2,1)} %copy.58), calls=%async_computation.7 | async-start | bytes 262144 | tf_op jit(solution)/shard_map/all_to_all | solution.py:25
  188.8 8.0 %copy-start.1 = (bf16[128,2048]{1,0:T(8,128)(2,1)S(1)}, bf16[128,2048]{1,0:T(8,128)(2,1)}, u32[]{:S(2)}) copy-start(bf16[128,2048]{1,0:T(8,128)(2,1)} %up_ref.1) | copy-start | bytes 1572868
  189.8 16.5 %all-to-all-start.8 = ((bf16[8,16,2048]{2,1,0:T(8,128)(2,1)}), bf16[8,16,2048]{2,1,0:T(8,128)(2,1)S(1)}, u32[]{:S(2)}, u32[]{:S(2)}) async-start(bf16[8,16,2048]{2,1,0:T(8,128)(2,1)} %broadcast_in_dim.107), calls=%async_computation.8 | async-start | bytes 1048576 | tf_op jit(solution)/shard_map/all_to_all | solution.py:25
  196.8 1.5 copy-start.6
Sparse Core Ops, SparseCore 0:
  10.7 35.9 all-gather.1

commit v10 on v9

--- a/solution.py
+++ b/solution.py
@@ -195,8 +195,10 @@
     )(core, sums, upstream, queries, own, across)
 
 
-def pick_kernel(core_ref, counts_ref, ids_ref, keys_ref, values_ref, *refs):
-    parts, (rows_ref, place_ref, own_ref) = refs[:-3], refs[-3:]
+def pick_kernel(
+    core_ref, counts_ref, ids_ref, keys_ref, values_ref, q_ref, states_ref, up_ref,
+    rows_ref, local_ref, place_ref, own_ref,
+):
     own_ref[...] = jnp.where(core_ref[0] == 0, keys_ref[...], values_ref[...])
     slots, tokens = place_ref.shape
     slot = lax.broadcasted_iota(jnp.int32, (slots, tokens), 0)
@@ -210,13 +212,13 @@
     rank = dot(named.astype(BF), earlier).astype(jnp.int32)
     place = (named & (rank == order) & (rank < count)).astype(BF)
     place_ref[...] = place
-    width = parts[0].shape[1]
-    for i, part in enumerate(parts):
-        rows = dot(place, part[...]).astype(BF)
-        for copy in range(rows_ref.shape[0]):
-            rows_ref[copy, :, i * width : (i + 1) * width] = rows
+    width = q_ref.shape[1]
+    rows = dot(place, q_ref[...]).astype(BF)
     for copy in range(rows_ref.shape[0]):
-        rows_ref[copy, :, len(parts) * width :] = count.astype(F32).astype(BF)
+        rows_ref[copy, :, :width] = rows
+        rows_ref[copy, :, width:] = count.astype(F32).astype(BF)
+    local_ref[:, :width] = dot(place, states_ref[...]).astype(BF)
+    local_ref[:, width:] = dot(place, up_ref[...]).astype(BF)
 
 
 def pick_rows(core, counts, ids, keys, values, parts, slots, copies):
@@ -225,9 +227,10 @@
     return pl.pallas_call(
         pick_kernel,
         in_specs=[pl.BlockSpec(memory_space=pltpu.SMEM)] * 2 + [vmem] * (3 + len(parts)),
-        out_specs=[vmem] * 3,
+        out_specs=[vmem] * 4,
         out_shape=[
-            jax.ShapeDtypeStruct((copies, slots, len(parts) * width + tokens), BF),
+            jax.ShapeDtypeStruct((copies, slots, width + tokens), BF),
+            jax.ShapeDtypeStruct((slots, 2 * width), BF),
             jax.ShapeDtypeStruct((slots, tokens), BF),
             jax.ShapeDtypeStruct(keys.shape, BF),
         ],
@@ -247,7 +250,7 @@
     experts = jnp.arange(window, dtype=jnp.int32)
     slot_ids = jnp.arange(slots, dtype=jnp.int32)
     core_id = core.reshape(1).astype(jnp.int32)
-    picked, place, own_memory = pick_rows(
+    picked, local, place, own_memory = pick_rows(
         core_id,
         send_counts,
         expert_ids.reshape(1, tokens),
@@ -260,7 +263,7 @@
     own_memory = lax.all_gather(own_memory, "y", axis=0, tiled=True)
     group = exchange(picked, "y").reshape(window * slots, -1)
 
-    counts = group[:, 3 * width].reshape(window, slots)[:, ::GCAP].astype(jnp.int32)
+    counts = group[:, width].reshape(window, slots)[:, ::GCAP].astype(jnp.int32)
     offsets = jnp.cumsum(counts, axis=0).astype(jnp.int32) - counts
     order = jnp.arange(GCAP, dtype=jnp.int32)
     position = offsets[:, :, None] + order
@@ -268,16 +271,17 @@
     target = jnp.where(kept, experts[None, :, None] * GCAP + position, -1).reshape(-1)
     pack = (slot_ids[:, None] == target[None, :]).astype(BF)
     filled = jnp.sum(pack.astype(F32), axis=1)
-    routed = dot(pack, group[:, : 3 * width]).astype(BF)
+    routed = dot(pack, group[:, :width]).astype(BF)
     own_target = lax.dynamic_slice_in_dim(target, mine * slots, slots, 0)
     own = (own_target[:, None] == slot_ids[None, :]).astype(BF)
+    local = dot(own, local, 0, 0)
     place_back = dot(place, own, 0, 0)
     taken = jnp.sum(place_back, axis=1, keepdims=True)
-    free = (1.0 - taken).astype(BF)
+    free = jnp.broadcast_to((1.0 - taken).astype(BF), (tokens, 2 * HEAD))
     place_back = place_back.astype(BF)
 
     in_head = jnp.arange(heads)[:, None] == (jnp.arange(width) // HEAD)[None, :]
-    by_head = jnp.where(in_head[:, None, :], routed[None, :, :width], 0).reshape(-1, width)
+    by_head = jnp.where(in_head[:, None, :], routed[None], 0).reshape(-1, width)
     scores = dot(by_head, mem_keys, 1, 1) * SCALE
     top = jnp.max(scores, axis=1, keepdims=True)
     exps = jnp.exp(scores - top)
@@ -286,7 +290,7 @@
     part = jnp.sum(jnp.where(in_head[:, None, :], part, 0.0), axis=0)
     tops, totals = top.reshape(heads, slots).T, total.reshape(heads, slots).T
     pad = jnp.zeros((slots, 128 - 2 * heads), F32)
-    parts = exchange(jnp.concatenate([part, tops, totals, pad], axis=1), "y")
+    parts = exchange(jnp.concatenate([part, tops, totals, pad, local], axis=1), "y")
     parts = parts.reshape(window, GCAP, -1)
     tops, totals = parts[:, :, width : width + heads], parts[:, :, width + heads : width + 2 * heads]
     share = jnp.exp(tops - jnp.max(tops, axis=0))
@@ -295,14 +299,15 @@
         share.reshape(-1, heads), in_head.astype(F32), precision=lax.Precision.HIGHEST
     ).reshape(window, GCAP, width)
     attended = jnp.sum(parts[:, :, :width] * share, axis=0)
+    local = jnp.sum(parts[:, :, width + 128 :], axis=0)
     here = lax.dynamic_slice_in_dim(routed, mine * GCAP, GCAP, 0)
     here_filled = lax.dynamic_slice_in_dim(filled, mine * GCAP, GCAP, 0)
-    row = (here[:, width : 2 * width].astype(F32) + attended) * here_filled[:, None]
-    pair = jnp.concatenate([row.astype(BF), here[:, 2 * width :]], axis=1)
+    row = (local[:, :width] + attended) * here_filled[:, None]
+    pair = jnp.concatenate([row, local[:, width:]], axis=1).astype(BF)
 
     depths = lax.axis_size("z")
     copies = jnp.broadcast_to(pair[None], (depths,) + pair.shape)
-    level = exchange(jnp.concatenate([copies, head_pairs(here[:, :width])], axis=2), "z")
+    level = exchange(jnp.concatenate([copies, head_pairs(here)], axis=2), "z")
     level = level.reshape(-1, level.shape[2])
     routed_queries = level[:, 2 * width :]
     level = level[:, : 2 * width]

time: 215 us -> 215 us (level)
    dot_general x16 -> x17, matrix products: 7.17 us -> 7.44 us  [dot(): lax.dot_general(left, right, (((left_dim,), (right_dim,)), ((), ())), pre...]
where the time goes in v10:
time: 215 us; the launch traced here: 214 us
  starting transfers between devices  86.2 us (40%)
  waiting for transfers between devices  51.2 us (24%)
  Pallas kernels  17.6 us (8%)
  blocking collectives  17.3 us (8%)
  between operations  14.7 us (7%)
  local copies, waits for them, and re-layouts  13.6 us (6%)
  matrix products  7.7 us (4%)
  other arithmetic  5.62 us (3%)
    all_to_all x8, starting transfers between devices, exchange(): return lax.all_to_all(values, axes, split_axis=0, concat_axis=0, tiled=True)  50.2 us
    all_to_all x8, waiting for transfers between devices, exchange(): return lax.all_to_all(values, axes, split_axis=0, concat_axis=0, tiled=True)  46.1 us
    ppermute x6, starting transfers between devices, other_core(): return lax.ppermute(values, 'c', [(0, 1), (1, 0)])  31 us
    all_to_all x1, blocking collectives, exchange(): return lax.all_to_all(values, axes, split_axis=0, concat_axis=0, tiled=True)  17.3 us
    pallas_call x1, Pallas kernels, bulk_backward(): pl.pallas_call(bulk_kernel, grid=(width // block,), in_specs=[pl.BlockSpe...  8.98 us
    dot_general x17, matrix products, dot(): lax.dot_general(left, right, (((left_dim,), (right_dim,)), ((), ())), pre...  7.44 us
    ppermute x2, starting transfers between devices, per_device(): lax.ppermute(blocks[d], 'y', [(i, i ^ d) for i in range(window)])  4.91 us
  transfers between devices with their start and end apart: 17, of which 10 were waited for; matrix products, arithmetic and copies ran while one was open for 9% of the time, Pallas kernels for 4%

profile of v10, /device:TPU:1, one launch (start us, length us, event | category | flops | bytes accessed | tf_op | source)
XLA Modules:
  0.0 213.8 jit_solution(15816945891136054319)
XLA Ops:
  7.2 2.7 %shard_map.136 = (bf16[4,8,2176]{2,1,0:T(8,128)(2,1)}, bf16[8,4096]{1,0:T(8,128)(2,1)}, bf16[8,128]{1,0:T(8,128)(2,1)}, bf16[64,2048]{1,0:T(8,128)(2,1)}) custom-call(s32[1]{0:T(128)} %bitcast.core_ref, s32[1,4]{1,0:T(1,128)} %counts_ref.1, s32[1,128]{1,0:T(1,128)} %bitcast.107, bf16[64,2048]{1,0:T(8,128)(2,1)} %keys_ref.1, bf16[64,2048]{1,0:T(8,128)(2,1)} %values_ref.1, ...), custom_call_target="tpu_custom_call" | custom-call | tf_op jit(solution)/shard_map/pallas_call | solution.py:227
  10.0 5.0 %all-to-all-start = ((bf16[4,8,2176]{2,1,0:T(8,128)(2,1)}), bf16[4,8,2176]{2,1,0:T(8,128)(2,1)S(1)}, u32[]{:S(2)}, u32[]{:S(2)}) async-start(bf16[4,8,2176]{2,1,0:T(8,128)(2,1)} %get-tuple-element.21), calls=%async_computation | async-start | bytes 278528 | tf_op jit(solution)/shard_map/all_to_all | solution.py:25
  15.1 4.8 %all-to-all-done = bf16[4,8,2176]{2,1,0:T(8,128)(2,1)S(1)} async-done(((bf16[4,8,2176]{2,1,0:T(8,128)(2,1)}), bf16[4,8,2176]{2,1,0:T(8,128)(2,1)S(1)}, u32[]{:S(2)}, u32[]{:S(2)}) %all-to-all-start) | async-done | bytes 139296 | tf_op jit(solution)/shard_map/all_to_all | solution.py:25
  20.6 0.5 fusion.103
  21.1 0.5 fusion.6
  22.0 0.3 fusion.83
  22.4 0.8 all_to_all.35
  23.2 3.4 %all-to-all-start.1 = ((f32[4,2,6272]{2,1,0:T(2,128)}), f32[4,2,6272]{2,1,0:T(2,128)S(1)}, u32[]{:S(2)}, u32[]{:S(2)}) async-start(f32[4,2,6272]{2,1,0:T(2,128)} %all_to_all.35), calls=%async_computation.1 | async-start | bytes 401408 | tf_op jit(solution)/shard_map/all_to_all | solution.py:25
  26.8 5.0 %all-to-all-done.1 = f32[4,2,6272]{2,1,0:T(2,128)S(1)} async-done(((f32[4,2,6272]{2,1,0:T(2,128)}), f32[4,2,6272]{2,1,0:T(2,128)S(1)}, u32[]{:S(2)}, u32[]{:S(2)}) %all-to-all-start.1) | async-done | bytes 200736 | tf_op jit(solution)/shard_map/all_to_all | solution.py:25
  32.5 1.0 pad_maximum_fusion.2
  33.4 14.9 %all-to-all-start.2 = ((bf16[16,2,4224]{2,1,0:T(2,128)(2,1)}), bf16[16,2,4224]{2,1,0:T(2,128)(2,1)S(1)}, u32[]{:S(2)}, u32[]{:S(2)}) async-start(bf16[16,2,4224]{2,1,0:T(2,128)(2,1)} %pad_maximum_fusion.2), calls=%async_computation.2 | async-start | bytes 540672 | tf_op jit(solution)/shard_map/all_to_all | solution.py:25
  48.4 1.3 fusion.99
  49.7 5.9 %collective-permute-start.1 = (bf16[128,2048]{1,0:T(8,128)(2,1)S(1)}, bf16[128,2048]{1,0:T(8,128)(2,1)S(1)}, u32[]{:S(2)}, u32[]{:S(2)}) collective-permute-start(bf16[128,2048]{1,0:T(8,128)(2,1)S(1)} %get-tuple-element.37), channel_id=1, source_target_pairs={{0,1},{1,0},{2,3},{3,2},{4,5},{5,4},{6,7},{7,6},{8,9},{9,8},{10,11... | collective-permute-start | bytes 1572872 | tf_op jit(solution)/shard_map/ppermute | solution.py:95
  55.6 1.9 collective-permute-start
  57.8 3.4 %all-to-all-done.2 = bf16[16,2,4224]{2,1,0:T(2,128)(2,1)S(1)} async-done(((bf16[16,2,4224]{2,1,0:T(2,128)(2,1)}), bf16[16,2,4224]{2,1,0:T(2,128)(2,1)S(1)}, u32[]{:S(2)}, u32[]{:S(2)}) %all-to-all-start.2) | async-done | bytes 270368 | tf_op jit(solution)/shard_map/all_to_all | solution.py:25
  61.4 0.9 broadcast_in_dim.108.free_ref
  62.3 1.1 broadcast_in_dim.109
  63.4 4.0 %all-to-all-start.3 = ((bf16[4,32,4096]{2,1,0:T(8,128)(2,1)}), bf16[4,32,4096]{2,1,0:T(8,128)(2,1)S(1)}, u32[]{:S(2)}, u32[]{:S(2)}) async-start(bf16[4,32,4096]{2,1,0:T(8,128)(2,1)} %broadcast_in_dim.109), calls=%async_computation.3 | async-start | bytes 2097152 | tf_op jit(solution)/shard_map/all_to_all | solution.py:25
  67.4 9.0 %shard_map.137 = (bf16[128,2048]{1,0:T(8,128)(2,1)}, bf16[256,2048]{1,0:T(8,128)(2,1)}, bf16[256,2048]{1,0:T(8,128)(2,1)}) custom-call(s32[1]{0:T(128)} %bitcast.core_ref, bf16[128,128]{1,0:T(8,128)(2,1)} %broadcast_in_dim.108.free_ref, bf16[128,2048]{1,0:T(8,128)(2,1)} %up_ref.3, bf16[128,2048]{1,0:T(8,128)(2,1)} %q_ref.3, ...), custom_call_target="tpu_custom_call" | custom-call | flops 805306368 | bytes 4194304 | tf_op jit(solution)/shard_map/pallas_call | solution.py:147
  76.4 9.6 %collective-permute-start.4 = (bf16[256,2048]{1,0:T(8,128)(2,1)}, bf16[256,2048]{1,0:T(8,128)(2,1)}, u32[]{:S(2)}, u32[]{:S(2)}) collective-permute-start(bf16[256,2048]{1,0:T(8,128)(2,1)} %get-tuple-element.26), channel_id=1, source_target_pairs={{0,1},{1,0},{2,3},{3,2},{4,5},{5,4},{6,7},{7,6},{8,9},{9,8},{10,11... | collective-permute-start | bytes 3145736 | tf_op jit(solution)/shard_map/ppermute | solution.py:95
  86.0 2.1 collective-permute-start.2
  88.1 0.3 fusion.21
  88.4 0.3 fusion.47
  88.8 1.6 add_convert_fusion
  90.5 2.4 %collective-permute-start.5 = (bf16[64,2048]{1,0:T(8,128)(2,1)S(1)}, bf16[64,2048]{1,0:T(8,128)(2,1)S(1)}, u32[]{:S(2)}, u32[]{:S(2)}) collective-permute-start(bf16[64,2048]{1,0:T(8,128)(2,1)S(1)} %get-tuple-element.34), channel_id=1, source_target_pairs={{0,128},{128,0},{256,384},{384,256},{1,129},{129,1},{257,385},{385... | collective-permute-start | bytes 786440 | tf_op jit(solution)/shard_map/ppermute | solution.py:330
  92.8 2.5 %collective-permute-start.6 = (bf16[64,2048]{1,0:T(8,128)(2,1)S(1)}, bf16[64,2048]{1,0:T(8,128)(2,1)S(1)}, u32[]{:S(2)}, u32[]{:S(2)}) collective-permute-start(bf16[64,2048]{1,0:T(8,128)(2,1)S(1)} %get-tuple-element.36), channel_id=1, source_target_pairs={{0,384},{128,256},{256,128},{384,0},{1,385},{129,257},{257,129},{3... | collective-permute-start | bytes 786440 | tf_op jit(solution)/shard_map/ppermute | solution.py:330
  95.4 0.3 fusion.14
  95.7 0.3 fusion.54
  96.0 0.3 fusion.27
  96.3 2.7 %collective-permute-start.3 = (bf16[128,2048]{1,0:T(8,128)(2,1)S(1)}, bf16[128,2048]{1,0:T(8,128)(2,1)S(1)}, u32[]{:S(2)}, u32[]{:S(2)}) collective-permute-start(bf16[128,2048]{1,0:T(8,128)(2,1)S(1)} %fusion.27), channel_id=1, source_target_pairs={{0,1},{1,0},{2,3},{3,2},{4,5},{5,4},{6,7},{7,6},{8,9},{9,8},{10,11... | collective-permute-start | bytes 1572872 | tf_op jit(solution)/shard_map/ppermute | solution.py:95
  99.0 0.7 collective-permute-done.5
  99.7 3.3 %collective-permute-done.6 = bf16[64,2048]{1,0:T(8,128)(2,1)S(1)} collective-permute-done((bf16[64,2048]{1,0:T(8,128)(2,1)S(1)}, bf16[64,2048]{1,0:T(8,128)(2,1)S(1)}, u32[]{:S(2)}, u32[]{:S(2)}) %collective-permute-start.6) | collective-permute-done | bytes 262176 | tf_op jit(solution)/shard_map/ppermute | solution.py:330
  103.2 0.3 add_convert_fusion.1
  103.6 17.3 %all_to_all.54.parts_ref = bf16[4,64,2048]{2,1,0:T(8,128)(2,1)} all-to-all(bf16[4,64,2048]{2,1,0:T(8,128)(2,1)S(1)} %pad_maximum_fusion), channel_id=1, replica_groups=mesh['y'=4,'z'=16,'x'=4,'c'=2] {'x'}, dimensions={0} | all-to-all | bytes 2097152 | tf_op jit(solution)/shard_map/all_to_all | solution.py:25
  120.9 2.1 shard_map.138
  123.0 7.1 %all-to-all-start.5 = ((bf16[16,64,128]{2,1,0:T(8,128)(2,1)}), bf16[16,64,128]{2,1,0:T(8,128)(2,1)S(1)}, u32[]{:S(2)}, u32[]{:S(2)}) async-start(bf16[16,64,128]{2,1,0:T(8,128)(2,1)} %shard_map.138), calls=%async_computation.5 | async-start | bytes 524288 | tf_op jit(solution)/shard_map/all_to_all | solution.py:25
  130.1 0.6 slice.110.q_ref
  130.7 0.6 constant_dynamic-slice_fusion.4.up_ref
  131.3 1.5 constant_dynamic-slice_fusion.3.own_ref
  132.8 0.8 constant_dynamic-slice_fusion.1
  133.5 0.8 constant_dynamic-slice_fusion.2
  134.3 0.6 pad_maximum_fusion.4.across_ref
  134.9 8.0 %all-to-all-done.5.sums_ref = bf16[16,64,128]{2,1,0:T(8,128)(2,1)S(1)} async-done(((bf16[16,64,128]{2,1,0:T(8,128)(2,1)}), bf16[16,64,128]{2,1,0:T(8,128)(2,1)S(1)}, u32[]{:S(2)}, u32[]{:S(2)}) %all-to-all-start.5) | async-done | bytes 262176 | tf_op jit(solution)/shard_map/all_to_all | solution.py:25
  142.9 0.7 copy-done.3
  143.6 2.2 %shard_map.139 = (bf16[64,128]{1,0:T(8,128)(2,1)}, bf16[256,128]{1,0:T(8,128)(2,1)}, bf16[256,128]{1,0:T(8,128)(2,1)}, f32[32,128]{1,0:T(8,128)}) custom-call(s32[1]{0:T(128)} %bitcast.core_ref, bf16[16,64,128]{2,1,0:T(8,128)(2,1)} %copy-done.3, bf16[32,128]{1,0:T(8,128)(2,1)} %constant_dynamic-slice_fusion.4.up_ref, bf16[32,128]{1,0:T(8,128)(2,1)} %slice.110.q_ref, ...), custom_call_target="tpu_custom_call" | custom-call | tf_op jit(solution)/shard_map/pallas_call | solution.py:188
  145.8 8.8 %collective-permute-start.7 = (bf16[256,128]{1,0:T(8,128)(2,1)}, bf16[256,128]{1,0:T(8,128)(2,1)S(1)}, u32[]{:S(2)}, u32[]{:S(2)}) collective-permute-start(bf16[256,128]{1,0:T(8,128)(2,1)} %get-tuple-element.30), channel_id=1, source_target_pairs={{0,1},{1,0},{2,3},{3,2},{4,5},{5,4},{6,7},{7,6},{8,9},{9,8},{10,11... | collective-permute-start | bytes 196616 | tf_op jit(solution)/shard_map/ppermute | solution.py:95
  154.7 1.1 collective-permute-done.7.got_ref
  155.7 0.6 copy-done.10
  156.4 1.6 shard_map.140
  158.0 3.7 %all-to-all-start.6 = ((bf16[16,80,128]{2,1,0:T(8,128)(2,1)}), bf16[16,80,128]{2,1,0:T(8,128)(2,1)S(1)}, u32[]{:S(2)}, u32[]{:S(2)}) async-start(bf16[16,80,128]{2,1,0:T(8,128)(2,1)} %shard_map.140), calls=%async_computation.6 | async-start | bytes 655360 | tf_op jit(solution)/shard_map/all_to_all | solution.py:25
  161.7 0.6 broadcast_compare_fusion
  162.6 8.0 %all-to-all-done.6 = bf16[16,80,128]{2,1,0:T(8,128)(2,1)S(1)} async-done(((bf16[16,80,128]{2,1,0:T(8,128)(2,1)}), bf16[16,80,128]{2,1,0:T(8,128)(2,1)S(1)}, u32[]{:S(2)}, u32[]{:S(2)}) %all-to-all-start.6) | async-done | bytes 327712 | tf_op jit(solution)/shard_map/all_to_all | solution.py:25
  170.8 0.7 copy.49
  171.5 5.1 %all-to-all-start.7 = ((bf16[16,32,128]{2,1,0:T(8,128)(2,1)}), bf16[16,32,128]{2,1,0:T(8,128)(2,1)S(1)}, u32[]{:S(2)}, u32[]{:S(2)}) async-start(bf16[16,32,128]{2,1,0:T(8,128)(2,1)} %copy.49), calls=%async_computation.7 | async-start | bytes 262144 | tf_op jit(solution)/shard_map/all_to_all | solution.py:25
  176.8 1.0 fusion.5
  177.8 1.0 fusion.4
  178.8 9.8 %all-to-all-done.7 = bf16[16,32,128]{2,1,0:T(8,128)(2,1)S(1)} async-done(((bf16[16,32,128]{2,1,0:T(8,128)(2,1)}), bf16[16,32,128]{2,1,0:T(8,128)(2,1)S(1)}, u32[]{:S(2)}, u32[]{:S(2)}) %all-to-all-start.7) | async-done | bytes 131104 | tf_op jit(solution)/shard_map/all_to_all | solution.py:25
  188.8 0.8 broadcast_in_dim.113
  189.6 7.0 %all-to-all-start.8 = ((bf16[8,16,2048]{2,1,0:T(8,128)(2,1)}), bf16[8,16,2048]{2,1,0:T(8,128)(2,1)S(1)}, u32[]{:S(2)}, u32[]{:S(2)}) async-start(bf16[8,16,2048]{2,1,0:T(8,128)(2,1)} %broadcast_in_dim.113), calls=%async_computation.8 | async-start | bytes 1048576 | tf_op jit(solution)/shard_map/all_to_all | solution.py:25
  196.6 1.1 fusion.1
  197.7 0.3 convolution_convert_fusion
  198.1 0.9 broadcast_select_fusion
  199.0 7.1 %all-to-all-done.8 = bf16[8,16,2048]{2,1,0:T(8,128)(2,1)S(1)} async-done(((bf16[8,16,2048]{2,1,0:T(8,128)(2,1)}), bf16[8,16,2048]{2,1,0:T(8,128)(2,1)S(1)}, u32[]{:S(2)}, u32[]{:S(2)}) %all-to-all-start.8) | async-done | bytes 524320 | tf_op jit(solution)/shard_map/all_to_all | solution.py:25
  206.1 0.8 fusion.100
  (94 shorter events, 3.7 us)
Async XLA Ops:
  7.2 80.9 %copy-start = (bf16[1,80,2048]{2,1,0:T(8,128)(2,1)S(1)}, bf16[1,80,2048]{2,1,0:T(8,128)(2,1)}, u32[]{:S(2)}) copy-start(bf16[1,80,2048]{2,1,0:T(8,128)(2,1)} %param.15) | copy-start | bytes 983044
  7.2 41.2 %all-gather.2.cloned.1.call-start = ((), (), s32[]{:S(2)}) async-start(), calls=%async_computation.9 | async-start | bytes 1310720 | tf_op jit(solution)/shard_map/all_gather | solution.py:263
  7.2 13.3 %copy-start.7 = (bf16[64,2048]{1,0:T(8,128)(2,1)S(1)}, bf16[64,2048]{1,0:T(8,128)(2,1)}, u32[]{:S(2)}) copy-start(bf16[64,2048]{1,0:T(8,128)(2,1)} %keys_ref.1) | copy-start | bytes 786436
  10.0 9.9 %all-to-all-start = ((bf16[4,8,2176]{2,1,0:T(8,128)(2,1)}), bf16[4,8,2176]{2,1,0:T(8,128)(2,1)S(1)}, u32[]{:S(2)}, u32[]{:S(2)}) async-start(bf16[4,8,2176]{2,1,0:T(8,128)(2,1)} %get-tuple-element.21), calls=%async_computation | async-start | bytes 278528 | tf_op jit(solution)/shard_map/all_to_all | solution.py:25
  15.0 6.1 %copy-start.8 = (bf16[64,2048]{1,0:T(8,128)(2,1)S(1)}, bf16[64,2048]{1,0:T(8,128)(2,1)}, u32[]{:S(2)}) copy-start(bf16[64,2048]{1,0:T(8,128)(2,1)} %values_ref.1) | copy-start | bytes 786436
  21.1 0.9 copy-start.9
  23.2 8.5 %all-to-all-start.1 = ((f32[4,2,6272]{2,1,0:T(2,128)}), f32[4,2,6272]{2,1,0:T(2,128)S(1)}, u32[]{:S(2)}, u32[]{:S(2)}) async-start(f32[4,2,6272]{2,1,0:T(2,128)} %all_to_all.35), calls=%async_computation.1 | async-start | bytes 401408 | tf_op jit(solution)/shard_map/all_to_all | solution.py:25
  33.4 27.8 %all-to-all-start.2 = ((bf16[16,2,4224]{2,1,0:T(2,128)(2,1)}), bf16[16,2,4224]{2,1,0:T(2,128)(2,1)S(1)}, u32[]{:S(2)}, u32[]{:S(2)}) async-start(bf16[16,2,4224]{2,1,0:T(2,128)(2,1)} %pad_maximum_fusion.2), calls=%async_computation.2 | async-start | bytes 540672 | tf_op jit(solution)/shard_map/all_to_all | solution.py:25
  48.4 9.2 %copy-start.13 = (bf16[8,128]{1,0:T(8,128)(2,1)S(1)}, bf16[8,128]{1,0:T(8,128)(2,1)}, u32[]{:S(2)}) copy-start(bf16[8,128]{1,0:T(8,128)(2,1)} %get-tuple-element.20) | copy-start | bytes 6148
  49.7 11.7 %collective-permute-start.1 = (bf16[128,2048]{1,0:T(8,128)(2,1)S(1)}, bf16[128,2048]{1,0:T(8,128)(2,1)S(1)}, u32[]{:S(2)}, u32[]{:S(2)}) collective-permute-start(bf16[128,2048]{1,0:T(8,128)(2,1)S(1)} %get-tuple-element.37), channel_id=1, source_target_pairs={{0,1},{1,0},{2,3},{3,2},{4,5},{5,4},{6,7},{7,6},{8,9},{9,8},{10,11... | collective-permute-start | bytes 1572872 | tf_op jit(solution)/shard_map/ppermute | solution.py:95
  55.6 5.8 %collective-permute-start = (bf16[128,2048]{1,0:T(8,128)(2,1)S(1)}, bf16[128,2048]{1,0:T(8,128)(2,1)S(1)}, u32[]{:S(2)}, u32[]{:S(2)}) collective-permute-start(bf16[128,2048]{1,0:T(8,128)(2,1)S(1)} %get-tuple-element.38), channel_id=1, source_target_pairs={{0,1},{1,0},{2,3},{3,2},{4,5},{5,4},{6,7},{7,6},{8,9},{9,8},{10,11... | collective-permute-start | bytes 1572872 | tf_op jit(solution)/shard_map/ppermute | solution.py:95
  57.8 5.6 %copy-start.14 = (f32[128]{0:T(128)}, f32[128]{0:T(128)S(1)}, u32[]{:S(2)}) copy-start(f32[128]{0:T(128)S(1)} %get-tuple-element.45) | copy-start | bytes 1540
  61.3 2.1 copy-start.4
  61.4 2.0 copy-start.5
  63.4 22.6 %all-to-all-start.3 = ((bf16[4,32,4096]{2,1,0:T(8,128)(2,1)}), bf16[4,32,4096]{2,1,0:T(8,128)(2,1)S(1)}, u32[]{:S(2)}, u32[]{:S(2)}) async-start(bf16[4,32,4096]{2,1,0:T(8,128)(2,1)} %broadcast_in_dim.109), calls=%async_computation.3 | async-start | bytes 2097152 | tf_op jit(solution)/shard_map/all_to_all | solution.py:25
  67.4 21.0 %copy-start.12 = (bf16[1,80,2048]{2,1,0:T(8,128)(2,1)S(1)}, bf16[1,80,2048]{2,1,0:T(8,128)(2,1)}, u32[]{:S(2)}) copy-start(bf16[1,80,2048]{2,1,0:T(8,128)(2,1)} %param.16) | copy-start | bytes 983044
  76.4 12.3 %collective-permute-start.4 = (bf16[256,2048]{1,0:T(8,128)(2,1)}, bf16[256,2048]{1,0:T(8,128)(2,1)}, u32[]{:S(2)}, u32[]{:S(2)}) collective-permute-start(bf16[256,2048]{1,0:T(8,128)(2,1)} %get-tuple-element.26), channel_id=1, source_target_pairs={{0,1},{1,0},{2,3},{3,2},{4,5},{5,4},{6,7},{7,6},{8,9},{9,8},{10,11... | collective-permute-start | bytes 3145736 | tf_op jit(solution)/shard_map/ppermute | solution.py:95
  86.0 2.7 %copy-start.2 = (bf16[256,2048]{1,0:T(8,128)(2,1)S(1)}, bf16[256,2048]{1,0:T(8,128)(2,1)}, u32[]{:S(2)}) copy-start(bf16[256,2048]{1,0:T(8,128)(2,1)} %get-tuple-element.25) | copy-start | bytes 3145732
  86.0 9.3 %collective-permute-start.2 = (bf16[128,4096]{1,0:T(8,128)(2,1)S(1)}, bf16[128,4096]{1,0:T(8,128)(2,1)S(1)}, u32[]{:S(2)}, u32[]{:S(2)}) collective-permute-start(bf16[128,4096]{1,0:T(8,128)(2,1)S(1)} %bitcast.87), channel_id=1, source_target_pairs={{0,1},{1,0},{2,3},{3,2},{4,5},{5,4},{6,7},{7,6},{8,9},{9,8},{10,11... | collective-permute-start | bytes 3145736 | tf_op jit(solution)/shard_map/ppermute | solution.py:95
  90.5 9.3 %collective-permute-start.5 = (bf16[64,2048]{1,0:T(8,128)(2,1)S(1)}, bf16[64,2048]{1,0:T(8,128)(2,1)S(1)}, u32[]{:S(2)}, u32[]{:S(2)}) collective-permute-start(bf16[64,2048]{1,0:T(8,128)(2,1)S(1)} %get-tuple-element.34), channel_id=1, source_target_pairs={{0,128},{128,0},{256,384},{384,256},{1,129},{129,1},{257,385},{385... | collective-permute-start | bytes 786440 | tf_op jit(solution)/shard_map/ppermute | solution.py:330
  92.8 10.2 %collective-permute-start.6 = (bf16[64,2048]{1,0:T(8,128)(2,1)S(1)}, bf16[64,2048]{1,0:T(8,128)(2,1)S(1)}, u32[]{:S(2)}, u32[]{:S(2)}) collective-permute-start(bf16[64,2048]{1,0:T(8,128)(2,1)S(1)} %get-tuple-element.36), channel_id=1, source_target_pairs={{0,384},{128,256},{256,128},{384,0},{1,385},{129,257},{257,129},{3... | collective-permute-start | bytes 786440 | tf_op jit(solution)/shard_map/ppermute | solution.py:330
  96.3 6.8 %collective-permute-start.3 = (bf16[128,2048]{1,0:T(8,128)(2,1)S(1)}, bf16[128,2048]{1,0:T(8,128)(2,1)S(1)}, u32[]{:S(2)}, u32[]{:S(2)}) collective-permute-start(bf16[128,2048]{1,0:T(8,128)(2,1)S(1)} %fusion.27), channel_id=1, source_target_pairs={{0,1},{1,0},{2,3},{3,2},{4,5},{5,4},{6,7},{7,6},{8,9},{9,8},{10,11... | collective-permute-start | bytes 1572872 | tf_op jit(solution)/shard_map/ppermute | solution.py:95
  123.0 19.9 %all-to-all-start.5 = ((bf16[16,64,128]{2,1,0:T(8,128)(2,1)}), bf16[16,64,128]{2,1,0:T(8,128)(2,1)S(1)}, u32[]{:S(2)}, u32[]{:S(2)}) async-start(bf16[16,64,128]{2,1,0:T(8,128)(2,1)} %shard_map.138), calls=%async_computation.5 | async-start | bytes 524288 | tf_op jit(solution)/shard_map/all_to_all | solution.py:25
  142.9 0.7 copy-start.3
  145.8 9.9 %collective-permute-start.7 = (bf16[256,128]{1,0:T(8,128)(2,1)}, bf16[256,128]{1,0:T(8,128)(2,1)S(1)}, u32[]{:S(2)}, u32[]{:S(2)}) collective-permute-start(bf16[256,128]{1,0:T(8,128)(2,1)} %get-tuple-element.30), channel_id=1, source_target_pairs={{0,1},{1,0},{2,3},{3,2},{4,5},{5,4},{6,7},{7,6},{8,9},{9,8},{10,11... | collective-permute-start | bytes 196616 | tf_op jit(solution)/shard_map/ppermute | solution.py:95
  155.7 0.6 copy-start.10
  158.0 12.6 %copy-start.11 = (f32[32,128]{1,0:T(8,128)S(1)}, f32[32,128]{1,0:T(8,128)}, u32[]{:S(2)}) copy-start(f32[32,128]{1,0:T(8,128)} %get-tuple-element.31.more_ref) | copy-start | bytes 49156
  158.0 12.6 %all-to-all-start.6 = ((bf16[16,80,128]{2,1,0:T(8,128)(2,1)}), bf16[16,80,128]{2,1,0:T(8,128)(2,1)S(1)}, u32[]{:S(2)}, u32[]{:S(2)}) async-start(bf16[16,80,128]{2,1,0:T(8,128)(2,1)} %shard_map.140), calls=%async_computation.6 | async-start | bytes 655360 | tf_op jit(solution)/shard_map/all_to_all | solution.py:25
  171.5 17.1 %all-to-all-start.7 = ((bf16[16,32,128]{2,1,0:T(8,128)(2,1)}), bf16[16,32,128]{2,1,0:T(8,128)(2,1)S(1)}, u32[]{:S(2)}, u32[]{:S(2)}) async-start(bf16[16,32,128]{2,1,0:T(8,128)(2,1)} %copy.49), calls=%async_computation.7 | async-start | bytes 262144 | tf_op jit(solution)/shard_map/all_to_all | solution.py:25
  188.6 8.0 %copy-start.1 = (bf16[128,2048]{1,0:T(8,128)(2,1)S(1)}, bf16[128,2048]{1,0:T(8,128)(2,1)}, u32[]{:S(2)}) copy-start(bf16[128,2048]{1,0:T(8,128)(2,1)} %up_ref.3) | copy-start | bytes 1572868
  189.6 16.5 %all-to-all-start.8 = ((bf16[8,16,2048]{2,1,0:T(8,128)(2,1)}), bf16[8,16,2048]{2,1,0:T(8,128)(2,1)S(1)}, u32[]{:S(2)}, u32[]{:S(2)}) async-start(bf16[8,16,2048]{2,1,0:T(8,128)(2,1)} %broadcast_in_dim.113), calls=%async_computation.8 | async-start | bytes 1048576 | tf_op jit(solution)/shard_map/all_to_all | solution.py:25
  196.6 1.5 copy-start.6
Sparse Core Ops, SparseCore 0:
  10.7 36.3 all-gather.1
